TPU v7x, 32 devices: a whole 2x2x4 slice. The times are simulated.
32 devices in a mesh: groups: 1, dp: 32 (over z, y, x, core).
Axes of the slice: x: 2, y: 2, z: 4, core: 2. Of those that a mesh axis runs over, the one named last changes fastest.
Arguments:
- queries: bfloat16 [128, 128, 576], P(('groups', 'dp')), may hold values from -900 to 900
- latent_cache: bfloat16 [128, 512, 576], P(('groups', 'dp')), may hold values from -6 to 6
- lengths: int32 [128], P(('groups', 'dp')), may hold values from 2 to 512, as said below
- hidden_in: bfloat16 [128, 7168], P(('groups', 'dp')), may hold values from -0.75 to 0.75
- route_ids: int32 [128, 2], P(('groups', 'dp')), may hold values from 0 to 3, all different within a row; in each aligned block of 4 rows (0 to 3, 4 to 7, ...) at most 2 rows name the same one
- route_weights: float32 [128, 2], P(('groups', 'dp')), may hold values from 0.3 to 1.5
- value_up: bfloat16 [128, 512, 128], P('dp'), may hold values from -0.25 to 0.25
- out_proj: bfloat16 [16384, 7168], P('dp'), may hold values from -0.046875 to 0.046875
- norm_gain: bfloat16 [7168], replicated, may hold values from 0.099609375 to 1.8984375
- gate_up: bfloat16 [2, 7168, 4096], P(None, None, 'dp'), may hold values from -0.0625 to 0.0625
- down_proj: bfloat16 [4096, 7168], P('dp'), may hold values from -0.1875 to 0.1875
Outputs:
- hidden_out: bfloat16 [128, 7168], P(('groups', 'dp'))
Inputs may be any that keep to these rules, and one draw needn't show every extreme that they name: `route_ids`: within one device's 4 rows no expert is picked more than 2 times; the picks of a row are distinct. `lengths`: some row has exactly 512 live slots.
All inputs are finite; a program needn't handle non-finite values.
Results may differ from a plain program's by a relative error of at most 0.011.
Values may be sent and summed in bfloat16 or wider, within the bound.
No kernel may reach another device: no remote copies, remote signals or barrier semaphores. Data moves between devices by JAX's collectives and lax.ppermute only.
A program may use at most 128 MiB of HBM per device.

v0:
```python
import jax
import jax.numpy as jnp
from jax import lax
from jax.sharding import PartitionSpec as P

LAT = 512
ROPE = 64
VH = 128
SPLIT = 8


MASKED = -1e30
EPSILON = 1e-06


def latent_attention(queries, latent_cache, lengths):
    row_count, head_count, unused_width = queries.shape
    max_length = latent_cache.shape[1]
    block_size = min(128, max_length)
    scale_factor = (VH + ROPE) ** (-0.5)
    length_limit = lengths[:, None, None]
    block_count = (jnp.max(lengths) + block_size - 1) // block_size

    def score_block(block_index, scores):
        block_keys = lax.dynamic_slice_in_dim(latent_cache, block_index * block_size, block_size, 1)
        block_scores = (
            jnp.einsum("rhc,rpc->rhp", queries, block_keys, preferred_element_type=jnp.float32)
            * scale_factor
        )
        position_ids = block_index * block_size + lax.broadcasted_iota(
            jnp.int32, (1, 1, block_size), 2
        )
        block_scores = jnp.where(position_ids < length_limit, block_scores, MASKED)
        return lax.dynamic_update_slice_in_dim(scores, block_scores, block_index * block_size, 2)

    scores = lax.fori_loop(
        0,
        block_count,
        score_block,
        jnp.full((row_count, head_count, max_length), MASKED, jnp.float32),
    )
    row_max = jnp.max(scores, axis=2, keepdims=True)
    exp_terms = jnp.exp(scores - row_max)
    exp_total = jnp.sum(exp_terms, axis=2, keepdims=True)
    prob_bf = exp_terms.astype(jnp.bfloat16)

    def value_block(block_index, numerator):
        block_probs = lax.dynamic_slice_in_dim(prob_bf, block_index * block_size, block_size, 2)
        block_values = lax.dynamic_slice(
            latent_cache, (0, block_index * block_size, 0), (row_count, block_size, LAT)
        )
        return numerator + jnp.einsum(
            "rhp,rpc->rhc", block_probs, block_values, preferred_element_type=jnp.float32
        )

    numerator = lax.fori_loop(
        0, block_count, value_block, jnp.zeros((row_count, head_count, LAT), jnp.float32)
    )
    return (numerator / exp_total).astype(jnp.bfloat16)


def expert_partial(inputs, gate_up, down_proj):
    gate_part = jnp.dot(inputs, gate_up[0], preferred_element_type=jnp.float32)
    up_part = jnp.dot(inputs, gate_up[1], preferred_element_type=jnp.float32)
    activated = (jax.nn.silu(gate_part) * up_part).astype(jnp.bfloat16)
    return jnp.dot(activated, down_proj, preferred_element_type=jnp.float32)


def body(
    queries,
    latent_cache,
    lengths,
    hidden_in,
    route_ids,
    route_weights,
    value_up,
    out_proj,
    norm_gain,
    gate_up,
    down_proj,
):
    row_count = hidden_in.shape[0]
    latent_out = latent_attention(queries, latent_cache, lengths)
    by_heads = lax.all_to_all(latent_out, "dp", split_axis=1, concat_axis=0, tiled=True)
    head_values = jnp.einsum(
        "rhc,hcv->rhv", by_heads, value_up, preferred_element_type=jnp.float32
    ).astype(jnp.bfloat16)
    flat_values = head_values.reshape(head_values.shape[0], -1)
    attention = lax.psum_scatter(
        jnp.dot(flat_values, out_proj, preferred_element_type=jnp.float32),
        "dp",
        scatter_dimension=0,
        tiled=True,
    )
    residual = (hidden_in.astype(jnp.float32) + attention).astype(jnp.bfloat16)
    resid_wide = residual.astype(jnp.float32)
    mean_square = jnp.mean(resid_wide * resid_wide, axis=1, keepdims=True)
    normed = (resid_wide * lax.rsqrt(mean_square + EPSILON) * norm_gain.astype(jnp.float32)).astype(
        jnp.bfloat16
    )
    devices = lax.axis_size("dp")
    experts = devices // SPLIT
    pick_count = route_ids.shape[1]
    capacity = max(2, (row_count * pick_count + experts - 1) // experts)
    flat_ids = route_ids.reshape(-1)
    pick_order = jnp.arange(flat_ids.shape[0])
    earlier = (pick_order[None, :] < pick_order[:, None]) & (flat_ids[None, :] == flat_ids[:, None])
    slot_index = jnp.sum(earlier.astype(jnp.int32), axis=1)
    slot_place = flat_ids * capacity + slot_index
    slot_hits = (
        slot_place[:, None] == jnp.arange(experts * capacity, dtype=jnp.int32)[None, :]
    ).reshape(row_count, pick_count, experts * capacity)
    send_table = jnp.sum(slot_hits.astype(jnp.float32), axis=1).astype(jnp.bfloat16)
    combine_table = jnp.sum(slot_hits.astype(jnp.float32) * route_weights[:, :, None], axis=1)
    packed = jnp.dot(send_table.T, normed, preferred_element_type=jnp.float32).astype(jnp.bfloat16)
    feature_count = packed.shape[1]
    outgoing = jnp.broadcast_to(
        packed.reshape(experts, 1, capacity, feature_count),
        (experts, SPLIT, capacity, feature_count),
    ).reshape(devices, capacity, feature_count)
    received = lax.all_to_all(outgoing, "dp", split_axis=0, concat_axis=0, tiled=True)
    source_count, slot_count, width_count = received.shape
    partial_value = expert_partial(
        received.reshape(source_count * slot_count, width_count), gate_up, down_proj
    )
    returned = lax.all_to_all(
        partial_value.reshape(source_count, slot_count, width_count).astype(jnp.bfloat16),
        "dp",
        split_axis=0,
        concat_axis=0,
        tiled=True,
    ).astype(jnp.float32)
    per_expert = jnp.sum(returned.reshape(experts, SPLIT, capacity, feature_count), axis=1).reshape(
        experts * capacity, feature_count
    )
    mixture = jnp.dot(
        combine_table,
        per_expert,
        precision=lax.Precision.HIGHEST,
        preferred_element_type=jnp.float32,
    )
    return (resid_wide + mixture).astype(jnp.bfloat16)


def solution(mesh):
    placed = (
        P(("groups", "dp"), None, None),
        P(("groups", "dp"), None, None),
        P(("groups", "dp")),
        P(("groups", "dp"), None),
        P(("groups", "dp"), None),
        P(("groups", "dp"), None),
        P("dp", None, None),
        P("dp", None),
        P(),
        P(None, None, "dp"),
        P("dp", None),
    )
    return jax.shard_map(
        body, mesh=mesh, in_specs=placed, out_specs=P(("groups", "dp"), None), check_vma=False
    )
```

profile of v0, /device:TPU:0, one launch (start us, length us, event | category | flops | bytes accessed | tf_op | source)
XLA Modules:
  0.0 268.4 jit_solution(13673915227770266543)
XLA Ops:
  6.5 1.4 reduce_max.18
  8.7 7.3 %while.20 = (s32[]{:T(128)}, f32[4,128,512]{1,2,0:T(8,128)S(1)}, s32[]{:T(128)}, s32[4,1,1]{0,2,1:T(1,128)}, bf16[4,512,576]{1,2,0:T(8,128)(2,1)}, /*index=5*/bf...) while((s32[]{:T(128)}, f32[4,128,512]{1,2,0:T(8,128)S(1)}, s32[]{:T(128)}, ...), condition=%wide.region_2.3_spmd, body=%wide.region_1.2_spmd.sunk | while | flops 75629192 | bytes 1445031 | solution.py:36
  9.5 1.7 fusion.62
  11.9 1.7 fusion.62
  14.4 1.7 fusion.62
  16.1 1.3 copy.43
  17.5 1.5 fusion.24
  19.1 4.3 %while.21 = (s32[]{:T(128)}, f32[4,128,512]{2,1,0:T(8,128)S(1)}, s32[]{:T(128)}, bf16[4,128,512]{2,1,0:T(8,128)(2,1)S(1)}, bf16[4,512,576]{1,2,0:T(8,128)(2,1)},...) while((s32[]{:T(128)}, f32[4,128,512]{2,1,0:T(8,128)S(1)}, s32[]{:T(128)}, ...), condition=%wide.region_5.6_spmd, body=%wide.region_4.5_spmd.sunk | while | flops 67371016 | bytes 2753675 | solution.py:56
  19.2 1.4 convolution_add_fusion.3
  20.6 1.4 convolution_add_fusion.3
  22.0 1.4 convolution_add_fusion.3
  23.6 0.7 fusion.23
  24.3 25.6 %all_to_all.28 = bf16[4,128,512]{2,0,1:T(4,128)(2,1)S(1)} all-to-all(bf16[4,128,512]{2,0,1:T(4,128)(2,1)S(1)} %fusion.23), channel_id=1, replica_groups=mesh['groups'=1,'dp'=32] {'dp'}, dimensions={1} | all-to-all | bytes 1048576 | tf_op jit(solution)/shard_map/all_to_all | solution.py:84
  50.6 6.1 %fusion.43 = f32[128,7168]{1,0:T(8,128)} fusion(bf16[128,512]{0,1:T(8,128)(2,1)S(1)} %bitcast.51, bf16[512,7168]{1,0:T(8,128)(2,1)} %param.22), kind=kOutput, calls=%fused_computation.57 | convolution fusion | flops 939524096 | bytes 11141120 | tf_op jit(solution)/shard_map/dot_general | solution.py:90
  58.0 136.7 %all-reduce.3.cloned.1.call-done = f32[128,7168]{1,0:T(8,128)} async-done(((f32[128,7168]{1,0:T(8,128)}), f32[128,7168]{1,0:T(8,128)}) %all-reduce.3.cloned.1.call-update) | async-done | bytes 3670032
  194.7 1.1 fusion.26
  196.6 26.9 %all_to_all.29 = bf16[32,2,7168]{2,1,0:T(2,128)(2,1)S(1)} all-to-all(bf16[32,2,7168]{2,1,0:T(2,128)(2,1)S(1)} %bitcast.48), channel_id=1, replica_groups=mesh['groups'=1,'dp'=32] {'dp'}, dimensions={0} | all-to-all | bytes 1835008 | tf_op jit(solution)/shard_map/all_to_all | solution.py:121
  223.6 1.3 reshape.92
  224.8 2.3 fusion.11
  227.2 3.3 %convolution_convert_fusion = bf16[64,7168]{1,0:T(8,128)(2,1)} fusion(bf16[128,7168]{1,0:T(8,128)(2,1)S(1)} %copy-done, bf16[64,7168]{1,0:T(8,128)(2,1)S(1)} %copy-done.1, bf16[2,7168,128]{2,1,0:T(8,128)(2,1)} %param.24, f32[64,128]{1,0:T(8,128)S(1)} %fusion.11), kind=kOutput, calls=%fused_computation.12 | convolution fusion | flops 235388928 | bytes 5537792 | tf_op jit(solution)/shard_map/dot_general | solution.py:66
  230.4 2.3 convert_element_type.68
  232.8 26.9 %all_to_all.30 = bf16[32,2,7168]{2,1,0:T(2,128)(2,1)S(1)} all-to-all(bf16[32,2,7168]{2,1,0:T(2,128)(2,1)S(1)} %convert_element_type.68), channel_id=1, replica_groups=mesh['groups'=1,'dp'=32] {'dp'}, dimensions={0} | all-to-all | bytes 1835008 | tf_op jit(solution)/shard_map/all_to_all | solution.py:126
  259.6 0.8 convert_reduce_fusion
  260.6 1.0 fusion.8
  (42 shorter events, 5.5 us)
Async XLA Ops:
  6.5 220.6 %copy-start = (bf16[128,7168]{1,0:T(8,128)(2,1)S(1)}, bf16[128,7168]{1,0:T(8,128)(2,1)}, u32[]{:S(2)}) copy-start(bf16[128,7168]{1,0:T(8,128)(2,1)} %param.25) | copy-start | bytes 5505028
  6.5 188.2 %all-reduce.3.cloned.1.call-start = ((), (), s32[]{:S(2)}) async-start(), calls=%async_computation.3 | async-start | bytes 7340032
  23.6 26.7 %copy-start.2 = (bf16[4,512,128]{2,1,0:T(8,128)(2,1)S(1)}, bf16[4,512,128]{2,1,0:T(8,128)(2,1)}, u32[]{:S(2)}) copy-start(bf16[4,512,128]{2,1,0:T(8,128)(2,1)} %param.21) | copy-start | bytes 1572868
  56.7 0.7 copy-start.5
  56.7 1.2 copy-start.4
  56.7 1.2 copy-start.6
  56.7 138.0 %copy-start.3 = (bf16[4,7168]{1,0:T(4,128)(2,1)S(1)}, bf16[4,7168]{1,0:T(4,128)(2,1)}, u32[]{:S(2)}) copy-start(bf16[4,7168]{1,0:T(4,128)(2,1)} %param.18) | copy-start | bytes 172036
  224.8 2.3 copy-start.1
Sparse Core Ops, SparseCore 0:
  56.9 137.8 all-reduce.2
where the time goes:
time: 268 us
  waiting for transfers between devices  137 us (51%)
  blocking collectives  79.4 us (30%)
  matrix products  22.5 us (8%)
  between operations  14.2 us (5%)
  other arithmetic  8.22 us (3%)
  local copies, waits for them, and re-layouts  7.25 us (3%)
    unnamed x2, waiting for transfers between devices  137 us
    all_to_all x1, blocking collectives, body(): lax.all_to_all(outgoing, 'dp', split_axis=0, concat_axis=0, tiled=True)  26.9 us
    all_to_all x1, blocking collectives, body(): lax.all_to_all(partial_value.reshape(source_count, slot_count, width_coun...  26.9 us
    all_to_all x1, blocking collectives, body(): lax.all_to_all(latent_out, 'dp', split_axis=1, concat_axis=0, tiled=True)  25.6 us
    dot_general x1, matrix products, body(): jnp.dot(flat_values, out_proj, preferred_element_type=jnp.float32)  6.1 us
  transfers between devices with their start and end apart: 1, of which 1 were waited for; matrix products, arithmetic and copies ran while one was open for 0% of the time, Pallas kernels for 0%

commit v1 on v0

v1 whole, which is shorter than its diff:
```python
import functools

import jax
import jax.numpy as jnp
from jax import lax
from jax.experimental import pallas as pl
from jax.experimental.pallas import tpu as pltpu
from jax.sharding import PartitionSpec as P

LAT = 512
ROPE = 64
VH = 128
SPLIT = 8

MASKED = -1e30
EPSILON = 1e-06
VMEM = 24 * 1024 * 1024

F32 = jnp.float32
BF16 = jnp.bfloat16
SCALARS = pl.BlockSpec(memory_space=pltpu.SMEM)


def sds(shape, dtype):
    return jax.ShapeDtypeStruct(shape, dtype)


def params():
    return pltpu.CompilerParams(vmem_limit_bytes=VMEM)


def whole(shape):
    return pl.BlockSpec(shape, lambda *_: (0,) * len(shape))


def attention_kernel(rows, lengths, q_ref, k_ref, o_ref, lat):
    row = pl.program_id(0)
    heads = q_ref.shape[2]
    slots = k_ref.shape[2]
    keys = k_ref[0]
    scores = lax.dot_general(
        q_ref[0], keys, (((0,), (0,)), ((), ())), preferred_element_type=F32
    ) * ((VH + ROPE) ** -0.5)
    position = lax.broadcasted_iota(jnp.int32, scores.shape, 1)
    scores = jnp.where(position < lengths[row], scores, MASKED)
    terms = jnp.exp(scores - jnp.max(scores, axis=1, keepdims=True))
    total = jnp.sum(terms, axis=1, keepdims=True)
    numerator = lax.dot_general(
        terms.astype(BF16), keys[:LAT], (((1,), (1,)), ((), ())), preferred_element_type=F32
    )
    lat[pl.ds(pl.multiple_of(row * heads, heads), heads), :] = (numerator / total).astype(BF16)

    @pl.when(row == rows - 1)
    def _():
        size = rows * heads
        i = lax.broadcasted_iota(jnp.int32, (size, size), 0)
        k = lax.broadcasted_iota(jnp.int32, (size, size), 1)
        pick = jnp.where(k == (i % rows) * heads + i // rows, 1.0, 0.0).astype(BF16)
        o_ref[...] = jnp.dot(pick, lat[...], preferred_element_type=F32).astype(BF16)


def attention(queries, latent_cache, lengths):
    rows, heads, width = queries.shape
    slots = latent_cache.shape[1]
    q_t = jnp.swapaxes(queries, 1, 2)
    k_t = jnp.swapaxes(latent_cache, 1, 2)
    return pl.pallas_call(
        functools.partial(attention_kernel, rows),
        grid=(rows,),
        in_specs=[
            SCALARS,
            pl.BlockSpec((1, width, heads), lambda r: (r, 0, 0)),
            pl.BlockSpec((1, width, slots), lambda r: (r, 0, 0)),
        ],
        out_specs=whole((rows * heads, LAT)),
        out_shape=sds((rows * heads, LAT), BF16),
        scratch_shapes=[pltpu.VMEM((rows * heads, LAT), BF16)],
        compiler_params=params(),
        name="latent_attention",
    )(lengths, q_t, k_t)


def project_kernel(planes, rows, me, x_ref, v_ref, w_ref, own_ref, other_ref, flat):
    heads = v_ref.shape[0]

    @pl.when(pl.program_id(0) == 0)
    def _():
        count = flat.shape[0]
        i = lax.broadcasted_iota(jnp.int32, (count, x_ref.shape[0]), 0)
        k = lax.broadcasted_iota(jnp.int32, (count, x_ref.shape[0]), 1)
        row = i % rows
        plane = (i // rows) % planes
        rest = i // (rows * planes)
        home = me[0] ^ (plane * 8 + (rest % 4) * 2 + rest // 4)
        target = home * (heads * rows) + row
        for h in range(heads):
            pick = jnp.where(k == target + h * rows, 1.0, 0.0).astype(BF16)
            mine = jnp.dot(pick, x_ref[...], preferred_element_type=F32).astype(BF16)
            flat[:, h * VH : (h + 1) * VH] = jnp.dot(
                mine, v_ref[h], preferred_element_type=F32
            ).astype(BF16)

    out = jnp.dot(flat[...], w_ref[...], preferred_element_type=F32)
    half = out.shape[0] // 2
    own_ref[...] = out[:half]
    other_ref[...] = out[half:].astype(BF16)


def project(me, by_heads, value_up, out_proj, planes, rows):
    count = planes * 8 * rows
    depth, features = out_proj.shape
    tile = features // 4
    half = count // 2
    return pl.pallas_call(
        functools.partial(project_kernel, planes, rows),
        grid=(features // tile,),
        in_specs=[
            SCALARS,
            whole(by_heads.shape),
            whole(value_up.shape),
            pl.BlockSpec((depth, tile), lambda t: (0, t)),
        ],
        out_specs=[
            pl.BlockSpec((half, tile), lambda t: (0, t)),
            pl.BlockSpec((half, tile), lambda t: (0, t)),
        ],
        out_shape=[sds((half, features), F32), sds((half, features), BF16)],
        scratch_shapes=[pltpu.VMEM((count, depth), BF16)],
        compiler_params=params(),
        name="projections",
    )(me, by_heads, value_up, out_proj)


def add_kernel(arrived, parts, *refs):
    total = refs[0][...]
    for ref in refs[1 : 1 + arrived]:
        total = total + ref[...].astype(F32)
    outs = refs[1 + arrived :]
    size = total.shape[0] // parts
    outs[0][...] = total[:size]
    for p in range(1, parts):
        outs[p][...] = total[p * size : (p + 1) * size].astype(BF16)


def add_and_cut(own, received, parts, name, steps=2):
    count, features = own.shape
    size = count // parts
    tile = features // steps
    return pl.pallas_call(
        functools.partial(add_kernel, len(received), parts),
        grid=(steps,),
        in_specs=[pl.BlockSpec((count, tile), lambda t: (0, t))] * (1 + len(received)),
        out_specs=[pl.BlockSpec((size, tile), lambda t: (0, t))] * parts,
        out_shape=[sds((size, features), F32)] + [sds((size, features), BF16)] * (parts - 1),
        compiler_params=params(),
        name=name,
    )(own, *received)


def norm_kernel(planes, cap, me, ids, own_ref, *refs):
    received = refs[: planes - 1]
    hidden_ref, gain_ref = refs[planes - 1 : planes + 1]
    resid_ref = refs[planes + 1]
    packs = refs[planes + 2 : 2 * planes + 2]
    normed, packed = refs[2 * planes + 2 :]
    total = own_ref[...]
    for ref in received:
        total = total + ref[...].astype(F32)
    resid = (hidden_ref[...].astype(F32) + total).astype(BF16)
    resid_ref[...] = resid
    wide = resid.astype(F32)
    scale = lax.rsqrt(jnp.mean(wide * wide, axis=1, keepdims=True) + EPSILON)
    normed[...] = (wide * scale * gain_ref[...].astype(F32)).astype(BF16).astype(F32)
    rows, picks = ids.shape
    plane = me[0] // 8
    for k in range(planes):
        expert = plane ^ k
        places = [jnp.int32(0)] * cap
        seen = jnp.int32(0)
        for r in range(rows):
            has = ids[r, 0] == expert
            for t in range(1, picks):
                has = has | (ids[r, t] == expert)
            for s in range(cap):
                places[s] = jnp.where(has & (seen == s), r, places[s])
            seen = seen + has.astype(jnp.int32)
        for s in range(cap):
            packed[k * cap + s : k * cap + s + 1, :] = normed[pl.ds(places[s], 1), :]
        packs[k][...] = packed[k * cap : (k + 1) * cap, :].astype(BF16)


def norm_and_pack(me, ids, own, received, hidden, gain, planes, cap):
    rows, features = own.shape
    vec = pl.BlockSpec(memory_space=pltpu.VMEM)
    return pl.pallas_call(
        functools.partial(norm_kernel, planes, cap),
        in_specs=[SCALARS, SCALARS] + [vec] * (2 + planes),
        out_specs=[vec] * (1 + planes),
        out_shape=[sds((rows, features), BF16)] + [sds((cap, features), BF16)] * planes,
        scratch_shapes=[
            pltpu.VMEM((rows, features), F32),
            pltpu.VMEM((planes * cap, features), F32),
        ],
        compiler_params=params(),
        name="norm_and_pack",
    )(me, ids, own, *received, hidden, gain)


def stack_kernel(*refs):
    wide = refs[-1]
    out = refs[-2]
    size = refs[0].shape[0]
    for k, ref in enumerate(refs[:-2]):
        wide[k * size : (k + 1) * size, :] = ref[...].astype(F32)
    out[...] = wide[...].astype(BF16)


def stack(pieces):
    size, features = pieces[0].shape
    vec = pl.BlockSpec(memory_space=pltpu.VMEM)
    shape = (size * len(pieces), features)
    return pl.pallas_call(
        stack_kernel,
        in_specs=[vec] * len(pieces),
        out_specs=vec,
        out_shape=sds(shape, BF16),
        scratch_shapes=[pltpu.VMEM(shape, F32)],
        compiler_params=params(),
        name="stack_rows",
    )(*pieces)


def expert_kernel(pieces, steps, *refs):
    xs = refs[:pieces]
    gu_ref, down_ref, own_ref, other_ref, gate, up, act = refs[pieces:]
    step = pl.program_id(0)

    @pl.when(step == 0)
    def _():
        gate[...] = jnp.zeros_like(gate)
        up[...] = jnp.zeros_like(up)

    @pl.when(step < steps)
    def _():
        x = jnp.concatenate([ref[...].astype(F32) for ref in xs], axis=0).astype(BF16)
        gate[...] += jnp.dot(x, gu_ref[0], preferred_element_type=F32)
        up[...] += jnp.dot(x, gu_ref[1], preferred_element_type=F32)

    @pl.when(step == steps - 1)
    def _():
        g = gate[...]
        act[...] = (g / (1.0 + jnp.exp(-g)) * up[...]).astype(BF16)

    @pl.when(step >= steps)
    def _():
        out = jnp.dot(act[...], down_ref[...], preferred_element_type=F32)
        half = out.shape[0] // 2
        own_ref[...] = out[:half]
        other_ref[...] = out[half:].astype(BF16)


def expert(pieces, gate_up, down_proj, steps=4):
    size, features = pieces[0].shape
    count = size * len(pieces)
    hidden = gate_up.shape[2]
    tile = features // steps
    half = count // 2
    return pl.pallas_call(
        functools.partial(expert_kernel, len(pieces), steps),
        grid=(2 * steps,),
        in_specs=[pl.BlockSpec((size, tile), lambda t: (0, jnp.minimum(t, steps - 1)))]
        * len(pieces)
        + [
            pl.BlockSpec((2, tile, hidden), lambda t: (0, jnp.minimum(t, steps - 1), 0)),
            pl.BlockSpec((hidden, tile), lambda t: (0, jnp.maximum(t - steps, 0))),
        ],
        out_specs=[pl.BlockSpec((half, tile), lambda t: (0, jnp.maximum(t - steps, 0)))] * 2,
        out_shape=[sds((half, features), F32), sds((half, features), BF16)],
        scratch_shapes=[
            pltpu.VMEM((count, hidden), F32),
            pltpu.VMEM((count, hidden), F32),
            pltpu.VMEM((count, hidden), BF16),
        ],
        compiler_params=params(),
        name="expert",
    )(*pieces, gate_up, down_proj)


def combine_kernel(planes, cap, me, ids, weights, own_ref, *refs):
    received = refs[: planes - 1]
    resid_ref, out_ref, table, mixed = refs[planes - 1 :]
    table[:cap, :] = own_ref[...]
    for k, ref in enumerate(received):
        table[(k + 1) * cap : (k + 2) * cap, :] = ref[...].astype(F32)
    rows, picks = ids.shape
    plane = me[0] // 8
    for r in range(rows):
        total = None
        for t in range(picks):
            expert_id = ids[r, t]
            seen = jnp.int32(0)
            for b in range(r):
                for u in range(picks):
                    seen = seen + (ids[b, u] == expert_id).astype(jnp.int32)
            place = (expert_id ^ plane) * cap + seen
            term = weights[r, t] * table[pl.ds(place, 1), :]
            total = term if total is None else total + term
        mixed[r : r + 1, :] = total
    out_ref[...] = (resid_ref[...].astype(F32) + mixed[...]).astype(BF16)


def combine(me, ids, weights, own, received, resid, planes, cap):
    rows, features = resid.shape
    vec = pl.BlockSpec(memory_space=pltpu.VMEM)
    return pl.pallas_call(
        functools.partial(combine_kernel, planes, cap),
        in_specs=[SCALARS] * 3 + [vec] * (1 + planes),
        out_specs=vec,
        out_shape=sds((rows, features), BF16),
        scratch_shapes=[
            pltpu.VMEM((planes * cap, features), F32),
            pltpu.VMEM((rows, features), F32),
        ],
        compiler_params=params(),
        name="combine",
    )(me, ids, weights, own, *received, resid)


def body(
    queries,
    latent_cache,
    lengths,
    hidden_in,
    route_ids,
    route_weights,
    value_up,
    out_proj,
    norm_gain,
    gate_up,
    down_proj,
):
    devices = lax.axis_size("dp")
    planes = devices // SPLIT
    rows = hidden_in.shape[0]
    picks = route_ids.shape[1]
    cap = max(2, (rows * picks + planes - 1) // planes)
    me = lax.axis_index("dp").astype(jnp.int32).reshape(1)

    def swap(x, mask):
        return lax.ppermute(x, "dp", [(i, i ^ mask) for i in range(devices)])

    def over_chips(messages):
        return [swap(x, k << 1) for k, x in enumerate(messages, 1)]

    def over_planes(messages):
        return [swap(x, k << 3) for k, x in enumerate(messages, 1)]

    latents = attention(queries, latent_cache, lengths)
    by_heads = lax.all_to_all(latents, "dp", split_axis=0, concat_axis=0, tiled=True)
    own, other = project(me, by_heads, value_up, out_proj, planes, rows)
    own, *out = add_and_cut(own, [swap(other, 1)], 4, "add_core")
    own, *out = add_and_cut(own, over_chips(out), planes, "add_chips", 1)
    resid, mine, *out = norm_and_pack(
        me, route_ids, own, over_planes(out), hidden_in, norm_gain[None], planes, cap
    )
    picked = stack([mine] + over_planes(out))
    chips = [picked] + over_chips([picked] * 3)
    pieces = chips + [swap(x, 1) for x in chips]
    own, other = expert(pieces, gate_up, down_proj)
    own, *out = add_and_cut(own, [swap(other, 1)], 4, "add_expert_core")
    own, *out = add_and_cut(own, over_chips(out), planes, "add_expert_chips", 1)
    return combine(me, route_ids, route_weights, own, over_planes(out), resid, planes, cap)


def solution(mesh):
    placed = (
        P(("groups", "dp"), None, None),
        P(("groups", "dp"), None, None),
        P(("groups", "dp")),
        P(("groups", "dp"), None),
        P(("groups", "dp"), None),
        P(("groups", "dp"), None),
        P("dp", None, None),
        P("dp", None),
        P(),
        P(None, None, "dp"),
        P("dp", None),
    )
    return jax.shard_map(
        body, mesh=mesh, in_specs=placed, out_specs=P(("groups", "dp"), None), check_vma=False
    )
```

time: 268 us -> 106 us (0.40)
  waiting for transfers between devices: 137 us -> 51.2 us
  blocking collectives: 79.4 us -> 0 us
  starting transfers between devices: 0.01 us -> 31.6 us
  matrix products: 22.5 us -> 0 us
  between operations: 14.2 us -> 0.17 us
  Pallas kernels: 0 us -> 13.7 us
  other arithmetic: 8.22 us -> 0 us
    unnamed x2 -> x0, waiting for transfers between devices: 137 us -> none
    all_to_all x3 -> x0, blocking collectives: 79.4 us -> none  [the longest x1 26.9 us: body(): lax.all_to_all(outgoing, 'dp', split_axis=0, concat_axis=0, tiled=True)]
    ppermute x0 -> x24, waiting for transfers between devices: none -> 35.7 us  [swap(): return lax.ppermute(x, 'dp', [(i, i ^ mask) for i in range(devices)])]
    ppermute x0 -> x24, starting transfers between devices: none -> 24.3 us  [swap(): return lax.ppermute(x, 'dp', [(i, i ^ mask) for i in range(devices)])]
    dot_general x12 -> x0, matrix products: 22.5 us -> none  [the longest x1 6.1 us: body(): jnp.dot(flat_values, out_proj, preferred_element_type=jnp.float32)]
    all_to_all x0 -> x1, waiting for transfers between devices: none -> 15.5 us  [body(): lax.all_to_all(latents, 'dp', split_axis=0, concat_axis=0, tiled=True)]
    pallas_call x0 -> x10, Pallas kernels: none -> 13.7 us  [the longest x1 4.21 us: attention(): pl.pallas_call(functools.partial(attention_kernel, rows), grid=(rows,), i...]
    unnamed x15 -> x24, local copies, waits for them, and re-layouts: 0.75 us -> 8.72 us
  transfers between devices with their start and end apart: 1 -> 25, of which waited for: 1 -> 17; matrix products, arithmetic and copies ran while one was open for 0% -> 0% of each run, Pallas kernels for 0% -> 0%
where the time goes in v1:
time: 106 us; the launch traced here: 105 us
  waiting for transfers between devices  51.2 us (48%)
  starting transfers between devices  31.6 us (30%)
  Pallas kernels  13.7 us (13%)
  local copies, waits for them, and re-layouts  8.74 us (8%)
    ppermute x24, waiting for transfers between devices, swap(): return lax.ppermute(x, 'dp', [(i, i ^ mask) for i in range(devices)])  35.7 us
    ppermute x24, starting transfers between devices, swap(): return lax.ppermute(x, 'dp', [(i, i ^ mask) for i in range(devices)])  24.3 us
    all_to_all x1, waiting for transfers between devices, body(): lax.all_to_all(latents, 'dp', split_axis=0, concat_axis=0, tiled=True)  15.5 us
    unnamed x24, local copies, waits for them, and re-layouts  8.72 us
    all_to_all x1, starting transfers between devices, body(): lax.all_to_all(latents, 'dp', split_axis=0, concat_axis=0, tiled=True)  7.3 us
    pallas_call x1, Pallas kernels, attention(): pl.pallas_call(functools.partial(attention_kernel, rows), grid=(rows,), i...  4.21 us
    pallas_call x1, Pallas kernels, project(): pl.pallas_call(functools.partial(project_kernel, planes, rows), grid=(fea...  3.34 us
    pallas_call x1, Pallas kernels, expert(): pl.pallas_call(functools.partial(expert_kernel, len(pieces), steps), grid...  2.91 us
  transfers between devices with their start and end apart: 25, of which 17 were waited for; matrix products, arithmetic and copies ran while one was open for 0% of the time, Pallas kernels for 0%

profile of v1, /device:TPU:0, one launch (start us, length us, event | category | flops | bytes accessed | tf_op | source)
XLA Modules:
  0.0 105.5 jit_solution(12925210785925732586)
XLA Ops:
  0.0 1.7 %copy-done.2 = bf16[4,512,576]{1,2,0:T(8,128)(2,1)S(1)} copy-done((bf16[4,512,576]{1,2,0:T(8,128)(2,1)S(1)}, bf16[4,512,576]{1,2,0:T(8,128)(2,1)}, u32[]{:S(2)}) %copy-start.2) | copy-done | bytes 2359320
  3.4 4.2 %latent_attention.1 = bf16[512,512]{1,0:T(8,128)(2,1)} custom-call(s32[4]{0:T(128)S(1)} %copy-done.7, bf16[4,576,128]{2,1,0:T(8,128)(2,1)S(1)} %bitcast.7, bf16[4,576,512]{2,1,0:T(8,128)(2,1)S(1)} %bitcast.5), custom_call_target="tpu_custom_call" | custom-call | tf_op jit(solution)/shard_map/latent_attention/pallas_call | solution.py:67
  7.6 7.3 %all-to-all-start = ((bf16[32,16,512]{2,1,0:T(8,128)(2,1)}), bf16[32,16,512]{2,1,0:T(8,128)(2,1)S(1)}, u32[]{:S(2)}, u32[]{:S(2)}) async-start(bf16[32,16,512]{2,1,0:T(8,128)(2,1)} %bitcast.3), calls=%async_computation | async-start | bytes 1048576 | tf_op jit(solution)/shard_map/all_to_all | solution.py:359
  14.9 15.5 %all-to-all-done = bf16[32,16,512]{2,1,0:T(8,128)(2,1)S(1)} async-done(((bf16[32,16,512]{2,1,0:T(8,128)(2,1)}), bf16[32,16,512]{2,1,0:T(8,128)(2,1)S(1)}, u32[]{:S(2)}, u32[]{:S(2)}) %all-to-all-start) | async-done | bytes 524320 | tf_op jit(solution)/shard_map/all_to_all | solution.py:359
  30.5 3.1 %copy-done = bf16[512,7168]{1,0:T(8,128)(2,1)S(1)} copy-done((bf16[512,7168]{1,0:T(8,128)(2,1)S(1)}, bf16[512,7168]{1,0:T(8,128)(2,1)}, u32[]{:S(2)}) %copy-start) | copy-done | bytes 7340056
  33.5 3.3 %projections.1 = (f32[64,7168]{1,0:T(8,128)S(1)}, bf16[64,7168]{1,0:T(8,128)(2,1)S(1)}) custom-call(s32[1]{0:T(128)} %bitcast.me, bf16[512,512]{1,0:T(8,128)(2,1)S(1)} %bitcast.6, bf16[4,512,128]{2,1,0:T(8,128)(2,1)S(1)} %copy-done.5, bf16[512,7168]{1,0:T(8,128)(2,1)S(1)} %copy-done), custom_call_target="tpu_custom_call" | custom-call | tf_op jit(solution)/shard_map/projections/pallas_call | solution.py:114
  37.0 2.5 %collective-permute-done.refs_1_ = bf16[64,7168]{1,0:T(8,128)(2,1)S(1)} collective-permute-done((bf16[64,7168]{1,0:T(8,128)(2,1)S(1)}, bf16[64,7168]{1,0:T(8,128)(2,1)S(1)}, u32[]{:S(2)}, u32[]{:S(2)}) %collective-permute-start) | collective-permute-done | bytes 917536 | tf_op jit(solution)/shard_map/ppermute | solution.py:350
  41.0 1.5 %collective-permute-start.2 = (bf16[16,7168]{1,0:T(8,128)(2,1)S(1)}, bf16[16,7168]{1,0:T(8,128)(2,1)S(1)}, u32[]{:S(2)}, u32[]{:S(2)}) collective-permute-start(bf16[16,7168]{1,0:T(8,128)(2,1)S(1)} %get-tuple-element.34), channel_id=1, source_target_pairs={{0,4},{1,5},{2,6},{3,7},{4,0},{5,1},{6,2},{7,3},{8,12},{9,13},{10,... | collective-permute-start | bytes 688136 | tf_op jit(solution)/shard_map/ppermute | solution.py:350
  43.5 5.0 %collective-permute-done.1.refs_1_ = bf16[16,7168]{1,0:T(8,128)(2,1)S(1)} collective-permute-done((bf16[16,7168]{1,0:T(8,128)(2,1)S(1)}, bf16[16,7168]{1,0:T(8,128)(2,1)S(1)}, u32[]{:S(2)}, u32[]{:S(2)}) %collective-permute-start.1) | collective-permute-done | bytes 229408 | tf_op jit(solution)/shard_map/ppermute | solution.py:350
  48.5 5.0 %collective-permute-done.2.refs_2_ = bf16[16,7168]{1,0:T(8,128)(2,1)S(1)} collective-permute-done((bf16[16,7168]{1,0:T(8,128)(2,1)S(1)}, bf16[16,7168]{1,0:T(8,128)(2,1)S(1)}, u32[]{:S(2)}, u32[]{:S(2)}) %collective-permute-start.2) | collective-permute-done | bytes 229408 | tf_op jit(solution)/shard_map/ppermute | solution.py:350
  55.5 2.6 %collective-permute-start.6 = (bf16[4,7168]{1,0:T(4,128)(2,1)S(1)}, bf16[4,7168]{1,0:T(4,128)(2,1)S(1)}, u32[]{:S(2)}, u32[]{:S(2)}) collective-permute-start(bf16[4,7168]{1,0:T(4,128)(2,1)S(1)} %get-tuple-element.39), channel_id=1, source_target_pairs={{0,24},{1,25},{2,26},{3,27},{4,28},{5,29},{6,30},{7,31},{8,16},{9,... | collective-permute-start | bytes 172040 | tf_op jit(solution)/shard_map/ppermute | solution.py:350
  58.2 2.3 %collective-permute-done.5.refs_1_ = bf16[4,7168]{1,0:T(4,128)(2,1)S(1)} collective-permute-done((bf16[4,7168]{1,0:T(4,128)(2,1)S(1)}, bf16[4,7168]{1,0:T(4,128)(2,1)S(1)}, u32[]{:S(2)}, u32[]{:S(2)}) %collective-permute-start.5) | collective-permute-done | bytes 57376 | tf_op jit(solution)/shard_map/ppermute | solution.py:350
  63.3 2.3 %collective-permute-start.8 = (bf16[2,7168]{1,0:T(2,128)(2,1)S(1)}, bf16[2,7168]{1,0:T(2,128)(2,1)S(1)}, u32[]{:S(2)}, u32[]{:S(2)}) collective-permute-start(bf16[2,7168]{1,0:T(2,128)(2,1)S(1)} %get-tuple-element.42), channel_id=1, source_target_pairs={{0,16},{1,17},{2,18},{3,19},{4,20},{5,21},{6,22},{7,23},{8,24},{9,... | collective-permute-start | bytes 86024 | tf_op jit(solution)/shard_map/ppermute | solution.py:350
  68.1 3.2 %collective-permute-done.9.refs_3_ = bf16[2,7168]{1,0:T(2,128)(2,1)S(1)} collective-permute-done((bf16[2,7168]{1,0:T(2,128)(2,1)S(1)}, bf16[2,7168]{1,0:T(2,128)(2,1)S(1)}, u32[]{:S(2)}, u32[]{:S(2)}) %collective-permute-start.9) | collective-permute-done | bytes 28704 | tf_op jit(solution)/shard_map/ppermute | solution.py:350
  77.2 2.0 %collective-permute-done.12.refs_3_ = bf16[8,7168]{1,0:T(8,128)(2,1)S(1)} collective-permute-done((bf16[8,7168]{1,0:T(8,128)(2,1)S(1)}, bf16[8,7168]{1,0:T(8,128)(2,1)S(1)}, u32[]{:S(2)}, u32[]{:S(2)}) %collective-permute-start.12) | collective-permute-done | bytes 114720 | tf_op jit(solution)/shard_map/ppermute | solution.py:350
  80.5 2.0 %copy-done.1 = bf16[2,7168,128]{2,1,0:T(8,128)(2,1)S(1)} copy-done((bf16[2,7168,128]{2,1,0:T(8,128)(2,1)S(1)}, bf16[2,7168,128]{2,1,0:T(8,128)(2,1)}, u32[]{:S(2)}) %copy-start.1) | copy-done | bytes 3670040
  82.6 2.9 %expert.1 = (f32[32,7168]{1,0:T(8,128)S(1)}, bf16[32,7168]{1,0:T(8,128)(2,1)S(1)}) custom-call(bf16[8,7168]{1,0:T(8,128)(2,1)S(1)} %stack_rows.1.refs_0_, bf16[8,7168]{1,0:T(8,128)(2,1)S(1)} %collective-permute-done.10.refs_1_, bf16[8,7168]{1,0:T(8,128)(2,1)S(1)} %collective-permute-done.11.refs_2_, bf16[8,7168]{1,0:T(8,128)(2,1)S(1)} %collective-permute-done.12.refs_3_, ...), custom_call_target="tpu_custom_call" | custom-call | tf_op jit(solution)/shard_map/expert/pallas_call | solution.py:268
  85.7 1.7 %collective-permute-done.17.refs_1_ = bf16[32,7168]{1,0:T(8,128)(2,1)S(1)} collective-permute-done((bf16[32,7168]{1,0:T(8,128)(2,1)S(1)}, bf16[32,7168]{1,0:T(8,128)(2,1)S(1)}, u32[]{:S(2)}, u32[]{:S(2)}) %collective-permute-start.17) | collective-permute-done | bytes 458784 | tf_op jit(solution)/shard_map/ppermute | solution.py:350
  89.6 1.5 %collective-permute-start.20 = (bf16[8,7168]{1,0:T(8,128)(2,1)S(1)}, bf16[8,7168]{1,0:T(8,128)(2,1)S(1)}, u32[]{:S(2)}, u32[]{:S(2)}) collective-permute-start(bf16[8,7168]{1,0:T(8,128)(2,1)S(1)} %get-tuple-element.49), channel_id=1, source_target_pairs={{0,6},{1,7},{2,4},{3,5},{4,2},{5,3},{6,0},{7,1},{8,14},{9,15},{10,... | collective-permute-start | bytes 344072 | tf_op jit(solution)/shard_map/ppermute | solution.py:350
  91.2 2.0 %collective-permute-done.18.refs_1_ = bf16[8,7168]{1,0:T(8,128)(2,1)S(1)} collective-permute-done((bf16[8,7168]{1,0:T(8,128)(2,1)S(1)}, bf16[8,7168]{1,0:T(8,128)(2,1)S(1)}, u32[]{:S(2)}, u32[]{:S(2)}) %collective-permute-start.18) | collective-permute-done | bytes 114720 | tf_op jit(solution)/shard_map/ppermute | solution.py:350
  93.2 3.0 %collective-permute-done.19.refs_2_ = bf16[8,7168]{1,0:T(8,128)(2,1)S(1)} collective-permute-done((bf16[8,7168]{1,0:T(8,128)(2,1)S(1)}, bf16[8,7168]{1,0:T(8,128)(2,1)S(1)}, u32[]{:S(2)}, u32[]{:S(2)}) %collective-permute-start.19) | collective-permute-done | bytes 114720 | tf_op jit(solution)/shard_map/ppermute | solution.py:350
  96.4 2.0 %collective-permute-start.22 = (bf16[2,7168]{1,0:T(2,128)(2,1)S(1)}, bf16[2,7168]{1,0:T(2,128)(2,1)S(1)}, u32[]{:S(2)}, u32[]{:S(2)}) collective-permute-start(bf16[2,7168]{1,0:T(2,128)(2,1)S(1)} %get-tuple-element.52), channel_id=1, source_target_pairs={{0,16},{1,17},{2,18},{3,19},{4,20},{5,21},{6,22},{7,23},{8,24},{9,... | collective-permute-start | bytes 86024 | tf_op jit(solution)/shard_map/ppermute | solution.py:350
  98.4 2.3 %collective-permute-start.23 = (bf16[2,7168]{1,0:T(2,128)(2,1)S(1)}, bf16[2,7168]{1,0:T(2,128)(2,1)S(1)}, u32[]{:S(2)}, u32[]{:S(2)}) collective-permute-start(bf16[2,7168]{1,0:T(2,128)(2,1)S(1)} %get-tuple-element.53), channel_id=1, source_target_pairs={{0,24},{1,25},{2,26},{3,27},{4,28},{5,29},{6,30},{7,31},{8,16},{9,... | collective-permute-start | bytes 86024 | tf_op jit(solution)/shard_map/ppermute | solution.py:350
  101.2 2.8 %collective-permute-done.23.refs_2_ = bf16[2,7168]{1,0:T(2,128)(2,1)S(1)} collective-permute-done((bf16[2,7168]{1,0:T(2,128)(2,1)S(1)}, bf16[2,7168]{1,0:T(2,128)(2,1)S(1)}, u32[]{:S(2)}, u32[]{:S(2)}) %collective-permute-start.23) | collective-permute-done | bytes 28704 | tf_op jit(solution)/shard_map/ppermute | solution.py:350
  (61 shorter events, 23.4 us)
Async XLA Ops:
  7.6 22.9 %all-to-all-start = ((bf16[32,16,512]{2,1,0:T(8,128)(2,1)}), bf16[32,16,512]{2,1,0:T(8,128)(2,1)S(1)}, u32[]{:S(2)}, u32[]{:S(2)}) async-start(bf16[32,16,512]{2,1,0:T(8,128)(2,1)} %bitcast.3), calls=%async_computation | async-start | bytes 1048576 | tf_op jit(solution)/shard_map/all_to_all | solution.py:359
  36.9 2.5 %collective-permute-start = (bf16[64,7168]{1,0:T(8,128)(2,1)S(1)}, bf16[64,7168]{1,0:T(8,128)(2,1)S(1)}, u32[]{:S(2)}, u32[]{:S(2)}) collective-permute-start(bf16[64,7168]{1,0:T(8,128)(2,1)S(1)} %get-tuple-element.31), channel_id=1, source_target_pairs={{0,1},{1,0},{2,3},{3,2},{4,5},{5,4},{6,7},{7,6},{8,9},{9,8},{10,11... | collective-permute-start | bytes 2752520 | tf_op jit(solution)/shard_map/ppermute | solution.py:350
  40.0 8.5 %collective-permute-start.1 = (bf16[16,7168]{1,0:T(8,128)(2,1)S(1)}, bf16[16,7168]{1,0:T(8,128)(2,1)S(1)}, u32[]{:S(2)}, u32[]{:S(2)}) collective-permute-start(bf16[16,7168]{1,0:T(8,128)(2,1)S(1)} %get-tuple-element.33), channel_id=1, source_target_pairs={{0,2},{1,3},{2,0},{3,1},{4,6},{5,7},{6,4},{7,5},{8,10},{9,11},{10,... | collective-permute-start | bytes 688136 | tf_op jit(solution)/shard_map/ppermute | solution.py:350
  41.0 12.5 %collective-permute-start.2 = (bf16[16,7168]{1,0:T(8,128)(2,1)S(1)}, bf16[16,7168]{1,0:T(8,128)(2,1)S(1)}, u32[]{:S(2)}, u32[]{:S(2)}) collective-permute-start(bf16[16,7168]{1,0:T(8,128)(2,1)S(1)} %get-tuple-element.34), channel_id=1, source_target_pairs={{0,4},{1,5},{2,6},{3,7},{4,0},{5,1},{6,2},{7,3},{8,12},{9,13},{10,... | collective-permute-start | bytes 688136 | tf_op jit(solution)/shard_map/ppermute | solution.py:350
  42.5 11.0 %collective-permute-start.3 = (bf16[16,7168]{1,0:T(8,128)(2,1)S(1)}, bf16[16,7168]{1,0:T(8,128)(2,1)S(1)}, u32[]{:S(2)}, u32[]{:S(2)}) collective-permute-start(bf16[16,7168]{1,0:T(8,128)(2,1)S(1)} %get-tuple-element.35), channel_id=1, source_target_pairs={{0,6},{1,7},{2,4},{3,5},{4,2},{5,3},{6,0},{7,1},{8,14},{9,15},{10,... | collective-permute-start | bytes 688136 | tf_op jit(solution)/shard_map/ppermute | solution.py:350
  53.6 4.6 %collective-permute-start.4 = (bf16[4,7168]{1,0:T(4,128)(2,1)S(1)}, bf16[4,7168]{1,0:T(4,128)(2,1)S(1)}, u32[]{:S(2)}, u32[]{:S(2)}) collective-permute-start(bf16[4,7168]{1,0:T(4,128)(2,1)S(1)} %get-tuple-element.37), channel_id=1, source_target_pairs={{0,8},{1,9},{2,10},{3,11},{4,12},{5,13},{6,14},{7,15},{8,0},{9,1},... | collective-permute-start | bytes 172040 | tf_op jit(solution)/shard_map/ppermute | solution.py:350
  54.4 6.1 %collective-permute-start.5 = (bf16[4,7168]{1,0:T(4,128)(2,1)S(1)}, bf16[4,7168]{1,0:T(4,128)(2,1)S(1)}, u32[]{:S(2)}, u32[]{:S(2)}) collective-permute-start(bf16[4,7168]{1,0:T(4,128)(2,1)S(1)} %get-tuple-element.38), channel_id=1, source_target_pairs={{0,16},{1,17},{2,18},{3,19},{4,20},{5,21},{6,22},{7,23},{8,24},{9,... | collective-permute-start | bytes 172040 | tf_op jit(solution)/shard_map/ppermute | solution.py:350
  55.5 6.1 %collective-permute-start.6 = (bf16[4,7168]{1,0:T(4,128)(2,1)S(1)}, bf16[4,7168]{1,0:T(4,128)(2,1)S(1)}, u32[]{:S(2)}, u32[]{:S(2)}) collective-permute-start(bf16[4,7168]{1,0:T(4,128)(2,1)S(1)} %get-tuple-element.39), channel_id=1, source_target_pairs={{0,24},{1,25},{2,26},{3,27},{4,28},{5,29},{6,30},{7,31},{8,16},{9,... | collective-permute-start | bytes 172040 | tf_op jit(solution)/shard_map/ppermute | solution.py:350
  62.5 4.5 %collective-permute-start.7 = (bf16[2,7168]{1,0:T(2,128)(2,1)S(1)}, bf16[2,7168]{1,0:T(2,128)(2,1)S(1)}, u32[]{:S(2)}, u32[]{:S(2)}) collective-permute-start(bf16[2,7168]{1,0:T(2,128)(2,1)S(1)} %get-tuple-element.41), channel_id=1, source_target_pairs={{0,8},{1,9},{2,10},{3,11},{4,12},{5,13},{6,14},{7,15},{8,0},{9,1},... | collective-permute-start | bytes 86024 | tf_op jit(solution)/shard_map/ppermute | solution.py:350
  63.3 4.8 %collective-permute-start.8 = (bf16[2,7168]{1,0:T(2,128)(2,1)S(1)}, bf16[2,7168]{1,0:T(2,128)(2,1)S(1)}, u32[]{:S(2)}, u32[]{:S(2)}) collective-permute-start(bf16[2,7168]{1,0:T(2,128)(2,1)S(1)} %get-tuple-element.42), channel_id=1, source_target_pairs={{0,16},{1,17},{2,18},{3,19},{4,20},{5,21},{6,22},{7,23},{8,24},{9,... | collective-permute-start | bytes 86024 | tf_op jit(solution)/shard_map/ppermute | solution.py:350
  65.6 5.7 %collective-permute-start.9 = (bf16[2,7168]{1,0:T(2,128)(2,1)S(1)}, bf16[2,7168]{1,0:T(2,128)(2,1)S(1)}, u32[]{:S(2)}, u32[]{:S(2)}) collective-permute-start(bf16[2,7168]{1,0:T(2,128)(2,1)S(1)} %get-tuple-element.43), channel_id=1, source_target_pairs={{0,24},{1,25},{2,26},{3,27},{4,28},{5,29},{6,30},{7,31},{8,16},{9,... | collective-permute-start | bytes 86024 | tf_op jit(solution)/shard_map/ppermute | solution.py:350
  71.3 4.9 %collective-permute-start.10 = (bf16[8,7168]{1,0:T(8,128)(2,1)S(1)}, bf16[8,7168]{1,0:T(8,128)(2,1)S(1)}, u32[]{:S(2)}, u32[]{:S(2)}) collective-permute-start(bf16[8,7168]{1,0:T(8,128)(2,1)S(1)} %stack_rows.1.refs_0_), channel_id=1, source_target_pairs={{0,2},{1,3},{2,0},{3,1},{4,6},{5,7},{6,4},{7,5},{8,10},{9,11},{10,... | collective-permute-start | bytes 344072 | tf_op jit(solution)/shard_map/ppermute | solution.py:350
  72.4 4.8 %collective-permute-start.11 = (bf16[8,7168]{1,0:T(8,128)(2,1)S(1)}, bf16[8,7168]{1,0:T(8,128)(2,1)S(1)}, u32[]{:S(2)}, u32[]{:S(2)}) collective-permute-start(bf16[8,7168]{1,0:T(8,128)(2,1)S(1)} %stack_rows.1.refs_0_), channel_id=1, source_target_pairs={{0,4},{1,5},{2,6},{3,7},{4,0},{5,1},{6,2},{7,3},{8,12},{9,13},{10,... | collective-permute-start | bytes 344072 | tf_op jit(solution)/shard_map/ppermute | solution.py:350
  73.5 5.7 %collective-permute-start.12 = (bf16[8,7168]{1,0:T(8,128)(2,1)S(1)}, bf16[8,7168]{1,0:T(8,128)(2,1)S(1)}, u32[]{:S(2)}, u32[]{:S(2)}) collective-permute-start(bf16[8,7168]{1,0:T(8,128)(2,1)S(1)} %stack_rows.1.refs_0_), channel_id=1, source_target_pairs={{0,6},{1,7},{2,4},{3,5},{4,2},{5,3},{6,0},{7,1},{8,14},{9,15},{10,... | collective-permute-start | bytes 344072 | tf_op jit(solution)/shard_map/ppermute | solution.py:350
  74.9 4.3 %collective-permute-start.13 = (bf16[8,7168]{1,0:T(8,128)(2,1)S(1)}, bf16[8,7168]{1,0:T(8,128)(2,1)S(1)}, u32[]{:S(2)}, u32[]{:S(2)}) collective-permute-start(bf16[8,7168]{1,0:T(8,128)(2,1)S(1)} %stack_rows.1.refs_0_), channel_id=1, source_target_pairs={{0,1},{1,0},{2,3},{3,2},{4,5},{5,4},{6,7},{7,6},{8,9},{9,8},{10,11... | collective-permute-start | bytes 344072 | tf_op jit(solution)/shard_map/ppermute | solution.py:350
  76.2 3.0 %collective-permute-start.14 = (bf16[8,7168]{1,0:T(8,128)(2,1)S(1)}, bf16[8,7168]{1,0:T(8,128)(2,1)S(1)}, u32[]{:S(2)}, u32[]{:S(2)}) collective-permute-start(bf16[8,7168]{1,0:T(8,128)(2,1)S(1)} %collective-permute-done.10.refs_1_), channel_id=1, source_target_pairs={{0,1},{1,0},{2,3},{3,2},{4,5},{5,4},{6,7},{7,6},{8,9},{9,8},{10,11... | collective-permute-start | bytes 344072 | tf_op jit(solution)/shard_map/ppermute | solution.py:350
  77.2 2.1 %collective-permute-start.15 = (bf16[8,7168]{1,0:T(8,128)(2,1)S(1)}, bf16[8,7168]{1,0:T(8,128)(2,1)S(1)}, u32[]{:S(2)}, u32[]{:S(2)}) collective-permute-start(bf16[8,7168]{1,0:T(8,128)(2,1)S(1)} %collective-permute-done.11.refs_2_), channel_id=1, source_target_pairs={{0,1},{1,0},{2,3},{3,2},{4,5},{5,4},{6,7},{7,6},{8,9},{9,8},{10,11... | collective-permute-start | bytes 344072 | tf_op jit(solution)/shard_map/ppermute | solution.py:350
  85.5 1.9 %collective-permute-start.17 = (bf16[32,7168]{1,0:T(8,128)(2,1)S(1)}, bf16[32,7168]{1,0:T(8,128)(2,1)S(1)}, u32[]{:S(2)}, u32[]{:S(2)}) collective-permute-start(bf16[32,7168]{1,0:T(8,128)(2,1)S(1)} %get-tuple-element.45), channel_id=1, source_target_pairs={{0,1},{1,0},{2,3},{3,2},{4,5},{5,4},{6,7},{7,6},{8,9},{9,8},{10,11... | collective-permute-start | bytes 1376264 | tf_op jit(solution)/shard_map/ppermute | solution.py:350
  87.6 5.6 %collective-permute-start.18 = (bf16[8,7168]{1,0:T(8,128)(2,1)S(1)}, bf16[8,7168]{1,0:T(8,128)(2,1)S(1)}, u32[]{:S(2)}, u32[]{:S(2)}) collective-permute-start(bf16[8,7168]{1,0:T(8,128)(2,1)S(1)} %get-tuple-element.47), channel_id=1, source_target_pairs={{0,2},{1,3},{2,0},{3,1},{4,6},{5,7},{6,4},{7,5},{8,10},{9,11},{10,... | collective-permute-start | bytes 344072 | tf_op jit(solution)/shard_map/ppermute | solution.py:350
  88.8 7.4 %collective-permute-start.19 = (bf16[8,7168]{1,0:T(8,128)(2,1)S(1)}, bf16[8,7168]{1,0:T(8,128)(2,1)S(1)}, u32[]{:S(2)}, u32[]{:S(2)}) collective-permute-start(bf16[8,7168]{1,0:T(8,128)(2,1)S(1)} %get-tuple-element.48), channel_id=1, source_target_pairs={{0,4},{1,5},{2,6},{3,7},{4,0},{5,1},{6,2},{7,3},{8,12},{9,13},{10,... | collective-permute-start | bytes 344072 | tf_op jit(solution)/shard_map/ppermute | solution.py:350
  89.6 6.6 %collective-permute-start.20 = (bf16[8,7168]{1,0:T(8,128)(2,1)S(1)}, bf16[8,7168]{1,0:T(8,128)(2,1)S(1)}, u32[]{:S(2)}, u32[]{:S(2)}) collective-permute-start(bf16[8,7168]{1,0:T(8,128)(2,1)S(1)} %get-tuple-element.49), channel_id=1, source_target_pairs={{0,6},{1,7},{2,4},{3,5},{4,2},{5,3},{6,0},{7,1},{8,14},{9,15},{10,... | collective-permute-start | bytes 344072 | tf_op jit(solution)/shard_map/ppermute | solution.py:350
  96.3 4.6 %collective-permute-start.21 = (bf16[2,7168]{1,0:T(2,128)(2,1)S(1)}, bf16[2,7168]{1,0:T(2,128)(2,1)S(1)}, u32[]{:S(2)}, u32[]{:S(2)}) collective-permute-start(bf16[2,7168]{1,0:T(2,128)(2,1)S(1)} %get-tuple-element.51), channel_id=1, source_target_pairs={{0,8},{1,9},{2,10},{3,11},{4,12},{5,13},{6,14},{7,15},{8,0},{9,1},... | collective-permute-start | bytes 86024 | tf_op jit(solution)/shard_map/ppermute | solution.py:350
  96.4 4.8 %collective-permute-start.22 = (bf16[2,7168]{1,0:T(2,128)(2,1)S(1)}, bf16[2,7168]{1,0:T(2,128)(2,1)S(1)}, u32[]{:S(2)}, u32[]{:S(2)}) collective-permute-start(bf16[2,7168]{1,0:T(2,128)(2,1)S(1)} %get-tuple-element.52), channel_id=1, source_target_pairs={{0,16},{1,17},{2,18},{3,19},{4,20},{5,21},{6,22},{7,23},{8,24},{9,... | collective-permute-start | bytes 86024 | tf_op jit(solution)/shard_map/ppermute | solution.py:350
  98.4 5.7 %collective-permute-start.23 = (bf16[2,7168]{1,0:T(2,128)(2,1)S(1)}, bf16[2,7168]{1,0:T(2,128)(2,1)S(1)}, u32[]{:S(2)}, u32[]{:S(2)}) collective-permute-start(bf16[2,7168]{1,0:T(2,128)(2,1)S(1)} %get-tuple-element.53), channel_id=1, source_target_pairs={{0,24},{1,25},{2,26},{3,27},{4,28},{5,29},{6,30},{7,31},{8,16},{9,... | collective-permute-start | bytes 86024 | tf_op jit(solution)/shard_map/ppermute | solution.py:350
  (12 other events, 177.1 us)

commit v2 on v1

--- a/solution.py
+++ b/solution.py
@@ -27,6 +27,10 @@
 
 def params():
     return pltpu.CompilerParams(vmem_limit_bytes=VMEM)
+
+
+def in_hbm(x):
+    return pltpu.with_memory_space_constraint(x, pltpu.HBM)
 
 
 def whole(shape):
@@ -77,7 +81,53 @@
         scratch_shapes=[pltpu.VMEM((rows * heads, LAT), BF16)],
         compiler_params=params(),
         name="latent_attention",
-    )(lengths, q_t, k_t)
+    )(
+        lengths,
+        in_hbm(q_t),
+        in_hbm(k_t),
+    )
+
+
+def fetch_kernel(parts, *refs):
+    count = len(parts)
+    ins, outs, sems = refs[:count], refs[count + 1 : -1], refs[-1]
+    copies = []
+    for ref, (axis, cuts) in zip(ins, parts):
+        size = ref.shape[axis] // cuts
+        for c in range(cuts):
+            at = (slice(None),) * axis + (pl.ds(c * size, size),)
+            src = ref.at[c] if axis == 0 and size == 1 else ref.at[at]
+            n = len(copies)
+            copies.append(pltpu.make_async_copy(src, outs[n], sems.at[n]))
+    for copy in copies:
+        copy.start()
+    for copy in copies:
+        copy.wait()
+
+
+def fetch(weights, parts, after):
+    shapes = []
+    for w, (axis, cuts) in zip(weights, parts):
+        shape = list(w.shape)
+        shape[axis] //= cuts
+        if shape[0] == 1:
+            shape = shape[1:]
+        shapes += [pltpu.VMEM(tuple(shape), w.dtype)] * cuts
+    out = pl.pallas_call(
+        functools.partial(fetch_kernel, parts),
+        in_specs=[pl.BlockSpec(memory_space=pltpu.HBM)] * len(weights)
+        + [pl.BlockSpec(memory_space=pl.ANY)],
+        out_specs=[pl.BlockSpec(memory_space=pltpu.VMEM)] * len(shapes),
+        out_shape=shapes,
+        scratch_shapes=[pltpu.SemaphoreType.DMA((len(shapes),))],
+        compiler_params=params(),
+        name="fetch_weights",
+    )(*[in_hbm(w) for w in weights], after)
+    result = []
+    for _, cuts in parts:
+        result.append(out[:cuts])
+        out = out[cuts:]
+    return result
 
 
 def project_kernel(planes, rows, me, x_ref, v_ref, w_ref, own_ref, other_ref, flat):
@@ -109,7 +159,7 @@
 def project(me, by_heads, value_up, out_proj, planes, rows):
     count = planes * 8 * rows
     depth, features = out_proj.shape
-    tile = features // 4
+    tile = features // 7
     half = count // 2
     return pl.pallas_call(
         functools.partial(project_kernel, planes, rows),
@@ -128,7 +178,7 @@
         scratch_shapes=[pltpu.VMEM((count, depth), BF16)],
         compiler_params=params(),
         name="projections",
-    )(me, by_heads, value_up, out_proj)
+    )(me, by_heads, value_up, in_hbm(out_proj))
 
 
 def add_kernel(arrived, parts, *refs):
@@ -230,60 +280,37 @@
     )(*pieces)
 
 
-def expert_kernel(pieces, steps, *refs):
+def expert_kernel(pieces, tiles, *refs):
     xs = refs[:pieces]
-    gu_ref, down_ref, own_ref, other_ref, gate, up, act = refs[pieces:]
-    step = pl.program_id(0)
-
-    @pl.when(step == 0)
-    def _():
-        gate[...] = jnp.zeros_like(gate)
-        up[...] = jnp.zeros_like(up)
-
-    @pl.when(step < steps)
-    def _():
-        x = jnp.concatenate([ref[...].astype(F32) for ref in xs], axis=0).astype(BF16)
-        gate[...] += jnp.dot(x, gu_ref[0], preferred_element_type=F32)
-        up[...] += jnp.dot(x, gu_ref[1], preferred_element_type=F32)
-
-    @pl.when(step == steps - 1)
-    def _():
-        g = gate[...]
-        act[...] = (g / (1.0 + jnp.exp(-g)) * up[...]).astype(BF16)
-
-    @pl.when(step >= steps)
-    def _():
-        out = jnp.dot(act[...], down_ref[...], preferred_element_type=F32)
-        half = out.shape[0] // 2
-        own_ref[...] = out[:half]
-        other_ref[...] = out[half:].astype(BF16)
-
-
-def expert(pieces, gate_up, down_proj, steps=4):
+    gate_ref, up_ref, down_ref, own_ref, other_ref = refs[pieces:]
+    tile = down_ref.shape[1] // tiles
+    gate, up = 0.0, 0.0
+    for t in range(tiles):
+        at = slice(t * tile, (t + 1) * tile)
+        x = jnp.concatenate([ref[:, at].astype(F32) for ref in xs], axis=0).astype(BF16)
+        gate += jnp.dot(x, gate_ref[at, :], preferred_element_type=F32)
+        up += jnp.dot(x, up_ref[at, :], preferred_element_type=F32)
+    act = (gate / (1.0 + jnp.exp(-gate)) * up).astype(BF16)
+    half = act.shape[0] // 2
+    for t in range(tiles):
+        at = slice(t * tile, (t + 1) * tile)
+        out = jnp.dot(act, down_ref[:, at], preferred_element_type=F32)
+        own_ref[:, at] = out[:half]
+        other_ref[:, at] = out[half:].astype(BF16)
+
+
+def expert(pieces, gate_up, down_proj, tiles=7):
     size, features = pieces[0].shape
-    count = size * len(pieces)
-    hidden = gate_up.shape[2]
-    tile = features // steps
-    half = count // 2
-    return pl.pallas_call(
-        functools.partial(expert_kernel, len(pieces), steps),
-        grid=(2 * steps,),
-        in_specs=[pl.BlockSpec((size, tile), lambda t: (0, jnp.minimum(t, steps - 1)))]
-        * len(pieces)
-        + [
-            pl.BlockSpec((2, tile, hidden), lambda t: (0, jnp.minimum(t, steps - 1), 0)),
-            pl.BlockSpec((hidden, tile), lambda t: (0, jnp.maximum(t - steps, 0))),
-        ],
-        out_specs=[pl.BlockSpec((half, tile), lambda t: (0, jnp.maximum(t - steps, 0)))] * 2,
+    half = size * len(pieces) // 2
+    vec = pl.BlockSpec(memory_space=pltpu.VMEM)
+    return pl.pallas_call(
+        functools.partial(expert_kernel, len(pieces), tiles),
+        in_specs=[vec] * (len(pieces) + 3),
+        out_specs=[vec, vec],
         out_shape=[sds((half, features), F32), sds((half, features), BF16)],
-        scratch_shapes=[
-            pltpu.VMEM((count, hidden), F32),
-            pltpu.VMEM((count, hidden), F32),
-            pltpu.VMEM((count, hidden), BF16),
-        ],
         compiler_params=params(),
         name="expert",
-    )(*pieces, gate_up, down_proj)
+    )(*pieces, *gate_up, down_proj)
 
 
 def combine_kernel(planes, cap, me, ids, weights, own_ref, *refs):
@@ -359,6 +386,7 @@
     by_heads = lax.all_to_all(latents, "dp", split_axis=0, concat_axis=0, tiled=True)
     own, other = project(me, by_heads, value_up, out_proj, planes, rows)
     own, *out = add_and_cut(own, [swap(other, 1)], 4, "add_core")
+    gate_up, (down_proj,) = fetch([gate_up, down_proj], [(0, 2), (0, 1)], own)
     own, *out = add_and_cut(own, over_chips(out), planes, "add_chips", 1)
     resid, mine, *out = norm_and_pack(
         me, route_ids, own, over_planes(out), hidden_in, norm_gain[None], planes, cap

time: 106 us -> 103 us (0.972)
  local copies, waits for them, and re-layouts: 8.74 us -> 0.88 us
  Pallas kernels: 13.7 us -> 19.7 us
  waiting for transfers between devices: 51.2 us -> 49.9 us
    unnamed x24 -> x14, local copies, waits for them, and re-layouts: 8.72 us -> 0.86 us
    pallas_call x1, Pallas kernels: 3.34 us -> 7.32 us  [project(): pl.pallas_call(functools.partial(project_kernel, planes, rows), grid=(fea...]
    ppermute x24, waiting for transfers between devices: 35.7 us -> 34.4 us  [swap(): return lax.ppermute(x, 'dp', [(i, i ^ mask) for i in range(devices)])]
    pallas_call x1, Pallas kernels: 4.21 us -> 5.43 us  [attention(): pl.pallas_call(functools.partial(attention_kernel, rows), grid=(rows,), i...]
    pallas_call x1 -> x2, Pallas kernels: 2.91 us -> 3.67 us  [the longest x1 2.63 us: fetch(): pl.pallas_call(functools.partial(fetch_kernel, parts), in_specs=[pl.Block...]
  transfers between devices with their start and end apart: 25 -> 25, of which waited for: 17 -> 16; matrix products, arithmetic and copies ran while one was open for 0% -> 0% of each run, Pallas kernels for 0% -> 3%
where the time goes in v2:
time: 103 us
  waiting for transfers between devices  49.9 us (48%)
  starting transfers between devices  32 us (31%)
  Pallas kernels  19.7 us (19%)
    ppermute x24, waiting for transfers between devices, swap(): return lax.ppermute(x, 'dp', [(i, i ^ mask) for i in range(devices)])  34.4 us
    ppermute x24, starting transfers between devices, swap(): return lax.ppermute(x, 'dp', [(i, i ^ mask) for i in range(devices)])  24.7 us
    all_to_all x1, waiting for transfers between devices, body(): lax.all_to_all(latents, 'dp', split_axis=0, concat_axis=0, tiled=True)  15.5 us
    pallas_call x1, Pallas kernels, project(): pl.pallas_call(functools.partial(project_kernel, planes, rows), grid=(fea...  7.32 us
    all_to_all x1, starting transfers between devices, body(): lax.all_to_all(latents, 'dp', split_axis=0, concat_axis=0, tiled=True)  7.3 us
    pallas_call x1, Pallas kernels, attention(): pl.pallas_call(functools.partial(attention_kernel, rows), grid=(rows,), i...  5.43 us
    pallas_call x1, Pallas kernels, fetch(): pl.pallas_call(functools.partial(fetch_kernel, parts), in_specs=[pl.Block...  2.63 us
  transfers between devices with their start and end apart: 25, of which 16 were waited for; matrix products, arithmetic and copies ran while one was open for 0% of the time, Pallas kernels for 3%

profile of v2, /device:TPU:0, one launch (start us, length us, event | category | flops | bytes accessed | tf_op | source)
XLA Modules:
  0.0 102.6 jit_solution(9510594713949397409)
XLA Ops:
  0.7 5.4 %latent_attention.1 = bf16[512,512]{1,0:T(8,128)(2,1)} custom-call(s32[4]{0:T(128)S(1)} %copy-done.2, bf16[4,576,128]{2,1,0:T(8,128)(2,1)} %bitcast.7, bf16[4,576,512]{2,1,0:T(8,128)(2,1)} %bitcast.6), custom_call_target="tpu_custom_call" | custom-call | tf_op jit(solution)/shard_map/latent_attention/pallas_call | solution.py:71
  6.1 7.3 %all-to-all-start = ((bf16[32,16,512]{2,1,0:T(8,128)(2,1)}), bf16[32,16,512]{2,1,0:T(8,128)(2,1)S(1)}, u32[]{:S(2)}, u32[]{:S(2)}) async-start(bf16[32,16,512]{2,1,0:T(8,128)(2,1)} %bitcast.3), calls=%async_computation | async-start | bytes 1048576 | tf_op jit(solution)/shard_map/all_to_all | solution.py:386
  13.4 15.5 %all-to-all-done = bf16[32,16,512]{2,1,0:T(8,128)(2,1)S(1)} async-done(((bf16[32,16,512]{2,1,0:T(8,128)(2,1)}), bf16[32,16,512]{2,1,0:T(8,128)(2,1)S(1)}, u32[]{:S(2)}, u32[]{:S(2)}) %all-to-all-start) | async-done | bytes 524320 | tf_op jit(solution)/shard_map/all_to_all | solution.py:386
  28.9 7.3 %projections.1 = (f32[64,7168]{1,0:T(8,128)S(1)}, bf16[64,7168]{1,0:T(8,128)(2,1)S(1)}) custom-call(s32[1]{0:T(128)} %bitcast.me, bf16[512,512]{1,0:T(8,128)(2,1)S(1)} %bitcast.5, bf16[4,512,128]{2,1,0:T(8,128)(2,1)S(1)} %copy-done, bf16[512,7168]{1,0:T(8,128)(2,1)} %w_ref.1), custom_call_target="tpu_custom_call" | custom-call | tf_op jit(solution)/shard_map/projections/pallas_call | solution.py:164
  36.4 2.5 %collective-permute-done.refs_1_ = bf16[64,7168]{1,0:T(8,128)(2,1)S(1)} collective-permute-done((bf16[64,7168]{1,0:T(8,128)(2,1)S(1)}, bf16[64,7168]{1,0:T(8,128)(2,1)S(1)}, u32[]{:S(2)}, u32[]{:S(2)}) %collective-permute-start) | collective-permute-done | bytes 917536 | tf_op jit(solution)/shard_map/ppermute | solution.py:377
  40.3 1.5 %collective-permute-start.2 = (bf16[16,7168]{1,0:T(8,128)(2,1)S(1)}, bf16[16,7168]{1,0:T(8,128)(2,1)S(1)}, u32[]{:S(2)}, u32[]{:S(2)}) collective-permute-start(bf16[16,7168]{1,0:T(8,128)(2,1)S(1)} %get-tuple-element.37), channel_id=1, source_target_pairs={{0,4},{1,5},{2,6},{3,7},{4,0},{5,1},{6,2},{7,3},{8,12},{9,13},{10,... | collective-permute-start | bytes 688136 | tf_op jit(solution)/shard_map/ppermute | solution.py:377
  42.9 5.0 %collective-permute-done.1.refs_1_ = bf16[16,7168]{1,0:T(8,128)(2,1)S(1)} collective-permute-done((bf16[16,7168]{1,0:T(8,128)(2,1)S(1)}, bf16[16,7168]{1,0:T(8,128)(2,1)S(1)}, u32[]{:S(2)}, u32[]{:S(2)}) %collective-permute-start.1) | collective-permute-done | bytes 229408 | tf_op jit(solution)/shard_map/ppermute | solution.py:377
  47.8 5.0 %collective-permute-done.2.refs_2_ = bf16[16,7168]{1,0:T(8,128)(2,1)S(1)} collective-permute-done((bf16[16,7168]{1,0:T(8,128)(2,1)S(1)}, bf16[16,7168]{1,0:T(8,128)(2,1)S(1)}, u32[]{:S(2)}, u32[]{:S(2)}) %collective-permute-start.2) | collective-permute-done | bytes 229408 | tf_op jit(solution)/shard_map/ppermute | solution.py:377
  54.8 2.6 %collective-permute-start.6 = (bf16[4,7168]{1,0:T(4,128)(2,1)S(1)}, bf16[4,7168]{1,0:T(4,128)(2,1)S(1)}, u32[]{:S(2)}, u32[]{:S(2)}) collective-permute-start(bf16[4,7168]{1,0:T(4,128)(2,1)S(1)} %get-tuple-element.42), channel_id=1, source_target_pairs={{0,24},{1,25},{2,26},{3,27},{4,28},{5,29},{6,30},{7,31},{8,16},{9,... | collective-permute-start | bytes 172040 | tf_op jit(solution)/shard_map/ppermute | solution.py:377
  57.5 2.3 %collective-permute-done.5.refs_1_ = bf16[4,7168]{1,0:T(4,128)(2,1)S(1)} collective-permute-done((bf16[4,7168]{1,0:T(4,128)(2,1)S(1)}, bf16[4,7168]{1,0:T(4,128)(2,1)S(1)}, u32[]{:S(2)}, u32[]{:S(2)}) %collective-permute-start.5) | collective-permute-done | bytes 57376 | tf_op jit(solution)/shard_map/ppermute | solution.py:377
  62.6 2.3 %collective-permute-start.8 = (bf16[2,7168]{1,0:T(2,128)(2,1)S(1)}, bf16[2,7168]{1,0:T(2,128)(2,1)S(1)}, u32[]{:S(2)}, u32[]{:S(2)}) collective-permute-start(bf16[2,7168]{1,0:T(2,128)(2,1)S(1)} %get-tuple-element.45), channel_id=1, source_target_pairs={{0,16},{1,17},{2,18},{3,19},{4,20},{5,21},{6,22},{7,23},{8,24},{9,... | collective-permute-start | bytes 86024 | tf_op jit(solution)/shard_map/ppermute | solution.py:377
  67.4 3.2 %collective-permute-done.9.refs_3_ = bf16[2,7168]{1,0:T(2,128)(2,1)S(1)} collective-permute-done((bf16[2,7168]{1,0:T(2,128)(2,1)S(1)}, bf16[2,7168]{1,0:T(2,128)(2,1)S(1)}, u32[]{:S(2)}, u32[]{:S(2)}) %collective-permute-start.9) | collective-permute-done | bytes 28704 | tf_op jit(solution)/shard_map/ppermute | solution.py:377
  72.8 1.4 %collective-permute-start.12 = (bf16[8,7168]{1,0:T(8,128)(2,1)S(1)}, bf16[8,7168]{1,0:T(8,128)(2,1)S(1)}, u32[]{:S(2)}, u32[]{:S(2)}) collective-permute-start(bf16[8,7168]{1,0:T(8,128)(2,1)S(1)} %stack_rows.1.refs_0_), channel_id=1, source_target_pairs={{0,6},{1,7},{2,4},{3,5},{4,2},{5,3},{6,0},{7,1},{8,14},{9,15},{10,... | collective-permute-start | bytes 344072 | tf_op jit(solution)/shard_map/ppermute | solution.py:377
  74.2 1.3 %collective-permute-done.10.refs_1_ = bf16[8,7168]{1,0:T(8,128)(2,1)S(1)} collective-permute-done((bf16[8,7168]{1,0:T(8,128)(2,1)S(1)}, bf16[8,7168]{1,0:T(8,128)(2,1)S(1)}, u32[]{:S(2)}, u32[]{:S(2)}) %collective-permute-start.10) | collective-permute-done | bytes 114720 | tf_op jit(solution)/shard_map/ppermute | solution.py:377
  76.5 2.0 %collective-permute-done.12.refs_3_ = bf16[8,7168]{1,0:T(8,128)(2,1)S(1)} collective-permute-done((bf16[8,7168]{1,0:T(8,128)(2,1)S(1)}, bf16[8,7168]{1,0:T(8,128)(2,1)S(1)}, u32[]{:S(2)}, u32[]{:S(2)}) %collective-permute-start.12) | collective-permute-done | bytes 114720 | tf_op jit(solution)/shard_map/ppermute | solution.py:377
  78.5 2.6 %fetch_weights.1 = (bf16[7168,128]{1,0:T(8,128)(2,1)S(1)}, bf16[7168,128]{1,0:T(8,128)(2,1)S(1)}, bf16[128,7168]{1,0:T(8,128)(2,1)S(1)}) custom-call(bf16[2,7168,128]{2,1,0:T(8,128)(2,1)} %refs_0_.1, bf16[128,7168]{1,0:T(8,128)(2,1)} %refs_1_.1, f32[16,7168]{1,0:T(8,128)S(1)} %get-tuple-element.35.refs_0_.refs_2_), custom_call_target="tpu_custom_call" | custom-call | tf_op jit(solution)/shard_map/fetch_weights/pallas_call | solution.py:116
  82.8 1.4 %collective-permute-done.17.refs_1_ = bf16[32,7168]{1,0:T(8,128)(2,1)S(1)} collective-permute-done((bf16[32,7168]{1,0:T(8,128)(2,1)S(1)}, bf16[32,7168]{1,0:T(8,128)(2,1)S(1)}, u32[]{:S(2)}, u32[]{:S(2)}) %collective-permute-start.17) | collective-permute-done | bytes 458784 | tf_op jit(solution)/shard_map/ppermute | solution.py:377
  86.6 1.5 %collective-permute-start.20 = (bf16[8,7168]{1,0:T(8,128)(2,1)S(1)}, bf16[8,7168]{1,0:T(8,128)(2,1)S(1)}, u32[]{:S(2)}, u32[]{:S(2)}) collective-permute-start(bf16[8,7168]{1,0:T(8,128)(2,1)S(1)} %get-tuple-element.55), channel_id=1, source_target_pairs={{0,6},{1,7},{2,4},{3,5},{4,2},{5,3},{6,0},{7,1},{8,14},{9,15},{10,... | collective-permute-start | bytes 344072 | tf_op jit(solution)/shard_map/ppermute | solution.py:377
  88.1 2.2 %collective-permute-done.18.refs_1_ = bf16[8,7168]{1,0:T(8,128)(2,1)S(1)} collective-permute-done((bf16[8,7168]{1,0:T(8,128)(2,1)S(1)}, bf16[8,7168]{1,0:T(8,128)(2,1)S(1)}, u32[]{:S(2)}, u32[]{:S(2)}) %collective-permute-start.18) | collective-permute-done | bytes 114720 | tf_op jit(solution)/shard_map/ppermute | solution.py:377
  90.3 3.0 %collective-permute-done.19.refs_2_ = bf16[8,7168]{1,0:T(8,128)(2,1)S(1)} collective-permute-done((bf16[8,7168]{1,0:T(8,128)(2,1)S(1)}, bf16[8,7168]{1,0:T(8,128)(2,1)S(1)}, u32[]{:S(2)}, u32[]{:S(2)}) %collective-permute-start.19) | collective-permute-done | bytes 114720 | tf_op jit(solution)/shard_map/ppermute | solution.py:377
  93.5 2.0 %collective-permute-start.22 = (bf16[2,7168]{1,0:T(2,128)(2,1)S(1)}, bf16[2,7168]{1,0:T(2,128)(2,1)S(1)}, u32[]{:S(2)}, u32[]{:S(2)}) collective-permute-start(bf16[2,7168]{1,0:T(2,128)(2,1)S(1)} %get-tuple-element.58), channel_id=1, source_target_pairs={{0,16},{1,17},{2,18},{3,19},{4,20},{5,21},{6,22},{7,23},{8,24},{9,... | collective-permute-start | bytes 86024 | tf_op jit(solution)/shard_map/ppermute | solution.py:377
  95.6 2.3 %collective-permute-start.23 = (bf16[2,7168]{1,0:T(2,128)(2,1)S(1)}, bf16[2,7168]{1,0:T(2,128)(2,1)S(1)}, u32[]{:S(2)}, u32[]{:S(2)}) collective-permute-start(bf16[2,7168]{1,0:T(2,128)(2,1)S(1)} %get-tuple-element.59), channel_id=1, source_target_pairs={{0,24},{1,25},{2,26},{3,27},{4,28},{5,29},{6,30},{7,31},{8,16},{9,... | collective-permute-start | bytes 86024 | tf_op jit(solution)/shard_map/ppermute | solution.py:377
  98.4 2.9 %collective-permute-done.23.refs_2_ = bf16[2,7168]{1,0:T(2,128)(2,1)S(1)} collective-permute-done((bf16[2,7168]{1,0:T(2,128)(2,1)S(1)}, bf16[2,7168]{1,0:T(2,128)(2,1)S(1)}, u32[]{:S(2)}, u32[]{:S(2)}) %collective-permute-start.23) | collective-permute-done | bytes 28704 | tf_op jit(solution)/shard_map/ppermute | solution.py:377
  101.2 1.4 %combine.1 = bf16[4,7168]{1,0:T(4,128)(2,1)} custom-call(s32[1]{0:T(128)} %bitcast.me, s32[4,2]{1,0:T(4,128)S(1)} %copy.13.ids, f32[4,2]{1,0:T(4,128)S(1)} %copy.14.weights, f32[2,7168]{1,0:T(2,128)S(1)} %get-tuple-element.56.own_ref, bf16[2,7168]{1,0:T(2,128)(2,1)S(1)} %collective-permute-done.21.refs_0_, ...), custom_call_target="tpu_custom_call" | custom-call | tf_op jit(solution)/shard_map/combine/pallas_call | solution.py:342
  (52 shorter events, 18.3 us)
Async XLA Ops:
  6.1 22.9 %all-to-all-start = ((bf16[32,16,512]{2,1,0:T(8,128)(2,1)}), bf16[32,16,512]{2,1,0:T(8,128)(2,1)S(1)}, u32[]{:S(2)}, u32[]{:S(2)}) async-start(bf16[32,16,512]{2,1,0:T(8,128)(2,1)} %bitcast.3), calls=%async_computation | async-start | bytes 1048576 | tf_op jit(solution)/shard_map/all_to_all | solution.py:386
  36.3 2.5 %collective-permute-start = (bf16[64,7168]{1,0:T(8,128)(2,1)S(1)}, bf16[64,7168]{1,0:T(8,128)(2,1)S(1)}, u32[]{:S(2)}, u32[]{:S(2)}) collective-permute-start(bf16[64,7168]{1,0:T(8,128)(2,1)S(1)} %get-tuple-element.34), channel_id=1, source_target_pairs={{0,1},{1,0},{2,3},{3,2},{4,5},{5,4},{6,7},{7,6},{8,9},{9,8},{10,11... | collective-permute-start | bytes 2752520 | tf_op jit(solution)/shard_map/ppermute | solution.py:377
  39.3 8.5 %collective-permute-start.1 = (bf16[16,7168]{1,0:T(8,128)(2,1)S(1)}, bf16[16,7168]{1,0:T(8,128)(2,1)S(1)}, u32[]{:S(2)}, u32[]{:S(2)}) collective-permute-start(bf16[16,7168]{1,0:T(8,128)(2,1)S(1)} %get-tuple-element.36), channel_id=1, source_target_pairs={{0,2},{1,3},{2,0},{3,1},{4,6},{5,7},{6,4},{7,5},{8,10},{9,11},{10,... | collective-permute-start | bytes 688136 | tf_op jit(solution)/shard_map/ppermute | solution.py:377
  40.3 12.5 %collective-permute-start.2 = (bf16[16,7168]{1,0:T(8,128)(2,1)S(1)}, bf16[16,7168]{1,0:T(8,128)(2,1)S(1)}, u32[]{:S(2)}, u32[]{:S(2)}) collective-permute-start(bf16[16,7168]{1,0:T(8,128)(2,1)S(1)} %get-tuple-element.37), channel_id=1, source_target_pairs={{0,4},{1,5},{2,6},{3,7},{4,0},{5,1},{6,2},{7,3},{8,12},{9,13},{10,... | collective-permute-start | bytes 688136 | tf_op jit(solution)/shard_map/ppermute | solution.py:377
  41.8 11.1 %collective-permute-start.3 = (bf16[16,7168]{1,0:T(8,128)(2,1)S(1)}, bf16[16,7168]{1,0:T(8,128)(2,1)S(1)}, u32[]{:S(2)}, u32[]{:S(2)}) collective-permute-start(bf16[16,7168]{1,0:T(8,128)(2,1)S(1)} %get-tuple-element.38), channel_id=1, source_target_pairs={{0,6},{1,7},{2,4},{3,5},{4,2},{5,3},{6,0},{7,1},{8,14},{9,15},{10,... | collective-permute-start | bytes 688136 | tf_op jit(solution)/shard_map/ppermute | solution.py:377
  53.0 4.6 %collective-permute-start.4 = (bf16[4,7168]{1,0:T(4,128)(2,1)S(1)}, bf16[4,7168]{1,0:T(4,128)(2,1)S(1)}, u32[]{:S(2)}, u32[]{:S(2)}) collective-permute-start(bf16[4,7168]{1,0:T(4,128)(2,1)S(1)} %get-tuple-element.40), channel_id=1, source_target_pairs={{0,8},{1,9},{2,10},{3,11},{4,12},{5,13},{6,14},{7,15},{8,0},{9,1},... | collective-permute-start | bytes 172040 | tf_op jit(solution)/shard_map/ppermute | solution.py:377
  53.8 6.1 %collective-permute-start.5 = (bf16[4,7168]{1,0:T(4,128)(2,1)S(1)}, bf16[4,7168]{1,0:T(4,128)(2,1)S(1)}, u32[]{:S(2)}, u32[]{:S(2)}) collective-permute-start(bf16[4,7168]{1,0:T(4,128)(2,1)S(1)} %get-tuple-element.41), channel_id=1, source_target_pairs={{0,16},{1,17},{2,18},{3,19},{4,20},{5,21},{6,22},{7,23},{8,24},{9,... | collective-permute-start | bytes 172040 | tf_op jit(solution)/shard_map/ppermute | solution.py:377
  54.8 6.1 %collective-permute-start.6 = (bf16[4,7168]{1,0:T(4,128)(2,1)S(1)}, bf16[4,7168]{1,0:T(4,128)(2,1)S(1)}, u32[]{:S(2)}, u32[]{:S(2)}) collective-permute-start(bf16[4,7168]{1,0:T(4,128)(2,1)S(1)} %get-tuple-element.42), channel_id=1, source_target_pairs={{0,24},{1,25},{2,26},{3,27},{4,28},{5,29},{6,30},{7,31},{8,16},{9,... | collective-permute-start | bytes 172040 | tf_op jit(solution)/shard_map/ppermute | solution.py:377
  61.8 4.5 %collective-permute-start.7 = (bf16[2,7168]{1,0:T(2,128)(2,1)S(1)}, bf16[2,7168]{1,0:T(2,128)(2,1)S(1)}, u32[]{:S(2)}, u32[]{:S(2)}) collective-permute-start(bf16[2,7168]{1,0:T(2,128)(2,1)S(1)} %get-tuple-element.44), channel_id=1, source_target_pairs={{0,8},{1,9},{2,10},{3,11},{4,12},{5,13},{6,14},{7,15},{8,0},{9,1},... | collective-permute-start | bytes 86024 | tf_op jit(solution)/shard_map/ppermute | solution.py:377
  62.6 4.8 %collective-permute-start.8 = (bf16[2,7168]{1,0:T(2,128)(2,1)S(1)}, bf16[2,7168]{1,0:T(2,128)(2,1)S(1)}, u32[]{:S(2)}, u32[]{:S(2)}) collective-permute-start(bf16[2,7168]{1,0:T(2,128)(2,1)S(1)} %get-tuple-element.45), channel_id=1, source_target_pairs={{0,16},{1,17},{2,18},{3,19},{4,20},{5,21},{6,22},{7,23},{8,24},{9,... | collective-permute-start | bytes 86024 | tf_op jit(solution)/shard_map/ppermute | solution.py:377
  64.9 5.7 %collective-permute-start.9 = (bf16[2,7168]{1,0:T(2,128)(2,1)S(1)}, bf16[2,7168]{1,0:T(2,128)(2,1)S(1)}, u32[]{:S(2)}, u32[]{:S(2)}) collective-permute-start(bf16[2,7168]{1,0:T(2,128)(2,1)S(1)} %get-tuple-element.46), channel_id=1, source_target_pairs={{0,24},{1,25},{2,26},{3,27},{4,28},{5,29},{6,30},{7,31},{8,16},{9,... | collective-permute-start | bytes 86024 | tf_op jit(solution)/shard_map/ppermute | solution.py:377
  70.7 4.9 %collective-permute-start.10 = (bf16[8,7168]{1,0:T(8,128)(2,1)S(1)}, bf16[8,7168]{1,0:T(8,128)(2,1)S(1)}, u32[]{:S(2)}, u32[]{:S(2)}) collective-permute-start(bf16[8,7168]{1,0:T(8,128)(2,1)S(1)} %stack_rows.1.refs_0_), channel_id=1, source_target_pairs={{0,2},{1,3},{2,0},{3,1},{4,6},{5,7},{6,4},{7,5},{8,10},{9,11},{10,... | collective-permute-start | bytes 344072 | tf_op jit(solution)/shard_map/ppermute | solution.py:377
  71.7 4.8 %collective-permute-start.11 = (bf16[8,7168]{1,0:T(8,128)(2,1)S(1)}, bf16[8,7168]{1,0:T(8,128)(2,1)S(1)}, u32[]{:S(2)}, u32[]{:S(2)}) collective-permute-start(bf16[8,7168]{1,0:T(8,128)(2,1)S(1)} %stack_rows.1.refs_0_), channel_id=1, source_target_pairs={{0,4},{1,5},{2,6},{3,7},{4,0},{5,1},{6,2},{7,3},{8,12},{9,13},{10,... | collective-permute-start | bytes 344072 | tf_op jit(solution)/shard_map/ppermute | solution.py:377
  72.8 5.7 %collective-permute-start.12 = (bf16[8,7168]{1,0:T(8,128)(2,1)S(1)}, bf16[8,7168]{1,0:T(8,128)(2,1)S(1)}, u32[]{:S(2)}, u32[]{:S(2)}) collective-permute-start(bf16[8,7168]{1,0:T(8,128)(2,1)S(1)} %stack_rows.1.refs_0_), channel_id=1, source_target_pairs={{0,6},{1,7},{2,4},{3,5},{4,2},{5,3},{6,0},{7,1},{8,14},{9,15},{10,... | collective-permute-start | bytes 344072 | tf_op jit(solution)/shard_map/ppermute | solution.py:377
  74.2 6.9 %collective-permute-start.13 = (bf16[8,7168]{1,0:T(8,128)(2,1)S(1)}, bf16[8,7168]{1,0:T(8,128)(2,1)S(1)}, u32[]{:S(2)}, u32[]{:S(2)}) collective-permute-start(bf16[8,7168]{1,0:T(8,128)(2,1)S(1)} %stack_rows.1.refs_0_), channel_id=1, source_target_pairs={{0,1},{1,0},{2,3},{3,2},{4,5},{5,4},{6,7},{7,6},{8,9},{9,8},{10,11... | collective-permute-start | bytes 344072 | tf_op jit(solution)/shard_map/ppermute | solution.py:377
  75.5 5.6 %collective-permute-start.14 = (bf16[8,7168]{1,0:T(8,128)(2,1)S(1)}, bf16[8,7168]{1,0:T(8,128)(2,1)S(1)}, u32[]{:S(2)}, u32[]{:S(2)}) collective-permute-start(bf16[8,7168]{1,0:T(8,128)(2,1)S(1)} %collective-permute-done.10.refs_1_), channel_id=1, source_target_pairs={{0,1},{1,0},{2,3},{3,2},{4,5},{5,4},{6,7},{7,6},{8,9},{9,8},{10,11... | collective-permute-start | bytes 344072 | tf_op jit(solution)/shard_map/ppermute | solution.py:377
  76.5 4.7 %collective-permute-start.15 = (bf16[8,7168]{1,0:T(8,128)(2,1)S(1)}, bf16[8,7168]{1,0:T(8,128)(2,1)S(1)}, u32[]{:S(2)}, u32[]{:S(2)}) collective-permute-start(bf16[8,7168]{1,0:T(8,128)(2,1)S(1)} %collective-permute-done.11.refs_2_), channel_id=1, source_target_pairs={{0,1},{1,0},{2,3},{3,2},{4,5},{5,4},{6,7},{7,6},{8,9},{9,8},{10,11... | collective-permute-start | bytes 344072 | tf_op jit(solution)/shard_map/ppermute | solution.py:377
  78.5 2.7 %collective-permute-start.16 = (bf16[8,7168]{1,0:T(8,128)(2,1)S(1)}, bf16[8,7168]{1,0:T(8,128)(2,1)S(1)}, u32[]{:S(2)}, u32[]{:S(2)}) collective-permute-start(bf16[8,7168]{1,0:T(8,128)(2,1)S(1)} %collective-permute-done.12.refs_3_), channel_id=1, source_target_pairs={{0,1},{1,0},{2,3},{3,2},{4,5},{5,4},{6,7},{7,6},{8,9},{9,8},{10,11... | collective-permute-start | bytes 344072 | tf_op jit(solution)/shard_map/ppermute | solution.py:377
  84.5 5.8 %collective-permute-start.18 = (bf16[8,7168]{1,0:T(8,128)(2,1)S(1)}, bf16[8,7168]{1,0:T(8,128)(2,1)S(1)}, u32[]{:S(2)}, u32[]{:S(2)}) collective-permute-start(bf16[8,7168]{1,0:T(8,128)(2,1)S(1)} %get-tuple-element.53), channel_id=1, source_target_pairs={{0,2},{1,3},{2,0},{3,1},{4,6},{5,7},{6,4},{7,5},{8,10},{9,11},{10,... | collective-permute-start | bytes 344072 | tf_op jit(solution)/shard_map/ppermute | solution.py:377
  85.8 7.6 %collective-permute-start.19 = (bf16[8,7168]{1,0:T(8,128)(2,1)S(1)}, bf16[8,7168]{1,0:T(8,128)(2,1)S(1)}, u32[]{:S(2)}, u32[]{:S(2)}) collective-permute-start(bf16[8,7168]{1,0:T(8,128)(2,1)S(1)} %get-tuple-element.54), channel_id=1, source_target_pairs={{0,4},{1,5},{2,6},{3,7},{4,0},{5,1},{6,2},{7,3},{8,12},{9,13},{10,... | collective-permute-start | bytes 344072 | tf_op jit(solution)/shard_map/ppermute | solution.py:377
  86.6 6.8 %collective-permute-start.20 = (bf16[8,7168]{1,0:T(8,128)(2,1)S(1)}, bf16[8,7168]{1,0:T(8,128)(2,1)S(1)}, u32[]{:S(2)}, u32[]{:S(2)}) collective-permute-start(bf16[8,7168]{1,0:T(8,128)(2,1)S(1)} %get-tuple-element.55), channel_id=1, source_target_pairs={{0,6},{1,7},{2,4},{3,5},{4,2},{5,3},{6,0},{7,1},{8,14},{9,15},{10,... | collective-permute-start | bytes 344072 | tf_op jit(solution)/shard_map/ppermute | solution.py:377
  93.4 4.6 %collective-permute-start.21 = (bf16[2,7168]{1,0:T(2,128)(2,1)S(1)}, bf16[2,7168]{1,0:T(2,128)(2,1)S(1)}, u32[]{:S(2)}, u32[]{:S(2)}) collective-permute-start(bf16[2,7168]{1,0:T(2,128)(2,1)S(1)} %get-tuple-element.57), channel_id=1, source_target_pairs={{0,8},{1,9},{2,10},{3,11},{4,12},{5,13},{6,14},{7,15},{8,0},{9,1},... | collective-permute-start | bytes 86024 | tf_op jit(solution)/shard_map/ppermute | solution.py:377
  93.5 4.8 %collective-permute-start.22 = (bf16[2,7168]{1,0:T(2,128)(2,1)S(1)}, bf16[2,7168]{1,0:T(2,128)(2,1)S(1)}, u32[]{:S(2)}, u32[]{:S(2)}) collective-permute-start(bf16[2,7168]{1,0:T(2,128)(2,1)S(1)} %get-tuple-element.58), channel_id=1, source_target_pairs={{0,16},{1,17},{2,18},{3,19},{4,20},{5,21},{6,22},{7,23},{8,24},{9,... | collective-permute-start | bytes 86024 | tf_op jit(solution)/shard_map/ppermute | solution.py:377
  95.6 5.7 %collective-permute-start.23 = (bf16[2,7168]{1,0:T(2,128)(2,1)S(1)}, bf16[2,7168]{1,0:T(2,128)(2,1)S(1)}, u32[]{:S(2)}, u32[]{:S(2)}) collective-permute-start(bf16[2,7168]{1,0:T(2,128)(2,1)S(1)} %get-tuple-element.59), channel_id=1, source_target_pairs={{0,24},{1,25},{2,26},{3,27},{4,28},{5,29},{6,30},{7,31},{8,16},{9,... | collective-permute-start | bytes 86024 | tf_op jit(solution)/shard_map/ppermute | solution.py:377
  (7 other events, 105.9 us)

commit v3 on v2

--- a/solution.py
+++ b/solution.py
@@ -37,54 +37,56 @@
     return pl.BlockSpec(shape, lambda *_: (0,) * len(shape))
 
 
-def attention_kernel(rows, lengths, q_ref, k_ref, o_ref, lat):
-    row = pl.program_id(0)
-    heads = q_ref.shape[2]
-    slots = k_ref.shape[2]
-    keys = k_ref[0]
-    scores = lax.dot_general(
-        q_ref[0], keys, (((0,), (0,)), ((), ())), preferred_element_type=F32
-    ) * ((VH + ROPE) ** -0.5)
-    position = lax.broadcasted_iota(jnp.int32, scores.shape, 1)
-    scores = jnp.where(position < lengths[row], scores, MASKED)
-    terms = jnp.exp(scores - jnp.max(scores, axis=1, keepdims=True))
-    total = jnp.sum(terms, axis=1, keepdims=True)
-    numerator = lax.dot_general(
-        terms.astype(BF16), keys[:LAT], (((1,), (1,)), ((), ())), preferred_element_type=F32
-    )
-    lat[pl.ds(pl.multiple_of(row * heads, heads), heads), :] = (numerator / total).astype(BF16)
-
-    @pl.when(row == rows - 1)
-    def _():
-        size = rows * heads
-        i = lax.broadcasted_iota(jnp.int32, (size, size), 0)
-        k = lax.broadcasted_iota(jnp.int32, (size, size), 1)
-        pick = jnp.where(k == (i % rows) * heads + i // rows, 1.0, 0.0).astype(BF16)
-        o_ref[...] = jnp.dot(pick, lat[...], preferred_element_type=F32).astype(BF16)
+def attention_kernel(lengths, q_hbm, k_hbm, o_ref, queries, keys, lat, sems):
+    rows, _, heads = queries.shape
+    copies = []
+    for r in range(rows):
+        for n, (src, dst) in enumerate(((q_hbm, queries), (k_hbm, keys))):
+            copy = pltpu.make_async_copy(src.at[r], dst.at[r], sems.at[2 * r + n])
+            copy.start()
+            copies.append(copy)
+    for r in range(rows):
+        copies[2 * r].wait()
+        copies[2 * r + 1].wait()
+        scores = lax.dot_general(
+            queries[r], keys[r], (((0,), (0,)), ((), ())), preferred_element_type=F32
+        ) * ((VH + ROPE) ** -0.5)
+        position = lax.broadcasted_iota(jnp.int32, scores.shape, 1)
+        scores = jnp.where(position < lengths[r], scores, MASKED)
+        terms = jnp.exp(scores - jnp.max(scores, axis=1, keepdims=True))
+        total = jnp.sum(terms, axis=1, keepdims=True)
+        numerator = lax.dot_general(
+            terms.astype(BF16), keys[r, :LAT], (((1,), (1,)), ((), ())), preferred_element_type=F32
+        )
+        lat[r * heads : (r + 1) * heads, :] = (numerator / total).astype(BF16)
+    size = rows * heads
+    i = lax.broadcasted_iota(jnp.int32, (size, 1), 0)
+    k = lax.broadcasted_iota(jnp.int32, (size, size), 1)
+    pick = jnp.where(k == (i % rows) * heads + i // rows, 1.0, 0.0).astype(BF16)
+    o_ref[...] = jnp.dot(pick, lat[...], preferred_element_type=F32).astype(BF16)
 
 
 def attention(queries, latent_cache, lengths):
     rows, heads, width = queries.shape
     slots = latent_cache.shape[1]
-    q_t = jnp.swapaxes(queries, 1, 2)
-    k_t = jnp.swapaxes(latent_cache, 1, 2)
-    return pl.pallas_call(
-        functools.partial(attention_kernel, rows),
-        grid=(rows,),
-        in_specs=[
-            SCALARS,
-            pl.BlockSpec((1, width, heads), lambda r: (r, 0, 0)),
-            pl.BlockSpec((1, width, slots), lambda r: (r, 0, 0)),
+    hbm = pl.BlockSpec(memory_space=pltpu.HBM)
+    return pl.pallas_call(
+        attention_kernel,
+        in_specs=[SCALARS, hbm, hbm],
+        out_specs=pl.BlockSpec(memory_space=pltpu.VMEM),
+        out_shape=sds((rows * heads, LAT), BF16),
+        scratch_shapes=[
+            pltpu.VMEM((rows, width, heads), BF16),
+            pltpu.VMEM((rows, width, slots), BF16),
+            pltpu.VMEM((rows * heads, LAT), BF16),
+            pltpu.SemaphoreType.DMA((2 * rows,)),
         ],
-        out_specs=whole((rows * heads, LAT)),
-        out_shape=sds((rows * heads, LAT), BF16),
-        scratch_shapes=[pltpu.VMEM((rows * heads, LAT), BF16)],
         compiler_params=params(),
         name="latent_attention",
     )(
         lengths,
-        in_hbm(q_t),
-        in_hbm(k_t),
+        in_hbm(jnp.swapaxes(queries, 1, 2)),
+        in_hbm(jnp.swapaxes(latent_cache, 1, 2)),
     )
 
 
@@ -130,91 +132,96 @@
     return result
 
 
-def project_kernel(planes, rows, me, x_ref, v_ref, w_ref, own_ref, other_ref, flat):
+def project_kernel(planes, rows, tiles, me, x_ref, v_ref, w_hbm, own_ref, other_ref, flat, w, sems):
+    tile = w.shape[2]
+    copies = []
+    for t in range(tiles):
+        copy = pltpu.make_async_copy(w_hbm.at[:, pl.ds(t * tile, tile)], w.at[t], sems.at[t])
+        copy.start()
+        copies.append(copy)
     heads = v_ref.shape[0]
-
-    @pl.when(pl.program_id(0) == 0)
-    def _():
-        count = flat.shape[0]
-        i = lax.broadcasted_iota(jnp.int32, (count, x_ref.shape[0]), 0)
-        k = lax.broadcasted_iota(jnp.int32, (count, x_ref.shape[0]), 1)
-        row = i % rows
-        plane = (i // rows) % planes
-        rest = i // (rows * planes)
-        home = me[0] ^ (plane * 8 + (rest % 4) * 2 + rest // 4)
-        target = home * (heads * rows) + row
-        for h in range(heads):
-            pick = jnp.where(k == target + h * rows, 1.0, 0.0).astype(BF16)
-            mine = jnp.dot(pick, x_ref[...], preferred_element_type=F32).astype(BF16)
-            flat[:, h * VH : (h + 1) * VH] = jnp.dot(
-                mine, v_ref[h], preferred_element_type=F32
-            ).astype(BF16)
-
-    out = jnp.dot(flat[...], w_ref[...], preferred_element_type=F32)
-    half = out.shape[0] // 2
-    own_ref[...] = out[:half]
-    other_ref[...] = out[half:].astype(BF16)
-
-
-def project(me, by_heads, value_up, out_proj, planes, rows):
+    count = flat.shape[0]
+    i = lax.broadcasted_iota(jnp.int32, (count, 1), 0)
+    k = lax.broadcasted_iota(jnp.int32, (count, x_ref.shape[0]), 1)
+    plane = (i // rows) % planes
+    rest = i // (rows * planes)
+    home = me[0] ^ (plane * 8 + (rest % 4) * 2 + rest // 4)
+    target = home * (heads * rows) + i % rows
+    for h in range(heads):
+        pick = jnp.where(k == target + h * rows, 1.0, 0.0).astype(BF16)
+        mine = jnp.dot(pick, x_ref[...], preferred_element_type=F32).astype(BF16)
+        flat[:, h * VH : (h + 1) * VH] = jnp.dot(
+            mine, v_ref[h], preferred_element_type=F32
+        ).astype(BF16)
+    half = count // 2
+    for t in range(tiles):
+        copies[t].wait()
+        at = slice(t * tile, (t + 1) * tile)
+        out = jnp.dot(flat[...], w[t], preferred_element_type=F32)
+        own_ref[:, at] = out[:half]
+        other_ref[:, at] = out[half:].astype(BF16)
+
+
+def project(me, by_heads, value_up, out_proj, planes, rows, tiles=7):
     count = planes * 8 * rows
     depth, features = out_proj.shape
-    tile = features // 7
     half = count // 2
-    return pl.pallas_call(
-        functools.partial(project_kernel, planes, rows),
-        grid=(features // tile,),
-        in_specs=[
-            SCALARS,
-            whole(by_heads.shape),
-            whole(value_up.shape),
-            pl.BlockSpec((depth, tile), lambda t: (0, t)),
+    vec = pl.BlockSpec(memory_space=pltpu.VMEM)
+    return pl.pallas_call(
+        functools.partial(project_kernel, planes, rows, tiles),
+        in_specs=[SCALARS, vec, vec, pl.BlockSpec(memory_space=pltpu.HBM)],
+        out_specs=[vec, vec],
+        out_shape=[sds((half, features), F32), sds((half, features), BF16)],
+        scratch_shapes=[
+            pltpu.VMEM((count, depth), BF16),
+            pltpu.VMEM((tiles, depth, features // tiles), BF16),
+            pltpu.SemaphoreType.DMA((tiles,)),
         ],
-        out_specs=[
-            pl.BlockSpec((half, tile), lambda t: (0, t)),
-            pl.BlockSpec((half, tile), lambda t: (0, t)),
-        ],
-        out_shape=[sds((half, features), F32), sds((half, features), BF16)],
-        scratch_shapes=[pltpu.VMEM((count, depth), BF16)],
         compiler_params=params(),
         name="projections",
     )(me, by_heads, value_up, in_hbm(out_proj))
 
 
-def add_kernel(arrived, parts, *refs):
-    total = refs[0][...]
-    for ref in refs[1 : 1 + arrived]:
-        total = total + ref[...].astype(F32)
-    outs = refs[1 + arrived :]
-    size = total.shape[0] // parts
-    outs[0][...] = total[:size]
-    for p in range(1, parts):
-        outs[p][...] = total[p * size : (p + 1) * size].astype(BF16)
-
-
-def add_and_cut(own, received, parts, name, steps=2):
+def add_kernel(arrived, parts, tile, *refs):
+    outs = refs[-parts:]
+    size = outs[0].shape[0]
+    for start in range(0, outs[0].shape[1], tile):
+        at = slice(start, start + tile)
+        for p in range(parts):
+            rows = slice(p * size, (p + 1) * size)
+            if arrived and size % 16 == 0:
+                total = refs[0][rows, at]
+                for ref in refs[1 : 1 + arrived]:
+                    total = total + ref[rows, at].astype(F32)
+            else:
+                if p == 0:
+                    full = refs[0][:, at]
+                    for ref in refs[1 : 1 + arrived]:
+                        full = full + ref[:, at].astype(F32)
+                total = full[rows]
+            outs[p][:, at] = total if p == 0 else total.astype(BF16)
+
+
+def add_and_cut(own, received, parts, name, after=()):
     count, features = own.shape
     size = count // parts
-    tile = features // steps
-    return pl.pallas_call(
-        functools.partial(add_kernel, len(received), parts),
-        grid=(steps,),
-        in_specs=[pl.BlockSpec((count, tile), lambda t: (0, t))] * (1 + len(received)),
-        out_specs=[pl.BlockSpec((size, tile), lambda t: (0, t))] * parts,
+    vec = pl.BlockSpec(memory_space=pltpu.VMEM)
+    return pl.pallas_call(
+        functools.partial(add_kernel, len(received), parts, 512),
+        in_specs=[vec] * (1 + len(received)) + [pl.BlockSpec(memory_space=pl.ANY)] * len(after),
+        out_specs=[vec] * parts,
         out_shape=[sds((size, features), F32)] + [sds((size, features), BF16)] * (parts - 1),
         compiler_params=params(),
         name=name,
-    )(own, *received)
-
-
-def norm_kernel(planes, cap, me, ids, own_ref, *refs):
-    received = refs[: planes - 1]
-    hidden_ref, gain_ref = refs[planes - 1 : planes + 1]
-    resid_ref = refs[planes + 1]
-    packs = refs[planes + 2 : 2 * planes + 2]
-    normed, packed = refs[2 * planes + 2 :]
-    total = own_ref[...]
-    for ref in received:
+    )(own, *received, *after)
+
+
+def norm_kernel(planes, cap, me, ids, *refs):
+    hidden_ref, gain_ref, resid_ref = refs[planes : planes + 3]
+    packs = refs[-2 - planes : -2]
+    normed, packed = refs[-2:]
+    total = refs[0][...]
+    for ref in refs[1:planes]:
         total = total + ref[...].astype(F32)
     resid = (hidden_ref[...].astype(F32) + total).astype(BF16)
     resid_ref[...] = resid
@@ -239,12 +246,12 @@
         packs[k][...] = packed[k * cap : (k + 1) * cap, :].astype(BF16)
 
 
-def norm_and_pack(me, ids, own, received, hidden, gain, planes, cap):
-    rows, features = own.shape
+def norm_and_pack(me, ids, sums, hidden, gain, planes, cap):
+    rows, features = hidden.shape
     vec = pl.BlockSpec(memory_space=pltpu.VMEM)
     return pl.pallas_call(
         functools.partial(norm_kernel, planes, cap),
-        in_specs=[SCALARS, SCALARS] + [vec] * (2 + planes),
+        in_specs=[SCALARS, SCALARS] + [vec] * (2 + len(sums)),
         out_specs=[vec] * (1 + planes),
         out_shape=[sds((rows, features), BF16)] + [sds((cap, features), BF16)] * planes,
         scratch_shapes=[
@@ -253,31 +260,31 @@
         ],
         compiler_params=params(),
         name="norm_and_pack",
-    )(me, ids, own, *received, hidden, gain)
-
-
-def stack_kernel(*refs):
+    )(me, ids, *sums, hidden, gain)
+
+
+def stack_kernel(count, *refs):
     wide = refs[-1]
     out = refs[-2]
     size = refs[0].shape[0]
-    for k, ref in enumerate(refs[:-2]):
+    for k, ref in enumerate(refs[:count]):
         wide[k * size : (k + 1) * size, :] = ref[...].astype(F32)
     out[...] = wide[...].astype(BF16)
 
 
-def stack(pieces):
+def stack(pieces, after):
     size, features = pieces[0].shape
     vec = pl.BlockSpec(memory_space=pltpu.VMEM)
     shape = (size * len(pieces), features)
     return pl.pallas_call(
-        stack_kernel,
-        in_specs=[vec] * len(pieces),
+        functools.partial(stack_kernel, len(pieces)),
+        in_specs=[vec] * len(pieces) + [pl.BlockSpec(memory_space=pl.ANY)] * len(after),
         out_specs=vec,
         out_shape=sds(shape, BF16),
         scratch_shapes=[pltpu.VMEM(shape, F32)],
         compiler_params=params(),
         name="stack_rows",
-    )(*pieces)
+    )(*pieces, *after)
 
 
 def expert_kernel(pieces, tiles, *refs):
@@ -386,17 +393,18 @@
     by_heads = lax.all_to_all(latents, "dp", split_axis=0, concat_axis=0, tiled=True)
     own, other = project(me, by_heads, value_up, out_proj, planes, rows)
     own, *out = add_and_cut(own, [swap(other, 1)], 4, "add_core")
-    gate_up, (down_proj,) = fetch([gate_up, down_proj], [(0, 2), (0, 1)], own)
-    own, *out = add_and_cut(own, over_chips(out), planes, "add_chips", 1)
+    own, *out = add_and_cut(own, over_chips(out), planes, "add_chips")
+    sums = [own] + over_planes(out)
     resid, mine, *out = norm_and_pack(
-        me, route_ids, own, over_planes(out), hidden_in, norm_gain[None], planes, cap
+        me, route_ids, sums, hidden_in, norm_gain[None], planes, cap
     )
-    picked = stack([mine] + over_planes(out))
+    gate_up, (down_proj,) = fetch([gate_up, down_proj], [(0, 2), (0, 1)], resid)
+    picked = stack([mine] + over_planes(out), gate_up[:1])
     chips = [picked] + over_chips([picked] * 3)
     pieces = chips + [swap(x, 1) for x in chips]
     own, other = expert(pieces, gate_up, down_proj)
     own, *out = add_and_cut(own, [swap(other, 1)], 4, "add_expert_core")
-    own, *out = add_and_cut(own, over_chips(out), planes, "add_expert_chips", 1)
+    own, *out = add_and_cut(own, over_chips(out), planes, "add_expert_chips")
     return combine(me, route_ids, route_weights, own, over_planes(out), resid, planes, cap)
 
 

time: 103 us -> 97.4 us (0.946)
  Pallas kernels: 19.7 us -> 15.9 us
  waiting for transfers between devices: 49.9 us -> 48.6 us
    pallas_call x7, Pallas kernels: 13.7 us -> 10 us  [the longest x1 5.22 us: attention(): pl.pallas_call(attention_kernel, in_specs=[SCALARS, hbm, hbm], out_specs=...]
    ppermute x24, waiting for transfers between devices: 34.4 us -> 33 us  [swap(): return lax.ppermute(x, 'dp', [(i, i ^ mask) for i in range(devices)])]
where the time goes in v3:
time: 97.4 us; the launch traced here: 97.2 us
  waiting for transfers between devices  48.6 us (50%)
  starting transfers between devices  31.6 us (32%)
  Pallas kernels  15.9 us (16%)
    ppermute x24, waiting for transfers between devices, swap(): return lax.ppermute(x, 'dp', [(i, i ^ mask) for i in range(devices)])  33 us
    ppermute x24, starting transfers between devices, swap(): return lax.ppermute(x, 'dp', [(i, i ^ mask) for i in range(devices)])  24.3 us
    all_to_all x1, waiting for transfers between devices, body(): lax.all_to_all(latents, 'dp', split_axis=0, concat_axis=0, tiled=True)  15.5 us
    all_to_all x1, starting transfers between devices, body(): lax.all_to_all(latents, 'dp', split_axis=0, concat_axis=0, tiled=True)  7.3 us
    pallas_call x1, Pallas kernels, attention(): pl.pallas_call(attention_kernel, in_specs=[SCALARS, hbm, hbm], out_specs=...  5.22 us
    pallas_call x1, Pallas kernels, project(): pl.pallas_call(functools.partial(project_kernel, planes, rows, tiles), in...  4.26 us
    pallas_call x1, Pallas kernels, fetch(): pl.pallas_call(functools.partial(fetch_kernel, parts), in_specs=[pl.Block...  2.63 us
  transfers between devices with their start and end apart: 25, of which 16 were waited for; matrix products, arithmetic and copies ran while one was open for 0% of the time, Pallas kernels for 3%

profile of v3, /device:TPU:0, one launch (start us, length us, event | category | flops | bytes accessed | tf_op | source)
XLA Modules:
  0.0 97.2 jit_solution(16965901953988238175)
XLA Ops:
  0.7 5.2 %latent_attention.1 = bf16[512,512]{1,0:T(8,128)(2,1)} custom-call(s32[4]{0:T(128)S(1)} %copy-done.2, bf16[4,576,128]{2,1,0:T(8,128)(2,1)} %bitcast.7, bf16[4,576,512]{2,1,0:T(8,128)(2,1)} %bitcast.6), custom_call_target="tpu_custom_call" | custom-call | tf_op jit(solution)/shard_map/latent_attention/pallas_call | solution.py:73
  5.9 7.3 %all-to-all-start = ((bf16[32,16,512]{2,1,0:T(8,128)(2,1)}), bf16[32,16,512]{2,1,0:T(8,128)(2,1)S(1)}, u32[]{:S(2)}, u32[]{:S(2)}) async-start(bf16[32,16,512]{2,1,0:T(8,128)(2,1)} %bitcast.3), calls=%async_computation | async-start | bytes 1048576 | tf_op jit(solution)/shard_map/all_to_all | solution.py:393
  13.2 15.5 %all-to-all-done = bf16[32,16,512]{2,1,0:T(8,128)(2,1)S(1)} async-done(((bf16[32,16,512]{2,1,0:T(8,128)(2,1)}), bf16[32,16,512]{2,1,0:T(8,128)(2,1)S(1)}, u32[]{:S(2)}, u32[]{:S(2)}) %all-to-all-start) | async-done | bytes 524320 | tf_op jit(solution)/shard_map/all_to_all | solution.py:393
  28.7 4.3 %projections.1 = (f32[64,7168]{1,0:T(8,128)S(1)}, bf16[64,7168]{1,0:T(8,128)(2,1)S(1)}) custom-call(s32[1]{0:T(128)} %bitcast.me, bf16[512,512]{1,0:T(8,128)(2,1)S(1)} %bitcast.5, bf16[4,512,128]{2,1,0:T(8,128)(2,1)S(1)} %copy-done, bf16[512,7168]{1,0:T(8,128)(2,1)} %w_hbm.1), custom_call_target="tpu_custom_call" | custom-call | tf_op jit(solution)/shard_map/projections/pallas_call | solution.py:170
  33.1 2.5 %collective-permute-done.refs_1_ = bf16[64,7168]{1,0:T(8,128)(2,1)S(1)} collective-permute-done((bf16[64,7168]{1,0:T(8,128)(2,1)S(1)}, bf16[64,7168]{1,0:T(8,128)(2,1)S(1)}, u32[]{:S(2)}, u32[]{:S(2)}) %collective-permute-start) | collective-permute-done | bytes 917536 | tf_op jit(solution)/shard_map/ppermute | solution.py:384
  36.7 1.5 %collective-permute-start.2 = (bf16[16,7168]{1,0:T(8,128)(2,1)S(1)}, bf16[16,7168]{1,0:T(8,128)(2,1)S(1)}, u32[]{:S(2)}, u32[]{:S(2)}) collective-permute-start(bf16[16,7168]{1,0:T(8,128)(2,1)S(1)} %get-tuple-element.37), channel_id=1, source_target_pairs={{0,4},{1,5},{2,6},{3,7},{4,0},{5,1},{6,2},{7,3},{8,12},{9,13},{10,... | collective-permute-start | bytes 688136 | tf_op jit(solution)/shard_map/ppermute | solution.py:384
  39.3 5.0 %collective-permute-done.1.refs_1_ = bf16[16,7168]{1,0:T(8,128)(2,1)S(1)} collective-permute-done((bf16[16,7168]{1,0:T(8,128)(2,1)S(1)}, bf16[16,7168]{1,0:T(8,128)(2,1)S(1)}, u32[]{:S(2)}, u32[]{:S(2)}) %collective-permute-start.1) | collective-permute-done | bytes 229408 | tf_op jit(solution)/shard_map/ppermute | solution.py:384
  44.2 5.0 %collective-permute-done.2.refs_2_ = bf16[16,7168]{1,0:T(8,128)(2,1)S(1)} collective-permute-done((bf16[16,7168]{1,0:T(8,128)(2,1)S(1)}, bf16[16,7168]{1,0:T(8,128)(2,1)S(1)}, u32[]{:S(2)}, u32[]{:S(2)}) %collective-permute-start.2) | collective-permute-done | bytes 229408 | tf_op jit(solution)/shard_map/ppermute | solution.py:384
  51.2 2.6 %collective-permute-start.6 = (bf16[4,7168]{1,0:T(4,128)(2,1)S(1)}, bf16[4,7168]{1,0:T(4,128)(2,1)S(1)}, u32[]{:S(2)}, u32[]{:S(2)}) collective-permute-start(bf16[4,7168]{1,0:T(4,128)(2,1)S(1)} %get-tuple-element.42), channel_id=1, source_target_pairs={{0,24},{1,25},{2,26},{3,27},{4,28},{5,29},{6,30},{7,31},{8,16},{9,... | collective-permute-start | bytes 172040 | tf_op jit(solution)/shard_map/ppermute | solution.py:384
  54.0 2.3 %collective-permute-done.5.refs_2_ = bf16[4,7168]{1,0:T(4,128)(2,1)S(1)} collective-permute-done((bf16[4,7168]{1,0:T(4,128)(2,1)S(1)}, bf16[4,7168]{1,0:T(4,128)(2,1)S(1)}, u32[]{:S(2)}, u32[]{:S(2)}) %collective-permute-start.5) | collective-permute-done | bytes 57376 | tf_op jit(solution)/shard_map/ppermute | solution.py:384
  59.0 2.3 %collective-permute-start.8 = (bf16[2,7168]{1,0:T(2,128)(2,1)S(1)}, bf16[2,7168]{1,0:T(2,128)(2,1)S(1)}, u32[]{:S(2)}, u32[]{:S(2)}) collective-permute-start(bf16[2,7168]{1,0:T(2,128)(2,1)S(1)} %get-tuple-element.45), channel_id=1, source_target_pairs={{0,16},{1,17},{2,18},{3,19},{4,20},{5,21},{6,22},{7,23},{8,24},{9,... | collective-permute-start | bytes 86024 | tf_op jit(solution)/shard_map/ppermute | solution.py:384
  62.6 2.6 %fetch_weights.1 = (bf16[7168,128]{1,0:T(8,128)(2,1)S(1)}, bf16[7168,128]{1,0:T(8,128)(2,1)S(1)}, bf16[128,7168]{1,0:T(8,128)(2,1)S(1)}) custom-call(bf16[2,7168,128]{2,1,0:T(8,128)(2,1)} %refs_0_.1, bf16[128,7168]{1,0:T(8,128)(2,1)} %refs_1_.1, bf16[4,7168]{1,0:T(4,128)(2,1)S(1)} %get-tuple-element.47.refs_2_.refs_3_), custom_call_target="tpu_custom_call" | custom-call | tf_op jit(solution)/shard_map/fetch_weights/pallas_call | solution.py:118
  65.3 1.7 %collective-permute-done.9.refs_3_ = bf16[2,7168]{1,0:T(2,128)(2,1)S(1)} collective-permute-done((bf16[2,7168]{1,0:T(2,128)(2,1)S(1)}, bf16[2,7168]{1,0:T(2,128)(2,1)S(1)}, u32[]{:S(2)}, u32[]{:S(2)}) %collective-permute-start.9) | collective-permute-done | bytes 28704 | tf_op jit(solution)/shard_map/ppermute | solution.py:384
  69.3 1.4 %collective-permute-start.12 = (bf16[8,7168]{1,0:T(8,128)(2,1)S(1)}, bf16[8,7168]{1,0:T(8,128)(2,1)S(1)}, u32[]{:S(2)}, u32[]{:S(2)}) collective-permute-start(bf16[8,7168]{1,0:T(8,128)(2,1)S(1)} %stack_rows.1.refs_0_), channel_id=1, source_target_pairs={{0,6},{1,7},{2,4},{3,5},{4,2},{5,3},{6,0},{7,1},{8,14},{9,15},{10,... | collective-permute-start | bytes 344072 | tf_op jit(solution)/shard_map/ppermute | solution.py:384
  72.9 2.0 %collective-permute-done.12.refs_3_ = bf16[8,7168]{1,0:T(8,128)(2,1)S(1)} collective-permute-done((bf16[8,7168]{1,0:T(8,128)(2,1)S(1)}, bf16[8,7168]{1,0:T(8,128)(2,1)S(1)}, u32[]{:S(2)}, u32[]{:S(2)}) %collective-permute-start.12) | collective-permute-done | bytes 114720 | tf_op jit(solution)/shard_map/ppermute | solution.py:384
  75.0 1.3 %collective-permute-done.16.refs_7_ = bf16[8,7168]{1,0:T(8,128)(2,1)S(1)} collective-permute-done((bf16[8,7168]{1,0:T(8,128)(2,1)S(1)}, bf16[8,7168]{1,0:T(8,128)(2,1)S(1)}, u32[]{:S(2)}, u32[]{:S(2)}) %collective-permute-start.16) | collective-permute-done | bytes 114720 | tf_op jit(solution)/shard_map/ppermute | solution.py:384
  77.5 1.7 %collective-permute-done.17.refs_1_ = bf16[32,7168]{1,0:T(8,128)(2,1)S(1)} collective-permute-done((bf16[32,7168]{1,0:T(8,128)(2,1)S(1)}, bf16[32,7168]{1,0:T(8,128)(2,1)S(1)}, u32[]{:S(2)}, u32[]{:S(2)}) %collective-permute-start.17) | collective-permute-done | bytes 458784 | tf_op jit(solution)/shard_map/ppermute | solution.py:384
  81.3 1.5 %collective-permute-start.20 = (bf16[8,7168]{1,0:T(8,128)(2,1)S(1)}, bf16[8,7168]{1,0:T(8,128)(2,1)S(1)}, u32[]{:S(2)}, u32[]{:S(2)}) collective-permute-start(bf16[8,7168]{1,0:T(8,128)(2,1)S(1)} %get-tuple-element.56), channel_id=1, source_target_pairs={{0,6},{1,7},{2,4},{3,5},{4,2},{5,3},{6,0},{7,1},{8,14},{9,15},{10,... | collective-permute-start | bytes 344072 | tf_op jit(solution)/shard_map/ppermute | solution.py:384
  82.8 2.1 %collective-permute-done.18.refs_1_ = bf16[8,7168]{1,0:T(8,128)(2,1)S(1)} collective-permute-done((bf16[8,7168]{1,0:T(8,128)(2,1)S(1)}, bf16[8,7168]{1,0:T(8,128)(2,1)S(1)}, u32[]{:S(2)}, u32[]{:S(2)}) %collective-permute-start.18) | collective-permute-done | bytes 114720 | tf_op jit(solution)/shard_map/ppermute | solution.py:384
  84.9 3.0 %collective-permute-done.19.refs_2_ = bf16[8,7168]{1,0:T(8,128)(2,1)S(1)} collective-permute-done((bf16[8,7168]{1,0:T(8,128)(2,1)S(1)}, bf16[8,7168]{1,0:T(8,128)(2,1)S(1)}, u32[]{:S(2)}, u32[]{:S(2)}) %collective-permute-start.19) | collective-permute-done | bytes 114720 | tf_op jit(solution)/shard_map/ppermute | solution.py:384
  88.1 2.0 %collective-permute-start.22 = (bf16[2,7168]{1,0:T(2,128)(2,1)S(1)}, bf16[2,7168]{1,0:T(2,128)(2,1)S(1)}, u32[]{:S(2)}, u32[]{:S(2)}) collective-permute-start(bf16[2,7168]{1,0:T(2,128)(2,1)S(1)} %get-tuple-element.59), channel_id=1, source_target_pairs={{0,16},{1,17},{2,18},{3,19},{4,20},{5,21},{6,22},{7,23},{8,24},{9,... | collective-permute-start | bytes 86024 | tf_op jit(solution)/shard_map/ppermute | solution.py:384
  90.1 2.3 %collective-permute-start.23 = (bf16[2,7168]{1,0:T(2,128)(2,1)S(1)}, bf16[2,7168]{1,0:T(2,128)(2,1)S(1)}, u32[]{:S(2)}, u32[]{:S(2)}) collective-permute-start(bf16[2,7168]{1,0:T(2,128)(2,1)S(1)} %get-tuple-element.60), channel_id=1, source_target_pairs={{0,24},{1,25},{2,26},{3,27},{4,28},{5,29},{6,30},{7,31},{8,16},{9,... | collective-permute-start | bytes 86024 | tf_op jit(solution)/shard_map/ppermute | solution.py:384
  93.2 2.6 %collective-permute-done.23.refs_2_ = bf16[2,7168]{1,0:T(2,128)(2,1)S(1)} collective-permute-done((bf16[2,7168]{1,0:T(2,128)(2,1)S(1)}, bf16[2,7168]{1,0:T(2,128)(2,1)S(1)}, u32[]{:S(2)}, u32[]{:S(2)}) %collective-permute-start.23) | collective-permute-done | bytes 28704 | tf_op jit(solution)/shard_map/ppermute | solution.py:384
  95.8 1.4 %combine.1 = bf16[4,7168]{1,0:T(4,128)(2,1)} custom-call(s32[1]{0:T(128)} %bitcast.me, s32[4,2]{1,0:T(4,128)S(1)} %copy.13.ids, f32[4,2]{1,0:T(4,128)S(1)} %copy.14.weights, f32[2,7168]{1,0:T(2,128)S(1)} %get-tuple-element.57.own_ref, bf16[2,7168]{1,0:T(2,128)(2,1)S(1)} %collective-permute-done.21.refs_0_, ...), custom_call_target="tpu_custom_call" | custom-call | tf_op jit(solution)/shard_map/combine/pallas_call | solution.py:349
  (52 shorter events, 17.9 us)
Async XLA Ops:
  5.9 22.9 %all-to-all-start = ((bf16[32,16,512]{2,1,0:T(8,128)(2,1)}), bf16[32,16,512]{2,1,0:T(8,128)(2,1)S(1)}, u32[]{:S(2)}, u32[]{:S(2)}) async-start(bf16[32,16,512]{2,1,0:T(8,128)(2,1)} %bitcast.3), calls=%async_computation | async-start | bytes 1048576 | tf_op jit(solution)/shard_map/all_to_all | solution.py:393
  33.0 2.5 %collective-permute-start = (bf16[64,7168]{1,0:T(8,128)(2,1)S(1)}, bf16[64,7168]{1,0:T(8,128)(2,1)S(1)}, u32[]{:S(2)}, u32[]{:S(2)}) collective-permute-start(bf16[64,7168]{1,0:T(8,128)(2,1)S(1)} %get-tuple-element.34), channel_id=1, source_target_pairs={{0,1},{1,0},{2,3},{3,2},{4,5},{5,4},{6,7},{7,6},{8,9},{9,8},{10,11... | collective-permute-start | bytes 2752520 | tf_op jit(solution)/shard_map/ppermute | solution.py:384
  35.7 8.5 %collective-permute-start.1 = (bf16[16,7168]{1,0:T(8,128)(2,1)S(1)}, bf16[16,7168]{1,0:T(8,128)(2,1)S(1)}, u32[]{:S(2)}, u32[]{:S(2)}) collective-permute-start(bf16[16,7168]{1,0:T(8,128)(2,1)S(1)} %get-tuple-element.36), channel_id=1, source_target_pairs={{0,2},{1,3},{2,0},{3,1},{4,6},{5,7},{6,4},{7,5},{8,10},{9,11},{10,... | collective-permute-start | bytes 688136 | tf_op jit(solution)/shard_map/ppermute | solution.py:384
  36.7 12.5 %collective-permute-start.2 = (bf16[16,7168]{1,0:T(8,128)(2,1)S(1)}, bf16[16,7168]{1,0:T(8,128)(2,1)S(1)}, u32[]{:S(2)}, u32[]{:S(2)}) collective-permute-start(bf16[16,7168]{1,0:T(8,128)(2,1)S(1)} %get-tuple-element.37), channel_id=1, source_target_pairs={{0,4},{1,5},{2,6},{3,7},{4,0},{5,1},{6,2},{7,3},{8,12},{9,13},{10,... | collective-permute-start | bytes 688136 | tf_op jit(solution)/shard_map/ppermute | solution.py:384
  38.2 11.0 %collective-permute-start.3 = (bf16[16,7168]{1,0:T(8,128)(2,1)S(1)}, bf16[16,7168]{1,0:T(8,128)(2,1)S(1)}, u32[]{:S(2)}, u32[]{:S(2)}) collective-permute-start(bf16[16,7168]{1,0:T(8,128)(2,1)S(1)} %get-tuple-element.38), channel_id=1, source_target_pairs={{0,6},{1,7},{2,4},{3,5},{4,2},{5,3},{6,0},{7,1},{8,14},{9,15},{10,... | collective-permute-start | bytes 688136 | tf_op jit(solution)/shard_map/ppermute | solution.py:384
  49.4 4.6 %collective-permute-start.4 = (bf16[4,7168]{1,0:T(4,128)(2,1)S(1)}, bf16[4,7168]{1,0:T(4,128)(2,1)S(1)}, u32[]{:S(2)}, u32[]{:S(2)}) collective-permute-start(bf16[4,7168]{1,0:T(4,128)(2,1)S(1)} %get-tuple-element.40), channel_id=1, source_target_pairs={{0,8},{1,9},{2,10},{3,11},{4,12},{5,13},{6,14},{7,15},{8,0},{9,1},... | collective-permute-start | bytes 172040 | tf_op jit(solution)/shard_map/ppermute | solution.py:384
  50.2 6.1 %collective-permute-start.5 = (bf16[4,7168]{1,0:T(4,128)(2,1)S(1)}, bf16[4,7168]{1,0:T(4,128)(2,1)S(1)}, u32[]{:S(2)}, u32[]{:S(2)}) collective-permute-start(bf16[4,7168]{1,0:T(4,128)(2,1)S(1)} %get-tuple-element.41), channel_id=1, source_target_pairs={{0,16},{1,17},{2,18},{3,19},{4,20},{5,21},{6,22},{7,23},{8,24},{9,... | collective-permute-start | bytes 172040 | tf_op jit(solution)/shard_map/ppermute | solution.py:384
  51.2 6.1 %collective-permute-start.6 = (bf16[4,7168]{1,0:T(4,128)(2,1)S(1)}, bf16[4,7168]{1,0:T(4,128)(2,1)S(1)}, u32[]{:S(2)}, u32[]{:S(2)}) collective-permute-start(bf16[4,7168]{1,0:T(4,128)(2,1)S(1)} %get-tuple-element.42), channel_id=1, source_target_pairs={{0,24},{1,25},{2,26},{3,27},{4,28},{5,29},{6,30},{7,31},{8,16},{9,... | collective-permute-start | bytes 172040 | tf_op jit(solution)/shard_map/ppermute | solution.py:384
  58.2 7.1 %collective-permute-start.7 = (bf16[2,7168]{1,0:T(2,128)(2,1)S(1)}, bf16[2,7168]{1,0:T(2,128)(2,1)S(1)}, u32[]{:S(2)}, u32[]{:S(2)}) collective-permute-start(bf16[2,7168]{1,0:T(2,128)(2,1)S(1)} %get-tuple-element.44), channel_id=1, source_target_pairs={{0,8},{1,9},{2,10},{3,11},{4,12},{5,13},{6,14},{7,15},{8,0},{9,1},... | collective-permute-start | bytes 86024 | tf_op jit(solution)/shard_map/ppermute | solution.py:384
  59.0 6.3 %collective-permute-start.8 = (bf16[2,7168]{1,0:T(2,128)(2,1)S(1)}, bf16[2,7168]{1,0:T(2,128)(2,1)S(1)}, u32[]{:S(2)}, u32[]{:S(2)}) collective-permute-start(bf16[2,7168]{1,0:T(2,128)(2,1)S(1)} %get-tuple-element.45), channel_id=1, source_target_pairs={{0,16},{1,17},{2,18},{3,19},{4,20},{5,21},{6,22},{7,23},{8,24},{9,... | collective-permute-start | bytes 86024 | tf_op jit(solution)/shard_map/ppermute | solution.py:384
  61.4 5.7 %collective-permute-start.9 = (bf16[2,7168]{1,0:T(2,128)(2,1)S(1)}, bf16[2,7168]{1,0:T(2,128)(2,1)S(1)}, u32[]{:S(2)}, u32[]{:S(2)}) collective-permute-start(bf16[2,7168]{1,0:T(2,128)(2,1)S(1)} %get-tuple-element.46), channel_id=1, source_target_pairs={{0,24},{1,25},{2,26},{3,27},{4,28},{5,29},{6,30},{7,31},{8,16},{9,... | collective-permute-start | bytes 86024 | tf_op jit(solution)/shard_map/ppermute | solution.py:384
  67.1 4.9 %collective-permute-start.10 = (bf16[8,7168]{1,0:T(8,128)(2,1)S(1)}, bf16[8,7168]{1,0:T(8,128)(2,1)S(1)}, u32[]{:S(2)}, u32[]{:S(2)}) collective-permute-start(bf16[8,7168]{1,0:T(8,128)(2,1)S(1)} %stack_rows.1.refs_0_), channel_id=1, source_target_pairs={{0,2},{1,3},{2,0},{3,1},{4,6},{5,7},{6,4},{7,5},{8,10},{9,11},{10,... | collective-permute-start | bytes 344072 | tf_op jit(solution)/shard_map/ppermute | solution.py:384
  68.1 4.8 %collective-permute-start.11 = (bf16[8,7168]{1,0:T(8,128)(2,1)S(1)}, bf16[8,7168]{1,0:T(8,128)(2,1)S(1)}, u32[]{:S(2)}, u32[]{:S(2)}) collective-permute-start(bf16[8,7168]{1,0:T(8,128)(2,1)S(1)} %stack_rows.1.refs_0_), channel_id=1, source_target_pairs={{0,4},{1,5},{2,6},{3,7},{4,0},{5,1},{6,2},{7,3},{8,12},{9,13},{10,... | collective-permute-start | bytes 344072 | tf_op jit(solution)/shard_map/ppermute | solution.py:384
  69.3 5.7 %collective-permute-start.12 = (bf16[8,7168]{1,0:T(8,128)(2,1)S(1)}, bf16[8,7168]{1,0:T(8,128)(2,1)S(1)}, u32[]{:S(2)}, u32[]{:S(2)}) collective-permute-start(bf16[8,7168]{1,0:T(8,128)(2,1)S(1)} %stack_rows.1.refs_0_), channel_id=1, source_target_pairs={{0,6},{1,7},{2,4},{3,5},{4,2},{5,3},{6,0},{7,1},{8,14},{9,15},{10,... | collective-permute-start | bytes 344072 | tf_op jit(solution)/shard_map/ppermute | solution.py:384
  70.7 4.3 %collective-permute-start.13 = (bf16[8,7168]{1,0:T(8,128)(2,1)S(1)}, bf16[8,7168]{1,0:T(8,128)(2,1)S(1)}, u32[]{:S(2)}, u32[]{:S(2)}) collective-permute-start(bf16[8,7168]{1,0:T(8,128)(2,1)S(1)} %stack_rows.1.refs_0_), channel_id=1, source_target_pairs={{0,1},{1,0},{2,3},{3,2},{4,5},{5,4},{6,7},{7,6},{8,9},{9,8},{10,11... | collective-permute-start | bytes 344072 | tf_op jit(solution)/shard_map/ppermute | solution.py:384
  72.0 3.0 %collective-permute-start.14 = (bf16[8,7168]{1,0:T(8,128)(2,1)S(1)}, bf16[8,7168]{1,0:T(8,128)(2,1)S(1)}, u32[]{:S(2)}, u32[]{:S(2)}) collective-permute-start(bf16[8,7168]{1,0:T(8,128)(2,1)S(1)} %collective-permute-done.10.refs_1_), channel_id=1, source_target_pairs={{0,1},{1,0},{2,3},{3,2},{4,5},{5,4},{6,7},{7,6},{8,9},{9,8},{10,11... | collective-permute-start | bytes 344072 | tf_op jit(solution)/shard_map/ppermute | solution.py:384
  72.9 2.0 %collective-permute-start.15 = (bf16[8,7168]{1,0:T(8,128)(2,1)S(1)}, bf16[8,7168]{1,0:T(8,128)(2,1)S(1)}, u32[]{:S(2)}, u32[]{:S(2)}) collective-permute-start(bf16[8,7168]{1,0:T(8,128)(2,1)S(1)} %collective-permute-done.11.refs_2_), channel_id=1, source_target_pairs={{0,1},{1,0},{2,3},{3,2},{4,5},{5,4},{6,7},{7,6},{8,9},{9,8},{10,11... | collective-permute-start | bytes 344072 | tf_op jit(solution)/shard_map/ppermute | solution.py:384
  77.3 1.9 %collective-permute-start.17 = (bf16[32,7168]{1,0:T(8,128)(2,1)S(1)}, bf16[32,7168]{1,0:T(8,128)(2,1)S(1)}, u32[]{:S(2)}, u32[]{:S(2)}) collective-permute-start(bf16[32,7168]{1,0:T(8,128)(2,1)S(1)} %get-tuple-element.52), channel_id=1, source_target_pairs={{0,1},{1,0},{2,3},{3,2},{4,5},{5,4},{6,7},{7,6},{8,9},{9,8},{10,11... | collective-permute-start | bytes 1376264 | tf_op jit(solution)/shard_map/ppermute | solution.py:384
  79.3 5.6 %collective-permute-start.18 = (bf16[8,7168]{1,0:T(8,128)(2,1)S(1)}, bf16[8,7168]{1,0:T(8,128)(2,1)S(1)}, u32[]{:S(2)}, u32[]{:S(2)}) collective-permute-start(bf16[8,7168]{1,0:T(8,128)(2,1)S(1)} %get-tuple-element.54), channel_id=1, source_target_pairs={{0,2},{1,3},{2,0},{3,1},{4,6},{5,7},{6,4},{7,5},{8,10},{9,11},{10,... | collective-permute-start | bytes 344072 | tf_op jit(solution)/shard_map/ppermute | solution.py:384
  80.5 7.4 %collective-permute-start.19 = (bf16[8,7168]{1,0:T(8,128)(2,1)S(1)}, bf16[8,7168]{1,0:T(8,128)(2,1)S(1)}, u32[]{:S(2)}, u32[]{:S(2)}) collective-permute-start(bf16[8,7168]{1,0:T(8,128)(2,1)S(1)} %get-tuple-element.55), channel_id=1, source_target_pairs={{0,4},{1,5},{2,6},{3,7},{4,0},{5,1},{6,2},{7,3},{8,12},{9,13},{10,... | collective-permute-start | bytes 344072 | tf_op jit(solution)/shard_map/ppermute | solution.py:384
  81.3 6.6 %collective-permute-start.20 = (bf16[8,7168]{1,0:T(8,128)(2,1)S(1)}, bf16[8,7168]{1,0:T(8,128)(2,1)S(1)}, u32[]{:S(2)}, u32[]{:S(2)}) collective-permute-start(bf16[8,7168]{1,0:T(8,128)(2,1)S(1)} %get-tuple-element.56), channel_id=1, source_target_pairs={{0,6},{1,7},{2,4},{3,5},{4,2},{5,3},{6,0},{7,1},{8,14},{9,15},{10,... | collective-permute-start | bytes 344072 | tf_op jit(solution)/shard_map/ppermute | solution.py:384
  88.0 4.6 %collective-permute-start.21 = (bf16[2,7168]{1,0:T(2,128)(2,1)S(1)}, bf16[2,7168]{1,0:T(2,128)(2,1)S(1)}, u32[]{:S(2)}, u32[]{:S(2)}) collective-permute-start(bf16[2,7168]{1,0:T(2,128)(2,1)S(1)} %get-tuple-element.58), channel_id=1, source_target_pairs={{0,8},{1,9},{2,10},{3,11},{4,12},{5,13},{6,14},{7,15},{8,0},{9,1},... | collective-permute-start | bytes 86024 | tf_op jit(solution)/shard_map/ppermute | solution.py:384
  88.1 5.1 %collective-permute-start.22 = (bf16[2,7168]{1,0:T(2,128)(2,1)S(1)}, bf16[2,7168]{1,0:T(2,128)(2,1)S(1)}, u32[]{:S(2)}, u32[]{:S(2)}) collective-permute-start(bf16[2,7168]{1,0:T(2,128)(2,1)S(1)} %get-tuple-element.59), channel_id=1, source_target_pairs={{0,16},{1,17},{2,18},{3,19},{4,20},{5,21},{6,22},{7,23},{8,24},{9,... | collective-permute-start | bytes 86024 | tf_op jit(solution)/shard_map/ppermute | solution.py:384
  90.1 5.7 %collective-permute-start.23 = (bf16[2,7168]{1,0:T(2,128)(2,1)S(1)}, bf16[2,7168]{1,0:T(2,128)(2,1)S(1)}, u32[]{:S(2)}, u32[]{:S(2)}) collective-permute-start(bf16[2,7168]{1,0:T(2,128)(2,1)S(1)} %get-tuple-element.60), channel_id=1, source_target_pairs={{0,24},{1,25},{2,26},{3,27},{4,28},{5,29},{6,30},{7,31},{8,16},{9,... | collective-permute-start | bytes 86024 | tf_op jit(solution)/shard_map/ppermute | solution.py:384
  (7 other events, 103.6 us)

commit v4 on v3

--- a/solution.py
+++ b/solution.py
@@ -132,7 +132,8 @@
     return result
 
 
-def project_kernel(planes, rows, tiles, me, x_ref, v_ref, w_hbm, own_ref, other_ref, flat, w, sems):
+def project_kernel(planes, rows, tiles, me, x_ref, v_ref, w_hbm, *refs):
+    own_ref, other_ref, flat, w, sems = refs[-5:]
     tile = w.shape[2]
     copies = []
     for t in range(tiles):
@@ -162,14 +163,15 @@
         other_ref[:, at] = out[half:].astype(BF16)
 
 
-def project(me, by_heads, value_up, out_proj, planes, rows, tiles=7):
+def project(me, by_heads, value_up, out_proj, planes, rows, after, tiles=7):
     count = planes * 8 * rows
     depth, features = out_proj.shape
     half = count // 2
     vec = pl.BlockSpec(memory_space=pltpu.VMEM)
     return pl.pallas_call(
         functools.partial(project_kernel, planes, rows, tiles),
-        in_specs=[SCALARS, vec, vec, pl.BlockSpec(memory_space=pltpu.HBM)],
+        in_specs=[SCALARS, vec, vec, pl.BlockSpec(memory_space=pltpu.HBM)]
+        + [pl.BlockSpec(memory_space=pl.ANY)] * len(after),
         out_specs=[vec, vec],
         out_shape=[sds((half, features), F32), sds((half, features), BF16)],
         scratch_shapes=[
@@ -179,7 +181,7 @@
         ],
         compiler_params=params(),
         name="projections",
-    )(me, by_heads, value_up, in_hbm(out_proj))
+    )(me, by_heads, value_up, in_hbm(out_proj), *after)
 
 
 def add_kernel(arrived, parts, tile, *refs):
@@ -216,75 +218,162 @@
     )(own, *received, *after)
 
 
-def norm_kernel(planes, cap, me, ids, *refs):
-    hidden_ref, gain_ref, resid_ref = refs[planes : planes + 3]
-    packs = refs[-2 - planes : -2]
-    normed, packed = refs[-2:]
+def routes_kernel(ids, weights, unused, out_ref):
+    rows, picks = ids.shape
+    i = lax.broadcasted_iota(jnp.int32, out_ref.shape, 0)
+    k = lax.broadcasted_iota(jnp.int32, out_ref.shape, 1)
+    table = jnp.zeros(out_ref.shape, F32)
+    for r in range(rows):
+        for t in range(picks):
+            table = jnp.where((i == r) & (k == t), ids[r, t].astype(F32), table)
+            table = jnp.where((i == r) & (k == picks + t), weights[r, t], table)
+    out_ref[...] = table
+
+
+def routes(ids, weights, after):
+    return pl.pallas_call(
+        routes_kernel,
+        in_specs=[SCALARS, SCALARS, pl.BlockSpec(memory_space=pl.ANY)],
+        out_specs=pl.BlockSpec(memory_space=pltpu.VMEM),
+        out_shape=sds((8, 128), F32),
+        compiler_params=params(),
+        name="routes",
+    )(ids, weights, after)
+
+
+def column(values, count):
+    i = lax.broadcasted_iota(jnp.int32, (count, 1), 0)
+    out = jnp.full((count, 1), values[0])
+    for n, value in enumerate(values[1:], 1):
+        out = jnp.where(i == n, value, out)
+    return out
+
+
+def tables_kernel(rows, picks, planes, cap, me, ids, *refs):
+    homes = refs[:planes]
+    pick_ref, weight_ref, merge_ref = refs[planes:]
+    plane = me[0] // 8
+    found = {}
+    for k in range(planes):
+        expert = (plane ^ k).astype(F32)
+        for h in range(planes):
+            home = homes[h]
+            places = [jnp.int32(-1)] * cap
+            scales = [jnp.float32(0.0)] * cap
+            seen = jnp.int32(0)
+            for r in range(rows):
+                has = home[r, 0] == expert
+                scale = home[r, picks]
+                for t in range(1, picks):
+                    here = home[r, t] == expert
+                    scale = jnp.where(here, home[r, picks + t], scale)
+                    has = has | here
+                for s in range(cap):
+                    hit = has & (seen == s)
+                    places[s] = jnp.where(hit, h * rows + r, places[s])
+                    scales[s] = jnp.where(hit, scale, scales[s])
+                seen = seen + has.astype(jnp.int32)
+            found[k, h] = places, scales
+    sources = [p for k in range(planes) for j in range(planes) for p in found[k, j ^ k][0]]
+    scales = [w for j in range(planes) for w in found[0, j][1]]
+    lane = lax.broadcasted_iota(jnp.int32, pick_ref.shape, 1)
+    pick_ref[...] = jnp.where(lane == column(sources, len(sources)), 1.0, 0.0)
+    weight_ref[...] = jnp.broadcast_to(column(scales, len(scales)), weight_ref.shape)
+    lane = lax.broadcasted_iota(jnp.int32, merge_ref.shape, 1)
+    merge = jnp.zeros(merge_ref.shape, jnp.bool_)
+    for t in range(picks):
+        slots = []
+        for r in range(rows):
+            seen = jnp.int32(0)
+            for b in range(r):
+                for u in range(picks):
+                    seen = seen + (ids[b, u] == ids[r, t]).astype(jnp.int32)
+            slots.append((ids[r, t] ^ plane) * cap + seen)
+        merge = merge | (lane == column(slots, rows))
+    merge_ref[...] = jnp.where(merge, 1.0, 0.0).astype(BF16)
+
+
+def tables(me, ids, homes, cap):
+    rows, picks = ids.shape
+    planes = len(homes)
+    vec = pl.BlockSpec(memory_space=pltpu.VMEM)
+    return pl.pallas_call(
+        functools.partial(tables_kernel, rows, picks, planes, cap),
+        in_specs=[SCALARS] * (2 + planes),
+        out_specs=[vec] * 3,
+        out_shape=[
+            sds((planes * planes * cap, planes * rows), F32),
+            sds((planes * cap, 128), F32),
+            sds((rows, planes * cap), BF16),
+        ],
+        compiler_params=params(),
+        name="route_tables",
+    )(me, ids, *homes)
+
+
+def pick_rows(pick, values):
+    high = values.astype(BF16)
+    low = (values - high.astype(F32)).astype(BF16)
+    return jnp.dot(pick, high, preferred_element_type=F32) + jnp.dot(
+        pick, low, preferred_element_type=F32
+    )
+
+
+def add_and_pick_kernel(planes, tile, own_ref, a_ref, b_ref, c_ref, hidden_ref, pick_ref, *outs):
+    size = outs[0].shape[0]
+    rows = hidden_ref.shape[0]
+    pick = pick_ref[...]
+    near, far = pick[:size].astype(BF16), pick[size:].astype(BF16)
+    for start in range(0, own_ref.shape[1], tile):
+        at = slice(start, start + tile)
+        total = own_ref[:, at]
+        for ref in (a_ref, b_ref, c_ref):
+            total = total + ref[:, at].astype(F32)
+        home = total[:rows] + hidden_ref[:, at].astype(F32)
+        total = jnp.concatenate([home, total[rows:]], axis=0)
+        outs[0][:, at] = pick_rows(near, total)
+        others = jnp.dot(far, total.astype(BF16), preferred_element_type=F32)
+        for k in range(1, planes):
+            outs[k][:, at] = others[(k - 1) * size : k * size].astype(BF16)
+
+
+def add_and_pick(own, received, hidden, pick, planes):
+    features = own.shape[1]
+    size = pick.shape[0] // planes
+    vec = pl.BlockSpec(memory_space=pltpu.VMEM)
+    return pl.pallas_call(
+        functools.partial(add_and_pick_kernel, planes, 1024),
+        in_specs=[vec] * 6,
+        out_specs=[vec] * planes,
+        out_shape=[sds((size, features), F32)] + [sds((size, features), BF16)] * (planes - 1),
+        compiler_params=params(),
+        name="add_chips",
+    )(own, *received, hidden, pick)
+
+
+def norm_kernel(planes, *refs):
+    gain_ref, resid_ref, normed_ref = refs[planes], refs[-2], refs[-1]
     total = refs[0][...]
     for ref in refs[1:planes]:
         total = total + ref[...].astype(F32)
-    resid = (hidden_ref[...].astype(F32) + total).astype(BF16)
+    resid = total.astype(BF16)
     resid_ref[...] = resid
     wide = resid.astype(F32)
     scale = lax.rsqrt(jnp.mean(wide * wide, axis=1, keepdims=True) + EPSILON)
-    normed[...] = (wide * scale * gain_ref[...].astype(F32)).astype(BF16).astype(F32)
-    rows, picks = ids.shape
-    plane = me[0] // 8
-    for k in range(planes):
-        expert = plane ^ k
-        places = [jnp.int32(0)] * cap
-        seen = jnp.int32(0)
-        for r in range(rows):
-            has = ids[r, 0] == expert
-            for t in range(1, picks):
-                has = has | (ids[r, t] == expert)
-            for s in range(cap):
-                places[s] = jnp.where(has & (seen == s), r, places[s])
-            seen = seen + has.astype(jnp.int32)
-        for s in range(cap):
-            packed[k * cap + s : k * cap + s + 1, :] = normed[pl.ds(places[s], 1), :]
-        packs[k][...] = packed[k * cap : (k + 1) * cap, :].astype(BF16)
-
-
-def norm_and_pack(me, ids, sums, hidden, gain, planes, cap):
-    rows, features = hidden.shape
-    vec = pl.BlockSpec(memory_space=pltpu.VMEM)
-    return pl.pallas_call(
-        functools.partial(norm_kernel, planes, cap),
-        in_specs=[SCALARS, SCALARS] + [vec] * (2 + len(sums)),
-        out_specs=[vec] * (1 + planes),
-        out_shape=[sds((rows, features), BF16)] + [sds((cap, features), BF16)] * planes,
-        scratch_shapes=[
-            pltpu.VMEM((rows, features), F32),
-            pltpu.VMEM((planes * cap, features), F32),
-        ],
-        compiler_params=params(),
-        name="norm_and_pack",
-    )(me, ids, *sums, hidden, gain)
-
-
-def stack_kernel(count, *refs):
-    wide = refs[-1]
-    out = refs[-2]
-    size = refs[0].shape[0]
-    for k, ref in enumerate(refs[:count]):
-        wide[k * size : (k + 1) * size, :] = ref[...].astype(F32)
-    out[...] = wide[...].astype(BF16)
-
-
-def stack(pieces, after):
-    size, features = pieces[0].shape
-    vec = pl.BlockSpec(memory_space=pltpu.VMEM)
-    shape = (size * len(pieces), features)
-    return pl.pallas_call(
-        functools.partial(stack_kernel, len(pieces)),
-        in_specs=[vec] * len(pieces) + [pl.BlockSpec(memory_space=pl.ANY)] * len(after),
-        out_specs=vec,
-        out_shape=sds(shape, BF16),
-        scratch_shapes=[pltpu.VMEM(shape, F32)],
-        compiler_params=params(),
-        name="stack_rows",
-    )(*pieces, *after)
+    normed_ref[...] = (wide * scale * gain_ref[...].astype(F32)).astype(BF16)
+
+
+def norm(sums, gain, after):
+    vec = pl.BlockSpec(memory_space=pltpu.VMEM)
+    shape = sums[0].shape
+    return pl.pallas_call(
+        functools.partial(norm_kernel, len(sums)),
+        in_specs=[vec] * (1 + len(sums)) + [pl.BlockSpec(memory_space=pl.ANY)] * len(after),
+        out_specs=[vec, vec],
+        out_shape=[sds(shape, BF16), sds(shape, BF16)],
+        compiler_params=params(),
+        name="norm",
+    )(*sums, gain, *after)
 
 
 def expert_kernel(pieces, tiles, *refs):
@@ -320,44 +409,49 @@
     )(*pieces, *gate_up, down_proj)
 
 
-def combine_kernel(planes, cap, me, ids, weights, own_ref, *refs):
-    received = refs[: planes - 1]
-    resid_ref, out_ref, table, mixed = refs[planes - 1 :]
-    table[:cap, :] = own_ref[...]
-    for k, ref in enumerate(received):
-        table[(k + 1) * cap : (k + 2) * cap, :] = ref[...].astype(F32)
-    rows, picks = ids.shape
-    plane = me[0] // 8
-    for r in range(rows):
-        total = None
-        for t in range(picks):
-            expert_id = ids[r, t]
-            seen = jnp.int32(0)
-            for b in range(r):
-                for u in range(picks):
-                    seen = seen + (ids[b, u] == expert_id).astype(jnp.int32)
-            place = (expert_id ^ plane) * cap + seen
-            term = weights[r, t] * table[pl.ds(place, 1), :]
-            total = term if total is None else total + term
-        mixed[r : r + 1, :] = total
-    out_ref[...] = (resid_ref[...].astype(F32) + mixed[...]).astype(BF16)
-
-
-def combine(me, ids, weights, own, received, resid, planes, cap):
-    rows, features = resid.shape
-    vec = pl.BlockSpec(memory_space=pltpu.VMEM)
-    return pl.pallas_call(
-        functools.partial(combine_kernel, planes, cap),
-        in_specs=[SCALARS] * 3 + [vec] * (1 + planes),
+def weigh_kernel(planes, share, tile, own_ref, a_ref, b_ref, c_ref, resid_ref, weight_ref, *outs):
+    cap = outs[0].shape[0]
+    for start in range(0, own_ref.shape[1], tile):
+        at = slice(start, start + tile)
+        total = own_ref[:, at]
+        for ref in (a_ref, b_ref, c_ref):
+            total = total + ref[:, at].astype(F32)
+        total = total * weight_ref[:, :1] + resid_ref[:, at].astype(F32) * share
+        outs[0][:, at] = total[:cap]
+        for k in range(1, planes):
+            outs[k][:, at] = total[k * cap : (k + 1) * cap].astype(BF16)
+
+
+def weigh(own, received, resid, weight, planes, picks):
+    count, features = own.shape
+    cap = count // planes
+    vec = pl.BlockSpec(memory_space=pltpu.VMEM)
+    return pl.pallas_call(
+        functools.partial(weigh_kernel, planes, 1.0 / picks, 1024),
+        in_specs=[vec] * 6,
+        out_specs=[vec] * planes,
+        out_shape=[sds((cap, features), F32)] + [sds((cap, features), BF16)] * (planes - 1),
+        compiler_params=params(),
+        name="weigh",
+    )(own, *received, resid, weight)
+
+
+def combine_kernel(planes, merge_ref, *refs):
+    out_ref = refs[planes]
+    table = jnp.concatenate([ref[...].astype(F32) for ref in refs[:planes]], axis=0)
+    out_ref[...] = pick_rows(merge_ref[...], table).astype(BF16)
+
+
+def combine(merge, pieces):
+    vec = pl.BlockSpec(memory_space=pltpu.VMEM)
+    return pl.pallas_call(
+        functools.partial(combine_kernel, len(pieces)),
+        in_specs=[vec] * (1 + len(pieces)),
         out_specs=vec,
-        out_shape=sds((rows, features), BF16),
-        scratch_shapes=[
-            pltpu.VMEM((planes * cap, features), F32),
-            pltpu.VMEM((rows, features), F32),
-        ],
+        out_shape=sds((merge.shape[0], pieces[0].shape[1]), BF16),
         compiler_params=params(),
         name="combine",
-    )(me, ids, weights, own, *received, resid)
+    )(merge, *pieces)
 
 
 def body(
@@ -391,21 +485,19 @@
 
     latents = attention(queries, latent_cache, lengths)
     by_heads = lax.all_to_all(latents, "dp", split_axis=0, concat_axis=0, tiled=True)
-    own, other = project(me, by_heads, value_up, out_proj, planes, rows)
+    mine = routes(route_ids, route_weights, latents)
+    pick, weight, merge = tables(me, route_ids, [mine] + over_planes([mine] * (planes - 1)), cap)
+    own, other = project(me, by_heads, value_up, out_proj, planes, rows, [pick])
     own, *out = add_and_cut(own, [swap(other, 1)], 4, "add_core")
-    own, *out = add_and_cut(own, over_chips(out), planes, "add_chips")
-    sums = [own] + over_planes(out)
-    resid, mine, *out = norm_and_pack(
-        me, route_ids, sums, hidden_in, norm_gain[None], planes, cap
-    )
-    gate_up, (down_proj,) = fetch([gate_up, down_proj], [(0, 2), (0, 1)], resid)
-    picked = stack([mine] + over_planes(out), gate_up[:1])
+    own, *out = add_and_pick(own, over_chips(out), hidden_in, pick, planes)
+    gate_up, (down_proj,) = fetch([gate_up, down_proj], [(0, 2), (0, 1)], own)
+    resid, picked = norm([own] + over_planes(out), norm_gain[None], gate_up[:1])
     chips = [picked] + over_chips([picked] * 3)
     pieces = chips + [swap(x, 1) for x in chips]
     own, other = expert(pieces, gate_up, down_proj)
     own, *out = add_and_cut(own, [swap(other, 1)], 4, "add_expert_core")
-    own, *out = add_and_cut(own, over_chips(out), planes, "add_expert_chips")
-    return combine(me, route_ids, route_weights, own, over_planes(out), resid, planes, cap)
+    own, *out = weigh(own, over_chips(out), resid, weight, planes, picks)
+    return combine(merge, [own] + over_planes(out))
 
 
 def solution(mesh):

time: 97.4 us -> 92.2 us (0.947)
  waiting for transfers between devices: 48.6 us -> 42.5 us
    all_to_all x1, waiting for transfers between devices: 15.5 us -> 0.01 us  [body(): lax.all_to_all(latents, 'dp', split_axis=0, concat_axis=0, tiled=True)]
    ppermute x24, waiting for transfers between devices: 33 us -> 42.5 us  [swap(): return lax.ppermute(x, 'dp', [(i, i ^ mask) for i in range(devices)])]
    pallas_call x3 -> x6, Pallas kernels: 2.36 us -> 3.41 us  [the longest x1 1.14 us: tables(): pl.pallas_call(functools.partial(tables_kernel, rows, picks, planes, cap)...]
  transfers between devices with their start and end apart: 25 -> 25, of which waited for: 16 -> 16; matrix products, arithmetic and copies ran while one was open for 0% -> 0% of each run, Pallas kernels for 3% -> 5%
where the time goes in v4:
time: 92.2 us; the launch traced here: 92 us
  waiting for transfers between devices  42.5 us (46%)
  starting transfers between devices  31.6 us (34%)
  Pallas kernels  16.8 us (18%)
    ppermute x24, waiting for transfers between devices, swap(): return lax.ppermute(x, 'dp', [(i, i ^ mask) for i in range(devices)])  42.5 us
    ppermute x24, starting transfers between devices, swap(): return lax.ppermute(x, 'dp', [(i, i ^ mask) for i in range(devices)])  24.3 us
    all_to_all x1, starting transfers between devices, body(): lax.all_to_all(latents, 'dp', split_axis=0, concat_axis=0, tiled=True)  7.3 us
    pallas_call x1, Pallas kernels, attention(): pl.pallas_call(attention_kernel, in_specs=[SCALARS, hbm, hbm], out_specs=...  5.23 us
    pallas_call x1, Pallas kernels, project(): pl.pallas_call(functools.partial(project_kernel, planes, rows, tiles), in...  4.28 us
    pallas_call x1, Pallas kernels, fetch(): pl.pallas_call(functools.partial(fetch_kernel, parts), in_specs=[pl.Block...  2.64 us
  transfers between devices with their start and end apart: 25, of which 16 were waited for; matrix products, arithmetic and copies ran while one was open for 0% of the time, Pallas kernels for 5%

profile of v4, /device:TPU:0, one launch (start us, length us, event | category | flops | bytes accessed | tf_op | source)
XLA Modules:
  0.0 92.0 jit_solution(16646314602803771345)
XLA Ops:
  0.7 5.2 %latent_attention.1.unused = bf16[512,512]{1,0:T(8,128)(2,1)} custom-call(s32[4]{0:T(128)S(1)} %copy-done.2, bf16[4,576,128]{2,1,0:T(8,128)(2,1)} %bitcast.7, bf16[4,576,512]{2,1,0:T(8,128)(2,1)} %bitcast.6), custom_call_target="tpu_custom_call" | custom-call | tf_op jit(solution)/shard_map/latent_attention/pallas_call | solution.py:73
  5.9 7.3 %all-to-all-start = ((bf16[32,16,512]{2,1,0:T(8,128)(2,1)}), bf16[32,16,512]{2,1,0:T(8,128)(2,1)S(1)}, u32[]{:S(2)}, u32[]{:S(2)}) async-start(bf16[32,16,512]{2,1,0:T(8,128)(2,1)} %bitcast.3), calls=%async_computation | async-start | bytes 1048576 | tf_op jit(solution)/shard_map/all_to_all | solution.py:487
  14.0 3.7 %collective-permute-start.2 = (f32[8,128]{1,0:T(8,128)S(1)}, f32[8,128]{1,0:T(8,128)S(1)}, u32[]{:S(2)}, u32[]{:S(2)}) collective-permute-start(f32[8,128]{1,0:T(8,128)S(1)} %routes.1.refs_0_), channel_id=1, source_target_pairs={{0,24},{1,25},{2,26},{3,27},{4,28},{5,29},{6,30},{7,31},{8,16},{9,... | collective-permute-start | bytes 12296 | tf_op jit(solution)/shard_map/ppermute | solution.py:478
  18.5 8.0 %collective-permute-done.2.refs_3_ = f32[8,128]{1,0:T(8,128)S(1)} collective-permute-done((f32[8,128]{1,0:T(8,128)S(1)}, f32[8,128]{1,0:T(8,128)S(1)}, u32[]{:S(2)}, u32[]{:S(2)}) %collective-permute-start.2) | collective-permute-done | bytes 4128 | tf_op jit(solution)/shard_map/ppermute | solution.py:478
  26.5 2.0 %collective-permute-done.1.refs_2_ = f32[8,128]{1,0:T(8,128)S(1)} collective-permute-done((f32[8,128]{1,0:T(8,128)S(1)}, f32[8,128]{1,0:T(8,128)S(1)}, u32[]{:S(2)}, u32[]{:S(2)}) %collective-permute-start.1) | collective-permute-done | bytes 4128 | tf_op jit(solution)/shard_map/ppermute | solution.py:478
  29.7 4.3 %projections.1 = (f32[64,7168]{1,0:T(8,128)S(1)}, bf16[64,7168]{1,0:T(8,128)(2,1)S(1)}) custom-call(s32[1]{0:T(128)} %bitcast.me, bf16[512,512]{1,0:T(8,128)(2,1)S(1)} %bitcast.5, bf16[4,512,128]{2,1,0:T(8,128)(2,1)S(1)} %copy-done, bf16[512,7168]{1,0:T(8,128)(2,1)} %w_hbm.1, f32[32,16]{1,0:T(8,128)S(1)} %get-tuple-element.34.refs_0_.pick_ref), custom_call_target="tpu_custom_call" | custom-call | tf_op jit(solution)/shard_map/projections/pallas_call | solution.py:171
  34.1 2.5 %collective-permute-done.3.refs_1_ = bf16[64,7168]{1,0:T(8,128)(2,1)S(1)} collective-permute-done((bf16[64,7168]{1,0:T(8,128)(2,1)S(1)}, bf16[64,7168]{1,0:T(8,128)(2,1)S(1)}, u32[]{:S(2)}, u32[]{:S(2)}) %collective-permute-start.3) | collective-permute-done | bytes 917536 | tf_op jit(solution)/shard_map/ppermute | solution.py:478
  36.7 1.5 %collective-permute-start.4 = (bf16[16,7168]{1,0:T(8,128)(2,1)S(1)}, bf16[16,7168]{1,0:T(8,128)(2,1)S(1)}, u32[]{:S(2)}, u32[]{:S(2)}) collective-permute-start(bf16[16,7168]{1,0:T(8,128)(2,1)S(1)} %get-tuple-element.38), channel_id=1, source_target_pairs={{0,2},{1,3},{2,0},{3,1},{4,6},{5,7},{6,4},{7,5},{8,10},{9,11},{10,... | collective-permute-start | bytes 688136 | tf_op jit(solution)/shard_map/ppermute | solution.py:478
  38.2 1.5 %collective-permute-start.5 = (bf16[16,7168]{1,0:T(8,128)(2,1)S(1)}, bf16[16,7168]{1,0:T(8,128)(2,1)S(1)}, u32[]{:S(2)}, u32[]{:S(2)}) collective-permute-start(bf16[16,7168]{1,0:T(8,128)(2,1)S(1)} %get-tuple-element.39), channel_id=1, source_target_pairs={{0,4},{1,5},{2,6},{3,7},{4,0},{5,1},{6,2},{7,3},{8,12},{9,13},{10,... | collective-permute-start | bytes 688136 | tf_op jit(solution)/shard_map/ppermute | solution.py:478
  40.3 5.0 %collective-permute-done.4.a_ref = bf16[16,7168]{1,0:T(8,128)(2,1)S(1)} collective-permute-done((bf16[16,7168]{1,0:T(8,128)(2,1)S(1)}, bf16[16,7168]{1,0:T(8,128)(2,1)S(1)}, u32[]{:S(2)}, u32[]{:S(2)}) %collective-permute-start.4) | collective-permute-done | bytes 229408 | tf_op jit(solution)/shard_map/ppermute | solution.py:478
  45.2 5.3 %collective-permute-done.5.b_ref = bf16[16,7168]{1,0:T(8,128)(2,1)S(1)} collective-permute-done((bf16[16,7168]{1,0:T(8,128)(2,1)S(1)}, bf16[16,7168]{1,0:T(8,128)(2,1)S(1)}, u32[]{:S(2)}, u32[]{:S(2)}) %collective-permute-start.5) | collective-permute-done | bytes 229408 | tf_op jit(solution)/shard_map/ppermute | solution.py:478
  51.5 1.5 %collective-permute-start.8 = (bf16[8,7168]{1,0:T(8,128)(2,1)S(1)}, bf16[8,7168]{1,0:T(8,128)(2,1)S(1)}, u32[]{:S(2)}, u32[]{:S(2)}) collective-permute-start(bf16[8,7168]{1,0:T(8,128)(2,1)S(1)} %get-tuple-element.43), channel_id=1, source_target_pairs={{0,16},{1,17},{2,18},{3,19},{4,20},{5,21},{6,22},{7,23},{8,24},{9,... | collective-permute-start | bytes 344072 | tf_op jit(solution)/shard_map/ppermute | solution.py:478
  53.0 2.4 %collective-permute-start.9 = (bf16[8,7168]{1,0:T(8,128)(2,1)S(1)}, bf16[8,7168]{1,0:T(8,128)(2,1)S(1)}, u32[]{:S(2)}, u32[]{:S(2)}) collective-permute-start(bf16[8,7168]{1,0:T(8,128)(2,1)S(1)} %get-tuple-element.44), channel_id=1, source_target_pairs={{0,24},{1,25},{2,26},{3,27},{4,28},{5,29},{6,30},{7,31},{8,16},{9,... | collective-permute-start | bytes 344072 | tf_op jit(solution)/shard_map/ppermute | solution.py:478
  55.4 2.6 %fetch_weights.1 = (bf16[7168,128]{1,0:T(8,128)(2,1)S(1)}, bf16[7168,128]{1,0:T(8,128)(2,1)S(1)}, bf16[128,7168]{1,0:T(8,128)(2,1)S(1)}) custom-call(bf16[2,7168,128]{2,1,0:T(8,128)(2,1)} %refs_0_.1, bf16[128,7168]{1,0:T(8,128)(2,1)} %refs_1_.1, f32[8,7168]{1,0:T(8,128)S(1)} %get-tuple-element.41.refs_2_.refs_0_), custom_call_target="tpu_custom_call" | custom-call | tf_op jit(solution)/shard_map/fetch_weights/pallas_call | solution.py:118
  58.1 4.4 %collective-permute-done.8.refs_2_ = bf16[8,7168]{1,0:T(8,128)(2,1)S(1)} collective-permute-done((bf16[8,7168]{1,0:T(8,128)(2,1)S(1)}, bf16[8,7168]{1,0:T(8,128)(2,1)S(1)}, u32[]{:S(2)}, u32[]{:S(2)}) %collective-permute-start.8) | collective-permute-done | bytes 114720 | tf_op jit(solution)/shard_map/ppermute | solution.py:478
  62.7 1.5 %collective-permute-start.12 = (bf16[8,7168]{1,0:T(8,128)(2,1)S(1)}, bf16[8,7168]{1,0:T(8,128)(2,1)S(1)}, u32[]{:S(2)}, u32[]{:S(2)}) collective-permute-start(bf16[8,7168]{1,0:T(8,128)(2,1)S(1)} %get-tuple-element.46.refs_0_), channel_id=1, source_target_pairs={{0,6},{1,7},{2,4},{3,5},{4,2},{5,3},{6,0},{7,1},{8,14},{9,15},{10,... | collective-permute-start | bytes 344072 | tf_op jit(solution)/shard_map/ppermute | solution.py:478
  66.2 2.3 %collective-permute-done.12.refs_3_ = bf16[8,7168]{1,0:T(8,128)(2,1)S(1)} collective-permute-done((bf16[8,7168]{1,0:T(8,128)(2,1)S(1)}, bf16[8,7168]{1,0:T(8,128)(2,1)S(1)}, u32[]{:S(2)}, u32[]{:S(2)}) %collective-permute-start.12) | collective-permute-done | bytes 114720 | tf_op jit(solution)/shard_map/ppermute | solution.py:478
  73.0 1.7 %collective-permute-done.17.refs_1_ = bf16[32,7168]{1,0:T(8,128)(2,1)S(1)} collective-permute-done((bf16[32,7168]{1,0:T(8,128)(2,1)S(1)}, bf16[32,7168]{1,0:T(8,128)(2,1)S(1)}, u32[]{:S(2)}, u32[]{:S(2)}) %collective-permute-start.17) | collective-permute-done | bytes 458784 | tf_op jit(solution)/shard_map/ppermute | solution.py:478
  76.2 2.1 %collective-permute-start.20 = (bf16[8,7168]{1,0:T(8,128)(2,1)S(1)}, bf16[8,7168]{1,0:T(8,128)(2,1)S(1)}, u32[]{:S(2)}, u32[]{:S(2)}) collective-permute-start(bf16[8,7168]{1,0:T(8,128)(2,1)S(1)} %get-tuple-element.54), channel_id=1, source_target_pairs={{0,6},{1,7},{2,4},{3,5},{4,2},{5,3},{6,0},{7,1},{8,14},{9,15},{10,... | collective-permute-start | bytes 344072 | tf_op jit(solution)/shard_map/ppermute | solution.py:478
  78.3 2.5 %collective-permute-done.18.a_ref = bf16[8,7168]{1,0:T(8,128)(2,1)S(1)} collective-permute-done((bf16[8,7168]{1,0:T(8,128)(2,1)S(1)}, bf16[8,7168]{1,0:T(8,128)(2,1)S(1)}, u32[]{:S(2)}, u32[]{:S(2)}) %collective-permute-start.18) | collective-permute-done | bytes 114720 | tf_op jit(solution)/shard_map/ppermute | solution.py:478
  80.8 2.1 %collective-permute-done.19.b_ref = bf16[8,7168]{1,0:T(8,128)(2,1)S(1)} collective-permute-done((bf16[8,7168]{1,0:T(8,128)(2,1)S(1)}, bf16[8,7168]{1,0:T(8,128)(2,1)S(1)}, u32[]{:S(2)}, u32[]{:S(2)}) %collective-permute-start.19) | collective-permute-done | bytes 114720 | tf_op jit(solution)/shard_map/ppermute | solution.py:478
  83.0 1.9 %collective-permute-start.21 = (bf16[2,7168]{1,0:T(2,128)(2,1)S(1)}, bf16[2,7168]{1,0:T(2,128)(2,1)S(1)}, u32[]{:S(2)}, u32[]{:S(2)}) collective-permute-start(bf16[2,7168]{1,0:T(2,128)(2,1)S(1)} %get-tuple-element.58), channel_id=1, source_target_pairs={{0,8},{1,9},{2,10},{3,11},{4,12},{5,13},{6,14},{7,15},{8,0},{9,1},... | collective-permute-start | bytes 86024 | tf_op jit(solution)/shard_map/ppermute | solution.py:478
  85.4 2.1 %collective-permute-start.23 = (bf16[2,7168]{1,0:T(2,128)(2,1)S(1)}, bf16[2,7168]{1,0:T(2,128)(2,1)S(1)}, u32[]{:S(2)}, u32[]{:S(2)}) collective-permute-start(bf16[2,7168]{1,0:T(2,128)(2,1)S(1)} %get-tuple-element.60), channel_id=1, source_target_pairs={{0,24},{1,25},{2,26},{3,27},{4,28},{5,29},{6,30},{7,31},{8,16},{9,... | collective-permute-start | bytes 86024 | tf_op jit(solution)/shard_map/ppermute | solution.py:478
  87.5 2.3 %collective-permute-done.22.refs_2_ = bf16[2,7168]{1,0:T(2,128)(2,1)S(1)} collective-permute-done((bf16[2,7168]{1,0:T(2,128)(2,1)S(1)}, bf16[2,7168]{1,0:T(2,128)(2,1)S(1)}, u32[]{:S(2)}, u32[]{:S(2)}) %collective-permute-start.22) | collective-permute-done | bytes 28704 | tf_op jit(solution)/shard_map/ppermute | solution.py:478
  (53 shorter events, 16.4 us)
Async XLA Ops:
  5.9 23.8 %all-to-all-start = ((bf16[32,16,512]{2,1,0:T(8,128)(2,1)}), bf16[32,16,512]{2,1,0:T(8,128)(2,1)S(1)}, u32[]{:S(2)}, u32[]{:S(2)}) async-start(bf16[32,16,512]{2,1,0:T(8,128)(2,1)} %bitcast.3), calls=%async_computation | async-start | bytes 1048576 | tf_op jit(solution)/shard_map/all_to_all | solution.py:487
  14.0 12.5 %collective-permute-start.2 = (f32[8,128]{1,0:T(8,128)S(1)}, f32[8,128]{1,0:T(8,128)S(1)}, u32[]{:S(2)}, u32[]{:S(2)}) collective-permute-start(f32[8,128]{1,0:T(8,128)S(1)} %routes.1.refs_0_), channel_id=1, source_target_pairs={{0,24},{1,25},{2,26},{3,27},{4,28},{5,29},{6,30},{7,31},{8,16},{9,... | collective-permute-start | bytes 12296 | tf_op jit(solution)/shard_map/ppermute | solution.py:478
  17.7 10.8 %collective-permute-start.1 = (f32[8,128]{1,0:T(8,128)S(1)}, f32[8,128]{1,0:T(8,128)S(1)}, u32[]{:S(2)}, u32[]{:S(2)}) collective-permute-start(f32[8,128]{1,0:T(8,128)S(1)} %routes.1.refs_0_), channel_id=1, source_target_pairs={{0,16},{1,17},{2,18},{3,19},{4,20},{5,21},{6,22},{7,23},{8,24},{9,... | collective-permute-start | bytes 12296 | tf_op jit(solution)/shard_map/ppermute | solution.py:478
  17.7 10.8 %collective-permute-start = (f32[8,128]{1,0:T(8,128)S(1)}, f32[8,128]{1,0:T(8,128)S(1)}, u32[]{:S(2)}, u32[]{:S(2)}) collective-permute-start(f32[8,128]{1,0:T(8,128)S(1)} %routes.1.refs_0_), channel_id=1, source_target_pairs={{0,8},{1,9},{2,10},{3,11},{4,12},{5,13},{6,14},{7,15},{8,0},{9,1},... | collective-permute-start | bytes 12296 | tf_op jit(solution)/shard_map/ppermute | solution.py:478
  34.0 2.5 %collective-permute-start.3 = (bf16[64,7168]{1,0:T(8,128)(2,1)S(1)}, bf16[64,7168]{1,0:T(8,128)(2,1)S(1)}, u32[]{:S(2)}, u32[]{:S(2)}) collective-permute-start(bf16[64,7168]{1,0:T(8,128)(2,1)S(1)} %get-tuple-element.36), channel_id=1, source_target_pairs={{0,1},{1,0},{2,3},{3,2},{4,5},{5,4},{6,7},{7,6},{8,9},{9,8},{10,11... | collective-permute-start | bytes 2752520 | tf_op jit(solution)/shard_map/ppermute | solution.py:478
  36.7 8.5 %collective-permute-start.4 = (bf16[16,7168]{1,0:T(8,128)(2,1)S(1)}, bf16[16,7168]{1,0:T(8,128)(2,1)S(1)}, u32[]{:S(2)}, u32[]{:S(2)}) collective-permute-start(bf16[16,7168]{1,0:T(8,128)(2,1)S(1)} %get-tuple-element.38), channel_id=1, source_target_pairs={{0,2},{1,3},{2,0},{3,1},{4,6},{5,7},{6,4},{7,5},{8,10},{9,11},{10,... | collective-permute-start | bytes 688136 | tf_op jit(solution)/shard_map/ppermute | solution.py:478
  38.2 12.3 %collective-permute-start.5 = (bf16[16,7168]{1,0:T(8,128)(2,1)S(1)}, bf16[16,7168]{1,0:T(8,128)(2,1)S(1)}, u32[]{:S(2)}, u32[]{:S(2)}) collective-permute-start(bf16[16,7168]{1,0:T(8,128)(2,1)S(1)} %get-tuple-element.39), channel_id=1, source_target_pairs={{0,4},{1,5},{2,6},{3,7},{4,0},{5,1},{6,2},{7,3},{8,12},{9,13},{10,... | collective-permute-start | bytes 688136 | tf_op jit(solution)/shard_map/ppermute | solution.py:478
  39.7 10.8 %collective-permute-start.6 = (bf16[16,7168]{1,0:T(8,128)(2,1)S(1)}, bf16[16,7168]{1,0:T(8,128)(2,1)S(1)}, u32[]{:S(2)}, u32[]{:S(2)}) collective-permute-start(bf16[16,7168]{1,0:T(8,128)(2,1)S(1)} %get-tuple-element.40), channel_id=1, source_target_pairs={{0,6},{1,7},{2,4},{3,5},{4,2},{5,3},{6,0},{7,1},{8,14},{9,15},{10,... | collective-permute-start | bytes 688136 | tf_op jit(solution)/shard_map/ppermute | solution.py:478
  50.9 7.1 %collective-permute-start.7 = (bf16[8,7168]{1,0:T(8,128)(2,1)S(1)}, bf16[8,7168]{1,0:T(8,128)(2,1)S(1)}, u32[]{:S(2)}, u32[]{:S(2)}) collective-permute-start(bf16[8,7168]{1,0:T(8,128)(2,1)S(1)} %get-tuple-element.42), channel_id=1, source_target_pairs={{0,8},{1,9},{2,10},{3,11},{4,12},{5,13},{6,14},{7,15},{8,0},{9,1},... | collective-permute-start | bytes 344072 | tf_op jit(solution)/shard_map/ppermute | solution.py:478
  51.5 10.9 %collective-permute-start.8 = (bf16[8,7168]{1,0:T(8,128)(2,1)S(1)}, bf16[8,7168]{1,0:T(8,128)(2,1)S(1)}, u32[]{:S(2)}, u32[]{:S(2)}) collective-permute-start(bf16[8,7168]{1,0:T(8,128)(2,1)S(1)} %get-tuple-element.43), channel_id=1, source_target_pairs={{0,16},{1,17},{2,18},{3,19},{4,20},{5,21},{6,22},{7,23},{8,24},{9,... | collective-permute-start | bytes 344072 | tf_op jit(solution)/shard_map/ppermute | solution.py:478
  53.0 9.4 %collective-permute-start.9 = (bf16[8,7168]{1,0:T(8,128)(2,1)S(1)}, bf16[8,7168]{1,0:T(8,128)(2,1)S(1)}, u32[]{:S(2)}, u32[]{:S(2)}) collective-permute-start(bf16[8,7168]{1,0:T(8,128)(2,1)S(1)} %get-tuple-element.44), channel_id=1, source_target_pairs={{0,24},{1,25},{2,26},{3,27},{4,28},{5,29},{6,30},{7,31},{8,16},{9,... | collective-permute-start | bytes 344072 | tf_op jit(solution)/shard_map/ppermute | solution.py:478
  62.7 5.8 %collective-permute-start.12 = (bf16[8,7168]{1,0:T(8,128)(2,1)S(1)}, bf16[8,7168]{1,0:T(8,128)(2,1)S(1)}, u32[]{:S(2)}, u32[]{:S(2)}) collective-permute-start(bf16[8,7168]{1,0:T(8,128)(2,1)S(1)} %get-tuple-element.46.refs_0_), channel_id=1, source_target_pairs={{0,6},{1,7},{2,4},{3,5},{4,2},{5,3},{6,0},{7,1},{8,14},{9,15},{10,... | collective-permute-start | bytes 344072 | tf_op jit(solution)/shard_map/ppermute | solution.py:478
  64.2 5.5 %collective-permute-start.11 = (bf16[8,7168]{1,0:T(8,128)(2,1)S(1)}, bf16[8,7168]{1,0:T(8,128)(2,1)S(1)}, u32[]{:S(2)}, u32[]{:S(2)}) collective-permute-start(bf16[8,7168]{1,0:T(8,128)(2,1)S(1)} %get-tuple-element.46.refs_0_), channel_id=1, source_target_pairs={{0,4},{1,5},{2,6},{3,7},{4,0},{5,1},{6,2},{7,3},{8,12},{9,13},{10,... | collective-permute-start | bytes 344072 | tf_op jit(solution)/shard_map/ppermute | solution.py:478
  65.6 4.8 %collective-permute-start.10 = (bf16[8,7168]{1,0:T(8,128)(2,1)S(1)}, bf16[8,7168]{1,0:T(8,128)(2,1)S(1)}, u32[]{:S(2)}, u32[]{:S(2)}) collective-permute-start(bf16[8,7168]{1,0:T(8,128)(2,1)S(1)} %get-tuple-element.46.refs_0_), channel_id=1, source_target_pairs={{0,2},{1,3},{2,0},{3,1},{4,6},{5,7},{6,4},{7,5},{8,10},{9,11},{10,... | collective-permute-start | bytes 344072 | tf_op jit(solution)/shard_map/ppermute | solution.py:478
  66.2 4.2 %collective-permute-start.13 = (bf16[8,7168]{1,0:T(8,128)(2,1)S(1)}, bf16[8,7168]{1,0:T(8,128)(2,1)S(1)}, u32[]{:S(2)}, u32[]{:S(2)}) collective-permute-start(bf16[8,7168]{1,0:T(8,128)(2,1)S(1)} %get-tuple-element.46.refs_0_), channel_id=1, source_target_pairs={{0,1},{1,0},{2,3},{3,2},{4,5},{5,4},{6,7},{7,6},{8,9},{9,8},{10,11... | collective-permute-start | bytes 344072 | tf_op jit(solution)/shard_map/ppermute | solution.py:478
  68.5 1.9 %collective-permute-start.16 = (bf16[8,7168]{1,0:T(8,128)(2,1)S(1)}, bf16[8,7168]{1,0:T(8,128)(2,1)S(1)}, u32[]{:S(2)}, u32[]{:S(2)}) collective-permute-start(bf16[8,7168]{1,0:T(8,128)(2,1)S(1)} %collective-permute-done.12.refs_3_), channel_id=1, source_target_pairs={{0,1},{1,0},{2,3},{3,2},{4,5},{5,4},{6,7},{7,6},{8,9},{9,8},{10,11... | collective-permute-start | bytes 344072 | tf_op jit(solution)/shard_map/ppermute | solution.py:478
  69.7 1.3 %collective-permute-start.15 = (bf16[8,7168]{1,0:T(8,128)(2,1)S(1)}, bf16[8,7168]{1,0:T(8,128)(2,1)S(1)}, u32[]{:S(2)}, u32[]{:S(2)}) collective-permute-start(bf16[8,7168]{1,0:T(8,128)(2,1)S(1)} %collective-permute-done.11.refs_2_), channel_id=1, source_target_pairs={{0,1},{1,0},{2,3},{3,2},{4,5},{5,4},{6,7},{7,6},{8,9},{9,8},{10,11... | collective-permute-start | bytes 344072 | tf_op jit(solution)/shard_map/ppermute | solution.py:478
  72.8 1.9 %collective-permute-start.17 = (bf16[32,7168]{1,0:T(8,128)(2,1)S(1)}, bf16[32,7168]{1,0:T(8,128)(2,1)S(1)}, u32[]{:S(2)}, u32[]{:S(2)}) collective-permute-start(bf16[32,7168]{1,0:T(8,128)(2,1)S(1)} %get-tuple-element.50), channel_id=1, source_target_pairs={{0,1},{1,0},{2,3},{3,2},{4,5},{5,4},{6,7},{7,6},{8,9},{9,8},{10,11... | collective-permute-start | bytes 1376264 | tf_op jit(solution)/shard_map/ppermute | solution.py:478
  74.7 6.1 %collective-permute-start.18 = (bf16[8,7168]{1,0:T(8,128)(2,1)S(1)}, bf16[8,7168]{1,0:T(8,128)(2,1)S(1)}, u32[]{:S(2)}, u32[]{:S(2)}) collective-permute-start(bf16[8,7168]{1,0:T(8,128)(2,1)S(1)} %get-tuple-element.52), channel_id=1, source_target_pairs={{0,2},{1,3},{2,0},{3,1},{4,6},{5,7},{6,4},{7,5},{8,10},{9,11},{10,... | collective-permute-start | bytes 344072 | tf_op jit(solution)/shard_map/ppermute | solution.py:478
  75.4 7.5 %collective-permute-start.19 = (bf16[8,7168]{1,0:T(8,128)(2,1)S(1)}, bf16[8,7168]{1,0:T(8,128)(2,1)S(1)}, u32[]{:S(2)}, u32[]{:S(2)}) collective-permute-start(bf16[8,7168]{1,0:T(8,128)(2,1)S(1)} %get-tuple-element.53), channel_id=1, source_target_pairs={{0,4},{1,5},{2,6},{3,7},{4,0},{5,1},{6,2},{7,3},{8,12},{9,13},{10,... | collective-permute-start | bytes 344072 | tf_op jit(solution)/shard_map/ppermute | solution.py:478
  76.2 6.7 %collective-permute-start.20 = (bf16[8,7168]{1,0:T(8,128)(2,1)S(1)}, bf16[8,7168]{1,0:T(8,128)(2,1)S(1)}, u32[]{:S(2)}, u32[]{:S(2)}) collective-permute-start(bf16[8,7168]{1,0:T(8,128)(2,1)S(1)} %get-tuple-element.54), channel_id=1, source_target_pairs={{0,6},{1,7},{2,4},{3,5},{4,2},{5,3},{6,0},{7,1},{8,14},{9,15},{10,... | collective-permute-start | bytes 344072 | tf_op jit(solution)/shard_map/ppermute | solution.py:478
  83.0 4.5 %collective-permute-start.21 = (bf16[2,7168]{1,0:T(2,128)(2,1)S(1)}, bf16[2,7168]{1,0:T(2,128)(2,1)S(1)}, u32[]{:S(2)}, u32[]{:S(2)}) collective-permute-start(bf16[2,7168]{1,0:T(2,128)(2,1)S(1)} %get-tuple-element.58), channel_id=1, source_target_pairs={{0,8},{1,9},{2,10},{3,11},{4,12},{5,13},{6,14},{7,15},{8,0},{9,1},... | collective-permute-start | bytes 86024 | tf_op jit(solution)/shard_map/ppermute | solution.py:478
  84.9 4.9 %collective-permute-start.22 = (bf16[2,7168]{1,0:T(2,128)(2,1)S(1)}, bf16[2,7168]{1,0:T(2,128)(2,1)S(1)}, u32[]{:S(2)}, u32[]{:S(2)}) collective-permute-start(bf16[2,7168]{1,0:T(2,128)(2,1)S(1)} %get-tuple-element.59), channel_id=1, source_target_pairs={{0,16},{1,17},{2,18},{3,19},{4,20},{5,21},{6,22},{7,23},{8,24},{9,... | collective-permute-start | bytes 86024 | tf_op jit(solution)/shard_map/ppermute | solution.py:478
  85.4 5.7 %collective-permute-start.23 = (bf16[2,7168]{1,0:T(2,128)(2,1)S(1)}, bf16[2,7168]{1,0:T(2,128)(2,1)S(1)}, u32[]{:S(2)}, u32[]{:S(2)}) collective-permute-start(bf16[2,7168]{1,0:T(2,128)(2,1)S(1)} %get-tuple-element.60), channel_id=1, source_target_pairs={{0,24},{1,25},{2,26},{3,27},{4,28},{5,29},{6,30},{7,31},{8,16},{9,... | collective-permute-start | bytes 86024 | tf_op jit(solution)/shard_map/ppermute | solution.py:478
  (7 other events, 91.6 us)

commit v5 on v4

--- a/solution.py
+++ b/solution.py
@@ -15,6 +15,8 @@
 MASKED = -1e30
 EPSILON = 1e-06
 VMEM = 24 * 1024 * 1024
+TILES = 7
+EARLY = 3
 
 F32 = jnp.float32
 BF16 = jnp.bfloat16
@@ -37,14 +39,19 @@
     return pl.BlockSpec(shape, lambda *_: (0,) * len(shape))
 
 
-def attention_kernel(lengths, q_hbm, k_hbm, o_ref, queries, keys, lat, sems):
+def attention_kernel(planes, me, lengths_hbm, q_hbm, k_hbm, *refs):
+    outs = refs[:planes]
+    lengths, queries, keys, lat, sems = refs[planes:]
     rows, _, heads = queries.shape
+    live = pltpu.make_async_copy(lengths_hbm, lengths, sems.at[2 * rows])
+    live.start()
     copies = []
     for r in range(rows):
         for n, (src, dst) in enumerate(((q_hbm, queries), (k_hbm, keys))):
             copy = pltpu.make_async_copy(src.at[r], dst.at[r], sems.at[2 * r + n])
             copy.start()
             copies.append(copy)
+    live.wait()
     for r in range(rows):
         copies[2 * r].wait()
         copies[2 * r + 1].wait()
@@ -59,44 +66,72 @@
             terms.astype(BF16), keys[r, :LAT], (((1,), (1,)), ((), ())), preferred_element_type=F32
         )
         lat[r * heads : (r + 1) * heads, :] = (numerator / total).astype(BF16)
-    size = rows * heads
+    each = heads // (planes * 8)
+    size = rows * heads // planes
     i = lax.broadcasted_iota(jnp.int32, (size, 1), 0)
-    k = lax.broadcasted_iota(jnp.int32, (size, size), 1)
-    pick = jnp.where(k == (i % rows) * heads + i // rows, 1.0, 0.0).astype(BF16)
-    o_ref[...] = jnp.dot(pick, lat[...], preferred_element_type=F32).astype(BF16)
-
-
-def attention(queries, latent_cache, lengths):
+    k = lax.broadcasted_iota(jnp.int32, (size, rows * heads), 1)
+    unit = i // (rows * each)
+    for p in range(planes):
+        head = (me[0] ^ (p * 8 + unit)) * each + (i // rows) % each
+        pick = jnp.where(k == (i % rows) * heads + head, 1.0, 0.0).astype(BF16)
+        outs[p][...] = jnp.dot(pick, lat[...], preferred_element_type=F32).astype(BF16)
+
+
+def attention(me, queries, latent_cache, lengths, planes):
     rows, heads, width = queries.shape
     slots = latent_cache.shape[1]
     hbm = pl.BlockSpec(memory_space=pltpu.HBM)
     return pl.pallas_call(
-        attention_kernel,
-        in_specs=[SCALARS, hbm, hbm],
-        out_specs=pl.BlockSpec(memory_space=pltpu.VMEM),
-        out_shape=sds((rows * heads, LAT), BF16),
+        functools.partial(attention_kernel, planes),
+        in_specs=[SCALARS, hbm, hbm, hbm],
+        out_specs=[pl.BlockSpec(memory_space=pltpu.VMEM)] * planes,
+        out_shape=[sds((rows * heads // planes, LAT), BF16)] * planes,
         scratch_shapes=[
+            pltpu.SMEM((rows,), jnp.int32),
             pltpu.VMEM((rows, width, heads), BF16),
             pltpu.VMEM((rows, width, slots), BF16),
             pltpu.VMEM((rows * heads, LAT), BF16),
-            pltpu.SemaphoreType.DMA((2 * rows,)),
+            pltpu.SemaphoreType.DMA((2 * rows + 1,)),
         ],
         compiler_params=params(),
         name="latent_attention",
     )(
-        lengths,
+        me,
+        in_hbm(lengths),
         in_hbm(jnp.swapaxes(queries, 1, 2)),
         in_hbm(jnp.swapaxes(latent_cache, 1, 2)),
     )
+
+
+def regroup_kernel(planes, chips, *refs):
+    outs = refs[-chips:]
+    size = refs[0].shape[0] // chips
+    for q in range(chips):
+        for p in range(planes):
+            outs[q][p * size : (p + 1) * size, :] = refs[p][q * size : (q + 1) * size, :]
+
+
+def regroup(pieces, chips, after):
+    vec = pl.BlockSpec(memory_space=pltpu.VMEM)
+    planes = len(pieces)
+    size, width = pieces[0].shape
+    return pl.pallas_call(
+        functools.partial(regroup_kernel, planes, chips),
+        in_specs=[vec] * planes + [pl.BlockSpec(memory_space=pl.ANY)] * len(after),
+        out_specs=[vec] * chips,
+        out_shape=[sds((planes * size // chips, width), BF16)] * chips,
+        compiler_params=params(),
+        name="regroup",
+    )(*pieces, *after)
 
 
 def fetch_kernel(parts, *refs):
     count = len(parts)
     ins, outs, sems = refs[:count], refs[count + 1 : -1], refs[-1]
     copies = []
-    for ref, (axis, cuts) in zip(ins, parts):
+    for ref, (axis, cuts, taken) in zip(ins, parts):
         size = ref.shape[axis] // cuts
-        for c in range(cuts):
+        for c in range(taken):
             at = (slice(None),) * axis + (pl.ds(c * size, size),)
             src = ref.at[c] if axis == 0 and size == 1 else ref.at[at]
             n = len(copies)
@@ -107,14 +142,14 @@
         copy.wait()
 
 
-def fetch(weights, parts, after):
+def fetch(weights, parts, after, name):
     shapes = []
-    for w, (axis, cuts) in zip(weights, parts):
+    for w, (axis, cuts, taken) in zip(weights, parts):
         shape = list(w.shape)
         shape[axis] //= cuts
         if shape[0] == 1:
             shape = shape[1:]
-        shapes += [pltpu.VMEM(tuple(shape), w.dtype)] * cuts
+        shapes += [pltpu.VMEM(tuple(shape), w.dtype)] * taken
     out = pl.pallas_call(
         functools.partial(fetch_kernel, parts),
         in_specs=[pl.BlockSpec(memory_space=pltpu.HBM)] * len(weights)
@@ -123,65 +158,69 @@
         out_shape=shapes,
         scratch_shapes=[pltpu.SemaphoreType.DMA((len(shapes),))],
         compiler_params=params(),
-        name="fetch_weights",
+        name=name,
     )(*[in_hbm(w) for w in weights], after)
     result = []
-    for _, cuts in parts:
-        result.append(out[:cuts])
-        out = out[cuts:]
+    for _, _, taken in parts:
+        result.append(list(out[:taken]))
+        out = out[taken:]
     return result
 
 
-def project_kernel(planes, rows, tiles, me, x_ref, v_ref, w_hbm, *refs):
-    own_ref, other_ref, flat, w, sems = refs[-5:]
-    tile = w.shape[2]
+def project_kernel(planes, rows, tiles, *refs):
+    pieces, v_ref, w_hbm, early = refs[:8], refs[8], refs[9], refs[10 : 10 + EARLY]
+    own_ref, other_ref, flat, late, sems = refs[-5:]
+    tile = late.shape[2]
     copies = []
-    for t in range(tiles):
-        copy = pltpu.make_async_copy(w_hbm.at[:, pl.ds(t * tile, tile)], w.at[t], sems.at[t])
+    for t in range(EARLY, tiles):
+        n = t - EARLY
+        copy = pltpu.make_async_copy(w_hbm.at[:, pl.ds(t * tile, tile)], late.at[n], sems.at[n])
         copy.start()
         copies.append(copy)
     heads = v_ref.shape[0]
-    count = flat.shape[0]
-    i = lax.broadcasted_iota(jnp.int32, (count, 1), 0)
-    k = lax.broadcasted_iota(jnp.int32, (count, x_ref.shape[0]), 1)
-    plane = (i // rows) % planes
-    rest = i // (rows * planes)
-    home = me[0] ^ (plane * 8 + (rest % 4) * 2 + rest // 4)
-    target = home * (heads * rows) + i % rows
-    for h in range(heads):
-        pick = jnp.where(k == target + h * rows, 1.0, 0.0).astype(BF16)
-        mine = jnp.dot(pick, x_ref[...], preferred_element_type=F32).astype(BF16)
-        flat[:, h * VH : (h + 1) * VH] = jnp.dot(
-            mine, v_ref[h], preferred_element_type=F32
-        ).astype(BF16)
-    half = count // 2
+    half = flat.shape[0] // 2
+    i = lax.broadcasted_iota(jnp.int32, (half, 1), 0)
+    k = lax.broadcasted_iota(jnp.int32, (half, half * 2 * heads), 1)
+    for core in range(2):
+        x = jnp.concatenate([ref[...] for ref in pieces[4 * core : 4 * core + 4]], axis=0)
+        target = ((i // rows) * 2 + core) * (heads * rows) + i % rows
+        for h in range(heads):
+            pick = jnp.where(k == target + h * rows, 1.0, 0.0).astype(BF16)
+            mine = jnp.dot(pick, x, preferred_element_type=F32).astype(BF16)
+            flat[core * half : (core + 1) * half, h * VH : (h + 1) * VH] = jnp.dot(
+                mine, v_ref[h], preferred_element_type=F32
+            ).astype(BF16)
     for t in range(tiles):
-        copies[t].wait()
+        if t >= EARLY:
+            copies[t - EARLY].wait()
+        w = early[t][...] if t < EARLY else late[t - EARLY]
         at = slice(t * tile, (t + 1) * tile)
-        out = jnp.dot(flat[...], w[t], preferred_element_type=F32)
+        out = jnp.dot(flat[...], w, preferred_element_type=F32)
         own_ref[:, at] = out[:half]
         other_ref[:, at] = out[half:].astype(BF16)
 
 
-def project(me, by_heads, value_up, out_proj, planes, rows, after, tiles=7):
+def project(pieces, value_up, early, out_proj, planes, rows):
     count = planes * 8 * rows
     depth, features = out_proj.shape
+    tile = features // TILES
     half = count // 2
     vec = pl.BlockSpec(memory_space=pltpu.VMEM)
     return pl.pallas_call(
-        functools.partial(project_kernel, planes, rows, tiles),
-        in_specs=[SCALARS, vec, vec, pl.BlockSpec(memory_space=pltpu.HBM)]
-        + [pl.BlockSpec(memory_space=pl.ANY)] * len(after),
+        functools.partial(project_kernel, planes, rows, TILES),
+        in_specs=[vec] * 9
+        + [pl.BlockSpec(memory_space=pltpu.HBM)]
+        + [vec] * EARLY,
         out_specs=[vec, vec],
         out_shape=[sds((half, features), F32), sds((half, features), BF16)],
         scratch_shapes=[
             pltpu.VMEM((count, depth), BF16),
-            pltpu.VMEM((tiles, depth, features // tiles), BF16),
-            pltpu.SemaphoreType.DMA((tiles,)),
+            pltpu.VMEM((TILES - EARLY, depth, tile), BF16),
+            pltpu.SemaphoreType.DMA((TILES - EARLY,)),
         ],
         compiler_params=params(),
         name="projections",
-    )(me, by_heads, value_up, in_hbm(out_proj), *after)
+    )(*pieces, value_up, in_hbm(out_proj), *early)
 
 
 def add_kernel(arrived, parts, tile, *refs):
@@ -483,14 +522,18 @@
     def over_planes(messages):
         return [swap(x, k << 3) for k, x in enumerate(messages, 1)]
 
-    latents = attention(queries, latent_cache, lengths)
-    by_heads = lax.all_to_all(latents, "dp", split_axis=0, concat_axis=0, tiled=True)
-    mine = routes(route_ids, route_weights, latents)
-    pick, weight, merge = tables(me, route_ids, [mine] + over_planes([mine] * (planes - 1)), cap)
-    own, other = project(me, by_heads, value_up, out_proj, planes, rows, [pick])
+    latents = attention(me, queries, latent_cache, lengths, planes)
+    (early,) = fetch([out_proj], [(1, TILES, EARLY)], latents[0], "fetch_projections")
+    by_chip = regroup([latents[0]] + over_planes(latents[1:]), 4, early[:1])
+    chips = [by_chip[0]] + over_chips(by_chip[1:])
+    pieces = chips + [swap(x, 1) for x in chips]
+    own, other = project(pieces, value_up, early, out_proj, planes, rows)
     own, *out = add_and_cut(own, [swap(other, 1)], 4, "add_core")
+    mine = routes(route_ids, route_weights, own)
+    homes = [mine] + over_planes([mine] * (planes - 1))
+    pick, weight, merge = tables(me, route_ids, homes, cap)
     own, *out = add_and_pick(own, over_chips(out), hidden_in, pick, planes)
-    gate_up, (down_proj,) = fetch([gate_up, down_proj], [(0, 2), (0, 1)], own)
+    gate_up, (down_proj,) = fetch([gate_up, down_proj], [(0, 2, 2), (0, 1, 1)], own, "fetch_experts")
     resid, picked = norm([own] + over_planes(out), norm_gain[None], gate_up[:1])
     chips = [picked] + over_chips([picked] * 3)
     pieces = chips + [swap(x, 1) for x in chips]

time: 92.2 us -> 95 us (1.030)
  starting transfers between devices: 31.6 us -> 33.7 us
    ppermute x24 -> x34, starting transfers between devices: 24.3 us -> 33.7 us  [swap(): return lax.ppermute(x, 'dp', [(i, i ^ mask) for i in range(devices)])]
    all_to_all x1 -> x0, starting transfers between devices: 7.3 us -> none  [body(): lax.all_to_all(latents, 'dp', split_axis=0, concat_axis=0, tiled=True)]
    pallas_call x1 -> x2, Pallas kernels: 2.64 us -> 4.53 us  [fetch(): pl.pallas_call(functools.partial(fetch_kernel, parts), in_specs=[pl.Block...]
    pallas_call x2 -> x3, Pallas kernels: 9.51 us -> 8.36 us  [the longest x1 4.31 us: project(): pl.pallas_call(functools.partial(project_kernel, planes, rows, TILES), in...]
    ppermute x24 -> x34, waiting for transfers between devices: 42.5 us -> 43.1 us  [swap(): return lax.ppermute(x, 'dp', [(i, i ^ mask) for i in range(devices)])]
  transfers between devices with their start and end apart: 25 -> 34, of which waited for: 16 -> 20; matrix products, arithmetic and copies ran while one was open for 0% -> 0% of each run, Pallas kernels for 5% -> 7%
where the time goes in v5:
time: 95 us; the launch traced here: 94.8 us
  waiting for transfers between devices  43.1 us (45%)
  starting transfers between devices  33.7 us (35%)
  Pallas kernels  17.5 us (18%)
    ppermute x34, waiting for transfers between devices, swap(): return lax.ppermute(x, 'dp', [(i, i ^ mask) for i in range(devices)])  43.1 us
    ppermute x34, starting transfers between devices, swap(): return lax.ppermute(x, 'dp', [(i, i ^ mask) for i in range(devices)])  33.7 us
    pallas_call x2, Pallas kernels, fetch(): pl.pallas_call(functools.partial(fetch_kernel, parts), in_specs=[pl.Block...  4.53 us
    pallas_call x1, Pallas kernels, project(): pl.pallas_call(functools.partial(project_kernel, planes, rows, TILES), in...  4.31 us
    pallas_call x1, Pallas kernels, attention(): pl.pallas_call(functools.partial(attention_kernel, planes), in_specs=[SCA...  4.01 us
  transfers between devices with their start and end apart: 34, of which 20 were waited for; matrix products, arithmetic and copies ran while one was open for 0% of the time, Pallas kernels for 7%

profile of v5, /device:TPU:0, one launch (start us, length us, event | category | flops | bytes accessed | tf_op | source)
XLA Modules:
  0.0 94.8 jit_solution(14489397778946817154)
XLA Ops:
  0.0 4.0 %latent_attention.1 = (bf16[128,512]{1,0:T(8,128)(2,1)S(1)}, bf16[128,512]{1,0:T(8,128)(2,1)S(1)}, bf16[128,512]{1,0:T(8,128)(2,1)S(1)}, bf16[128,512]{1,0:T(8,128)(2,1)S(1)}) custom-call(s32[1]{0:T(128)} %bitcast.me, s32[4]{0:T(128)} %lengths_hbm.1, bf16[4,576,128]{2,1,0:T(8,128)(2,1)} %bitcast.4, bf16[4,576,512]{2,1,0:T(8,128)(2,1)} %bitcast.3), custom_call_target="tpu_custom_call" | custom-call | tf_op jit(solution)/shard_map/latent_attention/pallas_call | solution.py:84
  4.0 3.1 %collective-permute-start = (bf16[128,512]{1,0:T(8,128)(2,1)S(1)}, bf16[128,512]{1,0:T(8,128)(2,1)S(1)}, u32[]{:S(2)}, u32[]{:S(2)}) collective-permute-start(bf16[128,512]{1,0:T(8,128)(2,1)S(1)} %get-tuple-element.45), channel_id=1, source_target_pairs={{0,8},{1,9},{2,10},{3,11},{4,12},{5,13},{6,14},{7,15},{8,0},{9,1},... | collective-permute-start | bytes 393224 | tf_op jit(solution)/shard_map/ppermute | solution.py:517
  7.1 2.6 %collective-permute-start.1 = (bf16[128,512]{1,0:T(8,128)(2,1)S(1)}, bf16[128,512]{1,0:T(8,128)(2,1)S(1)}, u32[]{:S(2)}, u32[]{:S(2)}) collective-permute-start(bf16[128,512]{1,0:T(8,128)(2,1)S(1)} %get-tuple-element.46), channel_id=1, source_target_pairs={{0,16},{1,17},{2,18},{3,19},{4,20},{5,21},{6,22},{7,23},{8,24},{9,... | collective-permute-start | bytes 393224 | tf_op jit(solution)/shard_map/ppermute | solution.py:517
  9.7 1.9 %fetch_projections.1 = (bf16[512,1024]{1,0:T(8,128)(2,1)S(1)}, bf16[512,1024]{1,0:T(8,128)(2,1)S(1)}, bf16[512,1024]{1,0:T(8,128)(2,1)S(1)}) custom-call(bf16[512,7168]{1,0:T(8,128)(2,1)} %refs_9_.1, bf16[128,512]{1,0:T(8,128)(2,1)S(1)} %get-tuple-element.44.refs_1_.refs_0_), custom_call_target="tpu_custom_call" | custom-call | tf_op jit(solution)/shard_map/fetch_projections/pallas_call | solution.py:153
  12.2 7.9 %collective-permute-done.1.refs_2_ = bf16[128,512]{1,0:T(8,128)(2,1)S(1)} collective-permute-done((bf16[128,512]{1,0:T(8,128)(2,1)S(1)}, bf16[128,512]{1,0:T(8,128)(2,1)S(1)}, u32[]{:S(2)}, u32[]{:S(2)}) %collective-permute-start.1) | collective-permute-done | bytes 131104 | tf_op jit(solution)/shard_map/ppermute | solution.py:517
  20.1 1.6 %collective-permute-start.3 = (bf16[128,512]{1,0:T(8,128)(2,1)S(1)}, bf16[128,512]{1,0:T(8,128)(2,1)S(1)}, u32[]{:S(2)}, u32[]{:S(2)}) collective-permute-start(bf16[128,512]{1,0:T(8,128)(2,1)S(1)} %get-tuple-element.50), channel_id=1, source_target_pairs={{0,2},{1,3},{2,0},{3,1},{4,6},{5,7},{6,4},{7,5},{8,10},{9,11},{10,... | collective-permute-start | bytes 393224 | tf_op jit(solution)/shard_map/ppermute | solution.py:517
  23.6 1.7 %collective-permute-done.3.refs_1_ = bf16[128,512]{1,0:T(8,128)(2,1)S(1)} collective-permute-done((bf16[128,512]{1,0:T(8,128)(2,1)S(1)}, bf16[128,512]{1,0:T(8,128)(2,1)S(1)}, u32[]{:S(2)}, u32[]{:S(2)}) %collective-permute-start.3) | collective-permute-done | bytes 131104 | tf_op jit(solution)/shard_map/ppermute | solution.py:517
  26.6 2.4 %collective-permute-done.5.refs_3_ = bf16[128,512]{1,0:T(8,128)(2,1)S(1)} collective-permute-done((bf16[128,512]{1,0:T(8,128)(2,1)S(1)}, bf16[128,512]{1,0:T(8,128)(2,1)S(1)}, u32[]{:S(2)}, u32[]{:S(2)}) %collective-permute-start.5) | collective-permute-done | bytes 131104 | tf_op jit(solution)/shard_map/ppermute | solution.py:517
  30.4 4.3 %projections.1 = (f32[64,7168]{1,0:T(8,128)S(1)}, bf16[64,7168]{1,0:T(8,128)(2,1)S(1)}) custom-call(bf16[128,512]{1,0:T(8,128)(2,1)S(1)} %get-tuple-element.49.refs_0_, bf16[128,512]{1,0:T(8,128)(2,1)S(1)} %collective-permute-done.3.refs_1_, bf16[128,512]{1,0:T(8,128)(2,1)S(1)} %collective-permute-done.4.refs_2_, ...), custom_call_target="tpu_custom_call" | custom-call | tf_op jit(solution)/shard_map/projections/pallas_call | solution.py:209
  34.9 2.3 %collective-permute-done.10.refs_1_ = bf16[64,7168]{1,0:T(8,128)(2,1)S(1)} collective-permute-done((bf16[64,7168]{1,0:T(8,128)(2,1)S(1)}, bf16[64,7168]{1,0:T(8,128)(2,1)S(1)}, u32[]{:S(2)}, u32[]{:S(2)}) %collective-permute-start.10) | collective-permute-done | bytes 917536 | tf_op jit(solution)/shard_map/ppermute | solution.py:517
  38.5 2.4 %collective-permute-start.16 = (bf16[16,7168]{1,0:T(8,128)(2,1)S(1)}, bf16[16,7168]{1,0:T(8,128)(2,1)S(1)}, u32[]{:S(2)}, u32[]{:S(2)}) collective-permute-start(bf16[16,7168]{1,0:T(8,128)(2,1)S(1)} %get-tuple-element.61), channel_id=1, source_target_pairs={{0,6},{1,7},{2,4},{3,5},{4,2},{5,3},{6,0},{7,1},{8,14},{9,15},{10,... | collective-permute-start | bytes 688136 | tf_op jit(solution)/shard_map/ppermute | solution.py:517
  41.8 2.4 %collective-permute-start.13 = (f32[8,128]{1,0:T(8,128)S(1)}, f32[8,128]{1,0:T(8,128)S(1)}, u32[]{:S(2)}, u32[]{:S(2)}) collective-permute-start(f32[8,128]{1,0:T(8,128)S(1)} %routes.1.refs_0_), channel_id=1, source_target_pairs={{0,24},{1,25},{2,26},{3,27},{4,28},{5,29},{6,30},{7,31},{8,16},{9,... | collective-permute-start | bytes 12296 | tf_op jit(solution)/shard_map/ppermute | solution.py:517
  45.4 1.9 %collective-permute-done.13.refs_3_ = f32[8,128]{1,0:T(8,128)S(1)} collective-permute-done((f32[8,128]{1,0:T(8,128)S(1)}, f32[8,128]{1,0:T(8,128)S(1)}, u32[]{:S(2)}, u32[]{:S(2)}) %collective-permute-start.13) | collective-permute-done | bytes 4128 | tf_op jit(solution)/shard_map/ppermute | solution.py:517
  48.7 2.2 %collective-permute-done.11.refs_1_ = f32[8,128]{1,0:T(8,128)S(1)} collective-permute-done((f32[8,128]{1,0:T(8,128)S(1)}, f32[8,128]{1,0:T(8,128)S(1)}, u32[]{:S(2)}, u32[]{:S(2)}) %collective-permute-start.11) | collective-permute-done | bytes 4128 | tf_op jit(solution)/shard_map/ppermute | solution.py:517
  53.2 2.1 %collective-permute-start.18 = (bf16[8,7168]{1,0:T(8,128)(2,1)S(1)}, bf16[8,7168]{1,0:T(8,128)(2,1)S(1)}, u32[]{:S(2)}, u32[]{:S(2)}) collective-permute-start(bf16[8,7168]{1,0:T(8,128)(2,1)S(1)} %get-tuple-element.65), channel_id=1, source_target_pairs={{0,16},{1,17},{2,18},{3,19},{4,20},{5,21},{6,22},{7,23},{8,24},{9,... | collective-permute-start | bytes 344072 | tf_op jit(solution)/shard_map/ppermute | solution.py:517
  56.9 2.6 %fetch_experts.1 = (bf16[7168,128]{1,0:T(8,128)(2,1)S(1)}, bf16[7168,128]{1,0:T(8,128)(2,1)S(1)}, bf16[128,7168]{1,0:T(8,128)(2,1)S(1)}) custom-call(bf16[2,7168,128]{2,1,0:T(8,128)(2,1)} %refs_0_.3, bf16[128,7168]{1,0:T(8,128)(2,1)} %refs_1_.1, f32[8,7168]{1,0:T(8,128)S(1)} %get-tuple-element.63.refs_2_.refs_0_), custom_call_target="tpu_custom_call" | custom-call | tf_op jit(solution)/shard_map/fetch_experts/pallas_call | solution.py:153
  59.6 5.2 %collective-permute-done.18.refs_2_ = bf16[8,7168]{1,0:T(8,128)(2,1)S(1)} collective-permute-done((bf16[8,7168]{1,0:T(8,128)(2,1)S(1)}, bf16[8,7168]{1,0:T(8,128)(2,1)S(1)}, u32[]{:S(2)}, u32[]{:S(2)}) %collective-permute-start.18) | collective-permute-done | bytes 114720 | tf_op jit(solution)/shard_map/ppermute | solution.py:517
  67.0 1.5 %collective-permute-start.20 = (bf16[8,7168]{1,0:T(8,128)(2,1)S(1)}, bf16[8,7168]{1,0:T(8,128)(2,1)S(1)}, u32[]{:S(2)}, u32[]{:S(2)}) collective-permute-start(bf16[8,7168]{1,0:T(8,128)(2,1)S(1)} %get-tuple-element.68.refs_0_), channel_id=1, source_target_pairs={{0,2},{1,3},{2,0},{3,1},{4,6},{5,7},{6,4},{7,5},{8,10},{9,11},{10,... | collective-permute-start | bytes 344072 | tf_op jit(solution)/shard_map/ppermute | solution.py:517
  68.5 2.3 %collective-permute-done.22.refs_3_ = bf16[8,7168]{1,0:T(8,128)(2,1)S(1)} collective-permute-done((bf16[8,7168]{1,0:T(8,128)(2,1)S(1)}, bf16[8,7168]{1,0:T(8,128)(2,1)S(1)}, u32[]{:S(2)}, u32[]{:S(2)}) %collective-permute-start.22) | collective-permute-done | bytes 114720 | tf_op jit(solution)/shard_map/ppermute | solution.py:517
  80.0 2.4 %collective-permute-done.28.a_ref = bf16[8,7168]{1,0:T(8,128)(2,1)S(1)} collective-permute-done((bf16[8,7168]{1,0:T(8,128)(2,1)S(1)}, bf16[8,7168]{1,0:T(8,128)(2,1)S(1)}, u32[]{:S(2)}, u32[]{:S(2)}) %collective-permute-start.28) | collective-permute-done | bytes 114720 | tf_op jit(solution)/shard_map/ppermute | solution.py:517
  82.4 2.7 %collective-permute-done.29.b_ref = bf16[8,7168]{1,0:T(8,128)(2,1)S(1)} collective-permute-done((bf16[8,7168]{1,0:T(8,128)(2,1)S(1)}, bf16[8,7168]{1,0:T(8,128)(2,1)S(1)}, u32[]{:S(2)}, u32[]{:S(2)}) %collective-permute-start.29) | collective-permute-done | bytes 114720 | tf_op jit(solution)/shard_map/ppermute | solution.py:517
  85.2 1.9 %collective-permute-start.31 = (bf16[2,7168]{1,0:T(2,128)(2,1)S(1)}, bf16[2,7168]{1,0:T(2,128)(2,1)S(1)}, u32[]{:S(2)}, u32[]{:S(2)}) collective-permute-start(bf16[2,7168]{1,0:T(2,128)(2,1)S(1)} %get-tuple-element.80), channel_id=1, source_target_pairs={{0,8},{1,9},{2,10},{3,11},{4,12},{5,13},{6,14},{7,15},{8,0},{9,1},... | collective-permute-start | bytes 86024 | tf_op jit(solution)/shard_map/ppermute | solution.py:517
  89.7 2.7 %collective-permute-done.32.refs_2_ = bf16[2,7168]{1,0:T(2,128)(2,1)S(1)} collective-permute-done((bf16[2,7168]{1,0:T(2,128)(2,1)S(1)}, bf16[2,7168]{1,0:T(2,128)(2,1)S(1)}, u32[]{:S(2)}, u32[]{:S(2)}) %collective-permute-start.32) | collective-permute-done | bytes 28704 | tf_op jit(solution)/shard_map/ppermute | solution.py:517
  92.4 1.5 %collective-permute-done.33.refs_3_ = bf16[2,7168]{1,0:T(2,128)(2,1)S(1)} collective-permute-done((bf16[2,7168]{1,0:T(2,128)(2,1)S(1)}, bf16[2,7168]{1,0:T(2,128)(2,1)S(1)}, u32[]{:S(2)}, u32[]{:S(2)}) %collective-permute-start.33) | collective-permute-done | bytes 28704 | tf_op jit(solution)/shard_map/ppermute | solution.py:517
  (71 shorter events, 29.0 us)
Async XLA Ops:
  4.0 8.1 %collective-permute-start = (bf16[128,512]{1,0:T(8,128)(2,1)S(1)}, bf16[128,512]{1,0:T(8,128)(2,1)S(1)}, u32[]{:S(2)}, u32[]{:S(2)}) collective-permute-start(bf16[128,512]{1,0:T(8,128)(2,1)S(1)} %get-tuple-element.45), channel_id=1, source_target_pairs={{0,8},{1,9},{2,10},{3,11},{4,12},{5,13},{6,14},{7,15},{8,0},{9,1},... | collective-permute-start | bytes 393224 | tf_op jit(solution)/shard_map/ppermute | solution.py:517
  7.1 12.9 %collective-permute-start.1 = (bf16[128,512]{1,0:T(8,128)(2,1)S(1)}, bf16[128,512]{1,0:T(8,128)(2,1)S(1)}, u32[]{:S(2)}, u32[]{:S(2)}) collective-permute-start(bf16[128,512]{1,0:T(8,128)(2,1)S(1)} %get-tuple-element.46), channel_id=1, source_target_pairs={{0,16},{1,17},{2,18},{3,19},{4,20},{5,21},{6,22},{7,23},{8,24},{9,... | collective-permute-start | bytes 393224 | tf_op jit(solution)/shard_map/ppermute | solution.py:517
  9.7 10.3 %collective-permute-start.2 = (bf16[128,512]{1,0:T(8,128)(2,1)S(1)}, bf16[128,512]{1,0:T(8,128)(2,1)S(1)}, u32[]{:S(2)}, u32[]{:S(2)}) collective-permute-start(bf16[128,512]{1,0:T(8,128)(2,1)S(1)} %get-tuple-element.47), channel_id=1, source_target_pairs={{0,24},{1,25},{2,26},{3,27},{4,28},{5,29},{6,30},{7,31},{8,16},{9,... | collective-permute-start | bytes 393224 | tf_op jit(solution)/shard_map/ppermute | solution.py:517
  20.1 5.3 %collective-permute-start.3 = (bf16[128,512]{1,0:T(8,128)(2,1)S(1)}, bf16[128,512]{1,0:T(8,128)(2,1)S(1)}, u32[]{:S(2)}, u32[]{:S(2)}) collective-permute-start(bf16[128,512]{1,0:T(8,128)(2,1)S(1)} %get-tuple-element.50), channel_id=1, source_target_pairs={{0,2},{1,3},{2,0},{3,1},{4,6},{5,7},{6,4},{7,5},{8,10},{9,11},{10,... | collective-permute-start | bytes 393224 | tf_op jit(solution)/shard_map/ppermute | solution.py:517
  21.6 5.0 %collective-permute-start.4 = (bf16[128,512]{1,0:T(8,128)(2,1)S(1)}, bf16[128,512]{1,0:T(8,128)(2,1)S(1)}, u32[]{:S(2)}, u32[]{:S(2)}) collective-permute-start(bf16[128,512]{1,0:T(8,128)(2,1)S(1)} %get-tuple-element.51), channel_id=1, source_target_pairs={{0,4},{1,5},{2,6},{3,7},{4,0},{5,1},{6,2},{7,3},{8,12},{9,13},{10,... | collective-permute-start | bytes 393224 | tf_op jit(solution)/shard_map/ppermute | solution.py:517
  23.2 5.9 %collective-permute-start.5 = (bf16[128,512]{1,0:T(8,128)(2,1)S(1)}, bf16[128,512]{1,0:T(8,128)(2,1)S(1)}, u32[]{:S(2)}, u32[]{:S(2)}) collective-permute-start(bf16[128,512]{1,0:T(8,128)(2,1)S(1)} %get-tuple-element.52), channel_id=1, source_target_pairs={{0,6},{1,7},{2,4},{3,5},{4,2},{5,3},{6,0},{7,1},{8,14},{9,15},{10,... | collective-permute-start | bytes 393224 | tf_op jit(solution)/shard_map/ppermute | solution.py:517
  23.6 5.4 %collective-permute-start.6 = (bf16[128,512]{1,0:T(8,128)(2,1)S(1)}, bf16[128,512]{1,0:T(8,128)(2,1)S(1)}, u32[]{:S(2)}, u32[]{:S(2)}) collective-permute-start(bf16[128,512]{1,0:T(8,128)(2,1)S(1)} %get-tuple-element.49.refs_0_), channel_id=1, source_target_pairs={{0,1},{1,0},{2,3},{3,2},{4,5},{5,4},{6,7},{7,6},{8,9},{9,8},{10,11... | collective-permute-start | bytes 393224 | tf_op jit(solution)/shard_map/ppermute | solution.py:517
  37.4 14.6 %collective-permute-start.14 = (bf16[16,7168]{1,0:T(8,128)(2,1)S(1)}, bf16[16,7168]{1,0:T(8,128)(2,1)S(1)}, u32[]{:S(2)}, u32[]{:S(2)}) collective-permute-start(bf16[16,7168]{1,0:T(8,128)(2,1)S(1)} %get-tuple-element.59), channel_id=1, source_target_pairs={{0,2},{1,3},{2,0},{3,1},{4,6},{5,7},{6,4},{7,5},{8,10},{9,11},{10,... | collective-permute-start | bytes 688136 | tf_op jit(solution)/shard_map/ppermute | solution.py:517
  38.0 14.0 %collective-permute-start.15 = (bf16[16,7168]{1,0:T(8,128)(2,1)S(1)}, bf16[16,7168]{1,0:T(8,128)(2,1)S(1)}, u32[]{:S(2)}, u32[]{:S(2)}) collective-permute-start(bf16[16,7168]{1,0:T(8,128)(2,1)S(1)} %get-tuple-element.60), channel_id=1, source_target_pairs={{0,4},{1,5},{2,6},{3,7},{4,0},{5,1},{6,2},{7,3},{8,12},{9,13},{10,... | collective-permute-start | bytes 688136 | tf_op jit(solution)/shard_map/ppermute | solution.py:517
  38.5 13.5 %collective-permute-start.16 = (bf16[16,7168]{1,0:T(8,128)(2,1)S(1)}, bf16[16,7168]{1,0:T(8,128)(2,1)S(1)}, u32[]{:S(2)}, u32[]{:S(2)}) collective-permute-start(bf16[16,7168]{1,0:T(8,128)(2,1)S(1)} %get-tuple-element.61), channel_id=1, source_target_pairs={{0,6},{1,7},{2,4},{3,5},{4,2},{5,3},{6,0},{7,1},{8,14},{9,15},{10,... | collective-permute-start | bytes 688136 | tf_op jit(solution)/shard_map/ppermute | solution.py:517
  41.8 5.5 %collective-permute-start.13 = (f32[8,128]{1,0:T(8,128)S(1)}, f32[8,128]{1,0:T(8,128)S(1)}, u32[]{:S(2)}, u32[]{:S(2)}) collective-permute-start(f32[8,128]{1,0:T(8,128)S(1)} %routes.1.refs_0_), channel_id=1, source_target_pairs={{0,24},{1,25},{2,26},{3,27},{4,28},{5,29},{6,30},{7,31},{8,16},{9,... | collective-permute-start | bytes 12296 | tf_op jit(solution)/shard_map/ppermute | solution.py:517
  44.2 4.5 %collective-permute-start.12 = (f32[8,128]{1,0:T(8,128)S(1)}, f32[8,128]{1,0:T(8,128)S(1)}, u32[]{:S(2)}, u32[]{:S(2)}) collective-permute-start(f32[8,128]{1,0:T(8,128)S(1)} %routes.1.refs_0_), channel_id=1, source_target_pairs={{0,16},{1,17},{2,18},{3,19},{4,20},{5,21},{6,22},{7,23},{8,24},{9,... | collective-permute-start | bytes 12296 | tf_op jit(solution)/shard_map/ppermute | solution.py:517
  52.4 7.1 %collective-permute-start.17 = (bf16[8,7168]{1,0:T(8,128)(2,1)S(1)}, bf16[8,7168]{1,0:T(8,128)(2,1)S(1)}, u32[]{:S(2)}, u32[]{:S(2)}) collective-permute-start(bf16[8,7168]{1,0:T(8,128)(2,1)S(1)} %get-tuple-element.64), channel_id=1, source_target_pairs={{0,8},{1,9},{2,10},{3,11},{4,12},{5,13},{6,14},{7,15},{8,0},{9,1},... | collective-permute-start | bytes 344072 | tf_op jit(solution)/shard_map/ppermute | solution.py:517
  53.2 11.5 %collective-permute-start.18 = (bf16[8,7168]{1,0:T(8,128)(2,1)S(1)}, bf16[8,7168]{1,0:T(8,128)(2,1)S(1)}, u32[]{:S(2)}, u32[]{:S(2)}) collective-permute-start(bf16[8,7168]{1,0:T(8,128)(2,1)S(1)} %get-tuple-element.65), channel_id=1, source_target_pairs={{0,16},{1,17},{2,18},{3,19},{4,20},{5,21},{6,22},{7,23},{8,24},{9,... | collective-permute-start | bytes 344072 | tf_op jit(solution)/shard_map/ppermute | solution.py:517
  55.4 9.4 %collective-permute-start.19 = (bf16[8,7168]{1,0:T(8,128)(2,1)S(1)}, bf16[8,7168]{1,0:T(8,128)(2,1)S(1)}, u32[]{:S(2)}, u32[]{:S(2)}) collective-permute-start(bf16[8,7168]{1,0:T(8,128)(2,1)S(1)} %get-tuple-element.66), channel_id=1, source_target_pairs={{0,24},{1,25},{2,26},{3,27},{4,28},{5,29},{6,30},{7,31},{8,16},{9,... | collective-permute-start | bytes 344072 | tf_op jit(solution)/shard_map/ppermute | solution.py:517
  65.0 5.9 %collective-permute-start.22 = (bf16[8,7168]{1,0:T(8,128)(2,1)S(1)}, bf16[8,7168]{1,0:T(8,128)(2,1)S(1)}, u32[]{:S(2)}, u32[]{:S(2)}) collective-permute-start(bf16[8,7168]{1,0:T(8,128)(2,1)S(1)} %get-tuple-element.68.refs_0_), channel_id=1, source_target_pairs={{0,6},{1,7},{2,4},{3,5},{4,2},{5,3},{6,0},{7,1},{8,14},{9,15},{10,... | collective-permute-start | bytes 344072 | tf_op jit(solution)/shard_map/ppermute | solution.py:517
  66.0 5.9 %collective-permute-start.21 = (bf16[8,7168]{1,0:T(8,128)(2,1)S(1)}, bf16[8,7168]{1,0:T(8,128)(2,1)S(1)}, u32[]{:S(2)}, u32[]{:S(2)}) collective-permute-start(bf16[8,7168]{1,0:T(8,128)(2,1)S(1)} %get-tuple-element.68.refs_0_), channel_id=1, source_target_pairs={{0,4},{1,5},{2,6},{3,7},{4,0},{5,1},{6,2},{7,3},{8,12},{9,13},{10,... | collective-permute-start | bytes 344072 | tf_op jit(solution)/shard_map/ppermute | solution.py:517
  67.0 5.0 %collective-permute-start.20 = (bf16[8,7168]{1,0:T(8,128)(2,1)S(1)}, bf16[8,7168]{1,0:T(8,128)(2,1)S(1)}, u32[]{:S(2)}, u32[]{:S(2)}) collective-permute-start(bf16[8,7168]{1,0:T(8,128)(2,1)S(1)} %get-tuple-element.68.refs_0_), channel_id=1, source_target_pairs={{0,2},{1,3},{2,0},{3,1},{4,6},{5,7},{6,4},{7,5},{8,10},{9,11},{10,... | collective-permute-start | bytes 344072 | tf_op jit(solution)/shard_map/ppermute | solution.py:517
  76.5 6.0 %collective-permute-start.28 = (bf16[8,7168]{1,0:T(8,128)(2,1)S(1)}, bf16[8,7168]{1,0:T(8,128)(2,1)S(1)}, u32[]{:S(2)}, u32[]{:S(2)}) collective-permute-start(bf16[8,7168]{1,0:T(8,128)(2,1)S(1)} %get-tuple-element.74), channel_id=1, source_target_pairs={{0,2},{1,3},{2,0},{3,1},{4,6},{5,7},{6,4},{7,5},{8,10},{9,11},{10,... | collective-permute-start | bytes 344072 | tf_op jit(solution)/shard_map/ppermute | solution.py:517
  77.7 7.4 %collective-permute-start.29 = (bf16[8,7168]{1,0:T(8,128)(2,1)S(1)}, bf16[8,7168]{1,0:T(8,128)(2,1)S(1)}, u32[]{:S(2)}, u32[]{:S(2)}) collective-permute-start(bf16[8,7168]{1,0:T(8,128)(2,1)S(1)} %get-tuple-element.75), channel_id=1, source_target_pairs={{0,4},{1,5},{2,6},{3,7},{4,0},{5,1},{6,2},{7,3},{8,12},{9,13},{10,... | collective-permute-start | bytes 344072 | tf_op jit(solution)/shard_map/ppermute | solution.py:517
  78.7 6.4 %collective-permute-start.30 = (bf16[8,7168]{1,0:T(8,128)(2,1)S(1)}, bf16[8,7168]{1,0:T(8,128)(2,1)S(1)}, u32[]{:S(2)}, u32[]{:S(2)}) collective-permute-start(bf16[8,7168]{1,0:T(8,128)(2,1)S(1)} %get-tuple-element.76), channel_id=1, source_target_pairs={{0,6},{1,7},{2,4},{3,5},{4,2},{5,3},{6,0},{7,1},{8,14},{9,15},{10,... | collective-permute-start | bytes 344072 | tf_op jit(solution)/shard_map/ppermute | solution.py:517
  85.2 4.5 %collective-permute-start.31 = (bf16[2,7168]{1,0:T(2,128)(2,1)S(1)}, bf16[2,7168]{1,0:T(2,128)(2,1)S(1)}, u32[]{:S(2)}, u32[]{:S(2)}) collective-permute-start(bf16[2,7168]{1,0:T(2,128)(2,1)S(1)} %get-tuple-element.80), channel_id=1, source_target_pairs={{0,8},{1,9},{2,10},{3,11},{4,12},{5,13},{6,14},{7,15},{8,0},{9,1},... | collective-permute-start | bytes 86024 | tf_op jit(solution)/shard_map/ppermute | solution.py:517
  87.1 5.3 %collective-permute-start.32 = (bf16[2,7168]{1,0:T(2,128)(2,1)S(1)}, bf16[2,7168]{1,0:T(2,128)(2,1)S(1)}, u32[]{:S(2)}, u32[]{:S(2)}) collective-permute-start(bf16[2,7168]{1,0:T(2,128)(2,1)S(1)} %get-tuple-element.81), channel_id=1, source_target_pairs={{0,16},{1,17},{2,18},{3,19},{4,20},{5,21},{6,22},{7,23},{8,24},{9,... | collective-permute-start | bytes 86024 | tf_op jit(solution)/shard_map/ppermute | solution.py:517
  88.2 5.7 %collective-permute-start.33 = (bf16[2,7168]{1,0:T(2,128)(2,1)S(1)}, bf16[2,7168]{1,0:T(2,128)(2,1)S(1)}, u32[]{:S(2)}, u32[]{:S(2)}) collective-permute-start(bf16[2,7168]{1,0:T(2,128)(2,1)S(1)} %get-tuple-element.82), channel_id=1, source_target_pairs={{0,24},{1,25},{2,26},{3,27},{4,28},{5,29},{6,30},{7,31},{8,16},{9,... | collective-permute-start | bytes 86024 | tf_op jit(solution)/shard_map/ppermute | solution.py:517
  (15 other events, 92.2 us)

commit v6 on v4

--- a/solution.py
+++ b/solution.py
@@ -15,6 +15,8 @@
 MASKED = -1e30
 EPSILON = 1e-06
 VMEM = 24 * 1024 * 1024
+TILES = 7
+EARLY = 2
 
 F32 = jnp.float32
 BF16 = jnp.bfloat16
@@ -37,14 +39,17 @@
     return pl.BlockSpec(shape, lambda *_: (0,) * len(shape))
 
 
-def attention_kernel(lengths, q_hbm, k_hbm, o_ref, queries, keys, lat, sems):
+def attention_kernel(lengths_hbm, q_hbm, k_hbm, o_ref, lengths, queries, keys, lat, sems):
     rows, _, heads = queries.shape
+    live = pltpu.make_async_copy(lengths_hbm, lengths, sems.at[2 * rows])
+    live.start()
     copies = []
     for r in range(rows):
         for n, (src, dst) in enumerate(((q_hbm, queries), (k_hbm, keys))):
             copy = pltpu.make_async_copy(src.at[r], dst.at[r], sems.at[2 * r + n])
             copy.start()
             copies.append(copy)
+    live.wait()
     for r in range(rows):
         copies[2 * r].wait()
         copies[2 * r + 1].wait()
@@ -72,19 +77,20 @@
     hbm = pl.BlockSpec(memory_space=pltpu.HBM)
     return pl.pallas_call(
         attention_kernel,
-        in_specs=[SCALARS, hbm, hbm],
+        in_specs=[hbm, hbm, hbm],
         out_specs=pl.BlockSpec(memory_space=pltpu.VMEM),
         out_shape=sds((rows * heads, LAT), BF16),
         scratch_shapes=[
+            pltpu.SMEM((rows,), jnp.int32),
             pltpu.VMEM((rows, width, heads), BF16),
             pltpu.VMEM((rows, width, slots), BF16),
             pltpu.VMEM((rows * heads, LAT), BF16),
-            pltpu.SemaphoreType.DMA((2 * rows,)),
+            pltpu.SemaphoreType.DMA((2 * rows + 1,)),
         ],
         compiler_params=params(),
         name="latent_attention",
     )(
-        lengths,
+        in_hbm(lengths),
         in_hbm(jnp.swapaxes(queries, 1, 2)),
         in_hbm(jnp.swapaxes(latent_cache, 1, 2)),
     )
@@ -94,9 +100,9 @@
     count = len(parts)
     ins, outs, sems = refs[:count], refs[count + 1 : -1], refs[-1]
     copies = []
-    for ref, (axis, cuts) in zip(ins, parts):
+    for ref, (axis, cuts, taken) in zip(ins, parts):
         size = ref.shape[axis] // cuts
-        for c in range(cuts):
+        for c in range(taken):
             at = (slice(None),) * axis + (pl.ds(c * size, size),)
             src = ref.at[c] if axis == 0 and size == 1 else ref.at[at]
             n = len(copies)
@@ -107,14 +113,14 @@
         copy.wait()
 
 
-def fetch(weights, parts, after):
+def fetch(weights, parts, after, name):
     shapes = []
-    for w, (axis, cuts) in zip(weights, parts):
+    for w, (axis, cuts, taken) in zip(weights, parts):
         shape = list(w.shape)
         shape[axis] //= cuts
         if shape[0] == 1:
             shape = shape[1:]
-        shapes += [pltpu.VMEM(tuple(shape), w.dtype)] * cuts
+        shapes += [pltpu.VMEM(tuple(shape), w.dtype)] * taken
     out = pl.pallas_call(
         functools.partial(fetch_kernel, parts),
         in_specs=[pl.BlockSpec(memory_space=pltpu.HBM)] * len(weights)
@@ -123,21 +129,23 @@
         out_shape=shapes,
         scratch_shapes=[pltpu.SemaphoreType.DMA((len(shapes),))],
         compiler_params=params(),
-        name="fetch_weights",
+        name=name,
     )(*[in_hbm(w) for w in weights], after)
     result = []
-    for _, cuts in parts:
-        result.append(out[:cuts])
-        out = out[cuts:]
+    for _, _, taken in parts:
+        result.append(list(out[:taken]))
+        out = out[taken:]
     return result
 
 
-def project_kernel(planes, rows, tiles, me, x_ref, v_ref, w_hbm, *refs):
-    own_ref, other_ref, flat, w, sems = refs[-5:]
-    tile = w.shape[2]
+def project_kernel(planes, rows, me, x_ref, v_ref, w_hbm, *refs):
+    early = refs[:EARLY]
+    own_ref, other_ref, flat, late, sems = refs[-5:]
+    tile = late.shape[2]
     copies = []
-    for t in range(tiles):
-        copy = pltpu.make_async_copy(w_hbm.at[:, pl.ds(t * tile, tile)], w.at[t], sems.at[t])
+    for t in range(EARLY, TILES):
+        n = t - EARLY
+        copy = pltpu.make_async_copy(w_hbm.at[:, pl.ds(t * tile, tile)], late.at[n], sems.at[n])
         copy.start()
         copies.append(copy)
     heads = v_ref.shape[0]
@@ -155,33 +163,36 @@
             mine, v_ref[h], preferred_element_type=F32
         ).astype(BF16)
     half = count // 2
-    for t in range(tiles):
-        copies[t].wait()
+    for t in range(TILES):
+        if t >= EARLY:
+            copies[t - EARLY].wait()
+        w = early[t][...] if t < EARLY else late[t - EARLY]
         at = slice(t * tile, (t + 1) * tile)
-        out = jnp.dot(flat[...], w[t], preferred_element_type=F32)
+        out = jnp.dot(flat[...], w, preferred_element_type=F32)
         own_ref[:, at] = out[:half]
         other_ref[:, at] = out[half:].astype(BF16)
 
 
-def project(me, by_heads, value_up, out_proj, planes, rows, after, tiles=7):
+def project(me, by_heads, value_up, out_proj, early, planes, rows, after):
     count = planes * 8 * rows
     depth, features = out_proj.shape
     half = count // 2
     vec = pl.BlockSpec(memory_space=pltpu.VMEM)
     return pl.pallas_call(
-        functools.partial(project_kernel, planes, rows, tiles),
+        functools.partial(project_kernel, planes, rows),
         in_specs=[SCALARS, vec, vec, pl.BlockSpec(memory_space=pltpu.HBM)]
+        + [vec] * EARLY
         + [pl.BlockSpec(memory_space=pl.ANY)] * len(after),
         out_specs=[vec, vec],
         out_shape=[sds((half, features), F32), sds((half, features), BF16)],
         scratch_shapes=[
             pltpu.VMEM((count, depth), BF16),
-            pltpu.VMEM((tiles, depth, features // tiles), BF16),
-            pltpu.SemaphoreType.DMA((tiles,)),
+            pltpu.VMEM((TILES - EARLY, depth, features // TILES), BF16),
+            pltpu.SemaphoreType.DMA((TILES - EARLY,)),
         ],
         compiler_params=params(),
         name="projections",
-    )(me, by_heads, value_up, in_hbm(out_proj), *after)
+    )(me, by_heads, value_up, in_hbm(out_proj), *early, *after)
 
 
 def add_kernel(arrived, parts, tile, *refs):
@@ -251,7 +262,7 @@
 
 def tables_kernel(rows, picks, planes, cap, me, ids, *refs):
     homes = refs[:planes]
-    pick_ref, weight_ref, merge_ref = refs[planes:]
+    pick_ref, weight_ref, merge_ref = refs[planes + 1 :]
     plane = me[0] // 8
     found = {}
     for k in range(planes):
@@ -293,13 +304,13 @@
     merge_ref[...] = jnp.where(merge, 1.0, 0.0).astype(BF16)
 
 
-def tables(me, ids, homes, cap):
+def tables(me, ids, homes, cap, after):
     rows, picks = ids.shape
     planes = len(homes)
     vec = pl.BlockSpec(memory_space=pltpu.VMEM)
     return pl.pallas_call(
         functools.partial(tables_kernel, rows, picks, planes, cap),
-        in_specs=[SCALARS] * (2 + planes),
+        in_specs=[SCALARS] * (2 + planes) + [pl.BlockSpec(memory_space=pl.ANY)],
         out_specs=[vec] * 3,
         out_shape=[
             sds((planes * planes * cap, planes * rows), F32),
@@ -308,7 +319,7 @@
         ],
         compiler_params=params(),
         name="route_tables",
-    )(me, ids, *homes)
+    )(me, ids, *homes, after)
 
 
 def pick_rows(pick, values):
@@ -485,12 +496,14 @@
 
     latents = attention(queries, latent_cache, lengths)
     by_heads = lax.all_to_all(latents, "dp", split_axis=0, concat_axis=0, tiled=True)
+    (early,) = fetch([out_proj], [(1, TILES, EARLY)], latents, "fetch_projections")
     mine = routes(route_ids, route_weights, latents)
-    pick, weight, merge = tables(me, route_ids, [mine] + over_planes([mine] * (planes - 1)), cap)
-    own, other = project(me, by_heads, value_up, out_proj, planes, rows, [pick])
+    homes = [mine] + over_planes([mine] * (planes - 1))
+    own, other = project(me, by_heads, value_up, out_proj, early, planes, rows, homes[1:])
     own, *out = add_and_cut(own, [swap(other, 1)], 4, "add_core")
+    pick, weight, merge = tables(me, route_ids, homes, cap, own)
     own, *out = add_and_pick(own, over_chips(out), hidden_in, pick, planes)
-    gate_up, (down_proj,) = fetch([gate_up, down_proj], [(0, 2), (0, 1)], own)
+    gate_up, (down_proj,) = fetch([gate_up, down_proj], [(0, 2, 2), (0, 1, 1)], own, "fetch_experts")
     resid, picked = norm([own] + over_planes(out), norm_gain[None], gate_up[:1])
     chips = [picked] + over_chips([picked] * 3)
     pieces = chips + [swap(x, 1) for x in chips]

time: 92.2 us -> 90.1 us (0.977)
  waiting for transfers between devices: 42.5 us -> 39.8 us
    ppermute x24, waiting for transfers between devices: 42.5 us -> 39.4 us  [swap(): return lax.ppermute(x, 'dp', [(i, i ^ mask) for i in range(devices)])]
    pallas_call x1 -> x2, Pallas kernels: 2.64 us -> 4.26 us  [fetch(): pl.pallas_call(functools.partial(fetch_kernel, parts), in_specs=[pl.Block...]
  transfers between devices with their start and end apart: 25 -> 25, of which waited for: 16 -> 17; matrix products, arithmetic and copies ran while one was open for 0% -> 0% of each run, Pallas kernels for 5% -> 7%
where the time goes in v6:
time: 90.1 us; the launch traced here: 89.8 us
  waiting for transfers between devices  39.8 us (44%)
  starting transfers between devices  32 us (36%)
  Pallas kernels  17.7 us (20%)
    ppermute x24, waiting for transfers between devices, swap(): return lax.ppermute(x, 'dp', [(i, i ^ mask) for i in range(devices)])  39.4 us
    ppermute x24, starting transfers between devices, swap(): return lax.ppermute(x, 'dp', [(i, i ^ mask) for i in range(devices)])  24.7 us
    all_to_all x1, starting transfers between devices, body(): lax.all_to_all(latents, 'dp', split_axis=0, concat_axis=0, tiled=True)  7.3 us
    pallas_call x1, Pallas kernels, attention(): pl.pallas_call(attention_kernel, in_specs=[hbm, hbm, hbm], out_specs=pl.B...  4.72 us
    pallas_call x2, Pallas kernels, fetch(): pl.pallas_call(functools.partial(fetch_kernel, parts), in_specs=[pl.Block...  4.26 us
    pallas_call x1, Pallas kernels, project(): pl.pallas_call(functools.partial(project_kernel, planes, rows), in_specs=...  4.05 us
  transfers between devices with their start and end apart: 25, of which 17 were waited for; matrix products, arithmetic and copies ran while one was open for 0% of the time, Pallas kernels for 7%

profile of v6, /device:TPU:0, one launch (start us, length us, event | category | flops | bytes accessed | tf_op | source)
XLA Modules:
  0.0 89.8 jit_solution(9631720037811999996)
XLA Ops:
  0.0 4.7 %latent_attention.1.unused.refs_1_ = bf16[512,512]{1,0:T(8,128)(2,1)} custom-call(s32[4]{0:T(128)} %lengths_hbm.1, bf16[4,576,128]{2,1,0:T(8,128)(2,1)} %bitcast.7, bf16[4,576,512]{2,1,0:T(8,128)(2,1)} %bitcast.6), custom_call_target="tpu_custom_call" | custom-call | tf_op jit(solution)/shard_map/latent_attention/pallas_call | solution.py:78
  4.7 7.3 %all-to-all-start = ((bf16[32,16,512]{2,1,0:T(8,128)(2,1)}), bf16[32,16,512]{2,1,0:T(8,128)(2,1)S(1)}, u32[]{:S(2)}, u32[]{:S(2)}) async-start(bf16[32,16,512]{2,1,0:T(8,128)(2,1)} %bitcast.3), calls=%async_computation | async-start | bytes 1048576 | tf_op jit(solution)/shard_map/all_to_all | solution.py:498
  12.9 3.7 %collective-permute-start.2 = (f32[8,128]{1,0:T(8,128)S(1)}, f32[8,128]{1,0:T(8,128)S(1)}, u32[]{:S(2)}, u32[]{:S(2)}) collective-permute-start(f32[8,128]{1,0:T(8,128)S(1)} %routes.1.refs_0_), channel_id=1, source_target_pairs={{0,24},{1,25},{2,26},{3,27},{4,28},{5,29},{6,30},{7,31},{8,16},{9,... | collective-permute-start | bytes 12296 | tf_op jit(solution)/shard_map/ppermute | solution.py:489
  17.3 1.6 %fetch_projections.1 = (bf16[512,1024]{1,0:T(8,128)(2,1)S(1)}, bf16[512,1024]{1,0:T(8,128)(2,1)S(1)}) custom-call(bf16[512,7168]{1,0:T(8,128)(2,1)} %w_hbm.1, bf16[512,512]{1,0:T(8,128)(2,1)} %latent_attention.1.unused.refs_1_), custom_call_target="tpu_custom_call" | custom-call | tf_op jit(solution)/shard_map/fetch_projections/pallas_call | solution.py:124
  18.9 6.4 %collective-permute-done.2.refs_4_.refs_3_ = f32[8,128]{1,0:T(8,128)S(1)} collective-permute-done((f32[8,128]{1,0:T(8,128)S(1)}, f32[8,128]{1,0:T(8,128)S(1)}, u32[]{:S(2)}, u32[]{:S(2)}) %collective-permute-start.2) | collective-permute-done | bytes 4128 | tf_op jit(solution)/shard_map/ppermute | solution.py:489
  25.4 2.0 %collective-permute-done.1.refs_3_.refs_2_ = f32[8,128]{1,0:T(8,128)S(1)} collective-permute-done((f32[8,128]{1,0:T(8,128)S(1)}, f32[8,128]{1,0:T(8,128)S(1)}, u32[]{:S(2)}, u32[]{:S(2)}) %collective-permute-start.1) | collective-permute-done | bytes 4128 | tf_op jit(solution)/shard_map/ppermute | solution.py:489
  27.8 4.1 %projections.1 = (f32[64,7168]{1,0:T(8,128)S(1)}, bf16[64,7168]{1,0:T(8,128)(2,1)S(1)}) custom-call(s32[1]{0:T(128)} %bitcast.me, bf16[512,512]{1,0:T(8,128)(2,1)S(1)} %bitcast.5, bf16[4,512,128]{2,1,0:T(8,128)(2,1)S(1)} %copy-done, bf16[512,7168]{1,0:T(8,128)(2,1)} %w_hbm.1, bf16[512,1024]{1,0:T(8,128)(2,1)S(1)} %get-tuple-element.35.refs_0_, ...), custom_call_target="tpu_custom_call" | custom-call | tf_op jit(solution)/shard_map/projections/pallas_call | solution.py:181
  31.9 2.5 %collective-permute-done.3.refs_1_ = bf16[64,7168]{1,0:T(8,128)(2,1)S(1)} collective-permute-done((bf16[64,7168]{1,0:T(8,128)(2,1)S(1)}, bf16[64,7168]{1,0:T(8,128)(2,1)S(1)}, u32[]{:S(2)}, u32[]{:S(2)}) %collective-permute-start.3) | collective-permute-done | bytes 917536 | tf_op jit(solution)/shard_map/ppermute | solution.py:489
  34.5 1.2 %collective-permute-start.4 = (bf16[16,7168]{1,0:T(8,128)(2,1)S(1)}, bf16[16,7168]{1,0:T(8,128)(2,1)S(1)}, u32[]{:S(2)}, u32[]{:S(2)}) collective-permute-start(bf16[16,7168]{1,0:T(8,128)(2,1)S(1)} %get-tuple-element.41), channel_id=1, source_target_pairs={{0,2},{1,3},{2,0},{3,1},{4,6},{5,7},{6,4},{7,5},{8,10},{9,11},{10,... | collective-permute-start | bytes 688136 | tf_op jit(solution)/shard_map/ppermute | solution.py:489
  35.7 1.5 %collective-permute-start.5 = (bf16[16,7168]{1,0:T(8,128)(2,1)S(1)}, bf16[16,7168]{1,0:T(8,128)(2,1)S(1)}, u32[]{:S(2)}, u32[]{:S(2)}) collective-permute-start(bf16[16,7168]{1,0:T(8,128)(2,1)S(1)} %get-tuple-element.42), channel_id=1, source_target_pairs={{0,4},{1,5},{2,6},{3,7},{4,0},{5,1},{6,2},{7,3},{8,12},{9,13},{10,... | collective-permute-start | bytes 688136 | tf_op jit(solution)/shard_map/ppermute | solution.py:489
  39.2 3.8 %collective-permute-done.4.a_ref = bf16[16,7168]{1,0:T(8,128)(2,1)S(1)} collective-permute-done((bf16[16,7168]{1,0:T(8,128)(2,1)S(1)}, bf16[16,7168]{1,0:T(8,128)(2,1)S(1)}, u32[]{:S(2)}, u32[]{:S(2)}) %collective-permute-start.4) | collective-permute-done | bytes 229408 | tf_op jit(solution)/shard_map/ppermute | solution.py:489
  43.0 5.1 %collective-permute-done.5.b_ref = bf16[16,7168]{1,0:T(8,128)(2,1)S(1)} collective-permute-done((bf16[16,7168]{1,0:T(8,128)(2,1)S(1)}, bf16[16,7168]{1,0:T(8,128)(2,1)S(1)}, u32[]{:S(2)}, u32[]{:S(2)}) %collective-permute-start.5) | collective-permute-done | bytes 229408 | tf_op jit(solution)/shard_map/ppermute | solution.py:489
  50.5 2.5 %collective-permute-start.9 = (bf16[8,7168]{1,0:T(8,128)(2,1)S(1)}, bf16[8,7168]{1,0:T(8,128)(2,1)S(1)}, u32[]{:S(2)}, u32[]{:S(2)}) collective-permute-start(bf16[8,7168]{1,0:T(8,128)(2,1)S(1)} %get-tuple-element.48), channel_id=1, source_target_pairs={{0,24},{1,25},{2,26},{3,27},{4,28},{5,29},{6,30},{7,31},{8,16},{9,... | collective-permute-start | bytes 344072 | tf_op jit(solution)/shard_map/ppermute | solution.py:489
  53.1 2.6 %fetch_experts.1 = (bf16[7168,128]{1,0:T(8,128)(2,1)S(1)}, bf16[7168,128]{1,0:T(8,128)(2,1)S(1)}, bf16[128,7168]{1,0:T(8,128)(2,1)S(1)}) custom-call(bf16[2,7168,128]{2,1,0:T(8,128)(2,1)} %refs_0_.3, bf16[128,7168]{1,0:T(8,128)(2,1)} %refs_1_.1, f32[8,7168]{1,0:T(8,128)S(1)} %get-tuple-element.45.refs_2_.refs_0_), custom_call_target="tpu_custom_call" | custom-call | tf_op jit(solution)/shard_map/fetch_experts/pallas_call | solution.py:124
  55.7 4.6 %collective-permute-done.8.refs_2_ = bf16[8,7168]{1,0:T(8,128)(2,1)S(1)} collective-permute-done((bf16[8,7168]{1,0:T(8,128)(2,1)S(1)}, bf16[8,7168]{1,0:T(8,128)(2,1)S(1)}, u32[]{:S(2)}, u32[]{:S(2)}) %collective-permute-start.8) | collective-permute-done | bytes 114720 | tf_op jit(solution)/shard_map/ppermute | solution.py:489
  60.6 1.7 %collective-permute-start.12 = (bf16[8,7168]{1,0:T(8,128)(2,1)S(1)}, bf16[8,7168]{1,0:T(8,128)(2,1)S(1)}, u32[]{:S(2)}, u32[]{:S(2)}) collective-permute-start(bf16[8,7168]{1,0:T(8,128)(2,1)S(1)} %get-tuple-element.50.refs_0_), channel_id=1, source_target_pairs={{0,6},{1,7},{2,4},{3,5},{4,2},{5,3},{6,0},{7,1},{8,14},{9,15},{10,... | collective-permute-start | bytes 344072 | tf_op jit(solution)/shard_map/ppermute | solution.py:489
  64.2 2.3 %collective-permute-done.12.refs_3_ = bf16[8,7168]{1,0:T(8,128)(2,1)S(1)} collective-permute-done((bf16[8,7168]{1,0:T(8,128)(2,1)S(1)}, bf16[8,7168]{1,0:T(8,128)(2,1)S(1)}, u32[]{:S(2)}, u32[]{:S(2)}) %collective-permute-start.12) | collective-permute-done | bytes 114720 | tf_op jit(solution)/shard_map/ppermute | solution.py:489
  70.5 1.7 %collective-permute-done.17.refs_1_ = bf16[32,7168]{1,0:T(8,128)(2,1)S(1)} collective-permute-done((bf16[32,7168]{1,0:T(8,128)(2,1)S(1)}, bf16[32,7168]{1,0:T(8,128)(2,1)S(1)}, u32[]{:S(2)}, u32[]{:S(2)}) %collective-permute-start.17) | collective-permute-done | bytes 458784 | tf_op jit(solution)/shard_map/ppermute | solution.py:489
  74.4 1.5 %collective-permute-start.20 = (bf16[8,7168]{1,0:T(8,128)(2,1)S(1)}, bf16[8,7168]{1,0:T(8,128)(2,1)S(1)}, u32[]{:S(2)}, u32[]{:S(2)}) collective-permute-start(bf16[8,7168]{1,0:T(8,128)(2,1)S(1)} %get-tuple-element.58), channel_id=1, source_target_pairs={{0,6},{1,7},{2,4},{3,5},{4,2},{5,3},{6,0},{7,1},{8,14},{9,15},{10,... | collective-permute-start | bytes 344072 | tf_op jit(solution)/shard_map/ppermute | solution.py:489
  75.8 2.2 %collective-permute-done.18.a_ref = bf16[8,7168]{1,0:T(8,128)(2,1)S(1)} collective-permute-done((bf16[8,7168]{1,0:T(8,128)(2,1)S(1)}, bf16[8,7168]{1,0:T(8,128)(2,1)S(1)}, u32[]{:S(2)}, u32[]{:S(2)}) %collective-permute-start.18) | collective-permute-done | bytes 114720 | tf_op jit(solution)/shard_map/ppermute | solution.py:489
  78.1 2.7 %collective-permute-done.19.b_ref = bf16[8,7168]{1,0:T(8,128)(2,1)S(1)} collective-permute-done((bf16[8,7168]{1,0:T(8,128)(2,1)S(1)}, bf16[8,7168]{1,0:T(8,128)(2,1)S(1)}, u32[]{:S(2)}, u32[]{:S(2)}) %collective-permute-start.19) | collective-permute-done | bytes 114720 | tf_op jit(solution)/shard_map/ppermute | solution.py:489
  80.9 2.2 %collective-permute-start.21 = (bf16[2,7168]{1,0:T(2,128)(2,1)S(1)}, bf16[2,7168]{1,0:T(2,128)(2,1)S(1)}, u32[]{:S(2)}, u32[]{:S(2)}) collective-permute-start(bf16[2,7168]{1,0:T(2,128)(2,1)S(1)} %get-tuple-element.62), channel_id=1, source_target_pairs={{0,8},{1,9},{2,10},{3,11},{4,12},{5,13},{6,14},{7,15},{8,0},{9,1},... | collective-permute-start | bytes 86024 | tf_op jit(solution)/shard_map/ppermute | solution.py:489
  83.2 2.3 %collective-permute-start.23 = (bf16[2,7168]{1,0:T(2,128)(2,1)S(1)}, bf16[2,7168]{1,0:T(2,128)(2,1)S(1)}, u32[]{:S(2)}, u32[]{:S(2)}) collective-permute-start(bf16[2,7168]{1,0:T(2,128)(2,1)S(1)} %get-tuple-element.64), channel_id=1, source_target_pairs={{0,24},{1,25},{2,26},{3,27},{4,28},{5,29},{6,30},{7,31},{8,16},{9,... | collective-permute-start | bytes 86024 | tf_op jit(solution)/shard_map/ppermute | solution.py:489
  85.5 2.3 %collective-permute-done.22.refs_2_ = bf16[2,7168]{1,0:T(2,128)(2,1)S(1)} collective-permute-done((bf16[2,7168]{1,0:T(2,128)(2,1)S(1)}, bf16[2,7168]{1,0:T(2,128)(2,1)S(1)}, u32[]{:S(2)}, u32[]{:S(2)}) %collective-permute-start.22) | collective-permute-done | bytes 28704 | tf_op jit(solution)/shard_map/ppermute | solution.py:489
  (52 shorter events, 17.2 us)
Async XLA Ops:
  4.7 23.0 %all-to-all-start = ((bf16[32,16,512]{2,1,0:T(8,128)(2,1)}), bf16[32,16,512]{2,1,0:T(8,128)(2,1)S(1)}, u32[]{:S(2)}, u32[]{:S(2)}) async-start(bf16[32,16,512]{2,1,0:T(8,128)(2,1)} %bitcast.3), calls=%async_computation | async-start | bytes 1048576 | tf_op jit(solution)/shard_map/all_to_all | solution.py:498
  12.9 12.5 %collective-permute-start.2 = (f32[8,128]{1,0:T(8,128)S(1)}, f32[8,128]{1,0:T(8,128)S(1)}, u32[]{:S(2)}, u32[]{:S(2)}) collective-permute-start(f32[8,128]{1,0:T(8,128)S(1)} %routes.1.refs_0_), channel_id=1, source_target_pairs={{0,24},{1,25},{2,26},{3,27},{4,28},{5,29},{6,30},{7,31},{8,16},{9,... | collective-permute-start | bytes 12296 | tf_op jit(solution)/shard_map/ppermute | solution.py:489
  16.5 10.8 %collective-permute-start.1 = (f32[8,128]{1,0:T(8,128)S(1)}, f32[8,128]{1,0:T(8,128)S(1)}, u32[]{:S(2)}, u32[]{:S(2)}) collective-permute-start(f32[8,128]{1,0:T(8,128)S(1)} %routes.1.refs_0_), channel_id=1, source_target_pairs={{0,16},{1,17},{2,18},{3,19},{4,20},{5,21},{6,22},{7,23},{8,24},{9,... | collective-permute-start | bytes 12296 | tf_op jit(solution)/shard_map/ppermute | solution.py:489
  16.6 10.8 %collective-permute-start = (f32[8,128]{1,0:T(8,128)S(1)}, f32[8,128]{1,0:T(8,128)S(1)}, u32[]{:S(2)}, u32[]{:S(2)}) collective-permute-start(f32[8,128]{1,0:T(8,128)S(1)} %routes.1.refs_0_), channel_id=1, source_target_pairs={{0,8},{1,9},{2,10},{3,11},{4,12},{5,13},{6,14},{7,15},{8,0},{9,1},... | collective-permute-start | bytes 12296 | tf_op jit(solution)/shard_map/ppermute | solution.py:489
  31.8 2.5 %collective-permute-start.3 = (bf16[64,7168]{1,0:T(8,128)(2,1)S(1)}, bf16[64,7168]{1,0:T(8,128)(2,1)S(1)}, u32[]{:S(2)}, u32[]{:S(2)}) collective-permute-start(bf16[64,7168]{1,0:T(8,128)(2,1)S(1)} %get-tuple-element.38), channel_id=1, source_target_pairs={{0,1},{1,0},{2,3},{3,2},{4,5},{5,4},{6,7},{7,6},{8,9},{9,8},{10,11... | collective-permute-start | bytes 2752520 | tf_op jit(solution)/shard_map/ppermute | solution.py:489
  34.5 8.5 %collective-permute-start.4 = (bf16[16,7168]{1,0:T(8,128)(2,1)S(1)}, bf16[16,7168]{1,0:T(8,128)(2,1)S(1)}, u32[]{:S(2)}, u32[]{:S(2)}) collective-permute-start(bf16[16,7168]{1,0:T(8,128)(2,1)S(1)} %get-tuple-element.41), channel_id=1, source_target_pairs={{0,2},{1,3},{2,0},{3,1},{4,6},{5,7},{6,4},{7,5},{8,10},{9,11},{10,... | collective-permute-start | bytes 688136 | tf_op jit(solution)/shard_map/ppermute | solution.py:489
  35.7 12.4 %collective-permute-start.5 = (bf16[16,7168]{1,0:T(8,128)(2,1)S(1)}, bf16[16,7168]{1,0:T(8,128)(2,1)S(1)}, u32[]{:S(2)}, u32[]{:S(2)}) collective-permute-start(bf16[16,7168]{1,0:T(8,128)(2,1)S(1)} %get-tuple-element.42), channel_id=1, source_target_pairs={{0,4},{1,5},{2,6},{3,7},{4,0},{5,1},{6,2},{7,3},{8,12},{9,13},{10,... | collective-permute-start | bytes 688136 | tf_op jit(solution)/shard_map/ppermute | solution.py:489
  37.2 11.0 %collective-permute-start.6 = (bf16[16,7168]{1,0:T(8,128)(2,1)S(1)}, bf16[16,7168]{1,0:T(8,128)(2,1)S(1)}, u32[]{:S(2)}, u32[]{:S(2)}) collective-permute-start(bf16[16,7168]{1,0:T(8,128)(2,1)S(1)} %get-tuple-element.43), channel_id=1, source_target_pairs={{0,6},{1,7},{2,4},{3,5},{4,2},{5,3},{6,0},{7,1},{8,14},{9,15},{10,... | collective-permute-start | bytes 688136 | tf_op jit(solution)/shard_map/ppermute | solution.py:489
  48.6 7.1 %collective-permute-start.7 = (bf16[8,7168]{1,0:T(8,128)(2,1)S(1)}, bf16[8,7168]{1,0:T(8,128)(2,1)S(1)}, u32[]{:S(2)}, u32[]{:S(2)}) collective-permute-start(bf16[8,7168]{1,0:T(8,128)(2,1)S(1)} %get-tuple-element.46), channel_id=1, source_target_pairs={{0,8},{1,9},{2,10},{3,11},{4,12},{5,13},{6,14},{7,15},{8,0},{9,1},... | collective-permute-start | bytes 344072 | tf_op jit(solution)/shard_map/ppermute | solution.py:489
  49.4 11.0 %collective-permute-start.8 = (bf16[8,7168]{1,0:T(8,128)(2,1)S(1)}, bf16[8,7168]{1,0:T(8,128)(2,1)S(1)}, u32[]{:S(2)}, u32[]{:S(2)}) collective-permute-start(bf16[8,7168]{1,0:T(8,128)(2,1)S(1)} %get-tuple-element.47), channel_id=1, source_target_pairs={{0,16},{1,17},{2,18},{3,19},{4,20},{5,21},{6,22},{7,23},{8,24},{9,... | collective-permute-start | bytes 344072 | tf_op jit(solution)/shard_map/ppermute | solution.py:489
  50.5 9.8 %collective-permute-start.9 = (bf16[8,7168]{1,0:T(8,128)(2,1)S(1)}, bf16[8,7168]{1,0:T(8,128)(2,1)S(1)}, u32[]{:S(2)}, u32[]{:S(2)}) collective-permute-start(bf16[8,7168]{1,0:T(8,128)(2,1)S(1)} %get-tuple-element.48), channel_id=1, source_target_pairs={{0,24},{1,25},{2,26},{3,27},{4,28},{5,29},{6,30},{7,31},{8,16},{9,... | collective-permute-start | bytes 344072 | tf_op jit(solution)/shard_map/ppermute | solution.py:489
  60.6 5.8 %collective-permute-start.12 = (bf16[8,7168]{1,0:T(8,128)(2,1)S(1)}, bf16[8,7168]{1,0:T(8,128)(2,1)S(1)}, u32[]{:S(2)}, u32[]{:S(2)}) collective-permute-start(bf16[8,7168]{1,0:T(8,128)(2,1)S(1)} %get-tuple-element.50.refs_0_), channel_id=1, source_target_pairs={{0,6},{1,7},{2,4},{3,5},{4,2},{5,3},{6,0},{7,1},{8,14},{9,15},{10,... | collective-permute-start | bytes 344072 | tf_op jit(solution)/shard_map/ppermute | solution.py:489
  62.3 5.3 %collective-permute-start.11 = (bf16[8,7168]{1,0:T(8,128)(2,1)S(1)}, bf16[8,7168]{1,0:T(8,128)(2,1)S(1)}, u32[]{:S(2)}, u32[]{:S(2)}) collective-permute-start(bf16[8,7168]{1,0:T(8,128)(2,1)S(1)} %get-tuple-element.50.refs_0_), channel_id=1, source_target_pairs={{0,4},{1,5},{2,6},{3,7},{4,0},{5,1},{6,2},{7,3},{8,12},{9,13},{10,... | collective-permute-start | bytes 344072 | tf_op jit(solution)/shard_map/ppermute | solution.py:489
  63.2 4.8 %collective-permute-start.10 = (bf16[8,7168]{1,0:T(8,128)(2,1)S(1)}, bf16[8,7168]{1,0:T(8,128)(2,1)S(1)}, u32[]{:S(2)}, u32[]{:S(2)}) collective-permute-start(bf16[8,7168]{1,0:T(8,128)(2,1)S(1)} %get-tuple-element.50.refs_0_), channel_id=1, source_target_pairs={{0,2},{1,3},{2,0},{3,1},{4,6},{5,7},{6,4},{7,5},{8,10},{9,11},{10,... | collective-permute-start | bytes 344072 | tf_op jit(solution)/shard_map/ppermute | solution.py:489
  64.2 3.9 %collective-permute-start.13 = (bf16[8,7168]{1,0:T(8,128)(2,1)S(1)}, bf16[8,7168]{1,0:T(8,128)(2,1)S(1)}, u32[]{:S(2)}, u32[]{:S(2)}) collective-permute-start(bf16[8,7168]{1,0:T(8,128)(2,1)S(1)} %get-tuple-element.50.refs_0_), channel_id=1, source_target_pairs={{0,1},{1,0},{2,3},{3,2},{4,5},{5,4},{6,7},{7,6},{8,9},{9,8},{10,11... | collective-permute-start | bytes 344072 | tf_op jit(solution)/shard_map/ppermute | solution.py:489
  66.4 1.7 %collective-permute-start.16 = (bf16[8,7168]{1,0:T(8,128)(2,1)S(1)}, bf16[8,7168]{1,0:T(8,128)(2,1)S(1)}, u32[]{:S(2)}, u32[]{:S(2)}) collective-permute-start(bf16[8,7168]{1,0:T(8,128)(2,1)S(1)} %collective-permute-done.12.refs_3_), channel_id=1, source_target_pairs={{0,1},{1,0},{2,3},{3,2},{4,5},{5,4},{6,7},{7,6},{8,9},{9,8},{10,11... | collective-permute-start | bytes 344072 | tf_op jit(solution)/shard_map/ppermute | solution.py:489
  67.6 1.3 %collective-permute-start.15 = (bf16[8,7168]{1,0:T(8,128)(2,1)S(1)}, bf16[8,7168]{1,0:T(8,128)(2,1)S(1)}, u32[]{:S(2)}, u32[]{:S(2)}) collective-permute-start(bf16[8,7168]{1,0:T(8,128)(2,1)S(1)} %collective-permute-done.11.refs_2_), channel_id=1, source_target_pairs={{0,1},{1,0},{2,3},{3,2},{4,5},{5,4},{6,7},{7,6},{8,9},{9,8},{10,11... | collective-permute-start | bytes 344072 | tf_op jit(solution)/shard_map/ppermute | solution.py:489
  70.3 1.9 %collective-permute-start.17 = (bf16[32,7168]{1,0:T(8,128)(2,1)S(1)}, bf16[32,7168]{1,0:T(8,128)(2,1)S(1)}, u32[]{:S(2)}, u32[]{:S(2)}) collective-permute-start(bf16[32,7168]{1,0:T(8,128)(2,1)S(1)} %get-tuple-element.54), channel_id=1, source_target_pairs={{0,1},{1,0},{2,3},{3,2},{4,5},{5,4},{6,7},{7,6},{8,9},{9,8},{10,11... | collective-permute-start | bytes 1376264 | tf_op jit(solution)/shard_map/ppermute | solution.py:489
  72.3 5.8 %collective-permute-start.18 = (bf16[8,7168]{1,0:T(8,128)(2,1)S(1)}, bf16[8,7168]{1,0:T(8,128)(2,1)S(1)}, u32[]{:S(2)}, u32[]{:S(2)}) collective-permute-start(bf16[8,7168]{1,0:T(8,128)(2,1)S(1)} %get-tuple-element.56), channel_id=1, source_target_pairs={{0,2},{1,3},{2,0},{3,1},{4,6},{5,7},{6,4},{7,5},{8,10},{9,11},{10,... | collective-permute-start | bytes 344072 | tf_op jit(solution)/shard_map/ppermute | solution.py:489
  73.3 7.4 %collective-permute-start.19 = (bf16[8,7168]{1,0:T(8,128)(2,1)S(1)}, bf16[8,7168]{1,0:T(8,128)(2,1)S(1)}, u32[]{:S(2)}, u32[]{:S(2)}) collective-permute-start(bf16[8,7168]{1,0:T(8,128)(2,1)S(1)} %get-tuple-element.57), channel_id=1, source_target_pairs={{0,4},{1,5},{2,6},{3,7},{4,0},{5,1},{6,2},{7,3},{8,12},{9,13},{10,... | collective-permute-start | bytes 344072 | tf_op jit(solution)/shard_map/ppermute | solution.py:489
  74.4 6.4 %collective-permute-start.20 = (bf16[8,7168]{1,0:T(8,128)(2,1)S(1)}, bf16[8,7168]{1,0:T(8,128)(2,1)S(1)}, u32[]{:S(2)}, u32[]{:S(2)}) collective-permute-start(bf16[8,7168]{1,0:T(8,128)(2,1)S(1)} %get-tuple-element.58), channel_id=1, source_target_pairs={{0,6},{1,7},{2,4},{3,5},{4,2},{5,3},{6,0},{7,1},{8,14},{9,15},{10,... | collective-permute-start | bytes 344072 | tf_op jit(solution)/shard_map/ppermute | solution.py:489
  80.9 4.7 %collective-permute-start.21 = (bf16[2,7168]{1,0:T(2,128)(2,1)S(1)}, bf16[2,7168]{1,0:T(2,128)(2,1)S(1)}, u32[]{:S(2)}, u32[]{:S(2)}) collective-permute-start(bf16[2,7168]{1,0:T(2,128)(2,1)S(1)} %get-tuple-element.62), channel_id=1, source_target_pairs={{0,8},{1,9},{2,10},{3,11},{4,12},{5,13},{6,14},{7,15},{8,0},{9,1},... | collective-permute-start | bytes 86024 | tf_op jit(solution)/shard_map/ppermute | solution.py:489
  83.1 4.8 %collective-permute-start.22 = (bf16[2,7168]{1,0:T(2,128)(2,1)S(1)}, bf16[2,7168]{1,0:T(2,128)(2,1)S(1)}, u32[]{:S(2)}, u32[]{:S(2)}) collective-permute-start(bf16[2,7168]{1,0:T(2,128)(2,1)S(1)} %get-tuple-element.63), channel_id=1, source_target_pairs={{0,16},{1,17},{2,18},{3,19},{4,20},{5,21},{6,22},{7,23},{8,24},{9,... | collective-permute-start | bytes 86024 | tf_op jit(solution)/shard_map/ppermute | solution.py:489
  83.2 5.7 %collective-permute-start.23 = (bf16[2,7168]{1,0:T(2,128)(2,1)S(1)}, bf16[2,7168]{1,0:T(2,128)(2,1)S(1)}, u32[]{:S(2)}, u32[]{:S(2)}) collective-permute-start(bf16[2,7168]{1,0:T(2,128)(2,1)S(1)} %get-tuple-element.64), channel_id=1, source_target_pairs={{0,24},{1,25},{2,26},{3,27},{4,28},{5,29},{6,30},{7,31},{8,16},{9,... | collective-permute-start | bytes 86024 | tf_op jit(solution)/shard_map/ppermute | solution.py:489
  (6 other events, 71.0 us)

commit v7 on v6

--- a/solution.py
+++ b/solution.py
@@ -50,14 +50,21 @@
             copy.start()
             copies.append(copy)
     live.wait()
-    for r in range(rows):
+
+    def score(r):
         copies[2 * r].wait()
         copies[2 * r + 1].wait()
         scores = lax.dot_general(
             queries[r], keys[r], (((0,), (0,)), ((), ())), preferred_element_type=F32
         ) * ((VH + ROPE) ** -0.5)
         position = lax.broadcasted_iota(jnp.int32, scores.shape, 1)
-        scores = jnp.where(position < lengths[r], scores, MASKED)
+        return jnp.where(position < lengths[r], scores, MASKED)
+
+    ready = score(0)
+    for r in range(rows):
+        scores = ready
+        if r + 1 < rows:
+            ready = score(r + 1)
         terms = jnp.exp(scores - jnp.max(scores, axis=1, keepdims=True))
         total = jnp.sum(terms, axis=1, keepdims=True)
         numerator = lax.dot_general(
@@ -150,17 +157,17 @@
         copies.append(copy)
     heads = v_ref.shape[0]
     count = flat.shape[0]
-    i = lax.broadcasted_iota(jnp.int32, (count, 1), 0)
-    k = lax.broadcasted_iota(jnp.int32, (count, x_ref.shape[0]), 1)
+    i = lax.broadcasted_iota(jnp.int32, (heads * count, 1), 0)
+    k = lax.broadcasted_iota(jnp.int32, (heads * count, x_ref.shape[0]), 1)
     plane = (i // rows) % planes
-    rest = i // (rows * planes)
+    rest = (i // (rows * planes)) % 8
     home = me[0] ^ (plane * 8 + (rest % 4) * 2 + rest // 4)
-    target = home * (heads * rows) + i % rows
+    target = (home * heads + i // count) * rows + i % rows
+    pick = jnp.where(k == target, 1.0, 0.0).astype(BF16)
+    mine = jnp.dot(pick, x_ref[...], preferred_element_type=F32).astype(BF16)
     for h in range(heads):
-        pick = jnp.where(k == target + h * rows, 1.0, 0.0).astype(BF16)
-        mine = jnp.dot(pick, x_ref[...], preferred_element_type=F32).astype(BF16)
         flat[:, h * VH : (h + 1) * VH] = jnp.dot(
-            mine, v_ref[h], preferred_element_type=F32
+            mine[h * count : (h + 1) * count], v_ref[h], preferred_element_type=F32
         ).astype(BF16)
     half = count // 2
     for t in range(TILES):
@@ -299,7 +306,9 @@
             for b in range(r):
                 for u in range(picks):
                     seen = seen + (ids[b, u] == ids[r, t]).astype(jnp.int32)
-            slots.append((ids[r, t] ^ plane) * cap + seen)
+            away = ids[r, t] ^ plane
+            spot = jnp.where(away == 0, 0, jnp.where(away == 1, planes - 1, planes - away))
+            slots.append(spot * cap + seen)
         merge = merge | (lane == column(slots, rows))
     merge_ref[...] = jnp.where(merge, 1.0, 0.0).astype(BF16)
 
@@ -488,24 +497,26 @@
     def swap(x, mask):
         return lax.ppermute(x, "dp", [(i, i ^ mask) for i in range(devices)])
 
+    def over_planes(messages):
+        moved = [swap(x, k << 3) for k, x in enumerate(messages, 1)]
+        return moved[1:][::-1] + moved[:1]
+
     def over_chips(messages):
         return [swap(x, k << 1) for k, x in enumerate(messages, 1)]
-
-    def over_planes(messages):
-        return [swap(x, k << 3) for k, x in enumerate(messages, 1)]
 
     latents = attention(queries, latent_cache, lengths)
     by_heads = lax.all_to_all(latents, "dp", split_axis=0, concat_axis=0, tiled=True)
     (early,) = fetch([out_proj], [(1, TILES, EARLY)], latents, "fetch_projections")
     mine = routes(route_ids, route_weights, latents)
-    homes = [mine] + over_planes([mine] * (planes - 1))
+    homes = over_planes([mine] * (planes - 1))
+    homes = [mine] + homes[::-1]
     own, other = project(me, by_heads, value_up, out_proj, early, planes, rows, homes[1:])
     own, *out = add_and_cut(own, [swap(other, 1)], 4, "add_core")
     pick, weight, merge = tables(me, route_ids, homes, cap, own)
     own, *out = add_and_pick(own, over_chips(out), hidden_in, pick, planes)
     gate_up, (down_proj,) = fetch([gate_up, down_proj], [(0, 2, 2), (0, 1, 1)], own, "fetch_experts")
     resid, picked = norm([own] + over_planes(out), norm_gain[None], gate_up[:1])
-    chips = [picked] + over_chips([picked] * 3)
+    chips = [picked] + [swap(picked, k << 1) for k in (1, 2, 3)]
     pieces = chips + [swap(x, 1) for x in chips]
     own, other = expert(pieces, gate_up, down_proj)
     own, *out = add_and_cut(own, [swap(other, 1)], 4, "add_expert_core")

time: 90.1 us -> 88.5 us (0.982)
  transfers between devices with their start and end apart: 25 -> 25, of which waited for: 17 -> 18; matrix products, arithmetic and copies ran while one was open for 0% -> 0% of each run, Pallas kernels for 7% -> 7%
where the time goes in v7:
time: 88.5 us; the launch traced here: 88.3 us
  waiting for transfers between devices  39.2 us (44%)
  starting transfers between devices  31.8 us (36%)
  Pallas kernels  16.9 us (19%)
    ppermute x24, waiting for transfers between devices, swap(): return lax.ppermute(x, 'dp', [(i, i ^ mask) for i in range(devices)])  38.8 us
    ppermute x24, starting transfers between devices, swap(): return lax.ppermute(x, 'dp', [(i, i ^ mask) for i in range(devices)])  24.5 us
    all_to_all x1, starting transfers between devices, body(): lax.all_to_all(latents, 'dp', split_axis=0, concat_axis=0, tiled=True)  7.3 us
    pallas_call x2, Pallas kernels, fetch(): pl.pallas_call(functools.partial(fetch_kernel, parts), in_specs=[pl.Block...  4.26 us
    pallas_call x1, Pallas kernels, attention(): pl.pallas_call(attention_kernel, in_specs=[hbm, hbm, hbm], out_specs=pl.B...  4.18 us
    pallas_call x1, Pallas kernels, project(): pl.pallas_call(functools.partial(project_kernel, planes, rows), in_specs=...  3.75 us
  transfers between devices with their start and end apart: 25, of which 18 were waited for; matrix products, arithmetic and copies ran while one was open for 0% of the time, Pallas kernels for 7%

profile of v7, /device:TPU:0, one launch (start us, length us, event | category | flops | bytes accessed | tf_op | source)
XLA Modules:
  0.0 88.3 jit_solution(1800970744429683873)
XLA Ops:
  0.0 4.2 %latent_attention.1.unused.refs_1_ = bf16[512,512]{1,0:T(8,128)(2,1)} custom-call(s32[4]{0:T(128)} %lengths_hbm.1, bf16[4,576,128]{2,1,0:T(8,128)(2,1)} %bitcast.7, bf16[4,576,512]{2,1,0:T(8,128)(2,1)} %bitcast.6), custom_call_target="tpu_custom_call" | custom-call | tf_op jit(solution)/shard_map/latent_attention/pallas_call | solution.py:85
  4.2 7.3 %all-to-all-start = ((bf16[32,16,512]{2,1,0:T(8,128)(2,1)}), bf16[32,16,512]{2,1,0:T(8,128)(2,1)S(1)}, u32[]{:S(2)}, u32[]{:S(2)}) async-start(bf16[32,16,512]{2,1,0:T(8,128)(2,1)} %bitcast.3), calls=%async_computation | async-start | bytes 1048576 | tf_op jit(solution)/shard_map/all_to_all | solution.py:508
  12.3 3.7 %collective-permute-start.2 = (f32[8,128]{1,0:T(8,128)S(1)}, f32[8,128]{1,0:T(8,128)S(1)}, u32[]{:S(2)}, u32[]{:S(2)}) collective-permute-start(f32[8,128]{1,0:T(8,128)S(1)} %routes.1.refs_0_), channel_id=1, source_target_pairs={{0,24},{1,25},{2,26},{3,27},{4,28},{5,29},{6,30},{7,31},{8,16},{9,... | collective-permute-start | bytes 12296 | tf_op jit(solution)/shard_map/ppermute | solution.py:498
  16.8 1.6 %fetch_projections.1 = (bf16[512,1024]{1,0:T(8,128)(2,1)S(1)}, bf16[512,1024]{1,0:T(8,128)(2,1)S(1)}) custom-call(bf16[512,7168]{1,0:T(8,128)(2,1)} %w_hbm.1, bf16[512,512]{1,0:T(8,128)(2,1)} %latent_attention.1.unused.refs_1_), custom_call_target="tpu_custom_call" | custom-call | tf_op jit(solution)/shard_map/fetch_projections/pallas_call | solution.py:131
  18.4 6.4 %collective-permute-done.2.refs_4_.refs_3_ = f32[8,128]{1,0:T(8,128)S(1)} collective-permute-done((f32[8,128]{1,0:T(8,128)S(1)}, f32[8,128]{1,0:T(8,128)S(1)}, u32[]{:S(2)}, u32[]{:S(2)}) %collective-permute-start.2) | collective-permute-done | bytes 4128 | tf_op jit(solution)/shard_map/ppermute | solution.py:498
  24.8 2.0 %collective-permute-done.1.refs_3_.refs_2_ = f32[8,128]{1,0:T(8,128)S(1)} collective-permute-done((f32[8,128]{1,0:T(8,128)S(1)}, f32[8,128]{1,0:T(8,128)S(1)}, u32[]{:S(2)}, u32[]{:S(2)}) %collective-permute-start.1) | collective-permute-done | bytes 4128 | tf_op jit(solution)/shard_map/ppermute | solution.py:498
  27.2 3.8 %projections.1 = (f32[64,7168]{1,0:T(8,128)S(1)}, bf16[64,7168]{1,0:T(8,128)(2,1)S(1)}) custom-call(s32[1]{0:T(128)} %bitcast.me, bf16[512,512]{1,0:T(8,128)(2,1)S(1)} %bitcast.5, bf16[4,512,128]{2,1,0:T(8,128)(2,1)S(1)} %copy-done, bf16[512,7168]{1,0:T(8,128)(2,1)} %w_hbm.1, bf16[512,1024]{1,0:T(8,128)(2,1)S(1)} %get-tuple-element.35.refs_0_, ...), custom_call_target="tpu_custom_call" | custom-call | tf_op jit(solution)/shard_map/projections/pallas_call | solution.py:188
  31.1 2.5 %collective-permute-done.3.refs_1_ = bf16[64,7168]{1,0:T(8,128)(2,1)S(1)} collective-permute-done((bf16[64,7168]{1,0:T(8,128)(2,1)S(1)}, bf16[64,7168]{1,0:T(8,128)(2,1)S(1)}, u32[]{:S(2)}, u32[]{:S(2)}) %collective-permute-start.3) | collective-permute-done | bytes 917536 | tf_op jit(solution)/shard_map/ppermute | solution.py:498
  34.9 1.5 %collective-permute-start.5 = (bf16[16,7168]{1,0:T(8,128)(2,1)S(1)}, bf16[16,7168]{1,0:T(8,128)(2,1)S(1)}, u32[]{:S(2)}, u32[]{:S(2)}) collective-permute-start(bf16[16,7168]{1,0:T(8,128)(2,1)S(1)} %get-tuple-element.42), channel_id=1, source_target_pairs={{0,4},{1,5},{2,6},{3,7},{4,0},{5,1},{6,2},{7,3},{8,12},{9,13},{10,... | collective-permute-start | bytes 688136 | tf_op jit(solution)/shard_map/ppermute | solution.py:498
  38.4 3.8 %collective-permute-done.4.a_ref = bf16[16,7168]{1,0:T(8,128)(2,1)S(1)} collective-permute-done((bf16[16,7168]{1,0:T(8,128)(2,1)S(1)}, bf16[16,7168]{1,0:T(8,128)(2,1)S(1)}, u32[]{:S(2)}, u32[]{:S(2)}) %collective-permute-start.4) | collective-permute-done | bytes 229408 | tf_op jit(solution)/shard_map/ppermute | solution.py:498
  42.2 5.1 %collective-permute-done.5.b_ref = bf16[16,7168]{1,0:T(8,128)(2,1)S(1)} collective-permute-done((bf16[16,7168]{1,0:T(8,128)(2,1)S(1)}, bf16[16,7168]{1,0:T(8,128)(2,1)S(1)}, u32[]{:S(2)}, u32[]{:S(2)}) %collective-permute-start.5) | collective-permute-done | bytes 229408 | tf_op jit(solution)/shard_map/ppermute | solution.py:498
  47.7 1.4 %collective-permute-start.7 = (bf16[8,7168]{1,0:T(8,128)(2,1)S(1)}, bf16[8,7168]{1,0:T(8,128)(2,1)S(1)}, u32[]{:S(2)}, u32[]{:S(2)}) collective-permute-start(bf16[8,7168]{1,0:T(8,128)(2,1)S(1)} %get-tuple-element.46), channel_id=1, source_target_pairs={{0,24},{1,25},{2,26},{3,27},{4,28},{5,29},{6,30},{7,31},{8,16},{9,... | collective-permute-start | bytes 344072 | tf_op jit(solution)/shard_map/ppermute | solution.py:498
  50.0 2.2 %collective-permute-start.9 = (bf16[8,7168]{1,0:T(8,128)(2,1)S(1)}, bf16[8,7168]{1,0:T(8,128)(2,1)S(1)}, u32[]{:S(2)}, u32[]{:S(2)}) collective-permute-start(bf16[8,7168]{1,0:T(8,128)(2,1)S(1)} %get-tuple-element.48), channel_id=1, source_target_pairs={{0,8},{1,9},{2,10},{3,11},{4,12},{5,13},{6,14},{7,15},{8,0},{9,1},... | collective-permute-start | bytes 344072 | tf_op jit(solution)/shard_map/ppermute | solution.py:498
  52.2 2.6 %fetch_experts.1 = (bf16[7168,128]{1,0:T(8,128)(2,1)S(1)}, bf16[7168,128]{1,0:T(8,128)(2,1)S(1)}, bf16[128,7168]{1,0:T(8,128)(2,1)S(1)}) custom-call(bf16[2,7168,128]{2,1,0:T(8,128)(2,1)} %refs_0_.3, bf16[128,7168]{1,0:T(8,128)(2,1)} %refs_1_.1, f32[8,7168]{1,0:T(8,128)S(1)} %get-tuple-element.45.refs_2_.refs_0_), custom_call_target="tpu_custom_call" | custom-call | tf_op jit(solution)/shard_map/fetch_experts/pallas_call | solution.py:131
  55.7 4.1 %collective-permute-done.8.refs_2_ = bf16[8,7168]{1,0:T(8,128)(2,1)S(1)} collective-permute-done((bf16[8,7168]{1,0:T(8,128)(2,1)S(1)}, bf16[8,7168]{1,0:T(8,128)(2,1)S(1)}, u32[]{:S(2)}, u32[]{:S(2)}) %collective-permute-start.8) | collective-permute-done | bytes 114720 | tf_op jit(solution)/shard_map/ppermute | solution.py:498
  60.0 1.7 %collective-permute-start.12 = (bf16[8,7168]{1,0:T(8,128)(2,1)S(1)}, bf16[8,7168]{1,0:T(8,128)(2,1)S(1)}, u32[]{:S(2)}, u32[]{:S(2)}) collective-permute-start(bf16[8,7168]{1,0:T(8,128)(2,1)S(1)} %get-tuple-element.50.refs_0_), channel_id=1, source_target_pairs={{0,6},{1,7},{2,4},{3,5},{4,2},{5,3},{6,0},{7,1},{8,14},{9,15},{10,... | collective-permute-start | bytes 344072 | tf_op jit(solution)/shard_map/ppermute | solution.py:498
  63.6 2.6 %collective-permute-done.12.refs_3_ = bf16[8,7168]{1,0:T(8,128)(2,1)S(1)} collective-permute-done((bf16[8,7168]{1,0:T(8,128)(2,1)S(1)}, bf16[8,7168]{1,0:T(8,128)(2,1)S(1)}, u32[]{:S(2)}, u32[]{:S(2)}) %collective-permute-start.12) | collective-permute-done | bytes 114720 | tf_op jit(solution)/shard_map/ppermute | solution.py:498
  70.3 1.6 %collective-permute-done.17.refs_1_ = bf16[32,7168]{1,0:T(8,128)(2,1)S(1)} collective-permute-done((bf16[32,7168]{1,0:T(8,128)(2,1)S(1)}, bf16[32,7168]{1,0:T(8,128)(2,1)S(1)}, u32[]{:S(2)}, u32[]{:S(2)}) %collective-permute-start.17) | collective-permute-done | bytes 458784 | tf_op jit(solution)/shard_map/ppermute | solution.py:498
  73.9 1.6 %collective-permute-start.20 = (bf16[8,7168]{1,0:T(8,128)(2,1)S(1)}, bf16[8,7168]{1,0:T(8,128)(2,1)S(1)}, u32[]{:S(2)}, u32[]{:S(2)}) collective-permute-start(bf16[8,7168]{1,0:T(8,128)(2,1)S(1)} %get-tuple-element.58), channel_id=1, source_target_pairs={{0,6},{1,7},{2,4},{3,5},{4,2},{5,3},{6,0},{7,1},{8,14},{9,15},{10,... | collective-permute-start | bytes 344072 | tf_op jit(solution)/shard_map/ppermute | solution.py:498
  75.6 2.2 %collective-permute-done.18.a_ref = bf16[8,7168]{1,0:T(8,128)(2,1)S(1)} collective-permute-done((bf16[8,7168]{1,0:T(8,128)(2,1)S(1)}, bf16[8,7168]{1,0:T(8,128)(2,1)S(1)}, u32[]{:S(2)}, u32[]{:S(2)}) %collective-permute-start.18) | collective-permute-done | bytes 114720 | tf_op jit(solution)/shard_map/ppermute | solution.py:498
  77.7 2.9 %collective-permute-done.19.b_ref = bf16[8,7168]{1,0:T(8,128)(2,1)S(1)} collective-permute-done((bf16[8,7168]{1,0:T(8,128)(2,1)S(1)}, bf16[8,7168]{1,0:T(8,128)(2,1)S(1)}, u32[]{:S(2)}, u32[]{:S(2)}) %collective-permute-start.19) | collective-permute-done | bytes 114720 | tf_op jit(solution)/shard_map/ppermute | solution.py:498
  80.7 1.8 %collective-permute-start.21 = (bf16[2,7168]{1,0:T(2,128)(2,1)S(1)}, bf16[2,7168]{1,0:T(2,128)(2,1)S(1)}, u32[]{:S(2)}, u32[]{:S(2)}) collective-permute-start(bf16[2,7168]{1,0:T(2,128)(2,1)S(1)} %get-tuple-element.62), channel_id=1, source_target_pairs={{0,24},{1,25},{2,26},{3,27},{4,28},{5,29},{6,30},{7,31},{8,16},{9,... | collective-permute-start | bytes 86024 | tf_op jit(solution)/shard_map/ppermute | solution.py:498
  82.5 2.6 %collective-permute-start.23 = (bf16[2,7168]{1,0:T(2,128)(2,1)S(1)}, bf16[2,7168]{1,0:T(2,128)(2,1)S(1)}, u32[]{:S(2)}, u32[]{:S(2)}) collective-permute-start(bf16[2,7168]{1,0:T(2,128)(2,1)S(1)} %get-tuple-element.64), channel_id=1, source_target_pairs={{0,8},{1,9},{2,10},{3,11},{4,12},{5,13},{6,14},{7,15},{8,0},{9,1},... | collective-permute-start | bytes 86024 | tf_op jit(solution)/shard_map/ppermute | solution.py:498
  85.2 1.3 %collective-permute-done.21.refs_1_ = bf16[2,7168]{1,0:T(2,128)(2,1)S(1)} collective-permute-done((bf16[2,7168]{1,0:T(2,128)(2,1)S(1)}, bf16[2,7168]{1,0:T(2,128)(2,1)S(1)}, u32[]{:S(2)}, u32[]{:S(2)}) %collective-permute-start.21) | collective-permute-done | bytes 28704 | tf_op jit(solution)/shard_map/ppermute | solution.py:498
  (52 shorter events, 17.7 us)
Async XLA Ops:
  4.2 23.0 %all-to-all-start = ((bf16[32,16,512]{2,1,0:T(8,128)(2,1)}), bf16[32,16,512]{2,1,0:T(8,128)(2,1)S(1)}, u32[]{:S(2)}, u32[]{:S(2)}) async-start(bf16[32,16,512]{2,1,0:T(8,128)(2,1)} %bitcast.3), calls=%async_computation | async-start | bytes 1048576 | tf_op jit(solution)/shard_map/all_to_all | solution.py:508
  12.3 12.5 %collective-permute-start.2 = (f32[8,128]{1,0:T(8,128)S(1)}, f32[8,128]{1,0:T(8,128)S(1)}, u32[]{:S(2)}, u32[]{:S(2)}) collective-permute-start(f32[8,128]{1,0:T(8,128)S(1)} %routes.1.refs_0_), channel_id=1, source_target_pairs={{0,24},{1,25},{2,26},{3,27},{4,28},{5,29},{6,30},{7,31},{8,16},{9,... | collective-permute-start | bytes 12296 | tf_op jit(solution)/shard_map/ppermute | solution.py:498
  16.0 10.8 %collective-permute-start.1 = (f32[8,128]{1,0:T(8,128)S(1)}, f32[8,128]{1,0:T(8,128)S(1)}, u32[]{:S(2)}, u32[]{:S(2)}) collective-permute-start(f32[8,128]{1,0:T(8,128)S(1)} %routes.1.refs_0_), channel_id=1, source_target_pairs={{0,16},{1,17},{2,18},{3,19},{4,20},{5,21},{6,22},{7,23},{8,24},{9,... | collective-permute-start | bytes 12296 | tf_op jit(solution)/shard_map/ppermute | solution.py:498
  16.0 10.8 %collective-permute-start = (f32[8,128]{1,0:T(8,128)S(1)}, f32[8,128]{1,0:T(8,128)S(1)}, u32[]{:S(2)}, u32[]{:S(2)}) collective-permute-start(f32[8,128]{1,0:T(8,128)S(1)} %routes.1.refs_0_), channel_id=1, source_target_pairs={{0,8},{1,9},{2,10},{3,11},{4,12},{5,13},{6,14},{7,15},{8,0},{9,1},... | collective-permute-start | bytes 12296 | tf_op jit(solution)/shard_map/ppermute | solution.py:498
  31.0 2.5 %collective-permute-start.3 = (bf16[64,7168]{1,0:T(8,128)(2,1)S(1)}, bf16[64,7168]{1,0:T(8,128)(2,1)S(1)}, u32[]{:S(2)}, u32[]{:S(2)}) collective-permute-start(bf16[64,7168]{1,0:T(8,128)(2,1)S(1)} %get-tuple-element.38), channel_id=1, source_target_pairs={{0,1},{1,0},{2,3},{3,2},{4,5},{5,4},{6,7},{7,6},{8,9},{9,8},{10,11... | collective-permute-start | bytes 2752520 | tf_op jit(solution)/shard_map/ppermute | solution.py:498
  33.7 8.5 %collective-permute-start.4 = (bf16[16,7168]{1,0:T(8,128)(2,1)S(1)}, bf16[16,7168]{1,0:T(8,128)(2,1)S(1)}, u32[]{:S(2)}, u32[]{:S(2)}) collective-permute-start(bf16[16,7168]{1,0:T(8,128)(2,1)S(1)} %get-tuple-element.41), channel_id=1, source_target_pairs={{0,2},{1,3},{2,0},{3,1},{4,6},{5,7},{6,4},{7,5},{8,10},{9,11},{10,... | collective-permute-start | bytes 688136 | tf_op jit(solution)/shard_map/ppermute | solution.py:498
  34.9 12.4 %collective-permute-start.5 = (bf16[16,7168]{1,0:T(8,128)(2,1)S(1)}, bf16[16,7168]{1,0:T(8,128)(2,1)S(1)}, u32[]{:S(2)}, u32[]{:S(2)}) collective-permute-start(bf16[16,7168]{1,0:T(8,128)(2,1)S(1)} %get-tuple-element.42), channel_id=1, source_target_pairs={{0,4},{1,5},{2,6},{3,7},{4,0},{5,1},{6,2},{7,3},{8,12},{9,13},{10,... | collective-permute-start | bytes 688136 | tf_op jit(solution)/shard_map/ppermute | solution.py:498
  36.3 11.0 %collective-permute-start.6 = (bf16[16,7168]{1,0:T(8,128)(2,1)S(1)}, bf16[16,7168]{1,0:T(8,128)(2,1)S(1)}, u32[]{:S(2)}, u32[]{:S(2)}) collective-permute-start(bf16[16,7168]{1,0:T(8,128)(2,1)S(1)} %get-tuple-element.43), channel_id=1, source_target_pairs={{0,6},{1,7},{2,4},{3,5},{4,2},{5,3},{6,0},{7,1},{8,14},{9,15},{10,... | collective-permute-start | bytes 688136 | tf_op jit(solution)/shard_map/ppermute | solution.py:498
  47.7 8.0 %collective-permute-start.7 = (bf16[8,7168]{1,0:T(8,128)(2,1)S(1)}, bf16[8,7168]{1,0:T(8,128)(2,1)S(1)}, u32[]{:S(2)}, u32[]{:S(2)}) collective-permute-start(bf16[8,7168]{1,0:T(8,128)(2,1)S(1)} %get-tuple-element.46), channel_id=1, source_target_pairs={{0,24},{1,25},{2,26},{3,27},{4,28},{5,29},{6,30},{7,31},{8,16},{9,... | collective-permute-start | bytes 344072 | tf_op jit(solution)/shard_map/ppermute | solution.py:498
  49.1 10.7 %collective-permute-start.8 = (bf16[8,7168]{1,0:T(8,128)(2,1)S(1)}, bf16[8,7168]{1,0:T(8,128)(2,1)S(1)}, u32[]{:S(2)}, u32[]{:S(2)}) collective-permute-start(bf16[8,7168]{1,0:T(8,128)(2,1)S(1)} %get-tuple-element.47), channel_id=1, source_target_pairs={{0,16},{1,17},{2,18},{3,19},{4,20},{5,21},{6,22},{7,23},{8,24},{9,... | collective-permute-start | bytes 344072 | tf_op jit(solution)/shard_map/ppermute | solution.py:498
  50.0 9.8 %collective-permute-start.9 = (bf16[8,7168]{1,0:T(8,128)(2,1)S(1)}, bf16[8,7168]{1,0:T(8,128)(2,1)S(1)}, u32[]{:S(2)}, u32[]{:S(2)}) collective-permute-start(bf16[8,7168]{1,0:T(8,128)(2,1)S(1)} %get-tuple-element.48), channel_id=1, source_target_pairs={{0,8},{1,9},{2,10},{3,11},{4,12},{5,13},{6,14},{7,15},{8,0},{9,1},... | collective-permute-start | bytes 344072 | tf_op jit(solution)/shard_map/ppermute | solution.py:498
  60.0 6.1 %collective-permute-start.12 = (bf16[8,7168]{1,0:T(8,128)(2,1)S(1)}, bf16[8,7168]{1,0:T(8,128)(2,1)S(1)}, u32[]{:S(2)}, u32[]{:S(2)}) collective-permute-start(bf16[8,7168]{1,0:T(8,128)(2,1)S(1)} %get-tuple-element.50.refs_0_), channel_id=1, source_target_pairs={{0,6},{1,7},{2,4},{3,5},{4,2},{5,3},{6,0},{7,1},{8,14},{9,15},{10,... | collective-permute-start | bytes 344072 | tf_op jit(solution)/shard_map/ppermute | solution.py:498
  61.7 5.6 %collective-permute-start.11 = (bf16[8,7168]{1,0:T(8,128)(2,1)S(1)}, bf16[8,7168]{1,0:T(8,128)(2,1)S(1)}, u32[]{:S(2)}, u32[]{:S(2)}) collective-permute-start(bf16[8,7168]{1,0:T(8,128)(2,1)S(1)} %get-tuple-element.50.refs_0_), channel_id=1, source_target_pairs={{0,4},{1,5},{2,6},{3,7},{4,0},{5,1},{6,2},{7,3},{8,12},{9,13},{10,... | collective-permute-start | bytes 344072 | tf_op jit(solution)/shard_map/ppermute | solution.py:498
  62.9 4.8 %collective-permute-start.10 = (bf16[8,7168]{1,0:T(8,128)(2,1)S(1)}, bf16[8,7168]{1,0:T(8,128)(2,1)S(1)}, u32[]{:S(2)}, u32[]{:S(2)}) collective-permute-start(bf16[8,7168]{1,0:T(8,128)(2,1)S(1)} %get-tuple-element.50.refs_0_), channel_id=1, source_target_pairs={{0,2},{1,3},{2,0},{3,1},{4,6},{5,7},{6,4},{7,5},{8,10},{9,11},{10,... | collective-permute-start | bytes 344072 | tf_op jit(solution)/shard_map/ppermute | solution.py:498
  63.6 4.3 %collective-permute-start.13 = (bf16[8,7168]{1,0:T(8,128)(2,1)S(1)}, bf16[8,7168]{1,0:T(8,128)(2,1)S(1)}, u32[]{:S(2)}, u32[]{:S(2)}) collective-permute-start(bf16[8,7168]{1,0:T(8,128)(2,1)S(1)} %get-tuple-element.50.refs_0_), channel_id=1, source_target_pairs={{0,1},{1,0},{2,3},{3,2},{4,5},{5,4},{6,7},{7,6},{8,9},{9,8},{10,11... | collective-permute-start | bytes 344072 | tf_op jit(solution)/shard_map/ppermute | solution.py:498
  66.2 1.7 %collective-permute-start.16 = (bf16[8,7168]{1,0:T(8,128)(2,1)S(1)}, bf16[8,7168]{1,0:T(8,128)(2,1)S(1)}, u32[]{:S(2)}, u32[]{:S(2)}) collective-permute-start(bf16[8,7168]{1,0:T(8,128)(2,1)S(1)} %collective-permute-done.12.refs_3_), channel_id=1, source_target_pairs={{0,1},{1,0},{2,3},{3,2},{4,5},{5,4},{6,7},{7,6},{8,9},{9,8},{10,11... | collective-permute-start | bytes 344072 | tf_op jit(solution)/shard_map/ppermute | solution.py:498
  67.4 1.3 %collective-permute-start.15 = (bf16[8,7168]{1,0:T(8,128)(2,1)S(1)}, bf16[8,7168]{1,0:T(8,128)(2,1)S(1)}, u32[]{:S(2)}, u32[]{:S(2)}) collective-permute-start(bf16[8,7168]{1,0:T(8,128)(2,1)S(1)} %collective-permute-done.11.refs_2_), channel_id=1, source_target_pairs={{0,1},{1,0},{2,3},{3,2},{4,5},{5,4},{6,7},{7,6},{8,9},{9,8},{10,11... | collective-permute-start | bytes 344072 | tf_op jit(solution)/shard_map/ppermute | solution.py:498
  70.0 1.9 %collective-permute-start.17 = (bf16[32,7168]{1,0:T(8,128)(2,1)S(1)}, bf16[32,7168]{1,0:T(8,128)(2,1)S(1)}, u32[]{:S(2)}, u32[]{:S(2)}) collective-permute-start(bf16[32,7168]{1,0:T(8,128)(2,1)S(1)} %get-tuple-element.54), channel_id=1, source_target_pairs={{0,1},{1,0},{2,3},{3,2},{4,5},{5,4},{6,7},{7,6},{8,9},{9,8},{10,11... | collective-permute-start | bytes 1376264 | tf_op jit(solution)/shard_map/ppermute | solution.py:498
  72.0 5.7 %collective-permute-start.18 = (bf16[8,7168]{1,0:T(8,128)(2,1)S(1)}, bf16[8,7168]{1,0:T(8,128)(2,1)S(1)}, u32[]{:S(2)}, u32[]{:S(2)}) collective-permute-start(bf16[8,7168]{1,0:T(8,128)(2,1)S(1)} %get-tuple-element.56), channel_id=1, source_target_pairs={{0,2},{1,3},{2,0},{3,1},{4,6},{5,7},{6,4},{7,5},{8,10},{9,11},{10,... | collective-permute-start | bytes 344072 | tf_op jit(solution)/shard_map/ppermute | solution.py:498
  73.0 7.6 %collective-permute-start.19 = (bf16[8,7168]{1,0:T(8,128)(2,1)S(1)}, bf16[8,7168]{1,0:T(8,128)(2,1)S(1)}, u32[]{:S(2)}, u32[]{:S(2)}) collective-permute-start(bf16[8,7168]{1,0:T(8,128)(2,1)S(1)} %get-tuple-element.57), channel_id=1, source_target_pairs={{0,4},{1,5},{2,6},{3,7},{4,0},{5,1},{6,2},{7,3},{8,12},{9,13},{10,... | collective-permute-start | bytes 344072 | tf_op jit(solution)/shard_map/ppermute | solution.py:498
  73.9 6.7 %collective-permute-start.20 = (bf16[8,7168]{1,0:T(8,128)(2,1)S(1)}, bf16[8,7168]{1,0:T(8,128)(2,1)S(1)}, u32[]{:S(2)}, u32[]{:S(2)}) collective-permute-start(bf16[8,7168]{1,0:T(8,128)(2,1)S(1)} %get-tuple-element.58), channel_id=1, source_target_pairs={{0,6},{1,7},{2,4},{3,5},{4,2},{5,3},{6,0},{7,1},{8,14},{9,15},{10,... | collective-permute-start | bytes 344072 | tf_op jit(solution)/shard_map/ppermute | solution.py:498
  80.7 5.7 %collective-permute-start.21 = (bf16[2,7168]{1,0:T(2,128)(2,1)S(1)}, bf16[2,7168]{1,0:T(2,128)(2,1)S(1)}, u32[]{:S(2)}, u32[]{:S(2)}) collective-permute-start(bf16[2,7168]{1,0:T(2,128)(2,1)S(1)} %get-tuple-element.62), channel_id=1, source_target_pairs={{0,24},{1,25},{2,26},{3,27},{4,28},{5,29},{6,30},{7,31},{8,16},{9,... | collective-permute-start | bytes 86024 | tf_op jit(solution)/shard_map/ppermute | solution.py:498
  82.5 4.8 %collective-permute-start.22 = (bf16[2,7168]{1,0:T(2,128)(2,1)S(1)}, bf16[2,7168]{1,0:T(2,128)(2,1)S(1)}, u32[]{:S(2)}, u32[]{:S(2)}) collective-permute-start(bf16[2,7168]{1,0:T(2,128)(2,1)S(1)} %get-tuple-element.63), channel_id=1, source_target_pairs={{0,16},{1,17},{2,18},{3,19},{4,20},{5,21},{6,22},{7,23},{8,24},{9,... | collective-permute-start | bytes 86024 | tf_op jit(solution)/shard_map/ppermute | solution.py:498
  82.5 4.8 %collective-permute-start.23 = (bf16[2,7168]{1,0:T(2,128)(2,1)S(1)}, bf16[2,7168]{1,0:T(2,128)(2,1)S(1)}, u32[]{:S(2)}, u32[]{:S(2)}) collective-permute-start(bf16[2,7168]{1,0:T(2,128)(2,1)S(1)} %get-tuple-element.64), channel_id=1, source_target_pairs={{0,8},{1,9},{2,10},{3,11},{4,12},{5,13},{6,14},{7,15},{8,0},{9,1},... | collective-permute-start | bytes 86024 | tf_op jit(solution)/shard_map/ppermute | solution.py:498
  (6 other events, 69.8 us)

commit v8 on v7

--- a/solution.py
+++ b/solution.py
@@ -17,6 +17,7 @@
 VMEM = 24 * 1024 * 1024
 TILES = 7
 EARLY = 2
+FIRST = 4
 
 F32 = jnp.float32
 BF16 = jnp.bfloat16
@@ -107,9 +108,9 @@
     count = len(parts)
     ins, outs, sems = refs[:count], refs[count + 1 : -1], refs[-1]
     copies = []
-    for ref, (axis, cuts, taken) in zip(ins, parts):
+    for ref, (axis, cuts, first, taken) in zip(ins, parts):
         size = ref.shape[axis] // cuts
-        for c in range(taken):
+        for c in range(first, first + taken):
             at = (slice(None),) * axis + (pl.ds(c * size, size),)
             src = ref.at[c] if axis == 0 and size == 1 else ref.at[at]
             n = len(copies)
@@ -122,7 +123,7 @@
 
 def fetch(weights, parts, after, name):
     shapes = []
-    for w, (axis, cuts, taken) in zip(weights, parts):
+    for w, (axis, cuts, _, taken) in zip(weights, parts):
         shape = list(w.shape)
         shape[axis] //= cuts
         if shape[0] == 1:
@@ -139,22 +140,46 @@
         name=name,
     )(*[in_hbm(w) for w in weights], after)
     result = []
-    for _, _, taken in parts:
+    for *_, taken in parts:
         result.append(list(out[:taken]))
         out = out[taken:]
     return result
 
 
-def project_kernel(planes, rows, me, x_ref, v_ref, w_hbm, *refs):
-    early = refs[:EARLY]
-    own_ref, other_ref, flat, late, sems = refs[-5:]
+def late_copies(w_hbm, tiles, late, sems):
     tile = late.shape[2]
     copies = []
-    for t in range(EARLY, TILES):
-        n = t - EARLY
+    for n, t in enumerate(tiles):
         copy = pltpu.make_async_copy(w_hbm.at[:, pl.ds(t * tile, tile)], late.at[n], sems.at[n])
         copy.start()
         copies.append(copy)
+    return copies
+
+
+def multiply(flat, weights, own_ref, other_ref):
+    half = flat.shape[0] // 2
+    tile = own_ref.shape[1] // len(weights)
+    for t, weight in enumerate(weights):
+        at = slice(t * tile, (t + 1) * tile)
+        out = jnp.dot(flat[...], weight(), preferred_element_type=F32)
+        own_ref[:, at] = out[:half]
+        other_ref[:, at] = out[half:].astype(BF16)
+
+
+def landed(copies, late):
+    def one(n):
+        def get():
+            copies[n].wait()
+            return late[n]
+
+        return get
+
+    return [one(n) for n in range(len(copies))]
+
+
+def project_first_kernel(planes, rows, me, x_ref, v_ref, w_hbm, *refs):
+    own_ref, other_ref, flat, late, sems = refs[-5:]
+    copies = late_copies(w_hbm, range(FIRST), late, sems)
     heads = v_ref.shape[0]
     count = flat.shape[0]
     i = lax.broadcasted_iota(jnp.int32, (heads * count, 1), 0)
@@ -169,71 +194,85 @@
         flat[:, h * VH : (h + 1) * VH] = jnp.dot(
             mine[h * count : (h + 1) * count], v_ref[h], preferred_element_type=F32
         ).astype(BF16)
-    half = count // 2
-    for t in range(TILES):
-        if t >= EARLY:
-            copies[t - EARLY].wait()
-        w = early[t][...] if t < EARLY else late[t - EARLY]
-        at = slice(t * tile, (t + 1) * tile)
-        out = jnp.dot(flat[...], w, preferred_element_type=F32)
-        own_ref[:, at] = out[:half]
-        other_ref[:, at] = out[half:].astype(BF16)
+    multiply(flat, landed(copies, late), own_ref, other_ref)
+
+
+def project_rest_kernel(flat, w_hbm, *refs):
+    early = refs[:EARLY]
+    own_ref, other_ref, late, sems = refs[-4:]
+    copies = late_copies(w_hbm, range(FIRST + EARLY, TILES), late, sems)
+    weights = [lambda ref=ref: ref[...] for ref in early]
+    multiply(flat, weights + landed(copies, late), own_ref, other_ref)
 
 
 def project(me, by_heads, value_up, out_proj, early, planes, rows, after):
     count = planes * 8 * rows
     depth, features = out_proj.shape
+    tile = features // TILES
     half = count // 2
     vec = pl.BlockSpec(memory_space=pltpu.VMEM)
-    return pl.pallas_call(
-        functools.partial(project_kernel, planes, rows),
-        in_specs=[SCALARS, vec, vec, pl.BlockSpec(memory_space=pltpu.HBM)]
-        + [vec] * EARLY
-        + [pl.BlockSpec(memory_space=pl.ANY)] * len(after),
-        out_specs=[vec, vec],
-        out_shape=[sds((half, features), F32), sds((half, features), BF16)],
-        scratch_shapes=[
-            pltpu.VMEM((count, depth), BF16),
-            pltpu.VMEM((TILES - EARLY, depth, features // TILES), BF16),
-            pltpu.SemaphoreType.DMA((TILES - EARLY,)),
-        ],
-        compiler_params=params(),
-        name="projections",
-    )(me, by_heads, value_up, in_hbm(out_proj), *early, *after)
-
-
-def add_kernel(arrived, parts, tile, *refs):
+    hbm = pl.BlockSpec(memory_space=pltpu.HBM)
+
+    def sums(tiles):
+        return [sds((half, tiles * tile), F32), sds((half, tiles * tile), BF16)]
+
+    def scratch(tiles):
+        return [pltpu.VMEM((tiles, depth, tile), BF16), pltpu.SemaphoreType.DMA((tiles,))]
+
+    own_a, other_a, flat = pl.pallas_call(
+        functools.partial(project_first_kernel, planes, rows),
+        in_specs=[SCALARS, vec, vec, hbm] + [pl.BlockSpec(memory_space=pl.ANY)] * len(after),
+        out_specs=[vec] * 3,
+        out_shape=sums(FIRST) + [sds((count, depth), BF16)],
+        scratch_shapes=scratch(FIRST),
+        compiler_params=params(),
+        name="project_first",
+    )(me, by_heads, value_up, in_hbm(out_proj), *after)
+    own_b, other_b = pl.pallas_call(
+        project_rest_kernel,
+        in_specs=[vec, hbm] + [vec] * EARLY,
+        out_specs=[vec] * 2,
+        out_shape=sums(TILES - FIRST),
+        scratch_shapes=scratch(TILES - FIRST - EARLY),
+        compiler_params=params(),
+        cost_estimate=pl.CostEstimate(
+            flops=2 * count * depth * (TILES - FIRST) * tile,
+            bytes_accessed=2 * depth * (TILES - FIRST) * tile * 2,
+            transcendentals=0,
+        ),
+        name="project_rest",
+    )(flat, in_hbm(out_proj), *early)
+    return (own_a, own_b), (other_a, other_b)
+
+
+def add_kernel(parts, tile, *refs):
     outs = refs[-parts:]
+    ranges = (len(refs) - parts) // 2
     size = outs[0].shape[0]
-    for start in range(0, outs[0].shape[1], tile):
-        at = slice(start, start + tile)
-        for p in range(parts):
-            rows = slice(p * size, (p + 1) * size)
-            if arrived and size % 16 == 0:
-                total = refs[0][rows, at]
-                for ref in refs[1 : 1 + arrived]:
-                    total = total + ref[rows, at].astype(F32)
-            else:
-                if p == 0:
-                    full = refs[0][:, at]
-                    for ref in refs[1 : 1 + arrived]:
-                        full = full + ref[:, at].astype(F32)
-                total = full[rows]
-            outs[p][:, at] = total if p == 0 else total.astype(BF16)
-
-
-def add_and_cut(own, received, parts, name, after=()):
-    count, features = own.shape
-    size = count // parts
-    vec = pl.BlockSpec(memory_space=pltpu.VMEM)
-    return pl.pallas_call(
-        functools.partial(add_kernel, len(received), parts, 512),
-        in_specs=[vec] * (1 + len(received)) + [pl.BlockSpec(memory_space=pl.ANY)] * len(after),
+    first = 0
+    for own_ref, other_ref in zip(refs[:ranges], refs[ranges : 2 * ranges]):
+        for start in range(0, own_ref.shape[1], tile):
+            at = slice(start, start + tile)
+            to = slice(first + start, first + start + tile)
+            total = own_ref[:, at] + other_ref[:, at].astype(F32)
+            outs[0][:, to] = total[:size]
+            for p in range(1, parts):
+                outs[p][:, to] = total[p * size : (p + 1) * size].astype(BF16)
+        first += own_ref.shape[1]
+
+
+def add_and_cut(own, received, parts, name):
+    size = own[0].shape[0] // parts
+    features = sum(x.shape[1] for x in own)
+    vec = pl.BlockSpec(memory_space=pltpu.VMEM)
+    return pl.pallas_call(
+        functools.partial(add_kernel, parts, 512),
+        in_specs=[vec] * (2 * len(own)),
         out_specs=[vec] * parts,
         out_shape=[sds((size, features), F32)] + [sds((size, features), BF16)] * (parts - 1),
         compiler_params=params(),
         name=name,
-    )(own, *received, *after)
+    )(*own, *received)
 
 
 def routes_kernel(ids, weights, unused, out_ref):
@@ -339,7 +378,7 @@
     )
 
 
-def add_and_pick_kernel(planes, tile, own_ref, a_ref, b_ref, c_ref, hidden_ref, pick_ref, *outs):
+def add_and_pick_kernel(planes, tile, first, own_ref, a_ref, b_ref, c_ref, hidden_ref, pick_ref, *outs):
     size = outs[0].shape[0]
     rows = hidden_ref.shape[0]
     pick = pick_ref[...]
@@ -349,7 +388,8 @@
         total = own_ref[:, at]
         for ref in (a_ref, b_ref, c_ref):
             total = total + ref[:, at].astype(F32)
-        home = total[:rows] + hidden_ref[:, at].astype(F32)
+        here = slice(first + start, first + start + tile)
+        home = total[:rows] + hidden_ref[:, here].astype(F32)
         total = jnp.concatenate([home, total[rows:]], axis=0)
         outs[0][:, at] = pick_rows(near, total)
         others = jnp.dot(far, total.astype(BF16), preferred_element_type=F32)
@@ -357,12 +397,12 @@
             outs[k][:, at] = others[(k - 1) * size : k * size].astype(BF16)
 
 
-def add_and_pick(own, received, hidden, pick, planes):
+def add_and_pick(own, received, hidden, pick, planes, first):
     features = own.shape[1]
     size = pick.shape[0] // planes
     vec = pl.BlockSpec(memory_space=pltpu.VMEM)
     return pl.pallas_call(
-        functools.partial(add_and_pick_kernel, planes, 1024),
+        functools.partial(add_and_pick_kernel, planes, 1024, first),
         in_specs=[vec] * 6,
         out_specs=[vec] * planes,
         out_shape=[sds((size, features), F32)] + [sds((size, features), BF16)] * (planes - 1),
@@ -371,12 +411,15 @@
     )(own, *received, hidden, pick)
 
 
-def norm_kernel(planes, *refs):
-    gain_ref, resid_ref, normed_ref = refs[planes], refs[-2], refs[-1]
-    total = refs[0][...]
-    for ref in refs[1:planes]:
-        total = total + ref[...].astype(F32)
-    resid = total.astype(BF16)
+def norm_kernel(planes, parts, *refs):
+    gain_ref, resid_ref, normed_ref = refs[planes * parts], refs[-2], refs[-1]
+    totals = []
+    for p in range(parts):
+        total = refs[p * planes][...]
+        for ref in refs[p * planes + 1 : (p + 1) * planes]:
+            total = total + ref[...].astype(F32)
+        totals.append(total)
+    resid = jnp.concatenate(totals[::-1], axis=1).astype(BF16)
     resid_ref[...] = resid
     wide = resid.astype(F32)
     scale = lax.rsqrt(jnp.mean(wide * wide, axis=1, keepdims=True) + EPSILON)
@@ -385,15 +428,17 @@
 
 def norm(sums, gain, after):
     vec = pl.BlockSpec(memory_space=pltpu.VMEM)
-    shape = sums[0].shape
-    return pl.pallas_call(
-        functools.partial(norm_kernel, len(sums)),
-        in_specs=[vec] * (1 + len(sums)) + [pl.BlockSpec(memory_space=pl.ANY)] * len(after),
+    planes = len(sums[0])
+    shape = (sums[0][0].shape[0], gain.shape[1])
+    return pl.pallas_call(
+        functools.partial(norm_kernel, planes, len(sums)),
+        in_specs=[vec] * (1 + planes * len(sums))
+        + [pl.BlockSpec(memory_space=pl.ANY)] * len(after),
         out_specs=[vec, vec],
         out_shape=[sds(shape, BF16), sds(shape, BF16)],
         compiler_params=params(),
         name="norm",
-    )(*sums, gain, *after)
+    )(*sums[1], *sums[0], gain, *after)
 
 
 def expert_kernel(pieces, tiles, *refs):
@@ -506,20 +551,30 @@
 
     latents = attention(queries, latent_cache, lengths)
     by_heads = lax.all_to_all(latents, "dp", split_axis=0, concat_axis=0, tiled=True)
-    (early,) = fetch([out_proj], [(1, TILES, EARLY)], latents, "fetch_projections")
+    (early,) = fetch([out_proj], [(1, TILES, FIRST, EARLY)], latents, "fetch_projections")
     mine = routes(route_ids, route_weights, latents)
     homes = over_planes([mine] * (planes - 1))
     homes = [mine] + homes[::-1]
-    own, other = project(me, by_heads, value_up, out_proj, early, planes, rows, homes[1:])
-    own, *out = add_and_cut(own, [swap(other, 1)], 4, "add_core")
+    own, other = project(me, by_heads, value_up, out_proj, early, planes, rows, homes[1:] + early[:1])
+    parts = []
+    for n in range(2):
+        part, *out = add_and_cut(own[n : n + 1], [swap(other[n], 1)], 4, "add_core")
+        parts.append((part, over_chips(out)))
+    own = parts[0][0]
     pick, weight, merge = tables(me, route_ids, homes, cap, own)
-    own, *out = add_and_pick(own, over_chips(out), hidden_in, pick, planes)
-    gate_up, (down_proj,) = fetch([gate_up, down_proj], [(0, 2, 2), (0, 1, 1)], own, "fetch_experts")
-    resid, picked = norm([own] + over_planes(out), norm_gain[None], gate_up[:1])
+    sums, first = [], 0
+    for own, received in parts:
+        own, *out = add_and_pick(own, received, hidden_in, pick, planes, first)
+        sums.append([own] + over_planes(out))
+        first += own.shape[1]
+    gate_up, (down_proj,) = fetch(
+        [gate_up, down_proj], [(0, 2, 0, 2), (0, 1, 0, 1)], sums[1][0], "fetch_experts"
+    )
+    resid, picked = norm(sums, norm_gain[None], gate_up[:1])
     chips = [picked] + [swap(picked, k << 1) for k in (1, 2, 3)]
     pieces = chips + [swap(x, 1) for x in chips]
     own, other = expert(pieces, gate_up, down_proj)
-    own, *out = add_and_cut(own, [swap(other, 1)], 4, "add_expert_core")
+    own, *out = add_and_cut([own], [swap(other, 1)], 4, "add_expert_core")
     own, *out = weigh(own, over_chips(out), resid, weight, planes, picks)
     return combine(merge, [own] + over_planes(out))
 

time: 88.5 us -> 87.8 us (level)
  waiting for transfers between devices: 39.2 us -> 30 us
  starting transfers between devices: 31.8 us -> 39.7 us
    ppermute x24 -> x31, waiting for transfers between devices: 38.8 us -> 29.6 us  [swap(): return lax.ppermute(x, 'dp', [(i, i ^ mask) for i in range(devices)])]
    ppermute x24 -> x31, starting transfers between devices: 24.5 us -> 32.4 us  [swap(): return lax.ppermute(x, 'dp', [(i, i ^ mask) for i in range(devices)])]
    pallas_call x5 -> x8, Pallas kernels: 4.61 us -> 5.11 us  [the longest x1 2.55 us: project(): pl.pallas_call(functools.partial(project_first_kernel, planes, rows), in_...]
  transfers between devices with their start and end apart: 25 -> 32, of which waited for: 18 -> 20; matrix products, arithmetic and copies ran while one was open for 0% -> 0% of each run, Pallas kernels for 7% -> 9%
where the time goes in v8:
time: 87.8 us; the launch traced here: 87.5 us
  starting transfers between devices  39.7 us (45%)
  waiting for transfers between devices  30 us (34%)
  Pallas kernels  17.4 us (20%)
    ppermute x31, starting transfers between devices, swap(): return lax.ppermute(x, 'dp', [(i, i ^ mask) for i in range(devices)])  32.4 us
    ppermute x31, waiting for transfers between devices, swap(): return lax.ppermute(x, 'dp', [(i, i ^ mask) for i in range(devices)])  29.6 us
    all_to_all x1, starting transfers between devices, body(): lax.all_to_all(latents, 'dp', split_axis=0, concat_axis=0, tiled=True)  7.3 us
    pallas_call x2, Pallas kernels, fetch(): pl.pallas_call(functools.partial(fetch_kernel, parts), in_specs=[pl.Block...  4.26 us
    pallas_call x1, Pallas kernels, attention(): pl.pallas_call(attention_kernel, in_specs=[hbm, hbm, hbm], out_specs=pl.B...  4.18 us
    pallas_call x1, Pallas kernels, project(): pl.pallas_call(functools.partial(project_first_kernel, planes, rows), in_...  2.55 us
  transfers between devices with their start and end apart: 32, of which 20 were waited for; matrix products, arithmetic and copies ran while one was open for 0% of the time, Pallas kernels for 9%

profile of v8, /device:TPU:0, one launch (start us, length us, event | category | flops | bytes accessed | tf_op | source)
XLA Modules:
  0.0 87.5 jit_solution(10682638913274415929)
XLA Ops:
  0.0 4.2 %latent_attention.1.unused.refs_1_ = bf16[512,512]{1,0:T(8,128)(2,1)} custom-call(s32[4]{0:T(128)} %lengths_hbm.1, bf16[4,576,128]{2,1,0:T(8,128)(2,1)} %bitcast.7, bf16[4,576,512]{2,1,0:T(8,128)(2,1)} %bitcast.6), custom_call_target="tpu_custom_call" | custom-call | tf_op jit(solution)/shard_map/latent_attention/pallas_call | solution.py:86
  4.2 7.3 %all-to-all-start = ((bf16[32,16,512]{2,1,0:T(8,128)(2,1)}), bf16[32,16,512]{2,1,0:T(8,128)(2,1)S(1)}, u32[]{:S(2)}, u32[]{:S(2)}) async-start(bf16[32,16,512]{2,1,0:T(8,128)(2,1)} %bitcast.3), calls=%async_computation | async-start | bytes 1048576 | tf_op jit(solution)/shard_map/all_to_all | solution.py:553
  12.3 3.7 %collective-permute-start.2 = (f32[8,128]{1,0:T(8,128)S(1)}, f32[8,128]{1,0:T(8,128)S(1)}, u32[]{:S(2)}, u32[]{:S(2)}) collective-permute-start(f32[8,128]{1,0:T(8,128)S(1)} %routes.1.refs_0_), channel_id=1, source_target_pairs={{0,24},{1,25},{2,26},{3,27},{4,28},{5,29},{6,30},{7,31},{8,16},{9,... | collective-permute-start | bytes 12296 | tf_op jit(solution)/shard_map/ppermute | solution.py:543
  16.8 1.6 %fetch_projections.1 = (bf16[512,1024]{1,0:T(8,128)(2,1)S(1)}, bf16[512,1024]{1,0:T(8,128)(2,1)S(1)}) custom-call(bf16[512,7168]{1,0:T(8,128)(2,1)} %w_hbm.3, bf16[512,512]{1,0:T(8,128)(2,1)} %latent_attention.1.unused.refs_1_), custom_call_target="tpu_custom_call" | custom-call | tf_op jit(solution)/shard_map/fetch_projections/pallas_call | solution.py:132
  18.4 6.4 %collective-permute-done.2.refs_2_.refs_3_ = f32[8,128]{1,0:T(8,128)S(1)} collective-permute-done((f32[8,128]{1,0:T(8,128)S(1)}, f32[8,128]{1,0:T(8,128)S(1)}, u32[]{:S(2)}, u32[]{:S(2)}) %collective-permute-start.2) | collective-permute-done | bytes 4128 | tf_op jit(solution)/shard_map/ppermute | solution.py:543
  24.8 2.0 %collective-permute-done.1.refs_1_.refs_2_ = f32[8,128]{1,0:T(8,128)S(1)} collective-permute-done((f32[8,128]{1,0:T(8,128)S(1)}, f32[8,128]{1,0:T(8,128)S(1)}, u32[]{:S(2)}, u32[]{:S(2)}) %collective-permute-start.1) | collective-permute-done | bytes 4128 | tf_op jit(solution)/shard_map/ppermute | solution.py:543
  27.2 2.6 %project_first.1 = (f32[64,4096]{1,0:T(8,128)S(1)}, bf16[64,4096]{1,0:T(8,128)(2,1)S(1)}, bf16[128,512]{1,0:T(8,128)(2,1)S(1)}) custom-call(s32[1]{0:T(128)} %bitcast.me, bf16[512,512]{1,0:T(8,128)(2,1)S(1)} %bitcast.5, bf16[4,512,128]{2,1,0:T(8,128)(2,1)S(1)} %copy-done, bf16[512,7168]{1,0:T(8,128)(2,1)} %w_hbm.3, ...), custom_call_target="tpu_custom_call" | custom-call | tf_op jit(solution)/shard_map/project_first/pallas_call | solution.py:222
  29.9 1.6 %project_rest.1 = (f32[64,3072]{1,0:T(8,128)S(1)}, bf16[64,3072]{1,0:T(8,128)(2,1)S(1)}) custom-call(bf16[128,512]{1,0:T(8,128)(2,1)S(1)} %get-tuple-element.51.flat, bf16[512,7168]{1,0:T(8,128)(2,1)} %w_hbm.3, bf16[512,1024]{1,0:T(8,128)(2,1)S(1)} %get-tuple-element.46.refs_3_.refs_0_, bf16[512,1024]{1,0:T(8,128)(2,1)S(1)} %get-tuple-element.52.refs_1_), custom_call_target="tpu_custom_call" | custom-call | flops 402653184 | bytes 6291456 | tf_op jit(solution)/shard_map/project_rest/pallas_call | solution.py:231
  39.8 1.4 %collective-permute-start.13 = (bf16[16,4096]{1,0:T(8,128)(2,1)S(1)}, bf16[16,4096]{1,0:T(8,128)(2,1)S(1)}, u32[]{:S(2)}, u32[]{:S(2)}) collective-permute-start(bf16[16,4096]{1,0:T(8,128)(2,1)S(1)} %get-tuple-element.66), channel_id=1, source_target_pairs={{0,6},{1,7},{2,4},{3,5},{4,2},{5,3},{6,0},{7,1},{8,14},{9,15},{10,... | collective-permute-start | bytes 393224 | tf_op jit(solution)/shard_map/ppermute | solution.py:543
  43.0 1.5 %collective-permute-start.8 = (bf16[8,3072]{1,0:T(8,128)(2,1)S(1)}, bf16[8,3072]{1,0:T(8,128)(2,1)S(1)}, u32[]{:S(2)}, u32[]{:S(2)}) collective-permute-start(bf16[8,3072]{1,0:T(8,128)(2,1)S(1)} %get-tuple-element.61), channel_id=1, source_target_pairs={{0,24},{1,25},{2,26},{3,27},{4,28},{5,29},{6,30},{7,31},{8,16},{9,... | collective-permute-start | bytes 147464 | tf_op jit(solution)/shard_map/ppermute | solution.py:543
  44.8 1.4 %collective-permute-done.12.b_ref = bf16[16,4096]{1,0:T(8,128)(2,1)S(1)} collective-permute-done((bf16[16,4096]{1,0:T(8,128)(2,1)S(1)}, bf16[16,4096]{1,0:T(8,128)(2,1)S(1)}, u32[]{:S(2)}, u32[]{:S(2)}) %collective-permute-start.12) | collective-permute-done | bytes 131104 | tf_op jit(solution)/shard_map/ppermute | solution.py:543
  47.5 1.5 %collective-permute-start.14 = (bf16[8,4096]{1,0:T(8,128)(2,1)S(1)}, bf16[8,4096]{1,0:T(8,128)(2,1)S(1)}, u32[]{:S(2)}, u32[]{:S(2)}) collective-permute-start(bf16[8,4096]{1,0:T(8,128)(2,1)S(1)} %get-tuple-element.68), channel_id=1, source_target_pairs={{0,24},{1,25},{2,26},{3,27},{4,28},{5,29},{6,30},{7,31},{8,16},{9,... | collective-permute-start | bytes 196616 | tf_op jit(solution)/shard_map/ppermute | solution.py:543
  49.7 2.2 %collective-permute-start.16 = (bf16[8,4096]{1,0:T(8,128)(2,1)S(1)}, bf16[8,4096]{1,0:T(8,128)(2,1)S(1)}, u32[]{:S(2)}, u32[]{:S(2)}) collective-permute-start(bf16[8,4096]{1,0:T(8,128)(2,1)S(1)} %get-tuple-element.70), channel_id=1, source_target_pairs={{0,8},{1,9},{2,10},{3,11},{4,12},{5,13},{6,14},{7,15},{8,0},{9,1},... | collective-permute-start | bytes 196616 | tf_op jit(solution)/shard_map/ppermute | solution.py:543
  51.9 2.0 %collective-permute-start.10 = (bf16[8,3072]{1,0:T(8,128)(2,1)S(1)}, bf16[8,3072]{1,0:T(8,128)(2,1)S(1)}, u32[]{:S(2)}, u32[]{:S(2)}) collective-permute-start(bf16[8,3072]{1,0:T(8,128)(2,1)S(1)} %get-tuple-element.63), channel_id=1, source_target_pairs={{0,8},{1,9},{2,10},{3,11},{4,12},{5,13},{6,14},{7,15},{8,0},{9,1},... | collective-permute-start | bytes 147464 | tf_op jit(solution)/shard_map/ppermute | solution.py:543
  53.9 2.6 %fetch_experts.1 = (bf16[7168,128]{1,0:T(8,128)(2,1)S(1)}, bf16[7168,128]{1,0:T(8,128)(2,1)S(1)}, bf16[128,7168]{1,0:T(8,128)(2,1)S(1)}) custom-call(bf16[2,7168,128]{2,1,0:T(8,128)(2,1)} %refs_0_.3, bf16[128,7168]{1,0:T(8,128)(2,1)} %refs_1_.1, f32[8,3072]{1,0:T(8,128)S(1)} %get-tuple-element.60.refs_2_.refs_0_), custom_call_target="tpu_custom_call" | custom-call | tf_op jit(solution)/shard_map/fetch_experts/pallas_call | solution.py:132
  58.1 1.6 %collective-permute-start.19 = (bf16[8,7168]{1,0:T(8,128)(2,1)S(1)}, bf16[8,7168]{1,0:T(8,128)(2,1)S(1)}, u32[]{:S(2)}, u32[]{:S(2)}) collective-permute-start(bf16[8,7168]{1,0:T(8,128)(2,1)S(1)} %get-tuple-element.72.refs_0_), channel_id=1, source_target_pairs={{0,6},{1,7},{2,4},{3,5},{4,2},{5,3},{6,0},{7,1},{8,14},{9,15},{10,... | collective-permute-start | bytes 344072 | tf_op jit(solution)/shard_map/ppermute | solution.py:543
  59.7 1.7 %collective-permute-start.18 = (bf16[8,7168]{1,0:T(8,128)(2,1)S(1)}, bf16[8,7168]{1,0:T(8,128)(2,1)S(1)}, u32[]{:S(2)}, u32[]{:S(2)}) collective-permute-start(bf16[8,7168]{1,0:T(8,128)(2,1)S(1)} %get-tuple-element.72.refs_0_), channel_id=1, source_target_pairs={{0,4},{1,5},{2,6},{3,7},{4,0},{5,1},{6,2},{7,3},{8,12},{9,13},{10,... | collective-permute-start | bytes 344072 | tf_op jit(solution)/shard_map/ppermute | solution.py:543
  61.7 3.0 %collective-permute-done.19.refs_3_ = bf16[8,7168]{1,0:T(8,128)(2,1)S(1)} collective-permute-done((bf16[8,7168]{1,0:T(8,128)(2,1)S(1)}, bf16[8,7168]{1,0:T(8,128)(2,1)S(1)}, u32[]{:S(2)}, u32[]{:S(2)}) %collective-permute-start.19) | collective-permute-done | bytes 114720 | tf_op jit(solution)/shard_map/ppermute | solution.py:543
  69.5 1.7 %collective-permute-done.24.refs_1_ = bf16[32,7168]{1,0:T(8,128)(2,1)S(1)} collective-permute-done((bf16[32,7168]{1,0:T(8,128)(2,1)S(1)}, bf16[32,7168]{1,0:T(8,128)(2,1)S(1)}, u32[]{:S(2)}, u32[]{:S(2)}) %collective-permute-start.24) | collective-permute-done | bytes 458784 | tf_op jit(solution)/shard_map/ppermute | solution.py:543
  73.0 1.8 %collective-permute-start.27 = (bf16[8,7168]{1,0:T(8,128)(2,1)S(1)}, bf16[8,7168]{1,0:T(8,128)(2,1)S(1)}, u32[]{:S(2)}, u32[]{:S(2)}) collective-permute-start(bf16[8,7168]{1,0:T(8,128)(2,1)S(1)} %get-tuple-element.80), channel_id=1, source_target_pairs={{0,6},{1,7},{2,4},{3,5},{4,2},{5,3},{6,0},{7,1},{8,14},{9,15},{10,... | collective-permute-start | bytes 344072 | tf_op jit(solution)/shard_map/ppermute | solution.py:543
  74.8 2.0 %collective-permute-done.25.a_ref = bf16[8,7168]{1,0:T(8,128)(2,1)S(1)} collective-permute-done((bf16[8,7168]{1,0:T(8,128)(2,1)S(1)}, bf16[8,7168]{1,0:T(8,128)(2,1)S(1)}, u32[]{:S(2)}, u32[]{:S(2)}) %collective-permute-start.25) | collective-permute-done | bytes 114720 | tf_op jit(solution)/shard_map/ppermute | solution.py:543
  78.0 1.9 %collective-permute-done.27.c_ref = bf16[8,7168]{1,0:T(8,128)(2,1)S(1)} collective-permute-done((bf16[8,7168]{1,0:T(8,128)(2,1)S(1)}, bf16[8,7168]{1,0:T(8,128)(2,1)S(1)}, u32[]{:S(2)}, u32[]{:S(2)}) %collective-permute-start.27) | collective-permute-done | bytes 114720 | tf_op jit(solution)/shard_map/ppermute | solution.py:543
  80.0 1.7 %collective-permute-start.28 = (bf16[2,7168]{1,0:T(2,128)(2,1)S(1)}, bf16[2,7168]{1,0:T(2,128)(2,1)S(1)}, u32[]{:S(2)}, u32[]{:S(2)}) collective-permute-start(bf16[2,7168]{1,0:T(2,128)(2,1)S(1)} %get-tuple-element.84), channel_id=1, source_target_pairs={{0,24},{1,25},{2,26},{3,27},{4,28},{5,29},{6,30},{7,31},{8,16},{9,... | collective-permute-start | bytes 86024 | tf_op jit(solution)/shard_map/ppermute | solution.py:543
  81.7 2.8 %collective-permute-start.30 = (bf16[2,7168]{1,0:T(2,128)(2,1)S(1)}, bf16[2,7168]{1,0:T(2,128)(2,1)S(1)}, u32[]{:S(2)}, u32[]{:S(2)}) collective-permute-start(bf16[2,7168]{1,0:T(2,128)(2,1)S(1)} %get-tuple-element.86), channel_id=1, source_target_pairs={{0,8},{1,9},{2,10},{3,11},{4,12},{5,13},{6,14},{7,15},{8,0},{9,1},... | collective-permute-start | bytes 86024 | tf_op jit(solution)/shard_map/ppermute | solution.py:543
  (69 shorter events, 27.3 us)
Async XLA Ops:
  4.2 23.0 %all-to-all-start = ((bf16[32,16,512]{2,1,0:T(8,128)(2,1)}), bf16[32,16,512]{2,1,0:T(8,128)(2,1)S(1)}, u32[]{:S(2)}, u32[]{:S(2)}) async-start(bf16[32,16,512]{2,1,0:T(8,128)(2,1)} %bitcast.3), calls=%async_computation | async-start | bytes 1048576 | tf_op jit(solution)/shard_map/all_to_all | solution.py:553
  12.3 12.5 %collective-permute-start.2 = (f32[8,128]{1,0:T(8,128)S(1)}, f32[8,128]{1,0:T(8,128)S(1)}, u32[]{:S(2)}, u32[]{:S(2)}) collective-permute-start(f32[8,128]{1,0:T(8,128)S(1)} %routes.1.refs_0_), channel_id=1, source_target_pairs={{0,24},{1,25},{2,26},{3,27},{4,28},{5,29},{6,30},{7,31},{8,16},{9,... | collective-permute-start | bytes 12296 | tf_op jit(solution)/shard_map/ppermute | solution.py:543
  16.0 10.8 %collective-permute-start.1 = (f32[8,128]{1,0:T(8,128)S(1)}, f32[8,128]{1,0:T(8,128)S(1)}, u32[]{:S(2)}, u32[]{:S(2)}) collective-permute-start(f32[8,128]{1,0:T(8,128)S(1)} %routes.1.refs_0_), channel_id=1, source_target_pairs={{0,16},{1,17},{2,18},{3,19},{4,20},{5,21},{6,22},{7,23},{8,24},{9,... | collective-permute-start | bytes 12296 | tf_op jit(solution)/shard_map/ppermute | solution.py:543
  16.0 10.8 %collective-permute-start = (f32[8,128]{1,0:T(8,128)S(1)}, f32[8,128]{1,0:T(8,128)S(1)}, u32[]{:S(2)}, u32[]{:S(2)}) collective-permute-start(f32[8,128]{1,0:T(8,128)S(1)} %routes.1.refs_0_), channel_id=1, source_target_pairs={{0,8},{1,9},{2,10},{3,11},{4,12},{5,13},{6,14},{7,15},{8,0},{9,1},... | collective-permute-start | bytes 12296 | tf_op jit(solution)/shard_map/ppermute | solution.py:543
  29.8 7.2 %collective-permute-start.3 = (bf16[64,4096]{1,0:T(8,128)(2,1)S(1)}, bf16[64,4096]{1,0:T(8,128)(2,1)S(1)}, u32[]{:S(2)}, u32[]{:S(2)}) collective-permute-start(bf16[64,4096]{1,0:T(8,128)(2,1)S(1)} %get-tuple-element.48), channel_id=1, source_target_pairs={{0,1},{1,0},{2,3},{3,2},{4,5},{5,4},{6,7},{7,6},{8,9},{9,8},{10,11... | collective-permute-start | bytes 1572872 | tf_op jit(solution)/shard_map/ppermute | solution.py:543
  33.5 6.3 %collective-permute-start.5 = (bf16[16,3072]{1,0:T(8,128)(2,1)S(1)}, bf16[16,3072]{1,0:T(8,128)(2,1)S(1)}, u32[]{:S(2)}, u32[]{:S(2)}) collective-permute-start(bf16[16,3072]{1,0:T(8,128)(2,1)S(1)} %get-tuple-element.56), channel_id=1, source_target_pairs={{0,2},{1,3},{2,0},{3,1},{4,6},{5,7},{6,4},{7,5},{8,10},{9,11},{10,... | collective-permute-start | bytes 294920 | tf_op jit(solution)/shard_map/ppermute | solution.py:543
  34.8 7.5 %collective-permute-start.6 = (bf16[16,3072]{1,0:T(8,128)(2,1)S(1)}, bf16[16,3072]{1,0:T(8,128)(2,1)S(1)}, u32[]{:S(2)}, u32[]{:S(2)}) collective-permute-start(bf16[16,3072]{1,0:T(8,128)(2,1)S(1)} %get-tuple-element.57), channel_id=1, source_target_pairs={{0,4},{1,5},{2,6},{3,7},{4,0},{5,1},{6,2},{7,3},{8,12},{9,13},{10,... | collective-permute-start | bytes 294920 | tf_op jit(solution)/shard_map/ppermute | solution.py:543
  36.2 6.6 %collective-permute-start.7 = (bf16[16,3072]{1,0:T(8,128)(2,1)S(1)}, bf16[16,3072]{1,0:T(8,128)(2,1)S(1)}, u32[]{:S(2)}, u32[]{:S(2)}) collective-permute-start(bf16[16,3072]{1,0:T(8,128)(2,1)S(1)} %get-tuple-element.58), channel_id=1, source_target_pairs={{0,6},{1,7},{2,4},{3,5},{4,2},{5,3},{6,0},{7,1},{8,14},{9,15},{10,... | collective-permute-start | bytes 294920 | tf_op jit(solution)/shard_map/ppermute | solution.py:543
  37.1 7.7 %collective-permute-start.11 = (bf16[16,4096]{1,0:T(8,128)(2,1)S(1)}, bf16[16,4096]{1,0:T(8,128)(2,1)S(1)}, u32[]{:S(2)}, u32[]{:S(2)}) collective-permute-start(bf16[16,4096]{1,0:T(8,128)(2,1)S(1)} %get-tuple-element.64), channel_id=1, source_target_pairs={{0,2},{1,3},{2,0},{3,1},{4,6},{5,7},{6,4},{7,5},{8,10},{9,11},{10,... | collective-permute-start | bytes 393224 | tf_op jit(solution)/shard_map/ppermute | solution.py:543
  38.5 7.7 %collective-permute-start.12 = (bf16[16,4096]{1,0:T(8,128)(2,1)S(1)}, bf16[16,4096]{1,0:T(8,128)(2,1)S(1)}, u32[]{:S(2)}, u32[]{:S(2)}) collective-permute-start(bf16[16,4096]{1,0:T(8,128)(2,1)S(1)} %get-tuple-element.65), channel_id=1, source_target_pairs={{0,4},{1,5},{2,6},{3,7},{4,0},{5,1},{6,2},{7,3},{8,12},{9,13},{10,... | collective-permute-start | bytes 393224 | tf_op jit(solution)/shard_map/ppermute | solution.py:543
  39.8 7.4 %collective-permute-start.13 = (bf16[16,4096]{1,0:T(8,128)(2,1)S(1)}, bf16[16,4096]{1,0:T(8,128)(2,1)S(1)}, u32[]{:S(2)}, u32[]{:S(2)}) collective-permute-start(bf16[16,4096]{1,0:T(8,128)(2,1)S(1)} %get-tuple-element.66), channel_id=1, source_target_pairs={{0,6},{1,7},{2,4},{3,5},{4,2},{5,3},{6,0},{7,1},{8,14},{9,15},{10,... | collective-permute-start | bytes 393224 | tf_op jit(solution)/shard_map/ppermute | solution.py:543
  43.0 8.9 %collective-permute-start.8 = (bf16[8,3072]{1,0:T(8,128)(2,1)S(1)}, bf16[8,3072]{1,0:T(8,128)(2,1)S(1)}, u32[]{:S(2)}, u32[]{:S(2)}) collective-permute-start(bf16[8,3072]{1,0:T(8,128)(2,1)S(1)} %get-tuple-element.61), channel_id=1, source_target_pairs={{0,24},{1,25},{2,26},{3,27},{4,28},{5,29},{6,30},{7,31},{8,16},{9,... | collective-permute-start | bytes 147464 | tf_op jit(solution)/shard_map/ppermute | solution.py:543
  47.5 10.4 %collective-permute-start.14 = (bf16[8,4096]{1,0:T(8,128)(2,1)S(1)}, bf16[8,4096]{1,0:T(8,128)(2,1)S(1)}, u32[]{:S(2)}, u32[]{:S(2)}) collective-permute-start(bf16[8,4096]{1,0:T(8,128)(2,1)S(1)} %get-tuple-element.68), channel_id=1, source_target_pairs={{0,24},{1,25},{2,26},{3,27},{4,28},{5,29},{6,30},{7,31},{8,16},{9,... | collective-permute-start | bytes 196616 | tf_op jit(solution)/shard_map/ppermute | solution.py:543
  49.0 8.9 %collective-permute-start.15 = (bf16[8,4096]{1,0:T(8,128)(2,1)S(1)}, bf16[8,4096]{1,0:T(8,128)(2,1)S(1)}, u32[]{:S(2)}, u32[]{:S(2)}) collective-permute-start(bf16[8,4096]{1,0:T(8,128)(2,1)S(1)} %get-tuple-element.69), channel_id=1, source_target_pairs={{0,16},{1,17},{2,18},{3,19},{4,20},{5,21},{6,22},{7,23},{8,24},{9,... | collective-permute-start | bytes 196616 | tf_op jit(solution)/shard_map/ppermute | solution.py:543
  49.7 8.2 %collective-permute-start.16 = (bf16[8,4096]{1,0:T(8,128)(2,1)S(1)}, bf16[8,4096]{1,0:T(8,128)(2,1)S(1)}, u32[]{:S(2)}, u32[]{:S(2)}) collective-permute-start(bf16[8,4096]{1,0:T(8,128)(2,1)S(1)} %get-tuple-element.70), channel_id=1, source_target_pairs={{0,8},{1,9},{2,10},{3,11},{4,12},{5,13},{6,14},{7,15},{8,0},{9,1},... | collective-permute-start | bytes 196616 | tf_op jit(solution)/shard_map/ppermute | solution.py:543
  51.9 5.9 %collective-permute-start.9 = (bf16[8,3072]{1,0:T(8,128)(2,1)S(1)}, bf16[8,3072]{1,0:T(8,128)(2,1)S(1)}, u32[]{:S(2)}, u32[]{:S(2)}) collective-permute-start(bf16[8,3072]{1,0:T(8,128)(2,1)S(1)} %get-tuple-element.62), channel_id=1, source_target_pairs={{0,16},{1,17},{2,18},{3,19},{4,20},{5,21},{6,22},{7,23},{8,24},{9,... | collective-permute-start | bytes 147464 | tf_op jit(solution)/shard_map/ppermute | solution.py:543
  51.9 5.9 %collective-permute-start.10 = (bf16[8,3072]{1,0:T(8,128)(2,1)S(1)}, bf16[8,3072]{1,0:T(8,128)(2,1)S(1)}, u32[]{:S(2)}, u32[]{:S(2)}) collective-permute-start(bf16[8,3072]{1,0:T(8,128)(2,1)S(1)} %get-tuple-element.63), channel_id=1, source_target_pairs={{0,8},{1,9},{2,10},{3,11},{4,12},{5,13},{6,14},{7,15},{8,0},{9,1},... | collective-permute-start | bytes 147464 | tf_op jit(solution)/shard_map/ppermute | solution.py:543
  58.1 6.5 %collective-permute-start.19 = (bf16[8,7168]{1,0:T(8,128)(2,1)S(1)}, bf16[8,7168]{1,0:T(8,128)(2,1)S(1)}, u32[]{:S(2)}, u32[]{:S(2)}) collective-permute-start(bf16[8,7168]{1,0:T(8,128)(2,1)S(1)} %get-tuple-element.72.refs_0_), channel_id=1, source_target_pairs={{0,6},{1,7},{2,4},{3,5},{4,2},{5,3},{6,0},{7,1},{8,14},{9,15},{10,... | collective-permute-start | bytes 344072 | tf_op jit(solution)/shard_map/ppermute | solution.py:543
  59.7 6.3 %collective-permute-start.18 = (bf16[8,7168]{1,0:T(8,128)(2,1)S(1)}, bf16[8,7168]{1,0:T(8,128)(2,1)S(1)}, u32[]{:S(2)}, u32[]{:S(2)}) collective-permute-start(bf16[8,7168]{1,0:T(8,128)(2,1)S(1)} %get-tuple-element.72.refs_0_), channel_id=1, source_target_pairs={{0,4},{1,5},{2,6},{3,7},{4,0},{5,1},{6,2},{7,3},{8,12},{9,13},{10,... | collective-permute-start | bytes 344072 | tf_op jit(solution)/shard_map/ppermute | solution.py:543
  61.4 5.5 %collective-permute-start.17 = (bf16[8,7168]{1,0:T(8,128)(2,1)S(1)}, bf16[8,7168]{1,0:T(8,128)(2,1)S(1)}, u32[]{:S(2)}, u32[]{:S(2)}) collective-permute-start(bf16[8,7168]{1,0:T(8,128)(2,1)S(1)} %get-tuple-element.72.refs_0_), channel_id=1, source_target_pairs={{0,2},{1,3},{2,0},{3,1},{4,6},{5,7},{6,4},{7,5},{8,10},{9,11},{10,... | collective-permute-start | bytes 344072 | tf_op jit(solution)/shard_map/ppermute | solution.py:543
  71.2 5.6 %collective-permute-start.25 = (bf16[8,7168]{1,0:T(8,128)(2,1)S(1)}, bf16[8,7168]{1,0:T(8,128)(2,1)S(1)}, u32[]{:S(2)}, u32[]{:S(2)}) collective-permute-start(bf16[8,7168]{1,0:T(8,128)(2,1)S(1)} %get-tuple-element.78), channel_id=1, source_target_pairs={{0,2},{1,3},{2,0},{3,1},{4,6},{5,7},{6,4},{7,5},{8,10},{9,11},{10,... | collective-permute-start | bytes 344072 | tf_op jit(solution)/shard_map/ppermute | solution.py:543
  72.3 5.7 %collective-permute-start.26 = (bf16[8,7168]{1,0:T(8,128)(2,1)S(1)}, bf16[8,7168]{1,0:T(8,128)(2,1)S(1)}, u32[]{:S(2)}, u32[]{:S(2)}) collective-permute-start(bf16[8,7168]{1,0:T(8,128)(2,1)S(1)} %get-tuple-element.79), channel_id=1, source_target_pairs={{0,4},{1,5},{2,6},{3,7},{4,0},{5,1},{6,2},{7,3},{8,12},{9,13},{10,... | collective-permute-start | bytes 344072 | tf_op jit(solution)/shard_map/ppermute | solution.py:543
  73.0 6.9 %collective-permute-start.27 = (bf16[8,7168]{1,0:T(8,128)(2,1)S(1)}, bf16[8,7168]{1,0:T(8,128)(2,1)S(1)}, u32[]{:S(2)}, u32[]{:S(2)}) collective-permute-start(bf16[8,7168]{1,0:T(8,128)(2,1)S(1)} %get-tuple-element.80), channel_id=1, source_target_pairs={{0,6},{1,7},{2,4},{3,5},{4,2},{5,3},{6,0},{7,1},{8,14},{9,15},{10,... | collective-permute-start | bytes 344072 | tf_op jit(solution)/shard_map/ppermute | solution.py:543
  80.0 5.8 %collective-permute-start.28 = (bf16[2,7168]{1,0:T(2,128)(2,1)S(1)}, bf16[2,7168]{1,0:T(2,128)(2,1)S(1)}, u32[]{:S(2)}, u32[]{:S(2)}) collective-permute-start(bf16[2,7168]{1,0:T(2,128)(2,1)S(1)} %get-tuple-element.84), channel_id=1, source_target_pairs={{0,24},{1,25},{2,26},{3,27},{4,28},{5,29},{6,30},{7,31},{8,16},{9,... | collective-permute-start | bytes 86024 | tf_op jit(solution)/shard_map/ppermute | solution.py:543
  (13 other events, 89.1 us)

commit v9 on v8

--- a/solution.py
+++ b/solution.py
@@ -346,7 +346,7 @@
                 for u in range(picks):
                     seen = seen + (ids[b, u] == ids[r, t]).astype(jnp.int32)
             away = ids[r, t] ^ plane
-            spot = jnp.where(away == 0, 0, jnp.where(away == 1, planes - 1, planes - away))
+            spot = jnp.where(away == 0, 0, jnp.where(away == 1, planes - 1, away - 1))
             slots.append(spot * cap + seen)
         merge = merge | (lane == column(slots, rows))
     merge_ref[...] = jnp.where(merge, 1.0, 0.0).astype(BF16)
@@ -544,7 +544,7 @@
 
     def over_planes(messages):
         moved = [swap(x, k << 3) for k, x in enumerate(messages, 1)]
-        return moved[1:][::-1] + moved[:1]
+        return moved[1:] + moved[:1]
 
     def over_chips(messages):
         return [swap(x, k << 1) for k, x in enumerate(messages, 1)]
@@ -554,7 +554,7 @@
     (early,) = fetch([out_proj], [(1, TILES, FIRST, EARLY)], latents, "fetch_projections")
     mine = routes(route_ids, route_weights, latents)
     homes = over_planes([mine] * (planes - 1))
-    homes = [mine] + homes[::-1]
+    homes = [mine] + homes[-1:] + homes[:-1]
     own, other = project(me, by_heads, value_up, out_proj, early, planes, rows, homes[1:] + early[:1])
     parts = []
     for n in range(2):

time: 87.8 us -> 87.3 us (level)
  starting transfers between devices: 39.7 us -> 37.2 us
  waiting for transfers between devices: 30 us -> 32 us
    ppermute x31, starting transfers between devices: 32.4 us -> 29.9 us  [swap(): return lax.ppermute(x, 'dp', [(i, i ^ mask) for i in range(devices)])]
    ppermute x31, waiting for transfers between devices: 29.6 us -> 31.7 us  [swap(): return lax.ppermute(x, 'dp', [(i, i ^ mask) for i in range(devices)])]
  transfers between devices with their start and end apart: 32 -> 32, of which waited for: 20 -> 19; matrix products, arithmetic and copies ran while one was open for 0% -> 0% of each run, Pallas kernels for 9% -> 10%
where the time goes in v9:
time: 87.3 us; the launch traced here: 87 us
  starting transfers between devices  37.2 us (43%)
  waiting for transfers between devices  32 us (37%)
  Pallas kernels  17.4 us (20%)
    ppermute x31, waiting for transfers between devices, swap(): return lax.ppermute(x, 'dp', [(i, i ^ mask) for i in range(devices)])  31.7 us
    ppermute x31, starting transfers between devices, swap(): return lax.ppermute(x, 'dp', [(i, i ^ mask) for i in range(devices)])  29.9 us
    all_to_all x1, starting transfers between devices, body(): lax.all_to_all(latents, 'dp', split_axis=0, concat_axis=0, tiled=True)  7.3 us
    pallas_call x2, Pallas kernels, fetch(): pl.pallas_call(functools.partial(fetch_kernel, parts), in_specs=[pl.Block...  4.26 us
    pallas_call x1, Pallas kernels, attention(): pl.pallas_call(attention_kernel, in_specs=[hbm, hbm, hbm], out_specs=pl.B...  4.18 us
    pallas_call x1, Pallas kernels, project(): pl.pallas_call(functools.partial(project_first_kernel, planes, rows), in_...  2.55 us
  transfers between devices with their start and end apart: 32, of which 19 were waited for; matrix products, arithmetic and copies ran while one was open for 0% of the time, Pallas kernels for 10%

profile of v9, /device:TPU:0, one launch (start us, length us, event | category | flops | bytes accessed | tf_op | source)
XLA Modules:
  0.0 87.0 jit_solution(6754812021572077090)
XLA Ops:
  0.0 4.2 %latent_attention.1.unused.refs_1_ = bf16[512,512]{1,0:T(8,128)(2,1)} custom-call(s32[4]{0:T(128)} %lengths_hbm.1, bf16[4,576,128]{2,1,0:T(8,128)(2,1)} %bitcast.7, bf16[4,576,512]{2,1,0:T(8,128)(2,1)} %bitcast.6), custom_call_target="tpu_custom_call" | custom-call | tf_op jit(solution)/shard_map/latent_attention/pallas_call | solution.py:86
  4.2 7.3 %all-to-all-start = ((bf16[32,16,512]{2,1,0:T(8,128)(2,1)}), bf16[32,16,512]{2,1,0:T(8,128)(2,1)S(1)}, u32[]{:S(2)}, u32[]{:S(2)}) async-start(bf16[32,16,512]{2,1,0:T(8,128)(2,1)} %bitcast.3), calls=%async_computation | async-start | bytes 1048576 | tf_op jit(solution)/shard_map/all_to_all | solution.py:553
  12.3 3.7 %collective-permute-start.2 = (f32[8,128]{1,0:T(8,128)S(1)}, f32[8,128]{1,0:T(8,128)S(1)}, u32[]{:S(2)}, u32[]{:S(2)}) collective-permute-start(f32[8,128]{1,0:T(8,128)S(1)} %routes.1.refs_0_), channel_id=1, source_target_pairs={{0,24},{1,25},{2,26},{3,27},{4,28},{5,29},{6,30},{7,31},{8,16},{9,... | collective-permute-start | bytes 12296 | tf_op jit(solution)/shard_map/ppermute | solution.py:543
  16.8 1.6 %fetch_projections.1 = (bf16[512,1024]{1,0:T(8,128)(2,1)S(1)}, bf16[512,1024]{1,0:T(8,128)(2,1)S(1)}) custom-call(bf16[512,7168]{1,0:T(8,128)(2,1)} %w_hbm.3, bf16[512,512]{1,0:T(8,128)(2,1)} %latent_attention.1.unused.refs_1_), custom_call_target="tpu_custom_call" | custom-call | tf_op jit(solution)/shard_map/fetch_projections/pallas_call | solution.py:132
  18.4 6.4 %collective-permute-done.2.refs_2_.refs_3_ = f32[8,128]{1,0:T(8,128)S(1)} collective-permute-done((f32[8,128]{1,0:T(8,128)S(1)}, f32[8,128]{1,0:T(8,128)S(1)}, u32[]{:S(2)}, u32[]{:S(2)}) %collective-permute-start.2) | collective-permute-done | bytes 4128 | tf_op jit(solution)/shard_map/ppermute | solution.py:543
  24.8 2.0 %collective-permute-done.1.refs_1_.refs_2_ = f32[8,128]{1,0:T(8,128)S(1)} collective-permute-done((f32[8,128]{1,0:T(8,128)S(1)}, f32[8,128]{1,0:T(8,128)S(1)}, u32[]{:S(2)}, u32[]{:S(2)}) %collective-permute-start.1) | collective-permute-done | bytes 4128 | tf_op jit(solution)/shard_map/ppermute | solution.py:543
  27.2 2.6 %project_first.1 = (f32[64,4096]{1,0:T(8,128)S(1)}, bf16[64,4096]{1,0:T(8,128)(2,1)S(1)}, bf16[128,512]{1,0:T(8,128)(2,1)S(1)}) custom-call(s32[1]{0:T(128)} %bitcast.me, bf16[512,512]{1,0:T(8,128)(2,1)S(1)} %bitcast.5, bf16[4,512,128]{2,1,0:T(8,128)(2,1)S(1)} %copy-done, bf16[512,7168]{1,0:T(8,128)(2,1)} %w_hbm.3, ...), custom_call_target="tpu_custom_call" | custom-call | tf_op jit(solution)/shard_map/project_first/pallas_call | solution.py:222
  29.9 1.6 %project_rest.1 = (f32[64,3072]{1,0:T(8,128)S(1)}, bf16[64,3072]{1,0:T(8,128)(2,1)S(1)}) custom-call(bf16[128,512]{1,0:T(8,128)(2,1)S(1)} %get-tuple-element.51.flat, bf16[512,7168]{1,0:T(8,128)(2,1)} %w_hbm.3, bf16[512,1024]{1,0:T(8,128)(2,1)S(1)} %get-tuple-element.46.refs_3_.refs_0_, bf16[512,1024]{1,0:T(8,128)(2,1)S(1)} %get-tuple-element.52.refs_1_), custom_call_target="tpu_custom_call" | custom-call | flops 402653184 | bytes 6291456 | tf_op jit(solution)/shard_map/project_rest/pallas_call | solution.py:231
  32.0 1.3 %collective-permute-done.4.refs_1_ = bf16[64,3072]{1,0:T(8,128)(2,1)S(1)} collective-permute-done((bf16[64,3072]{1,0:T(8,128)(2,1)S(1)}, bf16[64,3072]{1,0:T(8,128)(2,1)S(1)}, u32[]{:S(2)}, u32[]{:S(2)}) %collective-permute-start.4) | collective-permute-done | bytes 393248 | tf_op jit(solution)/shard_map/ppermute | solution.py:543
  39.8 1.4 %collective-permute-start.13 = (bf16[16,4096]{1,0:T(8,128)(2,1)S(1)}, bf16[16,4096]{1,0:T(8,128)(2,1)S(1)}, u32[]{:S(2)}, u32[]{:S(2)}) collective-permute-start(bf16[16,4096]{1,0:T(8,128)(2,1)S(1)} %get-tuple-element.66), channel_id=1, source_target_pairs={{0,6},{1,7},{2,4},{3,5},{4,2},{5,3},{6,0},{7,1},{8,14},{9,15},{10,... | collective-permute-start | bytes 393224 | tf_op jit(solution)/shard_map/ppermute | solution.py:543
  44.8 1.4 %collective-permute-done.12.b_ref = bf16[16,4096]{1,0:T(8,128)(2,1)S(1)} collective-permute-done((bf16[16,4096]{1,0:T(8,128)(2,1)S(1)}, bf16[16,4096]{1,0:T(8,128)(2,1)S(1)}, u32[]{:S(2)}, u32[]{:S(2)}) %collective-permute-start.12) | collective-permute-done | bytes 131104 | tf_op jit(solution)/shard_map/ppermute | solution.py:543
  48.3 2.3 %collective-permute-start.15 = (bf16[8,4096]{1,0:T(8,128)(2,1)S(1)}, bf16[8,4096]{1,0:T(8,128)(2,1)S(1)}, u32[]{:S(2)}, u32[]{:S(2)}) collective-permute-start(bf16[8,4096]{1,0:T(8,128)(2,1)S(1)} %get-tuple-element.69), channel_id=1, source_target_pairs={{0,24},{1,25},{2,26},{3,27},{4,28},{5,29},{6,30},{7,31},{8,16},{9,... | collective-permute-start | bytes 196616 | tf_op jit(solution)/shard_map/ppermute | solution.py:543
  51.0 1.4 %collective-permute-start.9 = (bf16[8,3072]{1,0:T(8,128)(2,1)S(1)}, bf16[8,3072]{1,0:T(8,128)(2,1)S(1)}, u32[]{:S(2)}, u32[]{:S(2)}) collective-permute-start(bf16[8,3072]{1,0:T(8,128)(2,1)S(1)} %get-tuple-element.62), channel_id=1, source_target_pairs={{0,24},{1,25},{2,26},{3,27},{4,28},{5,29},{6,30},{7,31},{8,16},{9,... | collective-permute-start | bytes 147464 | tf_op jit(solution)/shard_map/ppermute | solution.py:543
  53.2 2.6 %fetch_experts.1 = (bf16[7168,128]{1,0:T(8,128)(2,1)S(1)}, bf16[7168,128]{1,0:T(8,128)(2,1)S(1)}, bf16[128,7168]{1,0:T(8,128)(2,1)S(1)}) custom-call(bf16[2,7168,128]{2,1,0:T(8,128)(2,1)} %refs_0_.3, bf16[128,7168]{1,0:T(8,128)(2,1)} %refs_1_.1, f32[8,3072]{1,0:T(8,128)S(1)} %get-tuple-element.60.refs_2_.refs_0_), custom_call_target="tpu_custom_call" | custom-call | tf_op jit(solution)/shard_map/fetch_experts/pallas_call | solution.py:132
  57.3 1.7 %collective-permute-start.19 = (bf16[8,7168]{1,0:T(8,128)(2,1)S(1)}, bf16[8,7168]{1,0:T(8,128)(2,1)S(1)}, u32[]{:S(2)}, u32[]{:S(2)}) collective-permute-start(bf16[8,7168]{1,0:T(8,128)(2,1)S(1)} %get-tuple-element.72.refs_0_), channel_id=1, source_target_pairs={{0,6},{1,7},{2,4},{3,5},{4,2},{5,3},{6,0},{7,1},{8,14},{9,15},{10,... | collective-permute-start | bytes 344072 | tf_op jit(solution)/shard_map/ppermute | solution.py:543
  59.0 1.6 %collective-permute-start.18 = (bf16[8,7168]{1,0:T(8,128)(2,1)S(1)}, bf16[8,7168]{1,0:T(8,128)(2,1)S(1)}, u32[]{:S(2)}, u32[]{:S(2)}) collective-permute-start(bf16[8,7168]{1,0:T(8,128)(2,1)S(1)} %get-tuple-element.72.refs_0_), channel_id=1, source_target_pairs={{0,4},{1,5},{2,6},{3,7},{4,0},{5,1},{6,2},{7,3},{8,12},{9,13},{10,... | collective-permute-start | bytes 344072 | tf_op jit(solution)/shard_map/ppermute | solution.py:543
  60.9 3.0 %collective-permute-done.19.refs_3_ = bf16[8,7168]{1,0:T(8,128)(2,1)S(1)} collective-permute-done((bf16[8,7168]{1,0:T(8,128)(2,1)S(1)}, bf16[8,7168]{1,0:T(8,128)(2,1)S(1)}, u32[]{:S(2)}, u32[]{:S(2)}) %collective-permute-start.19) | collective-permute-done | bytes 114720 | tf_op jit(solution)/shard_map/ppermute | solution.py:543
  67.9 1.7 %collective-permute-done.24.refs_1_ = bf16[32,7168]{1,0:T(8,128)(2,1)S(1)} collective-permute-done((bf16[32,7168]{1,0:T(8,128)(2,1)S(1)}, bf16[32,7168]{1,0:T(8,128)(2,1)S(1)}, u32[]{:S(2)}, u32[]{:S(2)}) %collective-permute-start.24) | collective-permute-done | bytes 458784 | tf_op jit(solution)/shard_map/ppermute | solution.py:543
  73.2 1.8 %collective-permute-done.25.a_ref = bf16[8,7168]{1,0:T(8,128)(2,1)S(1)} collective-permute-done((bf16[8,7168]{1,0:T(8,128)(2,1)S(1)}, bf16[8,7168]{1,0:T(8,128)(2,1)S(1)}, u32[]{:S(2)}, u32[]{:S(2)}) %collective-permute-start.25) | collective-permute-done | bytes 114720 | tf_op jit(solution)/shard_map/ppermute | solution.py:543
  75.0 3.5 %collective-permute-done.26.b_ref = bf16[8,7168]{1,0:T(8,128)(2,1)S(1)} collective-permute-done((bf16[8,7168]{1,0:T(8,128)(2,1)S(1)}, bf16[8,7168]{1,0:T(8,128)(2,1)S(1)}, u32[]{:S(2)}, u32[]{:S(2)}) %collective-permute-start.26) | collective-permute-done | bytes 114720 | tf_op jit(solution)/shard_map/ppermute | solution.py:543
  78.6 1.8 %collective-permute-start.28 = (bf16[2,7168]{1,0:T(2,128)(2,1)S(1)}, bf16[2,7168]{1,0:T(2,128)(2,1)S(1)}, u32[]{:S(2)}, u32[]{:S(2)}) collective-permute-start(bf16[2,7168]{1,0:T(2,128)(2,1)S(1)} %get-tuple-element.84), channel_id=1, source_target_pairs={{0,16},{1,17},{2,18},{3,19},{4,20},{5,21},{6,22},{7,23},{8,24},{9,... | collective-permute-start | bytes 86024 | tf_op jit(solution)/shard_map/ppermute | solution.py:543
  80.5 1.5 %collective-permute-start.29 = (bf16[2,7168]{1,0:T(2,128)(2,1)S(1)}, bf16[2,7168]{1,0:T(2,128)(2,1)S(1)}, u32[]{:S(2)}, u32[]{:S(2)}) collective-permute-start(bf16[2,7168]{1,0:T(2,128)(2,1)S(1)} %get-tuple-element.85), channel_id=1, source_target_pairs={{0,24},{1,25},{2,26},{3,27},{4,28},{5,29},{6,30},{7,31},{8,16},{9,... | collective-permute-start | bytes 86024 | tf_op jit(solution)/shard_map/ppermute | solution.py:543
  82.2 1.4 %collective-permute-done.28.refs_1_ = bf16[2,7168]{1,0:T(2,128)(2,1)S(1)} collective-permute-done((bf16[2,7168]{1,0:T(2,128)(2,1)S(1)}, bf16[2,7168]{1,0:T(2,128)(2,1)S(1)}, u32[]{:S(2)}, u32[]{:S(2)}) %collective-permute-start.28) | collective-permute-done | bytes 28704 | tf_op jit(solution)/shard_map/ppermute | solution.py:543
  83.6 2.5 %collective-permute-done.29.refs_2_ = bf16[2,7168]{1,0:T(2,128)(2,1)S(1)} collective-permute-done((bf16[2,7168]{1,0:T(2,128)(2,1)S(1)}, bf16[2,7168]{1,0:T(2,128)(2,1)S(1)}, u32[]{:S(2)}, u32[]{:S(2)}) %collective-permute-start.29) | collective-permute-done | bytes 28704 | tf_op jit(solution)/shard_map/ppermute | solution.py:543
  (69 shorter events, 26.5 us)
Async XLA Ops:
  4.2 23.0 %all-to-all-start = ((bf16[32,16,512]{2,1,0:T(8,128)(2,1)}), bf16[32,16,512]{2,1,0:T(8,128)(2,1)S(1)}, u32[]{:S(2)}, u32[]{:S(2)}) async-start(bf16[32,16,512]{2,1,0:T(8,128)(2,1)} %bitcast.3), calls=%async_computation | async-start | bytes 1048576 | tf_op jit(solution)/shard_map/all_to_all | solution.py:553
  12.3 12.5 %collective-permute-start.2 = (f32[8,128]{1,0:T(8,128)S(1)}, f32[8,128]{1,0:T(8,128)S(1)}, u32[]{:S(2)}, u32[]{:S(2)}) collective-permute-start(f32[8,128]{1,0:T(8,128)S(1)} %routes.1.refs_0_), channel_id=1, source_target_pairs={{0,24},{1,25},{2,26},{3,27},{4,28},{5,29},{6,30},{7,31},{8,16},{9,... | collective-permute-start | bytes 12296 | tf_op jit(solution)/shard_map/ppermute | solution.py:543
  16.0 10.8 %collective-permute-start.1 = (f32[8,128]{1,0:T(8,128)S(1)}, f32[8,128]{1,0:T(8,128)S(1)}, u32[]{:S(2)}, u32[]{:S(2)}) collective-permute-start(f32[8,128]{1,0:T(8,128)S(1)} %routes.1.refs_0_), channel_id=1, source_target_pairs={{0,16},{1,17},{2,18},{3,19},{4,20},{5,21},{6,22},{7,23},{8,24},{9,... | collective-permute-start | bytes 12296 | tf_op jit(solution)/shard_map/ppermute | solution.py:543
  16.0 10.8 %collective-permute-start = (f32[8,128]{1,0:T(8,128)S(1)}, f32[8,128]{1,0:T(8,128)S(1)}, u32[]{:S(2)}, u32[]{:S(2)}) collective-permute-start(f32[8,128]{1,0:T(8,128)S(1)} %routes.1.refs_0_), channel_id=1, source_target_pairs={{0,8},{1,9},{2,10},{3,11},{4,12},{5,13},{6,14},{7,15},{8,0},{9,1},... | collective-permute-start | bytes 12296 | tf_op jit(solution)/shard_map/ppermute | solution.py:543
  29.8 7.2 %collective-permute-start.3 = (bf16[64,4096]{1,0:T(8,128)(2,1)S(1)}, bf16[64,4096]{1,0:T(8,128)(2,1)S(1)}, u32[]{:S(2)}, u32[]{:S(2)}) collective-permute-start(bf16[64,4096]{1,0:T(8,128)(2,1)S(1)} %get-tuple-element.48), channel_id=1, source_target_pairs={{0,1},{1,0},{2,3},{3,2},{4,5},{5,4},{6,7},{7,6},{8,9},{9,8},{10,11... | collective-permute-start | bytes 1572872 | tf_op jit(solution)/shard_map/ppermute | solution.py:543
  33.5 6.3 %collective-permute-start.5 = (bf16[16,3072]{1,0:T(8,128)(2,1)S(1)}, bf16[16,3072]{1,0:T(8,128)(2,1)S(1)}, u32[]{:S(2)}, u32[]{:S(2)}) collective-permute-start(bf16[16,3072]{1,0:T(8,128)(2,1)S(1)} %get-tuple-element.56), channel_id=1, source_target_pairs={{0,2},{1,3},{2,0},{3,1},{4,6},{5,7},{6,4},{7,5},{8,10},{9,11},{10,... | collective-permute-start | bytes 294920 | tf_op jit(solution)/shard_map/ppermute | solution.py:543
  34.8 7.5 %collective-permute-start.6 = (bf16[16,3072]{1,0:T(8,128)(2,1)S(1)}, bf16[16,3072]{1,0:T(8,128)(2,1)S(1)}, u32[]{:S(2)}, u32[]{:S(2)}) collective-permute-start(bf16[16,3072]{1,0:T(8,128)(2,1)S(1)} %get-tuple-element.57), channel_id=1, source_target_pairs={{0,4},{1,5},{2,6},{3,7},{4,0},{5,1},{6,2},{7,3},{8,12},{9,13},{10,... | collective-permute-start | bytes 294920 | tf_op jit(solution)/shard_map/ppermute | solution.py:543
  36.2 6.6 %collective-permute-start.7 = (bf16[16,3072]{1,0:T(8,128)(2,1)S(1)}, bf16[16,3072]{1,0:T(8,128)(2,1)S(1)}, u32[]{:S(2)}, u32[]{:S(2)}) collective-permute-start(bf16[16,3072]{1,0:T(8,128)(2,1)S(1)} %get-tuple-element.58), channel_id=1, source_target_pairs={{0,6},{1,7},{2,4},{3,5},{4,2},{5,3},{6,0},{7,1},{8,14},{9,15},{10,... | collective-permute-start | bytes 294920 | tf_op jit(solution)/shard_map/ppermute | solution.py:543
  37.1 7.7 %collective-permute-start.11 = (bf16[16,4096]{1,0:T(8,128)(2,1)S(1)}, bf16[16,4096]{1,0:T(8,128)(2,1)S(1)}, u32[]{:S(2)}, u32[]{:S(2)}) collective-permute-start(bf16[16,4096]{1,0:T(8,128)(2,1)S(1)} %get-tuple-element.64), channel_id=1, source_target_pairs={{0,2},{1,3},{2,0},{3,1},{4,6},{5,7},{6,4},{7,5},{8,10},{9,11},{10,... | collective-permute-start | bytes 393224 | tf_op jit(solution)/shard_map/ppermute | solution.py:543
  38.5 7.7 %collective-permute-start.12 = (bf16[16,4096]{1,0:T(8,128)(2,1)S(1)}, bf16[16,4096]{1,0:T(8,128)(2,1)S(1)}, u32[]{:S(2)}, u32[]{:S(2)}) collective-permute-start(bf16[16,4096]{1,0:T(8,128)(2,1)S(1)} %get-tuple-element.65), channel_id=1, source_target_pairs={{0,4},{1,5},{2,6},{3,7},{4,0},{5,1},{6,2},{7,3},{8,12},{9,13},{10,... | collective-permute-start | bytes 393224 | tf_op jit(solution)/shard_map/ppermute | solution.py:543
  39.8 7.4 %collective-permute-start.13 = (bf16[16,4096]{1,0:T(8,128)(2,1)S(1)}, bf16[16,4096]{1,0:T(8,128)(2,1)S(1)}, u32[]{:S(2)}, u32[]{:S(2)}) collective-permute-start(bf16[16,4096]{1,0:T(8,128)(2,1)S(1)} %get-tuple-element.66), channel_id=1, source_target_pairs={{0,6},{1,7},{2,4},{3,5},{4,2},{5,3},{6,0},{7,1},{8,14},{9,15},{10,... | collective-permute-start | bytes 393224 | tf_op jit(solution)/shard_map/ppermute | solution.py:543
  43.0 9.5 %collective-permute-start.8 = (bf16[8,3072]{1,0:T(8,128)(2,1)S(1)}, bf16[8,3072]{1,0:T(8,128)(2,1)S(1)}, u32[]{:S(2)}, u32[]{:S(2)}) collective-permute-start(bf16[8,3072]{1,0:T(8,128)(2,1)S(1)} %get-tuple-element.61), channel_id=1, source_target_pairs={{0,16},{1,17},{2,18},{3,19},{4,20},{5,21},{6,22},{7,23},{8,24},{9,... | collective-permute-start | bytes 147464 | tf_op jit(solution)/shard_map/ppermute | solution.py:543
  47.5 9.6 %collective-permute-start.14 = (bf16[8,4096]{1,0:T(8,128)(2,1)S(1)}, bf16[8,4096]{1,0:T(8,128)(2,1)S(1)}, u32[]{:S(2)}, u32[]{:S(2)}) collective-permute-start(bf16[8,4096]{1,0:T(8,128)(2,1)S(1)} %get-tuple-element.68), channel_id=1, source_target_pairs={{0,16},{1,17},{2,18},{3,19},{4,20},{5,21},{6,22},{7,23},{8,24},{9,... | collective-permute-start | bytes 196616 | tf_op jit(solution)/shard_map/ppermute | solution.py:543
  48.3 8.8 %collective-permute-start.15 = (bf16[8,4096]{1,0:T(8,128)(2,1)S(1)}, bf16[8,4096]{1,0:T(8,128)(2,1)S(1)}, u32[]{:S(2)}, u32[]{:S(2)}) collective-permute-start(bf16[8,4096]{1,0:T(8,128)(2,1)S(1)} %get-tuple-element.69), channel_id=1, source_target_pairs={{0,24},{1,25},{2,26},{3,27},{4,28},{5,29},{6,30},{7,31},{8,16},{9,... | collective-permute-start | bytes 196616 | tf_op jit(solution)/shard_map/ppermute | solution.py:543
  50.6 6.5 %collective-permute-start.16 = (bf16[8,4096]{1,0:T(8,128)(2,1)S(1)}, bf16[8,4096]{1,0:T(8,128)(2,1)S(1)}, u32[]{:S(2)}, u32[]{:S(2)}) collective-permute-start(bf16[8,4096]{1,0:T(8,128)(2,1)S(1)} %get-tuple-element.70), channel_id=1, source_target_pairs={{0,8},{1,9},{2,10},{3,11},{4,12},{5,13},{6,14},{7,15},{8,0},{9,1},... | collective-permute-start | bytes 196616 | tf_op jit(solution)/shard_map/ppermute | solution.py:543
  51.0 6.0 %collective-permute-start.9 = (bf16[8,3072]{1,0:T(8,128)(2,1)S(1)}, bf16[8,3072]{1,0:T(8,128)(2,1)S(1)}, u32[]{:S(2)}, u32[]{:S(2)}) collective-permute-start(bf16[8,3072]{1,0:T(8,128)(2,1)S(1)} %get-tuple-element.62), channel_id=1, source_target_pairs={{0,24},{1,25},{2,26},{3,27},{4,28},{5,29},{6,30},{7,31},{8,16},{9,... | collective-permute-start | bytes 147464 | tf_op jit(solution)/shard_map/ppermute | solution.py:543
  57.3 6.6 %collective-permute-start.19 = (bf16[8,7168]{1,0:T(8,128)(2,1)S(1)}, bf16[8,7168]{1,0:T(8,128)(2,1)S(1)}, u32[]{:S(2)}, u32[]{:S(2)}) collective-permute-start(bf16[8,7168]{1,0:T(8,128)(2,1)S(1)} %get-tuple-element.72.refs_0_), channel_id=1, source_target_pairs={{0,6},{1,7},{2,4},{3,5},{4,2},{5,3},{6,0},{7,1},{8,14},{9,15},{10,... | collective-permute-start | bytes 344072 | tf_op jit(solution)/shard_map/ppermute | solution.py:543
  59.0 5.6 %collective-permute-start.18 = (bf16[8,7168]{1,0:T(8,128)(2,1)S(1)}, bf16[8,7168]{1,0:T(8,128)(2,1)S(1)}, u32[]{:S(2)}, u32[]{:S(2)}) collective-permute-start(bf16[8,7168]{1,0:T(8,128)(2,1)S(1)} %get-tuple-element.72.refs_0_), channel_id=1, source_target_pairs={{0,4},{1,5},{2,6},{3,7},{4,0},{5,1},{6,2},{7,3},{8,12},{9,13},{10,... | collective-permute-start | bytes 344072 | tf_op jit(solution)/shard_map/ppermute | solution.py:543
  60.5 4.8 %collective-permute-start.17 = (bf16[8,7168]{1,0:T(8,128)(2,1)S(1)}, bf16[8,7168]{1,0:T(8,128)(2,1)S(1)}, u32[]{:S(2)}, u32[]{:S(2)}) collective-permute-start(bf16[8,7168]{1,0:T(8,128)(2,1)S(1)} %get-tuple-element.72.refs_0_), channel_id=1, source_target_pairs={{0,2},{1,3},{2,0},{3,1},{4,6},{5,7},{6,4},{7,5},{8,10},{9,11},{10,... | collective-permute-start | bytes 344072 | tf_op jit(solution)/shard_map/ppermute | solution.py:543
  69.7 5.4 %collective-permute-start.25 = (bf16[8,7168]{1,0:T(8,128)(2,1)S(1)}, bf16[8,7168]{1,0:T(8,128)(2,1)S(1)}, u32[]{:S(2)}, u32[]{:S(2)}) collective-permute-start(bf16[8,7168]{1,0:T(8,128)(2,1)S(1)} %get-tuple-element.78), channel_id=1, source_target_pairs={{0,2},{1,3},{2,0},{3,1},{4,6},{5,7},{6,4},{7,5},{8,10},{9,11},{10,... | collective-permute-start | bytes 344072 | tf_op jit(solution)/shard_map/ppermute | solution.py:543
  70.9 7.6 %collective-permute-start.26 = (bf16[8,7168]{1,0:T(8,128)(2,1)S(1)}, bf16[8,7168]{1,0:T(8,128)(2,1)S(1)}, u32[]{:S(2)}, u32[]{:S(2)}) collective-permute-start(bf16[8,7168]{1,0:T(8,128)(2,1)S(1)} %get-tuple-element.79), channel_id=1, source_target_pairs={{0,4},{1,5},{2,6},{3,7},{4,0},{5,1},{6,2},{7,3},{8,12},{9,13},{10,... | collective-permute-start | bytes 344072 | tf_op jit(solution)/shard_map/ppermute | solution.py:543
  72.0 6.5 %collective-permute-start.27 = (bf16[8,7168]{1,0:T(8,128)(2,1)S(1)}, bf16[8,7168]{1,0:T(8,128)(2,1)S(1)}, u32[]{:S(2)}, u32[]{:S(2)}) collective-permute-start(bf16[8,7168]{1,0:T(8,128)(2,1)S(1)} %get-tuple-element.80), channel_id=1, source_target_pairs={{0,6},{1,7},{2,4},{3,5},{4,2},{5,3},{6,0},{7,1},{8,14},{9,15},{10,... | collective-permute-start | bytes 344072 | tf_op jit(solution)/shard_map/ppermute | solution.py:543
  78.6 4.9 %collective-permute-start.28 = (bf16[2,7168]{1,0:T(2,128)(2,1)S(1)}, bf16[2,7168]{1,0:T(2,128)(2,1)S(1)}, u32[]{:S(2)}, u32[]{:S(2)}) collective-permute-start(bf16[2,7168]{1,0:T(2,128)(2,1)S(1)} %get-tuple-element.84), channel_id=1, source_target_pairs={{0,16},{1,17},{2,18},{3,19},{4,20},{5,21},{6,22},{7,23},{8,24},{9,... | collective-permute-start | bytes 86024 | tf_op jit(solution)/shard_map/ppermute | solution.py:543
  80.5 5.7 %collective-permute-start.29 = (bf16[2,7168]{1,0:T(2,128)(2,1)S(1)}, bf16[2,7168]{1,0:T(2,128)(2,1)S(1)}, u32[]{:S(2)}, u32[]{:S(2)}) collective-permute-start(bf16[2,7168]{1,0:T(2,128)(2,1)S(1)} %get-tuple-element.85), channel_id=1, source_target_pairs={{0,24},{1,25},{2,26},{3,27},{4,28},{5,29},{6,30},{7,31},{8,16},{9,... | collective-permute-start | bytes 86024 | tf_op jit(solution)/shard_map/ppermute | solution.py:543
  (13 other events, 85.8 us)

commit v10 on v9

--- a/solution.py
+++ b/solution.py
@@ -245,9 +245,8 @@
     return (own_a, own_b), (other_a, other_b)
 
 
-def add_kernel(parts, tile, *refs):
+def add_kernel(parts, ranges, tile, *refs):
     outs = refs[-parts:]
-    ranges = (len(refs) - parts) // 2
     size = outs[0].shape[0]
     first = 0
     for own_ref, other_ref in zip(refs[:ranges], refs[ranges : 2 * ranges]):
@@ -261,18 +260,18 @@
         first += own_ref.shape[1]
 
 
-def add_and_cut(own, received, parts, name):
+def add_and_cut(own, received, parts, name, after=()):
     size = own[0].shape[0] // parts
     features = sum(x.shape[1] for x in own)
     vec = pl.BlockSpec(memory_space=pltpu.VMEM)
     return pl.pallas_call(
-        functools.partial(add_kernel, parts, 512),
-        in_specs=[vec] * (2 * len(own)),
+        functools.partial(add_kernel, parts, len(own), 512),
+        in_specs=[vec] * (2 * len(own)) + [pl.BlockSpec(memory_space=pl.ANY)] * len(after),
         out_specs=[vec] * parts,
         out_shape=[sds((size, features), F32)] + [sds((size, features), BF16)] * (parts - 1),
         compiler_params=params(),
         name=name,
-    )(*own, *received)
+    )(*own, *received, *after)
 
 
 def routes_kernel(ids, weights, unused, out_ref):
@@ -556,12 +555,11 @@
     homes = over_planes([mine] * (planes - 1))
     homes = [mine] + homes[-1:] + homes[:-1]
     own, other = project(me, by_heads, value_up, out_proj, early, planes, rows, homes[1:] + early[:1])
+    pick, weight, merge = tables(me, route_ids, homes, cap, other[1])
     parts = []
     for n in range(2):
-        part, *out = add_and_cut(own[n : n + 1], [swap(other[n], 1)], 4, "add_core")
+        part, *out = add_and_cut(own[n : n + 1], [swap(other[n], 1)], 4, "add_core", [pick])
         parts.append((part, over_chips(out)))
-    own = parts[0][0]
-    pick, weight, merge = tables(me, route_ids, homes, cap, own)
     sums, first = [], 0
     for own, received in parts:
         own, *out = add_and_pick(own, received, hidden_in, pick, planes, first)

time: 87.3 us -> 87.3 us (level)
  no operation moved by 1% of the time
where the time goes in v10:
time: 87.3 us; the launch traced here: 87.1 us
  starting transfers between devices  37.2 us (43%)
  waiting for transfers between devices  32 us (37%)
  Pallas kernels  17.4 us (20%)
    ppermute x31, waiting for transfers between devices, swap(): return lax.ppermute(x, 'dp', [(i, i ^ mask) for i in range(devices)])  31.7 us
    ppermute x31, starting transfers between devices, swap(): return lax.ppermute(x, 'dp', [(i, i ^ mask) for i in range(devices)])  29.9 us
    all_to_all x1, starting transfers between devices, body(): lax.all_to_all(latents, 'dp', split_axis=0, concat_axis=0, tiled=True)  7.3 us
    pallas_call x2, Pallas kernels, fetch(): pl.pallas_call(functools.partial(fetch_kernel, parts), in_specs=[pl.Block...  4.26 us
    pallas_call x1, Pallas kernels, attention(): pl.pallas_call(attention_kernel, in_specs=[hbm, hbm, hbm], out_specs=pl.B...  4.18 us
    pallas_call x1, Pallas kernels, project(): pl.pallas_call(functools.partial(project_first_kernel, planes, rows), in_...  2.55 us
  transfers between devices with their start and end apart: 32, of which 19 were waited for; matrix products, arithmetic and copies ran while one was open for 0% of the time, Pallas kernels for 10%

profile of v10, /device:TPU:0, one launch (start us, length us, event | category | flops | bytes accessed | tf_op | source)
XLA Modules:
  0.0 87.1 jit_solution(10841163757359112986)
XLA Ops:
  0.0 4.2 %latent_attention.1.unused.refs_1_ = bf16[512,512]{1,0:T(8,128)(2,1)} custom-call(s32[4]{0:T(128)} %lengths_hbm.1, bf16[4,576,128]{2,1,0:T(8,128)(2,1)} %bitcast.7, bf16[4,576,512]{2,1,0:T(8,128)(2,1)} %bitcast.6), custom_call_target="tpu_custom_call" | custom-call | tf_op jit(solution)/shard_map/latent_attention/pallas_call | solution.py:86
  4.2 7.3 %all-to-all-start = ((bf16[32,16,512]{2,1,0:T(8,128)(2,1)}), bf16[32,16,512]{2,1,0:T(8,128)(2,1)S(1)}, u32[]{:S(2)}, u32[]{:S(2)}) async-start(bf16[32,16,512]{2,1,0:T(8,128)(2,1)} %bitcast.3), calls=%async_computation | async-start | bytes 1048576 | tf_op jit(solution)/shard_map/all_to_all | solution.py:552
  12.3 3.7 %collective-permute-start.2 = (f32[8,128]{1,0:T(8,128)S(1)}, f32[8,128]{1,0:T(8,128)S(1)}, u32[]{:S(2)}, u32[]{:S(2)}) collective-permute-start(f32[8,128]{1,0:T(8,128)S(1)} %routes.1.refs_0_), channel_id=1, source_target_pairs={{0,24},{1,25},{2,26},{3,27},{4,28},{5,29},{6,30},{7,31},{8,16},{9,... | collective-permute-start | bytes 12296 | tf_op jit(solution)/shard_map/ppermute | solution.py:542
  16.8 1.6 %fetch_projections.1 = (bf16[512,1024]{1,0:T(8,128)(2,1)S(1)}, bf16[512,1024]{1,0:T(8,128)(2,1)S(1)}) custom-call(bf16[512,7168]{1,0:T(8,128)(2,1)} %w_hbm.3, bf16[512,512]{1,0:T(8,128)(2,1)} %latent_attention.1.unused.refs_1_), custom_call_target="tpu_custom_call" | custom-call | tf_op jit(solution)/shard_map/fetch_projections/pallas_call | solution.py:132
  18.4 6.4 %collective-permute-done.2.refs_2_.refs_3_ = f32[8,128]{1,0:T(8,128)S(1)} collective-permute-done((f32[8,128]{1,0:T(8,128)S(1)}, f32[8,128]{1,0:T(8,128)S(1)}, u32[]{:S(2)}, u32[]{:S(2)}) %collective-permute-start.2) | collective-permute-done | bytes 4128 | tf_op jit(solution)/shard_map/ppermute | solution.py:542
  24.8 2.0 %collective-permute-done.1.refs_1_.refs_2_ = f32[8,128]{1,0:T(8,128)S(1)} collective-permute-done((f32[8,128]{1,0:T(8,128)S(1)}, f32[8,128]{1,0:T(8,128)S(1)}, u32[]{:S(2)}, u32[]{:S(2)}) %collective-permute-start.1) | collective-permute-done | bytes 4128 | tf_op jit(solution)/shard_map/ppermute | solution.py:542
  27.2 2.6 %project_first.1 = (f32[64,4096]{1,0:T(8,128)S(1)}, bf16[64,4096]{1,0:T(8,128)(2,1)S(1)}, bf16[128,512]{1,0:T(8,128)(2,1)S(1)}) custom-call(s32[1]{0:T(128)} %bitcast.me, bf16[512,512]{1,0:T(8,128)(2,1)S(1)} %bitcast.5, bf16[4,512,128]{2,1,0:T(8,128)(2,1)S(1)} %copy-done, bf16[512,7168]{1,0:T(8,128)(2,1)} %w_hbm.3, ...), custom_call_target="tpu_custom_call" | custom-call | tf_op jit(solution)/shard_map/project_first/pallas_call | solution.py:222
  29.9 1.6 %project_rest.1 = (f32[64,3072]{1,0:T(8,128)S(1)}, bf16[64,3072]{1,0:T(8,128)(2,1)S(1)}) custom-call(bf16[128,512]{1,0:T(8,128)(2,1)S(1)} %get-tuple-element.47.flat, bf16[512,7168]{1,0:T(8,128)(2,1)} %w_hbm.3, bf16[512,1024]{1,0:T(8,128)(2,1)S(1)} %get-tuple-element.46.refs_3_.refs_0_, bf16[512,1024]{1,0:T(8,128)(2,1)S(1)} %get-tuple-element.48.refs_1_), custom_call_target="tpu_custom_call" | custom-call | flops 402653184 | bytes 6291456 | tf_op jit(solution)/shard_map/project_rest/pallas_call | solution.py:231
  39.8 1.4 %collective-permute-start.13 = (bf16[16,4096]{1,0:T(8,128)(2,1)S(1)}, bf16[16,4096]{1,0:T(8,128)(2,1)S(1)}, u32[]{:S(2)}, u32[]{:S(2)}) collective-permute-start(bf16[16,4096]{1,0:T(8,128)(2,1)S(1)} %get-tuple-element.66), channel_id=1, source_target_pairs={{0,6},{1,7},{2,4},{3,5},{4,2},{5,3},{6,0},{7,1},{8,14},{9,15},{10,... | collective-permute-start | bytes 393224 | tf_op jit(solution)/shard_map/ppermute | solution.py:542
  41.2 1.5 %collective-permute-done.6.c_ref = bf16[16,3072]{1,0:T(8,128)(2,1)S(1)} collective-permute-done((bf16[16,3072]{1,0:T(8,128)(2,1)S(1)}, bf16[16,3072]{1,0:T(8,128)(2,1)S(1)}, u32[]{:S(2)}, u32[]{:S(2)}) %collective-permute-start.6) | collective-permute-done | bytes 98336 | tf_op jit(solution)/shard_map/ppermute | solution.py:542
  44.8 1.4 %collective-permute-done.12.b_ref = bf16[16,4096]{1,0:T(8,128)(2,1)S(1)} collective-permute-done((bf16[16,4096]{1,0:T(8,128)(2,1)S(1)}, bf16[16,4096]{1,0:T(8,128)(2,1)S(1)}, u32[]{:S(2)}, u32[]{:S(2)}) %collective-permute-start.12) | collective-permute-done | bytes 131104 | tf_op jit(solution)/shard_map/ppermute | solution.py:542
  48.3 2.3 %collective-permute-start.15 = (bf16[8,4096]{1,0:T(8,128)(2,1)S(1)}, bf16[8,4096]{1,0:T(8,128)(2,1)S(1)}, u32[]{:S(2)}, u32[]{:S(2)}) collective-permute-start(bf16[8,4096]{1,0:T(8,128)(2,1)S(1)} %get-tuple-element.69), channel_id=1, source_target_pairs={{0,24},{1,25},{2,26},{3,27},{4,28},{5,29},{6,30},{7,31},{8,16},{9,... | collective-permute-start | bytes 196616 | tf_op jit(solution)/shard_map/ppermute | solution.py:542
  51.0 1.4 %collective-permute-start.8 = (bf16[8,3072]{1,0:T(8,128)(2,1)S(1)}, bf16[8,3072]{1,0:T(8,128)(2,1)S(1)}, u32[]{:S(2)}, u32[]{:S(2)}) collective-permute-start(bf16[8,3072]{1,0:T(8,128)(2,1)S(1)} %get-tuple-element.59), channel_id=1, source_target_pairs={{0,24},{1,25},{2,26},{3,27},{4,28},{5,29},{6,30},{7,31},{8,16},{9,... | collective-permute-start | bytes 147464 | tf_op jit(solution)/shard_map/ppermute | solution.py:542
  53.2 2.6 %fetch_experts.1 = (bf16[7168,128]{1,0:T(8,128)(2,1)S(1)}, bf16[7168,128]{1,0:T(8,128)(2,1)S(1)}, bf16[128,7168]{1,0:T(8,128)(2,1)S(1)}) custom-call(bf16[2,7168,128]{2,1,0:T(8,128)(2,1)} %refs_0_.3, bf16[128,7168]{1,0:T(8,128)(2,1)} %refs_1_.1, f32[8,3072]{1,0:T(8,128)S(1)} %get-tuple-element.57.refs_2_.refs_0_), custom_call_target="tpu_custom_call" | custom-call | tf_op jit(solution)/shard_map/fetch_experts/pallas_call | solution.py:132
  57.3 1.7 %collective-permute-start.19 = (bf16[8,7168]{1,0:T(8,128)(2,1)S(1)}, bf16[8,7168]{1,0:T(8,128)(2,1)S(1)}, u32[]{:S(2)}, u32[]{:S(2)}) collective-permute-start(bf16[8,7168]{1,0:T(8,128)(2,1)S(1)} %get-tuple-element.72.refs_0_), channel_id=1, source_target_pairs={{0,6},{1,7},{2,4},{3,5},{4,2},{5,3},{6,0},{7,1},{8,14},{9,15},{10,... | collective-permute-start | bytes 344072 | tf_op jit(solution)/shard_map/ppermute | solution.py:542
  59.0 1.6 %collective-permute-start.18 = (bf16[8,7168]{1,0:T(8,128)(2,1)S(1)}, bf16[8,7168]{1,0:T(8,128)(2,1)S(1)}, u32[]{:S(2)}, u32[]{:S(2)}) collective-permute-start(bf16[8,7168]{1,0:T(8,128)(2,1)S(1)} %get-tuple-element.72.refs_0_), channel_id=1, source_target_pairs={{0,4},{1,5},{2,6},{3,7},{4,0},{5,1},{6,2},{7,3},{8,12},{9,13},{10,... | collective-permute-start | bytes 344072 | tf_op jit(solution)/shard_map/ppermute | solution.py:542
  60.9 3.0 %collective-permute-done.19.refs_3_ = bf16[8,7168]{1,0:T(8,128)(2,1)S(1)} collective-permute-done((bf16[8,7168]{1,0:T(8,128)(2,1)S(1)}, bf16[8,7168]{1,0:T(8,128)(2,1)S(1)}, u32[]{:S(2)}, u32[]{:S(2)}) %collective-permute-start.19) | collective-permute-done | bytes 114720 | tf_op jit(solution)/shard_map/ppermute | solution.py:542
  67.9 1.7 %collective-permute-done.24.refs_1_ = bf16[32,7168]{1,0:T(8,128)(2,1)S(1)} collective-permute-done((bf16[32,7168]{1,0:T(8,128)(2,1)S(1)}, bf16[32,7168]{1,0:T(8,128)(2,1)S(1)}, u32[]{:S(2)}, u32[]{:S(2)}) %collective-permute-start.24) | collective-permute-done | bytes 458784 | tf_op jit(solution)/shard_map/ppermute | solution.py:542
  73.2 1.8 %collective-permute-done.25.a_ref = bf16[8,7168]{1,0:T(8,128)(2,1)S(1)} collective-permute-done((bf16[8,7168]{1,0:T(8,128)(2,1)S(1)}, bf16[8,7168]{1,0:T(8,128)(2,1)S(1)}, u32[]{:S(2)}, u32[]{:S(2)}) %collective-permute-start.25) | collective-permute-done | bytes 114720 | tf_op jit(solution)/shard_map/ppermute | solution.py:542
  75.0 3.5 %collective-permute-done.26.b_ref = bf16[8,7168]{1,0:T(8,128)(2,1)S(1)} collective-permute-done((bf16[8,7168]{1,0:T(8,128)(2,1)S(1)}, bf16[8,7168]{1,0:T(8,128)(2,1)S(1)}, u32[]{:S(2)}, u32[]{:S(2)}) %collective-permute-start.26) | collective-permute-done | bytes 114720 | tf_op jit(solution)/shard_map/ppermute | solution.py:542
  78.6 1.8 %collective-permute-start.28 = (bf16[2,7168]{1,0:T(2,128)(2,1)S(1)}, bf16[2,7168]{1,0:T(2,128)(2,1)S(1)}, u32[]{:S(2)}, u32[]{:S(2)}) collective-permute-start(bf16[2,7168]{1,0:T(2,128)(2,1)S(1)} %get-tuple-element.84), channel_id=1, source_target_pairs={{0,16},{1,17},{2,18},{3,19},{4,20},{5,21},{6,22},{7,23},{8,24},{9,... | collective-permute-start | bytes 86024 | tf_op jit(solution)/shard_map/ppermute | solution.py:542
  80.5 1.5 %collective-permute-start.29 = (bf16[2,7168]{1,0:T(2,128)(2,1)S(1)}, bf16[2,7168]{1,0:T(2,128)(2,1)S(1)}, u32[]{:S(2)}, u32[]{:S(2)}) collective-permute-start(bf16[2,7168]{1,0:T(2,128)(2,1)S(1)} %get-tuple-element.85), channel_id=1, source_target_pairs={{0,24},{1,25},{2,26},{3,27},{4,28},{5,29},{6,30},{7,31},{8,16},{9,... | collective-permute-start | bytes 86024 | tf_op jit(solution)/shard_map/ppermute | solution.py:542
  82.2 1.4 %collective-permute-done.28.refs_1_ = bf16[2,7168]{1,0:T(2,128)(2,1)S(1)} collective-permute-done((bf16[2,7168]{1,0:T(2,128)(2,1)S(1)}, bf16[2,7168]{1,0:T(2,128)(2,1)S(1)}, u32[]{:S(2)}, u32[]{:S(2)}) %collective-permute-start.28) | collective-permute-done | bytes 28704 | tf_op jit(solution)/shard_map/ppermute | solution.py:542
  83.6 2.5 %collective-permute-done.29.refs_2_ = bf16[2,7168]{1,0:T(2,128)(2,1)S(1)} collective-permute-done((bf16[2,7168]{1,0:T(2,128)(2,1)S(1)}, bf16[2,7168]{1,0:T(2,128)(2,1)S(1)}, u32[]{:S(2)}, u32[]{:S(2)}) %collective-permute-start.29) | collective-permute-done | bytes 28704 | tf_op jit(solution)/shard_map/ppermute | solution.py:542
  (69 shorter events, 26.3 us)
Async XLA Ops:
  4.2 23.0 %all-to-all-start = ((bf16[32,16,512]{2,1,0:T(8,128)(2,1)}), bf16[32,16,512]{2,1,0:T(8,128)(2,1)S(1)}, u32[]{:S(2)}, u32[]{:S(2)}) async-start(bf16[32,16,512]{2,1,0:T(8,128)(2,1)} %bitcast.3), calls=%async_computation | async-start | bytes 1048576 | tf_op jit(solution)/shard_map/all_to_all | solution.py:552
  12.3 12.5 %collective-permute-start.2 = (f32[8,128]{1,0:T(8,128)S(1)}, f32[8,128]{1,0:T(8,128)S(1)}, u32[]{:S(2)}, u32[]{:S(2)}) collective-permute-start(f32[8,128]{1,0:T(8,128)S(1)} %routes.1.refs_0_), channel_id=1, source_target_pairs={{0,24},{1,25},{2,26},{3,27},{4,28},{5,29},{6,30},{7,31},{8,16},{9,... | collective-permute-start | bytes 12296 | tf_op jit(solution)/shard_map/ppermute | solution.py:542
  16.0 10.8 %collective-permute-start.1 = (f32[8,128]{1,0:T(8,128)S(1)}, f32[8,128]{1,0:T(8,128)S(1)}, u32[]{:S(2)}, u32[]{:S(2)}) collective-permute-start(f32[8,128]{1,0:T(8,128)S(1)} %routes.1.refs_0_), channel_id=1, source_target_pairs={{0,16},{1,17},{2,18},{3,19},{4,20},{5,21},{6,22},{7,23},{8,24},{9,... | collective-permute-start | bytes 12296 | tf_op jit(solution)/shard_map/ppermute | solution.py:542
  16.0 10.8 %collective-permute-start = (f32[8,128]{1,0:T(8,128)S(1)}, f32[8,128]{1,0:T(8,128)S(1)}, u32[]{:S(2)}, u32[]{:S(2)}) collective-permute-start(f32[8,128]{1,0:T(8,128)S(1)} %routes.1.refs_0_), channel_id=1, source_target_pairs={{0,8},{1,9},{2,10},{3,11},{4,12},{5,13},{6,14},{7,15},{8,0},{9,1},... | collective-permute-start | bytes 12296 | tf_op jit(solution)/shard_map/ppermute | solution.py:542
  29.8 7.3 %collective-permute-start.10 = (bf16[64,4096]{1,0:T(8,128)(2,1)S(1)}, bf16[64,4096]{1,0:T(8,128)(2,1)S(1)}, u32[]{:S(2)}, u32[]{:S(2)}) collective-permute-start(bf16[64,4096]{1,0:T(8,128)(2,1)S(1)} %get-tuple-element.62), channel_id=1, source_target_pairs={{0,1},{1,0},{2,3},{3,2},{4,5},{5,4},{6,7},{7,6},{8,9},{9,8},{10,11... | collective-permute-start | bytes 1572872 | tf_op jit(solution)/shard_map/ppermute | solution.py:542
  33.5 6.3 %collective-permute-start.4 = (bf16[16,3072]{1,0:T(8,128)(2,1)S(1)}, bf16[16,3072]{1,0:T(8,128)(2,1)S(1)}, u32[]{:S(2)}, u32[]{:S(2)}) collective-permute-start(bf16[16,3072]{1,0:T(8,128)(2,1)S(1)} %get-tuple-element.54), channel_id=1, source_target_pairs={{0,2},{1,3},{2,0},{3,1},{4,6},{5,7},{6,4},{7,5},{8,10},{9,11},{10,... | collective-permute-start | bytes 294920 | tf_op jit(solution)/shard_map/ppermute | solution.py:542
  34.8 6.4 %collective-permute-start.5 = (bf16[16,3072]{1,0:T(8,128)(2,1)S(1)}, bf16[16,3072]{1,0:T(8,128)(2,1)S(1)}, u32[]{:S(2)}, u32[]{:S(2)}) collective-permute-start(bf16[16,3072]{1,0:T(8,128)(2,1)S(1)} %get-tuple-element.55), channel_id=1, source_target_pairs={{0,4},{1,5},{2,6},{3,7},{4,0},{5,1},{6,2},{7,3},{8,12},{9,13},{10,... | collective-permute-start | bytes 294920 | tf_op jit(solution)/shard_map/ppermute | solution.py:542
  36.2 6.6 %collective-permute-start.6 = (bf16[16,3072]{1,0:T(8,128)(2,1)S(1)}, bf16[16,3072]{1,0:T(8,128)(2,1)S(1)}, u32[]{:S(2)}, u32[]{:S(2)}) collective-permute-start(bf16[16,3072]{1,0:T(8,128)(2,1)S(1)} %get-tuple-element.56), channel_id=1, source_target_pairs={{0,6},{1,7},{2,4},{3,5},{4,2},{5,3},{6,0},{7,1},{8,14},{9,15},{10,... | collective-permute-start | bytes 294920 | tf_op jit(solution)/shard_map/ppermute | solution.py:542
  37.1 7.7 %collective-permute-start.11 = (bf16[16,4096]{1,0:T(8,128)(2,1)S(1)}, bf16[16,4096]{1,0:T(8,128)(2,1)S(1)}, u32[]{:S(2)}, u32[]{:S(2)}) collective-permute-start(bf16[16,4096]{1,0:T(8,128)(2,1)S(1)} %get-tuple-element.64), channel_id=1, source_target_pairs={{0,2},{1,3},{2,0},{3,1},{4,6},{5,7},{6,4},{7,5},{8,10},{9,11},{10,... | collective-permute-start | bytes 393224 | tf_op jit(solution)/shard_map/ppermute | solution.py:542
  38.5 7.7 %collective-permute-start.12 = (bf16[16,4096]{1,0:T(8,128)(2,1)S(1)}, bf16[16,4096]{1,0:T(8,128)(2,1)S(1)}, u32[]{:S(2)}, u32[]{:S(2)}) collective-permute-start(bf16[16,4096]{1,0:T(8,128)(2,1)S(1)} %get-tuple-element.65), channel_id=1, source_target_pairs={{0,4},{1,5},{2,6},{3,7},{4,0},{5,1},{6,2},{7,3},{8,12},{9,13},{10,... | collective-permute-start | bytes 393224 | tf_op jit(solution)/shard_map/ppermute | solution.py:542
  39.8 7.4 %collective-permute-start.13 = (bf16[16,4096]{1,0:T(8,128)(2,1)S(1)}, bf16[16,4096]{1,0:T(8,128)(2,1)S(1)}, u32[]{:S(2)}, u32[]{:S(2)}) collective-permute-start(bf16[16,4096]{1,0:T(8,128)(2,1)S(1)} %get-tuple-element.66), channel_id=1, source_target_pairs={{0,6},{1,7},{2,4},{3,5},{4,2},{5,3},{6,0},{7,1},{8,14},{9,15},{10,... | collective-permute-start | bytes 393224 | tf_op jit(solution)/shard_map/ppermute | solution.py:542
  43.0 9.5 %collective-permute-start.7 = (bf16[8,3072]{1,0:T(8,128)(2,1)S(1)}, bf16[8,3072]{1,0:T(8,128)(2,1)S(1)}, u32[]{:S(2)}, u32[]{:S(2)}) collective-permute-start(bf16[8,3072]{1,0:T(8,128)(2,1)S(1)} %get-tuple-element.58), channel_id=1, source_target_pairs={{0,16},{1,17},{2,18},{3,19},{4,20},{5,21},{6,22},{7,23},{8,24},{9,... | collective-permute-start | bytes 147464 | tf_op jit(solution)/shard_map/ppermute | solution.py:542
  47.5 9.6 %collective-permute-start.14 = (bf16[8,4096]{1,0:T(8,128)(2,1)S(1)}, bf16[8,4096]{1,0:T(8,128)(2,1)S(1)}, u32[]{:S(2)}, u32[]{:S(2)}) collective-permute-start(bf16[8,4096]{1,0:T(8,128)(2,1)S(1)} %get-tuple-element.68), channel_id=1, source_target_pairs={{0,16},{1,17},{2,18},{3,19},{4,20},{5,21},{6,22},{7,23},{8,24},{9,... | collective-permute-start | bytes 196616 | tf_op jit(solution)/shard_map/ppermute | solution.py:542
  48.3 8.8 %collective-permute-start.15 = (bf16[8,4096]{1,0:T(8,128)(2,1)S(1)}, bf16[8,4096]{1,0:T(8,128)(2,1)S(1)}, u32[]{:S(2)}, u32[]{:S(2)}) collective-permute-start(bf16[8,4096]{1,0:T(8,128)(2,1)S(1)} %get-tuple-element.69), channel_id=1, source_target_pairs={{0,24},{1,25},{2,26},{3,27},{4,28},{5,29},{6,30},{7,31},{8,16},{9,... | collective-permute-start | bytes 196616 | tf_op jit(solution)/shard_map/ppermute | solution.py:542
  50.6 6.5 %collective-permute-start.16 = (bf16[8,4096]{1,0:T(8,128)(2,1)S(1)}, bf16[8,4096]{1,0:T(8,128)(2,1)S(1)}, u32[]{:S(2)}, u32[]{:S(2)}) collective-permute-start(bf16[8,4096]{1,0:T(8,128)(2,1)S(1)} %get-tuple-element.70), channel_id=1, source_target_pairs={{0,8},{1,9},{2,10},{3,11},{4,12},{5,13},{6,14},{7,15},{8,0},{9,1},... | collective-permute-start | bytes 196616 | tf_op jit(solution)/shard_map/ppermute | solution.py:542
  51.0 6.0 %collective-permute-start.8 = (bf16[8,3072]{1,0:T(8,128)(2,1)S(1)}, bf16[8,3072]{1,0:T(8,128)(2,1)S(1)}, u32[]{:S(2)}, u32[]{:S(2)}) collective-permute-start(bf16[8,3072]{1,0:T(8,128)(2,1)S(1)} %get-tuple-element.59), channel_id=1, source_target_pairs={{0,24},{1,25},{2,26},{3,27},{4,28},{5,29},{6,30},{7,31},{8,16},{9,... | collective-permute-start | bytes 147464 | tf_op jit(solution)/shard_map/ppermute | solution.py:542
  57.3 6.6 %collective-permute-start.19 = (bf16[8,7168]{1,0:T(8,128)(2,1)S(1)}, bf16[8,7168]{1,0:T(8,128)(2,1)S(1)}, u32[]{:S(2)}, u32[]{:S(2)}) collective-permute-start(bf16[8,7168]{1,0:T(8,128)(2,1)S(1)} %get-tuple-element.72.refs_0_), channel_id=1, source_target_pairs={{0,6},{1,7},{2,4},{3,5},{4,2},{5,3},{6,0},{7,1},{8,14},{9,15},{10,... | collective-permute-start | bytes 344072 | tf_op jit(solution)/shard_map/ppermute | solution.py:542
  59.0 5.6 %collective-permute-start.18 = (bf16[8,7168]{1,0:T(8,128)(2,1)S(1)}, bf16[8,7168]{1,0:T(8,128)(2,1)S(1)}, u32[]{:S(2)}, u32[]{:S(2)}) collective-permute-start(bf16[8,7168]{1,0:T(8,128)(2,1)S(1)} %get-tuple-element.72.refs_0_), channel_id=1, source_target_pairs={{0,4},{1,5},{2,6},{3,7},{4,0},{5,1},{6,2},{7,3},{8,12},{9,13},{10,... | collective-permute-start | bytes 344072 | tf_op jit(solution)/shard_map/ppermute | solution.py:542
  60.6 4.8 %collective-permute-start.17 = (bf16[8,7168]{1,0:T(8,128)(2,1)S(1)}, bf16[8,7168]{1,0:T(8,128)(2,1)S(1)}, u32[]{:S(2)}, u32[]{:S(2)}) collective-permute-start(bf16[8,7168]{1,0:T(8,128)(2,1)S(1)} %get-tuple-element.72.refs_0_), channel_id=1, source_target_pairs={{0,2},{1,3},{2,0},{3,1},{4,6},{5,7},{6,4},{7,5},{8,10},{9,11},{10,... | collective-permute-start | bytes 344072 | tf_op jit(solution)/shard_map/ppermute | solution.py:542
  69.7 5.3 %collective-permute-start.25 = (bf16[8,7168]{1,0:T(8,128)(2,1)S(1)}, bf16[8,7168]{1,0:T(8,128)(2,1)S(1)}, u32[]{:S(2)}, u32[]{:S(2)}) collective-permute-start(bf16[8,7168]{1,0:T(8,128)(2,1)S(1)} %get-tuple-element.78), channel_id=1, source_target_pairs={{0,2},{1,3},{2,0},{3,1},{4,6},{5,7},{6,4},{7,5},{8,10},{9,11},{10,... | collective-permute-start | bytes 344072 | tf_op jit(solution)/shard_map/ppermute | solution.py:542
  70.9 7.6 %collective-permute-start.26 = (bf16[8,7168]{1,0:T(8,128)(2,1)S(1)}, bf16[8,7168]{1,0:T(8,128)(2,1)S(1)}, u32[]{:S(2)}, u32[]{:S(2)}) collective-permute-start(bf16[8,7168]{1,0:T(8,128)(2,1)S(1)} %get-tuple-element.79), channel_id=1, source_target_pairs={{0,4},{1,5},{2,6},{3,7},{4,0},{5,1},{6,2},{7,3},{8,12},{9,13},{10,... | collective-permute-start | bytes 344072 | tf_op jit(solution)/shard_map/ppermute | solution.py:542
  72.0 6.5 %collective-permute-start.27 = (bf16[8,7168]{1,0:T(8,128)(2,1)S(1)}, bf16[8,7168]{1,0:T(8,128)(2,1)S(1)}, u32[]{:S(2)}, u32[]{:S(2)}) collective-permute-start(bf16[8,7168]{1,0:T(8,128)(2,1)S(1)} %get-tuple-element.80), channel_id=1, source_target_pairs={{0,6},{1,7},{2,4},{3,5},{4,2},{5,3},{6,0},{7,1},{8,14},{9,15},{10,... | collective-permute-start | bytes 344072 | tf_op jit(solution)/shard_map/ppermute | solution.py:542
  78.6 4.9 %collective-permute-start.28 = (bf16[2,7168]{1,0:T(2,128)(2,1)S(1)}, bf16[2,7168]{1,0:T(2,128)(2,1)S(1)}, u32[]{:S(2)}, u32[]{:S(2)}) collective-permute-start(bf16[2,7168]{1,0:T(2,128)(2,1)S(1)} %get-tuple-element.84), channel_id=1, source_target_pairs={{0,16},{1,17},{2,18},{3,19},{4,20},{5,21},{6,22},{7,23},{8,24},{9,... | collective-permute-start | bytes 86024 | tf_op jit(solution)/shard_map/ppermute | solution.py:542
  80.5 5.7 %collective-permute-start.29 = (bf16[2,7168]{1,0:T(2,128)(2,1)S(1)}, bf16[2,7168]{1,0:T(2,128)(2,1)S(1)}, u32[]{:S(2)}, u32[]{:S(2)}) collective-permute-start(bf16[2,7168]{1,0:T(2,128)(2,1)S(1)} %get-tuple-element.85), channel_id=1, source_target_pairs={{0,24},{1,25},{2,26},{3,27},{4,28},{5,29},{6,30},{7,31},{8,16},{9,... | collective-permute-start | bytes 86024 | tf_op jit(solution)/shard_map/ppermute | solution.py:542
  (13 other events, 85.9 us)
